TPU v7x, 32 devices: a whole 2x2x4 slice. The times are simulated.
32 devices in a mesh: space: 8 (over y, x, core), dp: 4 (over z).
Axes of the slice: x: 2, y: 2, z: 4, core: 2. Of those that a mesh axis runs over, the one named last changes fastest.
Arguments:
- volume: bfloat16 [4, 32, 96, 512], P('dp', 'space'), may hold values from -6 to 6
- neighbours: int32 [4, 32, 26], P('dp'), may hold values from -1 to 31, as said below
- active: int32 [4, 32], P('dp'), may hold values from 0 to 1, as said below
- cotangent: bfloat16 [4, 32, 96, 512], P('dp', 'space'), may hold values from -0.0234375 to 0.0234375
- weight_one: bfloat16 [96, 2592], replicated, may hold values from -0.125 to 0.125
- weight_two: bfloat16 [96, 2592], replicated, may hold values from -0.125 to 0.125
- bias_one: float32 [96], replicated, may hold values from -3 to 3
- bias_two: float32 [96], replicated, may hold values from -3 to 3
Outputs:
- output: bfloat16 [4, 32, 96, 512], P('dp', 'space')
- grad_weight_one: float32 [96, 2592], replicated
- grad_weight_two: float32 [96, 2592], replicated
- grad_bias_one: float32 [96], replicated
- grad_bias_two: float32 [96], replicated
Inputs may be any that keep to these rules, and one draw needn't show every extreme that they name: `neighbours`: each volume is a grid of 8 x 2 x 2 bricks; brick (l, y, z) sits in one slot, and slot g lies on space index g // 4. Entry k of a slot is the slot of the brick at the k-th offset, -1 where the offset leaves the grid. The bricks of brick layers 2m and 2m + 1 lie on space indices 2m and 2m + 1, one brick of each (y, z) on each of the two. `active`: the bricks on space indices 0 and 1 are all live.
All inputs are finite; a program needn't handle non-finite values.
Results may differ from a plain program's by a relative error of at most 0.0065.
Values may be sent and summed in bfloat16 or wider, within the bound.
No kernel may reach another device: no remote copies, remote signals or barrier semaphores. Data moves between devices by JAX's collectives and lax.ppermute only.
A program may use at most 128 MiB of HBM per device.

v0:
```python
import jax
import jax.numpy as jnp
import numpy as np
from jax import lax
from jax.experimental import pallas as pl
from jax.experimental.pallas import tpu as pltpu
from jax.sharding import PartitionSpec as P

EDGE = 8
PLANE = 256
CELLS = 512
KDIM = 896
TILES = 21
ROWS = 2048
NEAR_DOWN, NEAR_Y, NEAR_Z, NEAR_UP = 4, 10, 12, 21
F32 = jnp.float32
BF16 = jnp.bfloat16


def spread_matrix():
    move = np.zeros((256, 256), np.float32)
    for z in range(2):
        for p in range(2):
            for q in range(8):
                for r in range(8):
                    move[z * 128 + p * 64 + q * 8 + r, p * 128 + q * 16 + z * 8 + r] = 1.0
    return move


def tap_masks():
    masks = np.zeros((9, 16, 256), np.float32)
    for b in range(3):
        for c in range(3):
            for q in range(16):
                for r in range(16):
                    inside = 0 <= q + b - 1 < 16 and 0 <= r + c - 1 < 16
                    masks[b * 3 + c, :, q * 16 + r] = float(inside)
    return masks


def write_taps(dst, plane, masks_ref):
    channels = plane.shape[0]
    wide = plane.astype(F32)
    for k in range(9):
        step = (k // 3 - 1) * 16 + (k % 3 - 1)
        if step == 0:
            moved = plane
        else:
            moved = pltpu.roll(wide, (-step) % PLANE, 1).astype(BF16)
            moved = moved * jnp.concatenate([masks_ref[k]] * (channels // 16), axis=0)
        dst[k * channels : (k + 1) * channels, :] = moved


def slot_place(near_ref, slot, pair_slots):
    shift = pair_slots.bit_length() - 1
    up = near_ref[slot, NEAR_UP]
    inside = jnp.logical_and(up >= 0, up >> shift == slot >> shift)
    parity = jnp.where(inside, 0, 1)
    column = jnp.where(near_ref[slot, NEAR_Y] >= 0, 2, 0) + jnp.where(
        near_ref[slot, NEAR_Z] >= 0, 1, 0
    )
    return parity, column


def lane_mask(scalars):
    lane = lax.broadcasted_iota(jnp.int32, (8, PLANE), 1)
    high_y = lane >= 128
    high_z = (lane & 8) != 0
    s = [jnp.full((8, PLANE), v, F32) for v in scalars]
    return jnp.where(high_y, jnp.where(high_z, s[3], s[2]), jnp.where(high_z, s[1], s[0]))


def plane_product(weight_ref, taps):
    return jnp.dot(weight_ref[...], taps, preferred_element_type=F32)


def add_planes(acc, at, product, channels):
    acc[at + 1] = product[:channels]
    acc[at] = acc[at] + product[channels : 2 * channels]
    acc[at - 1] = acc[at - 1] + product[2 * channels :]


def weight_products(total, grads, taps, first_grad, first_tap, pairs):
    for j in range(0, 2 * pairs, 2):
        left = jnp.concatenate([grads[first_grad + j], grads[first_grad + j + 1]], axis=1)
        right = jnp.concatenate([taps[first_tap + j], taps[first_tap + j + 1]], axis=1)
        part = lax.dot_general(left, right, (((1,), (1,)), ((), ())), preferred_element_type=F32)
        total[...] = part if j == 0 else total[...] + part


def write_tiles(flat, total, channels):
    lane = lax.broadcasted_iota(jnp.int32, (channels, 128), 1)
    blank = jnp.zeros((channels, 128), F32)
    first = total[:channels, :]
    second = jnp.concatenate([total[channels : 2 * channels, :], blank], axis=1)
    third = jnp.concatenate([total[2 * channels :, :], blank], axis=1)
    second = pltpu.roll(second, 96, 1)
    third = pltpu.roll(third, 64, 1)

    def cut(value, k):
        return value[:, k * 128 : (k + 1) * 128]

    tiles = [cut(first, k) for k in range(6)]
    tiles.append(jnp.where(lane < 96, cut(first, 6), cut(second, 0)))
    tiles += [cut(second, k) for k in range(1, 7)]
    tiles.append(jnp.where(lane < 64, cut(second, 7), cut(third, 0)))
    tiles += [cut(third, k) for k in range(1, 8)]
    for k in range(TILES):
        flat[k * channels : (k + 1) * channels, :] = tiles[k]
    flat[TILES * channels :, :] = jnp.zeros((ROWS - TILES * channels, 128), F32)


def split_tiles(keep_ref, send_ref, flat, me):
    chips, rows = keep_ref.shape[0], keep_ref.shape[1]
    core, chip = me & 1, me >> 1
    for r in range(chips):
        at = jnp.clip(chip ^ r, 0, chips - 1) * rows
        here = at + jnp.where(core == 1, chips * rows, 0)
        there = at + jnp.where(core == 1, 0, chips * rows)
        keep_ref[r] = flat[pl.ds(pl.multiple_of(here, rows), rows), :]
        send_ref[r] = flat[pl.ds(pl.multiple_of(there, rows), rows), :]


def layout_kernel(
    me_ref, near_ref, active_ref, own_ref, pair_ref, cot_own_ref, cot_pair_ref, move_ref,
    x_ref, cot_ref, edge_ref, mask_ref, bricks, cots,
):
    slots, channels = own_ref.shape[0], own_ref.shape[1]
    all_slots = near_ref.shape[0]
    me = jnp.clip(me_ref[0], 0, all_slots // slots - 1)
    core = me & 1
    even = core == 0

    live = [[jnp.float32(0)] * 4 for _ in range(2)]
    beyond = [jnp.float32(0)] * 4
    for device, source, cot_source in (
        (me, own_ref, cot_own_ref), (me ^ 1, pair_ref, cot_pair_ref),
    ):
        for s in range(slots):
            slot = jnp.clip(device * slots + s, 0, all_slots - 1)
            parity, column = slot_place(near_ref, slot, 2 * slots)
            alive = active_ref[slot].astype(F32)
            scale = jnp.full((channels, CELLS), alive, F32).astype(BF16)
            bricks[parity, column] = source[s] * scale
            cots[parity, column] = cot_source[s] * scale
            outer = jnp.where(even, near_ref[slot, NEAR_DOWN], near_ref[slot, NEAR_UP])
            alive_outer = active_ref[jnp.clip(outer, 0, all_slots - 1)].astype(F32)
            alive_outer = jnp.where(outer >= 0, alive_outer, 0.0)
            for k in range(4):
                for p in range(2):
                    here = jnp.logical_and(parity == p, column == k)
                    live[p][k] = jnp.where(here, alive, live[p][k])
                here = jnp.logical_and(parity == core, column == k)
                beyond[k] = jnp.where(here, alive_outer, beyond[k])
    inner = [jnp.where(even, live[1][k], live[0][k]) for k in range(4)]
    mask_ref[0] = lane_mask([jnp.where(even, beyond[k], inner[k]) for k in range(4)])
    mask_ref[1] = lane_mask([jnp.where(even, live[0][k], live[1][k]) for k in range(4)])
    mask_ref[2] = lane_mask([jnp.where(even, inner[k], beyond[k]) for k in range(4)])

    move = move_ref[...]
    mine = jnp.where(even, 0, 1)

    def spread(left, right):
        two = jnp.concatenate([left, right], axis=1)
        return jnp.dot(two, move, preferred_element_type=F32).astype(BF16)

    for y in range(2):
        row = slice(y * 128, (y + 1) * 128)
        for j in range(4):
            pair = slice(j * 128, (j + 1) * 128)
            both = spread(bricks[mine, 2 * y, :, pair], bricks[mine, 2 * y + 1, :, pair])
            x_ref[4 + 2 * j, :, row] = both[:, :128]
            x_ref[5 + 2 * j, :, row] = both[:, 128:]
            both = spread(cots[mine, 2 * y, :, pair], cots[mine, 2 * y + 1, :, pair])
            cot_ref[1 + 2 * j, :, row] = both[:, :128]
            cot_ref[2 + 2 * j, :, row] = both[:, 128:]
        inner_at = jnp.where(even, 12, 0)
        for j in range(2):
            start = pl.multiple_of(jnp.where(even, j * 128, 256 + j * 128), 128)
            pair = pl.ds(start, 128)
            both = spread(
                bricks[1 - mine, 2 * y, :, pair], bricks[1 - mine, 2 * y + 1, :, pair]
            )
            x_ref[inner_at + 2 * j, :, row] = both[:, :128]
            x_ref[inner_at + 2 * j + 1, :, row] = both[:, 128:]
        pair = pl.ds(pl.multiple_of(jnp.where(even, 0, 384), 128), 128)
        both = spread(cots[1 - mine, 2 * y, :, pair], cots[1 - mine, 2 * y + 1, :, pair])

        @pl.when(even)
        def _(both=both, row=row):
            cot_ref[9, :, row] = both[:, :128]

        @pl.when(core == 1)
        def _(both=both, row=row):
            cot_ref[0, :, row] = both[:, 128:]

    edge_ref[:3] = x_ref[pl.ds(jnp.where(even, 4, 9), 3)]
    edge_ref[3] = cot_ref[jnp.where(even, 1, 8)]


def forward_kernel(
    me_ref, near_ref, x_in_ref, cot_in_ref, outer_ref, layer_mask, w1_ref, w2_ref, b1_ref, b2_ref,
    back_ref, masks_ref,
    keep_ref, send_ref, grad_keep_ref, grad_send_ref, g_ref, slope_ref, x_ref,
    bricks, planes, cot_planes, xc, hc, acc_one, acc_two, outs, gs, total, flat,
):
    slots, channels = keep_ref.shape[0], keep_ref.shape[1]
    me = jnp.clip(me_ref[0], 0, near_ref.shape[0] // slots - 1)
    core = me & 1
    even = core == 0
    planes[...] = x_in_ref[...]
    cot_planes[...] = cot_in_ref[...]
    planes[pl.ds(jnp.where(even, 1, 12), 3)] = outer_ref[:3]
    cot_planes[jnp.where(even, 0, 9)] = outer_ref[3]
    bias_one = jnp.broadcast_to(b1_ref[...], (8, channels)).T[:, :1]
    bias_two = jnp.broadcast_to(b2_ref[...], (8, channels)).T[:, :1]
    x_ref[...] = planes[3:13]

    ones = jnp.ones((KDIM - 9 * channels, PLANE), BF16)
    for k in range(2):
        xc[k, 9 * channels :, :] = ones
    for k in range(12):
        hc[k, 9 * channels :, :] = ones
    gs[1, 2 * channels :, :] = jnp.zeros((channels, PLANE), BF16)
    gs[10, :channels, :] = jnp.zeros((channels, PLANE), BF16)

    def which_layer(q):
        return 0 if q < 0 else 1 if q < EDGE else 2

    def finish_one(q):
        pre = acc_one[q + 4] + bias_one
        mask = layer_mask[which_layer(q)][:1]
        sigma = jax.nn.sigmoid(pre)
        slope_ref[q + 2] = sigma * (1.0 + pre * (1.0 - sigma)) * mask
        hidden = (pre * sigma * mask).astype(BF16)
        write_taps(hc.at[q + 2], hidden, masks_ref)

    def step_one(p, finish):
        now = (p + 3) & 1
        product = plane_product(w1_ref, xc[now])
        write_taps(xc.at[1 - now], planes[p + 5], masks_ref)
        if finish:
            finish_one(p - 2)
        add_planes(acc_one, p + 4, product, channels)

    write_taps(xc.at[0], planes[1], masks_ref)
    for p in range(-3, 0):
        step_one(p, False)
    for p in range(0, 11):
        step_one(p, True)
    finish_one(9)

    def finish_two(q):
        pre = acc_two[q + 3] + bias_two
        sigma = jax.nn.sigmoid(pre)
        outs[q + 1] = (pre * sigma * layer_mask[which_layer(q)][:1]).astype(BF16)
        grad = cot_planes[q + 1].astype(F32) * (sigma * (1.0 + pre * (1.0 - sigma)))
        g_ref[q + 1] = grad.astype(BF16)
        kept = grad.astype(BF16)
        if not 0 <= q < EDGE:
            kept = jnp.zeros_like(kept)
        gs[q + 1, :channels, :] = kept
        gs[q + 2, channels : 2 * channels, :] = kept
        gs[q + 3, 2 * channels :, :] = kept

    def step_two(p, finish):
        product = plane_product(w2_ref, hc[p + 2])
        if finish:
            finish_two(p - 2)
        add_planes(acc_two, p + 3, product, channels)

    for p in range(-2, 1):
        step_two(p, False)
    for p in range(1, 10):
        step_two(p, True)
    finish_two(8)

    weight_products(total, gs, hc, 1, 1, 5)
    write_tiles(flat, total, channels)
    split_tiles(grad_keep_ref, grad_send_ref, flat, me)

    back = back_ref[...]
    for y in range(2):
        row = slice(y * 128, (y + 1) * 128)
        for j in range(4):
            two = jnp.concatenate([outs[1 + 2 * j, :, row], outs[2 + 2 * j, :, row]], axis=1)
            both = jnp.dot(two, back, preferred_element_type=F32).astype(BF16)
            pair = slice(j * 128, (j + 1) * 128)
            bricks[2 * y, :, pair] = both[:, :128]
            bricks[2 * y + 1, :, pair] = both[:, 128:]
    for target, device in ((keep_ref, me), (send_ref, me ^ 1)):
        for s in range(slots):
            slot = jnp.clip(device * slots + s, 0, near_ref.shape[0] - 1)
            parity, column = slot_place(near_ref, slot, 2 * slots)
            scale = jnp.where(parity == core, 1.0, 0.0)
            target[s] = bricks[column] * jnp.full((channels, CELLS), scale, F32).astype(BF16)


def backward_kernel(
    me_ref, g_ref, slope_ref, x_ref, w2t_ref, masks_ref, grad_keep_ref, grad_send_ref,
    gc, xc, acc, gs, total, flat,
):
    channels = g_ref.shape[1]
    blank = jnp.zeros((channels, PLANE), BF16)
    ones = jnp.ones((KDIM - 9 * channels, PLANE), BF16)
    for k in range(2):
        gc[k, 9 * channels :, :] = ones
    for k in range(10):
        xc[k, 9 * channels :, :] = ones
    for at, a in ((1, 1), (1, 2), (2, 2), (9, 0), (10, 0), (10, 1)):
        gs[at, a * channels : (a + 1) * channels, :] = blank

    def finish(q):
        grad = (acc[q + 2] * slope_ref[q + 2]).astype(BF16)
        gs[q + 1, :channels, :] = grad
        gs[q + 2, channels : 2 * channels, :] = grad
        gs[q + 3, 2 * channels :, :] = grad

    def step(p, done):
        now = (p + 1) & 1
        product = plane_product(w2t_ref, gc[now])
        write_taps(gc.at[1 - now], g_ref[min(p + 2, 9)], masks_ref)
        write_taps(xc.at[p + 1], x_ref[p + 1], masks_ref)
        if done:
            finish(p - 2)
        add_planes(acc, p + 2, product, channels)

    write_taps(gc.at[0], g_ref[0], masks_ref)
    for p in range(-1, 2):
        step(p, False)
    for p in range(2, 9):
        step(p, True)
    finish(7)
    weight_products(total, gs, xc, 1, 0, 5)
    write_tiles(flat, total, channels)
    split_tiles(grad_keep_ref, grad_send_ref, flat, jnp.clip(me_ref[0], 0, 2**15))


def gather_kernel(me_ref, *refs):
    chips = (len(refs) - 5) // 2
    w_one_ref, w_two_ref, b_one_ref, b_two_ref, flat = refs[2 * chips :]
    rows = refs[0].shape[1]
    channels = w_one_ref.shape[0]
    me = jnp.clip(me_ref[0], 0, 2 * chips - 1)
    core, chip = me & 1, me >> 1
    for half in range(2):
        base = jnp.where(core == half, 0, chips * rows)
        for r in range(chips):
            at = base + jnp.clip(chip ^ r, 0, chips - 1) * rows
            flat[:, pl.ds(pl.multiple_of(at, rows), rows), :] = refs[half * chips + r][...]
    for n, (weight, bias) in enumerate(((w_one_ref, b_one_ref), (w_two_ref, b_two_ref))):
        for k in range(TILES - 1):
            tile = flat[n, k * channels : (k + 1) * channels, :]
            weight[:, k * 128 : (k + 1) * 128] = tile.astype(F32)
        last = flat[n, (TILES - 1) * channels : TILES * channels, :].astype(F32)
        weight[:, 2560:2592] = last[:, :32]
        bias[...] = last.T[32:33, :]


VMEM = pl.BlockSpec(memory_space=pltpu.VMEM)
SMEM = pl.BlockSpec(memory_space=pltpu.SMEM)


def vmem(mebibytes):
    return pltpu.CompilerParams(vmem_limit_bytes=mebibytes * 2**20)


def shared_sum(keeps, sends, send_two_done):
    chips = keeps[0].shape[0]
    count = 2 * chips
    volumes = lax.axis_size("dp")
    swap = [(d, d ^ 1) for d in range(count)]
    halves = [keeps[0] + lax.ppermute(sends[0], "space", swap)]
    halves.append(keeps[1] + send_two_done)
    total = jnp.stack([half[0] for half in halves])
    for r in range(chips - 1, 0, -1):
        part = jnp.stack([half[r] for half in halves]).astype(BF16)
        hop = [(d, d ^ (2 * r)) for d in range(count)]
        total = total + lax.ppermute(part, "space", hop).astype(F32)
    total = total.astype(BF16)
    step = 1
    while step < volumes:
        hop = [(d, d ^ step) for d in range(volumes)]
        moved = lax.ppermute(total, "dp", hop)
        total = (total.astype(F32) + moved.astype(F32)).astype(BF16)
        step *= 2
    parts = [total]
    for r in range(chips - 1, 0, -1):
        parts.insert(1, lax.ppermute(total, "space", [(d, d ^ (2 * r)) for d in range(count)]))
    return parts + [lax.ppermute(part, "space", swap) for part in parts]


def local(volume, neighbours, active, cotangent, weight_one, weight_two, bias_one, bias_two):
    volume, cotangent = volume[0], cotangent[0]
    slots, channels = volume.shape[0], volume.shape[1]
    near = neighbours[0]
    count = lax.axis_size("space")
    chips = count // 2
    me = lax.axis_index("space").astype(jnp.int32)[None]

    swap = [(d, d ^ 1) for d in range(count)]
    hop = [(d, d + 1) for d in range(1, count - 1, 2)] + [(d, d - 1) for d in range(2, count, 2)]
    pair_volume = lax.ppermute(volume, "space", swap)
    pair_cot = lax.ppermute(cotangent, "space", swap)

    def by_plane(weight):
        weight = weight.reshape(channels, 3, 9 * channels).transpose(1, 0, 2)
        weight = weight.reshape(3 * channels, 9 * channels)
        return jnp.pad(weight, ((0, 0), (0, KDIM - 9 * channels)))

    w1 = by_plane(weight_one)
    w2 = by_plane(weight_two)
    w2t = weight_two.reshape(channels, 3, 3, 3, channels)[:, ::-1, ::-1, ::-1]
    w2t = w2t.transpose(1, 4, 2, 3, 0).reshape(3 * channels, 9 * channels)
    w2t = jnp.pad(w2t, ((0, 0), (0, KDIM - 9 * channels)))
    move = spread_matrix()
    masks = jnp.asarray(tap_masks(), BF16)

    def planes(number, dtype=BF16):
        return jax.ShapeDtypeStruct((number, channels, PLANE), dtype)

    bricks = (slots, channels, CELLS)
    x_planes, cot_planes, edge, layer_mask = pl.pallas_call(
        layout_kernel,
        out_shape=(planes(16), planes(10), planes(4), jax.ShapeDtypeStruct((3, 8, PLANE), F32)),
        in_specs=[SMEM] * 3 + [VMEM] * 5,
        out_specs=(VMEM,) * 4,
        scratch_shapes=[pltpu.VMEM((2, *bricks), BF16), pltpu.VMEM((2, *bricks), BF16)],
        compiler_params=vmem(8),
        name="layout",
    )(me, near, active[0], volume, pair_volume, cotangent, pair_cot, jnp.asarray(move, BF16))
    outer = lax.ppermute(edge, "space", hop)

    half = (chips, ROWS // count, 128)
    keep, send, keep_two, send_two, grad_out, slope, x_inner = pl.pallas_call(
        forward_kernel,
        out_shape=(
            jax.ShapeDtypeStruct(bricks, BF16),
            jax.ShapeDtypeStruct(bricks, BF16),
            jax.ShapeDtypeStruct(half, F32),
            jax.ShapeDtypeStruct(half, F32),
            planes(10),
            planes(12, F32),
            planes(10),
        ),
        in_specs=[SMEM] * 2 + [VMEM] * 10,
        out_specs=(VMEM,) * 7,
        scratch_shapes=[
            pltpu.VMEM(bricks, BF16),
            pltpu.VMEM((16, channels, PLANE), BF16),
            pltpu.VMEM((10, channels, PLANE), BF16),
            pltpu.VMEM((2, KDIM, PLANE), BF16),
            pltpu.VMEM((12, KDIM, PLANE), BF16),
            pltpu.VMEM((16, channels, PLANE), F32),
            pltpu.VMEM((14, channels, PLANE), F32),
            pltpu.VMEM((10, channels, PLANE), BF16),
            pltpu.VMEM((12, 3 * channels, PLANE), BF16),
            pltpu.VMEM((3 * channels, KDIM), F32),
            pltpu.VMEM((ROWS, 128), F32),
        ],
        compiler_params=vmem(26),
        cost_estimate=pl.CostEstimate(flops=2**33, bytes_accessed=2**23, transcendentals=2**20),
        name="forward",
    )(
        me, near, x_planes, cot_planes, outer, layer_mask, w1, w2, bias_one[None], bias_two[None],
        jnp.asarray(move.T, BF16), masks,
    )
    got_two = lax.ppermute(send_two, "space", swap)
    keep_one, send_one = pl.pallas_call(
        backward_kernel,
        out_shape=(jax.ShapeDtypeStruct(half, F32), jax.ShapeDtypeStruct(half, F32)),
        in_specs=[SMEM] + [VMEM] * 5,
        out_specs=(VMEM,) * 2,
        scratch_shapes=[
            pltpu.VMEM((2, KDIM, PLANE), BF16),
            pltpu.VMEM((10, KDIM, PLANE), BF16),
            pltpu.VMEM((12, channels, PLANE), F32),
            pltpu.VMEM((12, 3 * channels, PLANE), BF16),
            pltpu.VMEM((3 * channels, KDIM), F32),
            pltpu.VMEM((ROWS, 128), F32),
        ],
        compiler_params=vmem(22),
        cost_estimate=pl.CostEstimate(flops=2**32, bytes_accessed=2**22, transcendentals=0),
        name="backward",
    )(me, grad_out, slope, x_inner, w2t, masks)

    output = (keep + lax.ppermute(send, "space", swap))[None]
    parts = shared_sum([keep_one, keep_two], [send_one, send_two], got_two)
    weight_shape = jax.ShapeDtypeStruct((channels, 27 * channels), F32)
    bias_shape = jax.ShapeDtypeStruct((1, channels), F32)
    total_w_one, total_w_two, total_b_one, total_b_two = pl.pallas_call(
        gather_kernel,
        out_shape=(weight_shape, weight_shape, bias_shape, bias_shape),
        in_specs=[SMEM] + [VMEM] * len(parts),
        out_specs=(VMEM,) * 4,
        scratch_shapes=[pltpu.VMEM((2, ROWS, 128), BF16)],
        compiler_params=vmem(8),
        name="gather",
    )(me, *parts)
    return (output, total_w_one, total_w_two, total_b_one[0], total_b_two[0])


def solution(mesh):
    in_specs = (
        P("dp", "space", None, None),
        P("dp", None, None),
        P("dp", None),
        P("dp", "space", None, None),
        P(),
        P(),
        P(),
        P(),
    )
    out_specs = (P("dp", "space", None, None), P(), P(), P(), P())
    return jax.shard_map(local, mesh=mesh, in_specs=in_specs, out_specs=out_specs, check_vma=False)
```

profile of v0, /device:TPU:0, one launch (start us, length us, event | category | flops | bytes accessed | tf_op | source)
XLA Modules:
  0.0 75.2 jit_solution(15708261232961710693)
XLA Ops:
  3.3 1.0 %copy-done = bf16[1,4,96,512]{3,2,1,0:T(8,128)(2,1)S(1)} copy-done((bf16[1,4,96,512]{3,2,1,0:T(8,128)(2,1)S(1)}, bf16[1,4,96,512]{3,2,1,0:T(8,128)(2,1)}, u32[]{:S(2)}) %copy-start) | copy-done | bytes 393240
  6.8 1.8 %layout.1 = (bf16[16,96,256]{2,1,0:T(8,128)(2,1)S(1)}, bf16[10,96,256]{2,1,0:T(8,128)(2,1)S(1)}, bf16[4,96,256]{2,1,0:T(8,128)(2,1)S(1)}, f32[3,8,256]{2,1,0:T(8,128)S(1)}) custom-call(s32[1]{0:T(128)} %bitcast.me_ref, s32[32,26]{1,0:T(8,128)S(1)} %bitcast.22, s32[32]{0:T(128)S(1)} %bitcast.24, bf16[4,96,512]{2,1,0:T(8,128)(2,1)S(1)} %bitcast.19, ...), custom_call_target="tpu_custom_call" | custom-call | tf_op jit(solution)/shard_map/layout/pallas_call | solution.py:423
  9.9 1.1 %copy.23 = bf16[96,2592]{0,1:T(8,128)(2,1)} copy(bf16[96,2592]{1,0:T(8,128)(2,1)S(1)} %copy-done.9) | data formatting | bytes 995328 | tf_op args[5]
  11.0 1.2 %reshape.28 = bf16[96,3,864]{2,1,0:T(4,128)(2,1)} reshape(bf16[96,2592]{1,0:T(8,128)(2,1)S(1)} %copy-done.10) | data formatting | bytes 995328 | tf_op jit(solution)/shard_map/reshape | solution.py:407
  12.3 1.2 %copy.21 = bf16[3,96,864]{2,1,0:T(8,128)(2,1)S(1)} copy(bf16[3,96,864]{2,0,1:T(4,128)(2,1)} %bitcast.28) | data formatting | bytes 995328 | tf_op jit(solution)/shard_map/transpose | solution.py:407
  14.6 1.4 %copy.24 = bf16[3,96,3,3,96]{4,3,2,1,0:T(4,128)(2,1)} copy(bf16[3,96,3,3,96]{4,1,3,2,0:T(8,128)(2,1)S(1)} %reverse_bitcast_fusion) | data formatting | bytes 995328 | tf_op jit(solution)/shard_map/transpose | solution.py:414
  16.0 2.5 %reshape.33 = bf16[288,864]{1,0:T(8,128)(2,1)S(1)} reshape(bf16[3,96,3,3,96]{4,3,2,1,0:T(4,128)(2,1)} %copy.24) | data formatting | bytes 995328 | tf_op jit(solution)/shard_map/reshape | solution.py:414
  18.6 10.2 %forward.1 = (bf16[4,96,512]{2,1,0:T(8,128)(2,1)S(1)}, bf16[4,96,512]{2,1,0:T(8,128)(2,1)S(1)}, f32[4,256,128]{2,1,0:T(8,128)S(1)}, f32[4,256,128]{2,1,0:T(8,128...) custom-call(s32[1]{0:T(128)} %bitcast.me_ref, ...), custom_call_target="tpu_custom_call" | custom-call | flops 8589934592 | bytes 8388608 | tf_op jit(solution)/shard_map/forward/pallas_call | solution.py:435
  28.8 4.7 %backward.1 = (f32[4,256,128]{2,1,0:T(8,128)S(1)}, f32[4,256,128]{2,1,0:T(8,128)S(1)}) custom-call(s32[1]{0:T(128)} %bitcast.me_ref, bf16[10,96,256]{2,1,0:T(8,128)(2,1)S(1)} %get-tuple-element.28.g_ref, f32[12,96,256]{2,1,0:T(8,128)S(1)} %get-tuple-element.29.slope_ref, bf16[10,96,256]{2,1,0:T(8,128)(2,1)S(1)} %get-tuple-element.30.x_ref, ...), custom_call_target="tpu_custom_call" | custom-call | flops 4294967296 | bytes 4194304 | tf_op jit(solution)/shard_map/backward/pallas_call | solution.py:469
  33.5 4.3 %collective-permute-start.4 = (f32[4,256,128]{2,1,0:T(8,128)S(1)}, f32[4,256,128]{2,1,0:T(8,128)S(1)}, u32[]{:S(2)}, u32[]{:S(2)}) collective-permute-start(f32[4,256,128]{2,1,0:T(8,128)S(1)} %get-tuple-element.32), channel_id=1, source_target_pairs={{0,4},{4,0},{8,12},{12,8},{16,20},{20,16},{24,28},{28,24},{1,5},{5... | collective-permute-start | bytes 1572872 | tf_op jit(solution)/shard_map/ppermute | solution.py:373
  37.9 1.5 %collective-permute-done.4 = f32[4,256,128]{2,1,0:T(8,128)S(1)} collective-permute-done((f32[4,256,128]{2,1,0:T(8,128)S(1)}, f32[4,256,128]{2,1,0:T(8,128)S(1)}, u32[]{:S(2)}, u32[]{:S(2)}) %collective-permute-start.4) | collective-permute-done | bytes 524320 | tf_op jit(solution)/shard_map/ppermute | solution.py:373
  40.2 1.6 %collective-permute-start.6 = (bf16[2,256,128]{2,1,0:T(8,128)(2,1)S(1)}, bf16[2,256,128]{2,1,0:T(8,128)(2,1)S(1)}, u32[]{:S(2)}, u32[]{:S(2)}) collective-permute-start(bf16[2,256,128]{2,1,0:T(8,128)(2,1)S(1)} %pad_maximum_fusion), channel_id=1, source_target_pairs={{0,24},{4,28},{8,16},{12,20},{16,8},{20,12},{24,0},{28,4},{1,25},{... | collective-permute-start | bytes 393224 | tf_op jit(solution)/shard_map/ppermute | solution.py:379
  41.8 1.5 %collective-permute-start.7 = (bf16[2,256,128]{2,1,0:T(8,128)(2,1)S(1)}, bf16[2,256,128]{2,1,0:T(8,128)(2,1)S(1)}, u32[]{:S(2)}, u32[]{:S(2)}) collective-permute-start(bf16[2,256,128]{2,1,0:T(8,128)(2,1)S(1)} %pad_maximum_fusion.1), channel_id=1, source_target_pairs={{0,16},{4,20},{8,24},{12,28},{16,0},{20,4},{24,8},{28,12},{1,17},{... | collective-permute-start | bytes 393224 | tf_op jit(solution)/shard_map/ppermute | solution.py:379
  44.0 3.6 %collective-permute-done.6 = bf16[2,256,128]{2,1,0:T(8,128)(2,1)S(1)} collective-permute-done((bf16[2,256,128]{2,1,0:T(8,128)(2,1)S(1)}, bf16[2,256,128]{2,1,0:T(8,128)(2,1)S(1)}, u32[]{:S(2)}, u32[]{:S(2)}) %collective-permute-start.6) | collective-permute-done | bytes 131104 | tf_op jit(solution)/shard_map/ppermute | solution.py:379
  47.6 2.2 %collective-permute-done.7 = bf16[2,256,128]{2,1,0:T(8,128)(2,1)S(1)} collective-permute-done((bf16[2,256,128]{2,1,0:T(8,128)(2,1)S(1)}, bf16[2,256,128]{2,1,0:T(8,128)(2,1)S(1)}, u32[]{:S(2)}, u32[]{:S(2)}) %collective-permute-start.7) | collective-permute-done | bytes 131104 | tf_op jit(solution)/shard_map/ppermute | solution.py:379
  50.0 1.6 %collective-permute-start.9 = (bf16[2,256,128]{2,1,0:T(8,128)(2,1)S(1)}, bf16[2,256,128]{2,1,0:T(8,128)(2,1)S(1)}, u32[]{:S(2)}, u32[]{:S(2)}) collective-permute-start(bf16[2,256,128]{2,1,0:T(8,128)(2,1)S(1)} %fusion.2), channel_id=1, source_target_pairs={{0,1},{1,0},{2,3},{3,2},{4,5},{5,4},{6,7},{7,6},{8,9},{9,8},{10,11... | collective-permute-start | bytes 393224 | tf_op jit(solution)/shard_map/ppermute | solution.py:384
  51.6 3.7 %collective-permute-done.9 = bf16[2,256,128]{2,1,0:T(8,128)(2,1)S(1)} collective-permute-done((bf16[2,256,128]{2,1,0:T(8,128)(2,1)S(1)}, bf16[2,256,128]{2,1,0:T(8,128)(2,1)S(1)}, u32[]{:S(2)}, u32[]{:S(2)}) %collective-permute-start.9) | collective-permute-done | bytes 131104 | tf_op jit(solution)/shard_map/ppermute | solution.py:384
  55.4 2.7 %collective-permute-start.10 = (bf16[2,256,128]{2,1,0:T(8,128)(2,1)S(1)}, bf16[2,256,128]{2,1,0:T(8,128)(2,1)S(1)}, u32[]{:S(2)}, u32[]{:S(2)}) collective-permute-start(bf16[2,256,128]{2,1,0:T(8,128)(2,1)S(1)} %add_convert_fusion.1), channel_id=1, source_target_pairs={{0,2},{1,3},{2,0},{3,1},{4,6},{5,7},{6,4},{7,5},{8,10},{9,11},{10,... | collective-permute-start | bytes 393224 | tf_op jit(solution)/shard_map/ppermute | solution.py:384
  58.1 5.6 %collective-permute-done.10 = bf16[2,256,128]{2,1,0:T(8,128)(2,1)S(1)} collective-permute-done((bf16[2,256,128]{2,1,0:T(8,128)(2,1)S(1)}, bf16[2,256,128]{2,1,0:T(8,128)(2,1)S(1)}, u32[]{:S(2)}, u32[]{:S(2)}) %collective-permute-start.10) | collective-permute-done | bytes 131104 | tf_op jit(solution)/shard_map/ppermute | solution.py:384
  63.7 1.7 %collective-permute-start.11 = (bf16[2,256,128]{2,1,0:T(8,128)(2,1)S(1)}, bf16[2,256,128]{2,1,0:T(8,128)(2,1)S(1)}, u32[]{:S(2)}, u32[]{:S(2)}) collective-permute-start(bf16[2,256,128]{2,1,0:T(8,128)(2,1)S(1)} %add_convert_fusion.refs_0_), channel_id=1, source_target_pairs={{0,8},{4,12},{8,0},{12,4},{16,24},{20,28},{24,16},{28,20},{1,9},{5... | collective-permute-start | bytes 393224 | tf_op jit(solution)/shard_map/ppermute | solution.py:389
  65.5 1.8 %collective-permute-start.13 = (bf16[2,256,128]{2,1,0:T(8,128)(2,1)S(1)}, bf16[2,256,128]{2,1,0:T(8,128)(2,1)S(1)}, u32[]{:S(2)}, u32[]{:S(2)}) collective-permute-start(bf16[2,256,128]{2,1,0:T(8,128)(2,1)S(1)} %add_convert_fusion.refs_0_), channel_id=1, source_target_pairs={{0,24},{4,28},{8,16},{12,20},{16,8},{20,12},{24,0},{28,4},{1,25},{... | collective-permute-start | bytes 393224 | tf_op jit(solution)/shard_map/ppermute | solution.py:389
  67.2 2.4 %collective-permute-done.11.refs_1_ = bf16[2,256,128]{2,1,0:T(8,128)(2,1)S(1)} collective-permute-done((bf16[2,256,128]{2,1,0:T(8,128)(2,1)S(1)}, bf16[2,256,128]{2,1,0:T(8,128)(2,1)S(1)}, u32[]{:S(2)}, u32[]{:S(2)}) %collective-permute-start.11) | collective-permute-done | bytes 131104 | tf_op jit(solution)/shard_map/ppermute | solution.py:389
  69.7 2.6 %collective-permute-done.12.refs_2_ = bf16[2,256,128]{2,1,0:T(8,128)(2,1)S(1)} collective-permute-done((bf16[2,256,128]{2,1,0:T(8,128)(2,1)S(1)}, bf16[2,256,128]{2,1,0:T(8,128)(2,1)S(1)}, u32[]{:S(2)}, u32[]{:S(2)}) %collective-permute-start.12) | collective-permute-done | bytes 131104 | tf_op jit(solution)/shard_map/ppermute | solution.py:389
  73.8 1.5 %gather.1 = (f32[96,2592]{1,0:T(8,128)}, f32[96,2592]{1,0:T(8,128)}, f32[1,96]{1,0:T(1,128)}, f32[1,96]{1,0:T(1,128)}) custom-call(s32[1]{0:T(128)} %bitcast.me_ref, bf16[2,256,128]{2,1,0:T(8,128)(2,1)S(1)} %add_convert_fusion.refs_0_, bf16[2,256,128]{2,1,0:T(8,128)(2,1)S(1)} %collective-permute-done.11.refs_1_, ...), custom_call_target="tpu_custom_call" | custom-call | tf_op jit(solution)/shard_map/gather/pallas_call | solution.py:491
  (62 shorter events, 11.1 us)
Async XLA Ops:
  0.6 2.1 %collective-permute-start = (bf16[4,96,512]{2,1,0:T(8,128)(2,1)}, bf16[4,96,512]{2,1,0:T(8,128)(2,1)S(1)}, u32[]{:S(2)}, u32[]{:S(2)}) collective-permute-start(bf16[4,96,512]{2,1,0:T(8,128)(2,1)} %bitcast.18), channel_id=1, source_target_pairs={{0,4},{4,0},{8,12},{12,8},{16,20},{20,16},{24,28},{28,24},{1,5},{5... | collective-permute-start | bytes 1179656 | tf_op jit(solution)/shard_map/ppermute | solution.py:403
  1.1 2.1 %collective-permute-start.1 = (bf16[4,96,512]{2,1,0:T(8,128)(2,1)}, bf16[4,96,512]{2,1,0:T(8,128)(2,1)S(1)}, u32[]{:S(2)}, u32[]{:S(2)}) collective-permute-start(bf16[4,96,512]{2,1,0:T(8,128)(2,1)} %bitcast.20), channel_id=1, source_target_pairs={{0,4},{4,0},{8,12},{12,8},{16,20},{20,16},{24,28},{28,24},{1,5},{5... | collective-permute-start | bytes 1179656 | tf_op jit(solution)/shard_map/ppermute | solution.py:404
  6.8 2.7 %copy-start.9 = (bf16[96,2592]{1,0:T(8,128)(2,1)S(1)}, bf16[96,2592]{1,0:T(8,128)(2,1)}, u32[]{:S(2)}) copy-start(bf16[96,2592]{1,0:T(8,128)(2,1)} %param.16) | copy-start | bytes 1492996
  8.7 2.3 %copy-start.10 = (bf16[96,2592]{1,0:T(8,128)(2,1)S(1)}, bf16[96,2592]{1,0:T(8,128)(2,1)}, u32[]{:S(2)}) copy-start(bf16[96,2592]{1,0:T(8,128)(2,1)} %param.15) | copy-start | bytes 1492996
  8.7 9.9 %collective-permute-start.2 = (bf16[4,96,256]{2,1,0:T(8,128)(2,1)S(1)}, bf16[4,96,256]{2,1,0:T(8,128)(2,1)S(1)}, u32[]{:S(2)}, u32[]{:S(2)}) collective-permute-start(bf16[4,96,256]{2,1,0:T(8,128)(2,1)S(1)} %get-tuple-element.24), channel_id=1, source_target_pairs={{4,8},{12,16},{20,24},{8,4},{16,12},{24,20},{5,9},{13,17},{21,25},... | collective-permute-start | bytes 589832 | tf_op jit(solution)/shard_map/ppermute | solution.py:432
  16.0 2.6 %copy-start.4 = (f32[96]{0:T(128)S(1)}, f32[96]{0:T(128)}, u32[]{:S(2)}) copy-start(f32[96]{0:T(128)} %param.17) | copy-start | bytes 1156
  16.0 2.6 %copy-start.5 = (f32[96]{0:T(128)S(1)}, f32[96]{0:T(128)}, u32[]{:S(2)}) copy-start(f32[96]{0:T(128)} %param.18) | copy-start | bytes 1156
  16.0 2.6 %copy-start.6 = (bf16[256,256]{1,0:T(8,128)(2,1)S(1)}, bf16[256,256]{1,0:T(8,128)(2,1)}, u32[]{:S(2)}) copy-start(bf16[256,256]{1,0:T(8,128)(2,1)} %constant.17.clone.back_ref) | copy-start | bytes 393220
  16.0 2.6 %copy-start.7 = (bf16[9,16,256]{2,1,0:T(8,128)(2,1)S(1)}, bf16[9,16,256]{2,1,0:T(8,128)(2,1)}, u32[]{:S(2)}) copy-start(bf16[9,16,256]{2,1,0:T(8,128)(2,1)} %constant.15.clone.masks_ref) | copy-start | bytes 221188
  33.5 5.8 %collective-permute-start.4 = (f32[4,256,128]{2,1,0:T(8,128)S(1)}, f32[4,256,128]{2,1,0:T(8,128)S(1)}, u32[]{:S(2)}, u32[]{:S(2)}) collective-permute-start(f32[4,256,128]{2,1,0:T(8,128)S(1)} %get-tuple-element.32), channel_id=1, source_target_pairs={{0,4},{4,0},{8,12},{12,8},{16,20},{20,16},{24,28},{28,24},{1,5},{5... | collective-permute-start | bytes 1572872 | tf_op jit(solution)/shard_map/ppermute | solution.py:373
  37.8 2.3 %collective-permute-start.5 = (f32[4,256,128]{2,1,0:T(8,128)S(1)}, f32[4,256,128]{2,1,0:T(8,128)S(1)}, u32[]{:S(2)}, u32[]{:S(2)}) collective-permute-start(f32[4,256,128]{2,1,0:T(8,128)S(1)} %get-tuple-element.34), channel_id=1, source_target_pairs={{0,4},{4,0},{8,12},{12,8},{16,20},{20,16},{24,28},{28,24},{1,5},{5... | collective-permute-start | bytes 1572872 | tf_op jit(solution)/shard_map/ppermute | solution.py:468
  40.2 7.3 %collective-permute-start.6 = (bf16[2,256,128]{2,1,0:T(8,128)(2,1)S(1)}, bf16[2,256,128]{2,1,0:T(8,128)(2,1)S(1)}, u32[]{:S(2)}, u32[]{:S(2)}) collective-permute-start(bf16[2,256,128]{2,1,0:T(8,128)(2,1)S(1)} %pad_maximum_fusion), channel_id=1, source_target_pairs={{0,24},{4,28},{8,16},{12,20},{16,8},{20,12},{24,0},{28,4},{1,25},{... | collective-permute-start | bytes 393224 | tf_op jit(solution)/shard_map/ppermute | solution.py:379
  41.8 8.0 %collective-permute-start.7 = (bf16[2,256,128]{2,1,0:T(8,128)(2,1)S(1)}, bf16[2,256,128]{2,1,0:T(8,128)(2,1)S(1)}, u32[]{:S(2)}, u32[]{:S(2)}) collective-permute-start(bf16[2,256,128]{2,1,0:T(8,128)(2,1)S(1)} %pad_maximum_fusion.1), channel_id=1, source_target_pairs={{0,16},{4,20},{8,24},{12,28},{16,0},{20,4},{24,8},{28,12},{1,17},{... | collective-permute-start | bytes 393224 | tf_op jit(solution)/shard_map/ppermute | solution.py:379
  43.4 6.5 %collective-permute-start.8 = (bf16[2,256,128]{2,1,0:T(8,128)(2,1)S(1)}, bf16[2,256,128]{2,1,0:T(8,128)(2,1)S(1)}, u32[]{:S(2)}, u32[]{:S(2)}) collective-permute-start(bf16[2,256,128]{2,1,0:T(8,128)(2,1)S(1)} %pad_maximum_fusion.2), channel_id=1, source_target_pairs={{0,8},{4,12},{8,0},{12,4},{16,24},{20,28},{24,16},{28,20},{1,9},{5... | collective-permute-start | bytes 393224 | tf_op jit(solution)/shard_map/ppermute | solution.py:379
  50.0 5.4 %collective-permute-start.9 = (bf16[2,256,128]{2,1,0:T(8,128)(2,1)S(1)}, bf16[2,256,128]{2,1,0:T(8,128)(2,1)S(1)}, u32[]{:S(2)}, u32[]{:S(2)}) collective-permute-start(bf16[2,256,128]{2,1,0:T(8,128)(2,1)S(1)} %fusion.2), channel_id=1, source_target_pairs={{0,1},{1,0},{2,3},{3,2},{4,5},{5,4},{6,7},{7,6},{8,9},{9,8},{10,11... | collective-permute-start | bytes 393224 | tf_op jit(solution)/shard_map/ppermute | solution.py:384
  55.4 8.2 %collective-permute-start.10 = (bf16[2,256,128]{2,1,0:T(8,128)(2,1)S(1)}, bf16[2,256,128]{2,1,0:T(8,128)(2,1)S(1)}, u32[]{:S(2)}, u32[]{:S(2)}) collective-permute-start(bf16[2,256,128]{2,1,0:T(8,128)(2,1)S(1)} %add_convert_fusion.1), channel_id=1, source_target_pairs={{0,2},{1,3},{2,0},{3,1},{4,6},{5,7},{6,4},{7,5},{8,10},{9,11},{10,... | collective-permute-start | bytes 393224 | tf_op jit(solution)/shard_map/ppermute | solution.py:384
  58.0 14.7 %collective-permute-start.3 = (bf16[4,96,512]{2,1,0:T(8,128)(2,1)S(1)}, bf16[4,96,512]{2,1,0:T(8,128)(2,1)S(1)}, u32[]{:S(2)}, u32[]{:S(2)}) collective-permute-start(bf16[4,96,512]{2,1,0:T(8,128)(2,1)S(1)} %get-tuple-element.27), channel_id=1, source_target_pairs={{0,4},{4,0},{8,12},{12,8},{16,20},{20,16},{24,28},{28,24},{1,5},{5... | collective-permute-start | bytes 1179656 | tf_op jit(solution)/shard_map/ppermute | solution.py:487
  63.7 6.0 %collective-permute-start.11 = (bf16[2,256,128]{2,1,0:T(8,128)(2,1)S(1)}, bf16[2,256,128]{2,1,0:T(8,128)(2,1)S(1)}, u32[]{:S(2)}, u32[]{:S(2)}) collective-permute-start(bf16[2,256,128]{2,1,0:T(8,128)(2,1)S(1)} %add_convert_fusion.refs_0_), channel_id=1, source_target_pairs={{0,8},{4,12},{8,0},{12,4},{16,24},{20,28},{24,16},{28,20},{1,9},{5... | collective-permute-start | bytes 393224 | tf_op jit(solution)/shard_map/ppermute | solution.py:389
  65.4 6.9 %collective-permute-start.12 = (bf16[2,256,128]{2,1,0:T(8,128)(2,1)S(1)}, bf16[2,256,128]{2,1,0:T(8,128)(2,1)S(1)}, u32[]{:S(2)}, u32[]{:S(2)}) collective-permute-start(bf16[2,256,128]{2,1,0:T(8,128)(2,1)S(1)} %add_convert_fusion.refs_0_), channel_id=1, source_target_pairs={{0,16},{4,20},{8,24},{12,28},{16,0},{20,4},{24,8},{28,12},{1,17},{... | collective-permute-start | bytes 393224 | tf_op jit(solution)/shard_map/ppermute | solution.py:389
  65.5 6.8 %collective-permute-start.13 = (bf16[2,256,128]{2,1,0:T(8,128)(2,1)S(1)}, bf16[2,256,128]{2,1,0:T(8,128)(2,1)S(1)}, u32[]{:S(2)}, u32[]{:S(2)}) collective-permute-start(bf16[2,256,128]{2,1,0:T(8,128)(2,1)S(1)} %add_convert_fusion.refs_0_), channel_id=1, source_target_pairs={{0,24},{4,28},{8,16},{12,20},{16,8},{20,12},{24,0},{28,4},{1,25},{... | collective-permute-start | bytes 393224 | tf_op jit(solution)/shard_map/ppermute | solution.py:389
  67.2 6.3 %collective-permute-start.14 = (bf16[2,256,128]{2,1,0:T(8,128)(2,1)S(1)}, bf16[2,256,128]{2,1,0:T(8,128)(2,1)S(1)}, u32[]{:S(2)}, u32[]{:S(2)}) collective-permute-start(bf16[2,256,128]{2,1,0:T(8,128)(2,1)S(1)} %add_convert_fusion.refs_0_), channel_id=1, source_target_pairs={{0,4},{4,0},{8,12},{12,8},{16,20},{20,16},{24,28},{28,24},{1,5},{5... | collective-permute-start | bytes 393224 | tf_op jit(solution)/shard_map/ppermute | solution.py:390
  69.7 3.9 %collective-permute-start.15 = (bf16[2,256,128]{2,1,0:T(8,128)(2,1)S(1)}, bf16[2,256,128]{2,1,0:T(8,128)(2,1)S(1)}, u32[]{:S(2)}, u32[]{:S(2)}) collective-permute-start(bf16[2,256,128]{2,1,0:T(8,128)(2,1)S(1)} %collective-permute-done.11.refs_1_), channel_id=1, source_target_pairs={{0,4},{4,0},{8,12},{12,8},{16,20},{20,16},{24,28},{28,24},{1,5},{5... | collective-permute-start | bytes 393224 | tf_op jit(solution)/shard_map/ppermute | solution.py:390
  72.2 1.3 %collective-permute-start.16 = (bf16[2,256,128]{2,1,0:T(8,128)(2,1)S(1)}, bf16[2,256,128]{2,1,0:T(8,128)(2,1)S(1)}, u32[]{:S(2)}, u32[]{:S(2)}) collective-permute-start(bf16[2,256,128]{2,1,0:T(8,128)(2,1)S(1)} %collective-permute-done.12.refs_2_), channel_id=1, source_target_pairs={{0,4},{4,0},{8,12},{12,8},{16,20},{20,16},{24,28},{28,24},{1,5},{5... | collective-permute-start | bytes 393224 | tf_op jit(solution)/shard_map/ppermute | solution.py:390
  72.2 1.5 %collective-permute-start.17 = (bf16[2,256,128]{2,1,0:T(8,128)(2,1)S(1)}, bf16[2,256,128]{2,1,0:T(8,128)(2,1)S(1)}, u32[]{:S(2)}, u32[]{:S(2)}) collective-permute-start(bf16[2,256,128]{2,1,0:T(8,128)(2,1)S(1)} %collective-permute-done.13.refs_3_), channel_id=1, source_target_pairs={{0,4},{4,0},{8,12},{12,8},{16,20},{20,16},{24,28},{28,24},{1,5},{5... | collective-permute-start | bytes 393224 | tf_op jit(solution)/shard_map/ppermute | solution.py:390
  (5 other events, 4.6 us)
where the time goes:
time: 75.7 us; the launch traced here: 75.2 us
  waiting for transfers between devices  23.8 us (31%)
  Pallas kernels  18.2 us (24%)
  starting transfers between devices  17.8 us (24%)
  local copies, waits for them, and re-layouts  13.4 us (18%)
  other arithmetic  1.13 us (1%)
  between operations  0.86 us (1%)
    pallas_call x1, Pallas kernels, local(): pl.pallas_call(forward_kernel, out_shape=(jax.ShapeDtypeStruct(bricks, BF...  10.2 us
    ppermute x2, waiting for transfers between devices, shared_sum(): moved = lax.ppermute(total, 'dp', hop)  9.32 us
    unnamed x24, local copies, waits for them, and re-layouts  6.43 us
    ppermute x3, waiting for transfers between devices, shared_sum(): total = total + lax.ppermute(part, 'space', hop).astype(F32)  5.88 us
    ppermute x3, waiting for transfers between devices, shared_sum(): lax.ppermute(total, 'space', [(d, d ^ 2 * r) for d in range(count)])  5.01 us
    pallas_call x1, Pallas kernels, local(): pl.pallas_call(backward_kernel, out_shape=(jax.ShapeDtypeStruct(half, F32...  4.73 us
    ppermute x2, starting transfers between devices, shared_sum(): moved = lax.ppermute(total, 'dp', hop)  4.29 us
    ppermute x1, starting transfers between devices, shared_sum(): halves = [keeps[0] + lax.ppermute(sends[0], 'space', swap)]  4.28 us
  transfers between devices with their start and end apart: 18, of which 12 were waited for; matrix products, arithmetic and copies ran while one was open for 13% of the time, Pallas kernels for 0%

commit v1 on v0

v1 whole, which is shorter than its diff:
```python
import jax
import jax.numpy as jnp
import numpy as np
from jax import lax
from jax.experimental import pallas as pl
from jax.experimental.pallas import tpu as pltpu
from jax.sharding import PartitionSpec as P

EDGE = 8
PLANE = 256
CELLS = 512
KDIM = 896
TILES = 21
ROWS = 2048
OFFSETS = (4, 10, 12, 21)
DOWN, NEAR_Y, NEAR_Z, UP, LIVE, DEVICE = range(6)
F32 = jnp.float32
BF16 = jnp.bfloat16


def spread_matrix():
    move = np.zeros((256, 256), np.float32)
    for z in range(2):
        for p in range(2):
            for q in range(8):
                for r in range(8):
                    move[z * 128 + p * 64 + q * 8 + r, p * 128 + q * 16 + z * 8 + r] = 1.0
    return move


def tap_masks():
    masks = np.zeros((9, 16, 256), np.float32)
    for b in range(3):
        for c in range(3):
            for q in range(16):
                for r in range(16):
                    inside = 0 <= q + b - 1 < 16 and 0 <= r + c - 1 < 16
                    masks[b * 3 + c, :, q * 16 + r] = float(inside)
    return masks


def write_taps(dst, plane, masks_ref):
    channels = plane.shape[0]
    wide = plane.astype(F32)
    for k in range(9):
        step = (k // 3 - 1) * 16 + (k % 3 - 1)
        if step == 0:
            moved = plane
        else:
            moved = pltpu.roll(wide, (-step) % PLANE, 1).astype(BF16)
            moved = moved * jnp.concatenate([masks_ref[k]] * (channels // 16), axis=0)
        dst[k * channels : (k + 1) * channels, :] = moved


def slot_place(table, slot, pair_slots):
    shift = pair_slots.bit_length() - 1
    up = table[UP, slot]
    inside = jnp.logical_and(up >= 0, up >> shift == slot >> shift)
    parity = jnp.where(inside, 0, 1)
    place = jnp.where(table[NEAR_Y, slot] >= 0, 2, 0) + jnp.where(table[NEAR_Z, slot] >= 0, 1, 0)
    return parity, place


def lane_mask(scalars):
    lane = lax.broadcasted_iota(jnp.int32, (8, PLANE), 1)
    high_y = lane >= 128
    high_z = (lane & 8) != 0
    s = [jnp.full((8, PLANE), v, F32) for v in scalars]
    return jnp.where(high_y, jnp.where(high_z, s[3], s[2]), jnp.where(high_z, s[1], s[0]))


def plane_product(weight_ref, taps):
    blocks, channels = weight_ref.shape[0], weight_ref.shape[1]
    left = weight_ref[...].reshape(blocks * channels, KDIM)
    return jnp.dot(left, taps, preferred_element_type=F32)


def add_planes(acc, at, product, fresh=()):
    channels = acc.shape[1]
    for a in range(3):
        k = at + 1 - a
        if not 0 <= k < acc.shape[0]:
            continue
        part = product[a * channels : (a + 1) * channels]
        acc[k] = part if k in fresh else acc[k] + part


def weight_products(total, grads, taps):
    blank = jnp.zeros((total.shape[0] // 3, PLANE), BF16)

    def left(p):
        inside = [grads(p + 1 - a) if 0 <= p + 1 - a < EDGE else blank for a in range(3)]
        return jnp.concatenate(inside, axis=0)

    for p in range(-1, EDGE + 1, 2):
        both_left = jnp.concatenate([left(p), left(p + 1)], axis=1)
        both_right = jnp.concatenate([taps(p), taps(p + 1)], axis=1)
        part = lax.dot_general(
            both_left, both_right, (((1,), (1,)), ((), ())), preferred_element_type=F32
        )
        total[...] = part if p == -1 else total[...] + part


def write_tiles(flat, total, channels, even):
    lane = lax.broadcasted_iota(jnp.int32, (channels, 128), 1)
    blank = jnp.zeros((channels, 128), F32)
    low = total[pl.ds(pl.multiple_of(jnp.where(even, 0, 2 * channels), channels), channels), :]
    high = total[pl.ds(pl.multiple_of(jnp.where(even, 2 * channels, 0), channels), channels), :]
    second = jnp.concatenate([total[channels : 2 * channels, :], blank], axis=1)
    third = jnp.concatenate([high, blank], axis=1)
    second = pltpu.roll(second, 96, 1)
    third = pltpu.roll(third, 64, 1)

    def cut(value, k):
        return value[:, k * 128 : (k + 1) * 128]

    tiles = [cut(low, k) for k in range(6)]
    tiles.append(jnp.where(lane < 96, cut(low, 6), cut(second, 0)))
    tiles += [cut(second, k) for k in range(1, 7)]
    tiles.append(jnp.where(lane < 64, cut(second, 7), cut(third, 0)))
    tiles += [cut(third, k) for k in range(1, 8)]
    for k in range(TILES):
        flat[k * channels : (k + 1) * channels, :] = tiles[k]
    flat[TILES * channels :, :] = jnp.zeros((ROWS - TILES * channels, 128), F32)


def split_tiles(keep_ref, send_ref, flat, me):
    chips, rows = keep_ref.shape[0], keep_ref.shape[1]
    core, chip = me & 1, me >> 1
    for r in range(chips):
        at = jnp.clip(chip ^ r, 0, chips - 1) * rows
        here = at + jnp.where(core == 1, chips * rows, 0)
        there = at + jnp.where(core == 1, 0, chips * rows)
        keep_ref[r] = flat[pl.ds(pl.multiple_of(here, rows), rows), :]
        send_ref[r] = flat[pl.ds(pl.multiple_of(there, rows), rows), :]


def layout_kernel(
    table, own_ref, pair_ref, cot_own_ref, cot_pair_ref, move_ref,
    x_ref, cot_ref, edge_ref, mask_ref, bricks, cots,
):
    slots, channels = pair_ref.shape[0], pair_ref.shape[1]
    all_slots = table.shape[1]
    me = jnp.clip(table[DEVICE, 0], 0, all_slots // slots - 1)
    core = me & 1
    even = core == 0

    live = [[jnp.float32(0)] * 4 for _ in range(2)]
    beyond = [jnp.float32(0)] * 4
    for device, source, cot_source in (
        (me, own_ref, cot_own_ref), (me ^ 1, pair_ref, cot_pair_ref),
    ):
        for s in range(slots):
            slot = jnp.clip(device * slots + s, 0, all_slots - 1)
            parity, place = slot_place(table, slot, 2 * slots)
            alive = table[LIVE, slot].astype(F32)
            if source is own_ref:
                bricks[parity, place] = source[s]
                cots[parity, place] = cot_source[s]
            else:
                scale = jnp.full((channels, CELLS), alive, F32).astype(BF16)
                bricks[parity, place] = source[s] * scale
                cots[parity, place] = cot_source[s] * scale
            outer = jnp.where(even, table[DOWN, slot], table[UP, slot])
            alive_outer = table[LIVE, jnp.clip(outer, 0, all_slots - 1)].astype(F32)
            alive_outer = jnp.where(outer >= 0, alive_outer, 0.0)
            for k in range(4):
                for p in range(2):
                    here = jnp.logical_and(parity == p, place == k)
                    live[p][k] = jnp.where(here, alive, live[p][k])
                here = jnp.logical_and(parity == core, place == k)
                beyond[k] = jnp.where(here, alive_outer, beyond[k])
    mask_ref[0] = lane_mask(beyond)
    mask_ref[1] = lane_mask([jnp.where(even, live[0][k], live[1][k]) for k in range(4)])
    mask_ref[2] = lane_mask([jnp.where(even, live[1][k], live[0][k]) for k in range(4)])

    move = move_ref[...]
    mine = jnp.where(even, 0, 1)

    def spread(left, right):
        two = jnp.concatenate([left, right], axis=1)
        return jnp.dot(two, move, preferred_element_type=F32).astype(BF16)

    for y in range(2):
        row = slice(y * 128, (y + 1) * 128)
        for j in range(4):
            pair = slice(j * 128, (j + 1) * 128)
            first = jnp.where(even, 2 * j, 7 - 2 * j)
            second = jnp.where(even, 2 * j + 1, 6 - 2 * j)
            both = spread(bricks[mine, 2 * y, :, pair], bricks[mine, 2 * y + 1, :, pair])
            x_ref[first, :, row] = both[:, :128]
            x_ref[second, :, row] = both[:, 128:]
            both = spread(cots[mine, 2 * y, :, pair], cots[mine, 2 * y + 1, :, pair])
            cot_ref[first, :, row] = both[:, :128]
            cot_ref[second, :, row] = both[:, 128:]
        for j in range(2):
            start = pl.multiple_of(jnp.where(even, j * 128, 256 + j * 128), 128)
            pair = pl.ds(start, 128)
            both = spread(
                bricks[1 - mine, 2 * y, :, pair], bricks[1 - mine, 2 * y + 1, :, pair]
            )
            x_ref[jnp.where(even, 8 + 2 * j, 11 - 2 * j), :, row] = both[:, :128]
            x_ref[jnp.where(even, 9 + 2 * j, 10 - 2 * j), :, row] = both[:, 128:]
        pair = pl.ds(pl.multiple_of(jnp.where(even, 0, 384), 128), 128)
        both = spread(cots[1 - mine, 2 * y, :, pair], cots[1 - mine, 2 * y + 1, :, pair])
        side = jnp.full((channels, 128), jnp.where(even, 1.0, 0.0), F32).astype(BF16)
        cot_ref[8, :, row] = both[:, :128] * side + both[:, 128:] * (1 - side)
    edge_ref[:3] = x_ref[:3]
    edge_ref[3] = cot_ref[0]


def tap_weights(out_ref, weight_ref, wide, even):
    channels, width = weight_ref.shape
    wide[:, :width] = weight_ref[...]
    lane = lax.broadcasted_iota(jnp.int32, (channels, 128), 1)
    for a, (tile, moved) in enumerate(((0, 0), (6, 96), (13, 64))):
        span = wide[:, tile * 128 : (tile + 8) * 128].astype(F32)
        if moved:
            span = pltpu.roll(span, 1024 - moved, 1)
        last = jnp.where(lane < 96, span[:, 768:KDIM], 0.0)
        span = jnp.concatenate([span[:, :768], last], axis=1)
        at = a if a == 1 else jnp.where(even, a, 2 - a)
        out_ref[at] = span.astype(BF16)


def back_weights(out_ref, taps_ref):
    channels = taps_ref.shape[1]
    lane = lax.broadcasted_iota(jnp.int32, (channels, 128), 1)
    more = jnp.zeros((128 - channels, KDIM), F32)
    for a in range(3):
        block = jnp.concatenate([taps_ref[2 - a].astype(F32), more], axis=0)
        turned = block.T
        tiles = [jnp.zeros((channels, 128), F32)] * 7
        for k in range(9):
            piece = turned[(8 - k) * channels : (9 - k) * channels, :]
            tile, moved = divmod(k * channels, 128)
            if moved:
                piece = pltpu.roll(piece, moved, 1)
            tiles[tile] = tiles[tile] + jnp.where(lane >= moved, piece, 0.0)
            if moved + channels > 128:
                tiles[tile + 1] = tiles[tile + 1] + jnp.where(lane < moved, piece, 0.0)
        out_ref[a] = jnp.concatenate(tiles, axis=1).astype(BF16)


def column(row):
    return jnp.broadcast_to(row, (8, row.shape[1])).T[:, :1]


def layer_of(q):
    return 0 if q < 0 else 1 if q < EDGE else 2


def hidden_plane(pre, mask):
    sigma = jax.nn.sigmoid(pre)
    return (pre * sigma * mask).astype(BF16), sigma * (1.0 + pre * (1.0 - sigma)) * mask


def out_plane(pre, mask, cot):
    sigma = jax.nn.sigmoid(pre)
    grad = cot.astype(F32) * (sigma * (1.0 + pre * (1.0 - sigma)))
    return (pre * sigma * mask).astype(BF16), grad.astype(BF16)


def inner_kernel(
    table, x_ref, cot_ref, layer_mask, w1_ref, w2_ref, bias_ref, masks_ref,
    taps_ref, one_ref, two_ref, slope_ref, g_ref, out_ref, w1_taps, w2_taps, w2_back,
    wide, xc, acc_one, acc_two,
):
    channels = x_ref.shape[1]
    even = (table[DEVICE, 0] & 1) == 0
    tap_weights(w1_taps, w1_ref, wide, even)
    bias_one, bias_two = column(bias_ref[0:1]), column(bias_ref[1:2])
    ones = jnp.ones((KDIM - 9 * channels, PLANE), BF16)
    for k in range(2):
        xc[k, 9 * channels :, :] = ones
    for k in range(9):
        taps_ref[k, 9 * channels :, :] = ones
    write_taps(xc.at[0], x_ref[0], masks_ref)

    for p in range(15):
        if p <= 10:
            product = plane_product(w1_taps, xc[p & 1])
            if p < 10:
                write_taps(xc.at[1 - (p & 1)], x_ref[p + 1], masks_ref)
            add_planes(acc_one, p + 1, product, fresh=(0, 1, 2) if p == 0 else (p + 2,))
        if p == 1:
            tap_weights(w2_taps, w2_ref, wide, even)
        if p == 3:
            back_weights(w2_back, w2_taps)
        q = p - 2
        if 1 <= q <= 9:
            hidden, slope = hidden_plane(acc_one[q + 1] + bias_one, layer_mask[layer_of(q)][:1])
            write_taps(taps_ref.at[q - 1], hidden, masks_ref)
            if q < EDGE:
                slope_ref[q - 1] = slope
        q = p - 4
        if 1 <= q <= 9:
            product = plane_product(w2_taps, taps_ref[q - 1])
            add_planes(acc_two, q, product, fresh=(0, 1, 2) if q == 1 else (q + 1,))
        q = p - 6
        if 2 <= q <= 8:
            mask = layer_mask[layer_of(q)][:1]
            out, grad = out_plane(acc_two[q] + bias_two, mask, cot_ref[q])
            g_ref[q - 2] = grad
            if q < EDGE:
                out_ref[q - 2] = out
    one_ref[...] = acc_one[:2]
    two_ref[...] = acc_two[:2]


def outer_kernel(
    table, edge_ref, cot_ref, layer_mask, w1_taps, w2_taps, bias_ref, masks_ref,
    taps_ref, one_ref, two_ref, g_in_ref,
    keep_ref, send_ref, slope_ref, g_ref, out_ref,
    xc, hc, acc_one, acc_two, total, flat,
):
    channels = cot_ref.shape[1]
    me = jnp.clip(table[DEVICE, 0], 0, 2**15)
    bias_one, bias_two = column(bias_ref[0:1]), column(bias_ref[1:2])
    ones = jnp.ones((KDIM - 9 * channels, PLANE), BF16)
    for k in range(3):
        xc[k, 9 * channels :, :] = ones
        hc[k, 9 * channels :, :] = ones
        write_taps(xc.at[k], edge_ref[2 - k], masks_ref)
    acc_one[1:] = one_ref[...]
    acc_two[1:] = two_ref[...]
    for p in range(-3, 0):
        add_planes(acc_one, p + 2, plane_product(w1_taps, xc[p + 3]), fresh=(0,) if p == -3 else ())
    for q in range(-2, 1):
        hidden, slope = hidden_plane(acc_one[q + 2] + bias_one, layer_mask[layer_of(q)][:1])
        write_taps(hc.at[q + 2], hidden, masks_ref)
        if q == 0:
            slope_ref[0] = slope
    for q in range(-2, 1):
        add_planes(acc_two, q + 1, plane_product(w2_taps, hc[q + 2]), fresh=(0,) if q == -2 else ())
    for q in range(-1, 2):
        cot = edge_ref[3] if q < 0 else cot_ref[q]
        out, grad = out_plane(acc_two[q + 1] + bias_two, layer_mask[layer_of(q)][:1], cot)
        g_ref[q + 1] = grad
        if q >= 0:
            out_ref[q] = out

    def grads(q):
        return g_ref[q + 1] if q < 2 else g_in_ref[q - 2]

    def taps(q):
        return hc[q + 2] if q < 1 else taps_ref[q - 1]

    weight_products(total, grads, taps)
    write_tiles(flat, total, channels, (me & 1) == 0)
    split_tiles(keep_ref, send_ref, flat, me)


def output_kernel(table, first_ref, second_ref, back_ref, keep_ref, send_ref, outs, bricks):
    slots, channels = keep_ref.shape[0], keep_ref.shape[1]
    me = jnp.clip(table[DEVICE, 0], 0, table.shape[1] // slots - 1)
    core = me & 1
    even = core == 0
    outs[:2] = first_ref[...]
    outs[2:] = second_ref[...]
    back = back_ref[...]
    for y in range(2):
        row = slice(y * 128, (y + 1) * 128)
        for j in range(4):
            first = jnp.where(even, 2 * j, 7 - 2 * j)
            second = jnp.where(even, 2 * j + 1, 6 - 2 * j)
            two = jnp.concatenate([outs[first, :, row], outs[second, :, row]], axis=1)
            both = jnp.dot(two, back, preferred_element_type=F32).astype(BF16)
            pair = slice(j * 128, (j + 1) * 128)
            bricks[2 * y, :, pair] = both[:, :128]
            bricks[2 * y + 1, :, pair] = both[:, 128:]
    for target, device in ((keep_ref, me), (send_ref, me ^ 1)):
        for s in range(slots):
            slot = jnp.clip(device * slots + s, 0, table.shape[1] - 1)
            parity, place = slot_place(table, slot, 2 * slots)
            scale = jnp.where(parity == core, 1.0, 0.0)
            target[s] = bricks[place] * jnp.full((channels, CELLS), scale, F32).astype(BF16)


def backward_kernel(
    table, g_out_ref, g_in_ref, slope_out_ref, slope_in_ref, x_ref, edge_ref, w2_back, masks_ref,
    keep_ref, send_ref, gc, xc, acc, grad, total, flat,
):
    channels = x_ref.shape[1]
    me = jnp.clip(table[DEVICE, 0], 0, 2**15)
    ones = jnp.ones((KDIM - 9 * channels, PLANE), BF16)
    for k in range(2):
        gc[k, 9 * channels :, :] = ones
    for k in range(10):
        xc[k, 9 * channels :, :] = ones

    def g_plane(q):
        return g_out_ref[q + 1] if q < 2 else g_in_ref[q - 2]

    write_taps(gc.at[0], g_plane(-1), masks_ref)
    for p in range(-1, 10):
        if p <= 8:
            now = (p + 1) & 1
            product = plane_product(w2_back, gc[now])
            if p < 8:
                write_taps(gc.at[1 - now], g_plane(p + 1), masks_ref)
            write_taps(xc.at[p + 1], edge_ref[0] if p < 0 else x_ref[p], masks_ref)
            add_planes(acc, p + 2, product, fresh=(0, 1, 2) if p == -1 else (p + 3,))
        q = p - 2
        if 0 <= q < EDGE:
            slope = slope_out_ref[0] if q == 0 else slope_in_ref[q - 1]
            grad[q] = (acc[q + 2] * slope).astype(BF16)
    weight_products(total, lambda q: grad[q], lambda q: xc[q + 1])
    write_tiles(flat, total, channels, (me & 1) == 0)
    split_tiles(keep_ref, send_ref, flat, me)


def gather_kernel(table, *refs):
    chips = (len(refs) - 5) // 2
    w_one_ref, w_two_ref, b_one_ref, b_two_ref, flat = refs[2 * chips :]
    rows = refs[0].shape[1]
    channels = w_one_ref.shape[0]
    me = jnp.clip(table[DEVICE, 0], 0, 2 * chips - 1)
    core, chip = me & 1, me >> 1
    for half in range(2):
        base = jnp.where(core == half, 0, chips * rows)
        for r in range(chips):
            at = base + jnp.clip(chip ^ r, 0, chips - 1) * rows
            flat[:, pl.ds(pl.multiple_of(at, rows), rows), :] = refs[half * chips + r][...]
    for n, (weight, bias) in enumerate(((w_one_ref, b_one_ref), (w_two_ref, b_two_ref))):
        for k in range(TILES - 1):
            tile = flat[n, k * channels : (k + 1) * channels, :]
            weight[:, k * 128 : (k + 1) * 128] = tile.astype(F32)
        last = flat[n, (TILES - 1) * channels : TILES * channels, :].astype(F32)
        weight[:, 2560:2592] = last[:, :32]
        bias[...] = last.T[32:33, :]


VMEM = pl.BlockSpec(memory_space=pltpu.VMEM)
SMEM = pl.BlockSpec(memory_space=pltpu.SMEM)


def vmem(mebibytes):
    return pltpu.CompilerParams(vmem_limit_bytes=mebibytes * 2**20)


def shared_sum(keeps, sends, send_two_done):
    chips = keeps[0].shape[0]
    count = 2 * chips
    volumes = lax.axis_size("dp")
    swap = [(d, d ^ 1) for d in range(count)]
    halves = [keeps[0] + lax.ppermute(sends[0], "space", swap)]
    halves.append(keeps[1] + send_two_done)
    total = jnp.stack([half[0] for half in halves])
    for r in range(chips - 1, 0, -1):
        part = jnp.stack([half[r] for half in halves]).astype(BF16)
        hop = [(d, d ^ (2 * r)) for d in range(count)]
        total = total + lax.ppermute(part, "space", hop).astype(F32)
    total = total.astype(BF16)
    step = 1
    while step < volumes:
        hop = [(d, d ^ step) for d in range(volumes)]
        moved = lax.ppermute(total, "dp", hop)
        total = (total.astype(F32) + moved.astype(F32)).astype(BF16)
        step *= 2
    parts = [total]
    for r in range(chips - 1, 0, -1):
        parts.insert(1, lax.ppermute(total, "space", [(d, d ^ (2 * r)) for d in range(count)]))
    return parts + [lax.ppermute(part, "space", swap) for part in parts]


def local(volume, neighbours, active, cotangent, weight_one, weight_two, bias_one, bias_two):
    volume, cotangent = volume[0], cotangent[0]
    slots, channels = volume.shape[0], volume.shape[1]
    count = lax.axis_size("space")
    chips = count // 2
    me = lax.axis_index("space").astype(jnp.int32)

    swap = [(d, d ^ 1) for d in range(count)]
    hop = [(d, d + 1) for d in range(1, count - 1, 2)] + [(d, d - 1) for d in range(2, count, 2)]
    pair_volume = lax.ppermute(volume, "space", swap)
    pair_cot = lax.ppermute(cotangent, "space", swap)
    move = spread_matrix()
    masks = jnp.asarray(tap_masks(), BF16)
    biases = jnp.stack([bias_one, bias_two])
    near = neighbours[0].T
    table = [near[k : k + 1] for k in OFFSETS]
    table = jnp.concatenate([*table, active, jnp.full_like(active, me)], axis=0)
    alive = lax.dynamic_slice_in_dim(active[0], me * slots, slots, 0)
    alive = alive.astype(BF16)[:, None, None]

    def planes(number, dtype=BF16):
        return jax.ShapeDtypeStruct((number, channels, PLANE), dtype)

    def plane_space(number, dtype=BF16):
        return pltpu.VMEM((number, channels, PLANE), dtype)

    def tap_space(number):
        return pltpu.VMEM((number, KDIM, PLANE), BF16)

    bricks = (slots, channels, CELLS)
    x_planes, cot_planes, edge, layer_mask = pl.pallas_call(
        layout_kernel,
        out_shape=(planes(12), planes(9), planes(4), jax.ShapeDtypeStruct((3, 8, PLANE), F32)),
        in_specs=[SMEM] + [VMEM] * 5,
        out_specs=(VMEM,) * 4,
        scratch_shapes=[
            pltpu.VMEM((2, *bricks), BF16),
            pltpu.VMEM((2, *bricks), BF16),
        ],
        compiler_params=vmem(8),
        name="layout",
    )(table, volume * alive, pair_volume, cotangent * alive, pair_cot, jnp.asarray(move, BF16))
    outer = lax.ppermute(edge, "space", hop)

    weights = jax.ShapeDtypeStruct((3, channels, KDIM), BF16)
    taps, one, two, slope_in, g_in, out_in, w1, w2, w2_back = pl.pallas_call(
        inner_kernel,
        out_shape=(
            jax.ShapeDtypeStruct((9, KDIM, PLANE), BF16),
            planes(2, F32),
            planes(2, F32),
            planes(7, F32),
            planes(7),
            planes(6),
            weights,
            weights,
            weights,
        ),
        in_specs=[SMEM] + [VMEM] * 7,
        out_specs=(VMEM,) * 9,
        scratch_shapes=[
            pltpu.VMEM((channels, 21 * 128), BF16),
            tap_space(2),
            plane_space(13, F32),
            plane_space(11, F32),
        ],
        compiler_params=vmem(20),
        cost_estimate=pl.CostEstimate(flops=2**33, bytes_accessed=2**23, transcendentals=2**20),
        name="inner",
    )(table, x_planes, cot_planes, layer_mask, weight_one, weight_two, biases, masks)

    half = jax.ShapeDtypeStruct((chips, ROWS // count, 128), F32)
    keep_two, send_two, slope_out, g_out, out_out = pl.pallas_call(
        outer_kernel,
        out_shape=(half, half, planes(1, F32), planes(3), planes(2)),
        in_specs=[SMEM] + [VMEM] * 11,
        out_specs=(VMEM,) * 5,
        scratch_shapes=[
            tap_space(3),
            tap_space(3),
            plane_space(3, F32),
            plane_space(3, F32),
            pltpu.VMEM((3 * channels, KDIM), F32),
            pltpu.VMEM((ROWS, 128), F32),
        ],
        compiler_params=vmem(16),
        cost_estimate=pl.CostEstimate(flops=2**32, bytes_accessed=2**23, transcendentals=2**18),
        name="outer",
    )(
        table, outer, cot_planes, layer_mask, w1, w2, biases, masks, taps, one, two, g_in,
    )
    got_two = lax.ppermute(send_two, "space", swap)
    keep_one, send_one = pl.pallas_call(
        backward_kernel,
        out_shape=(half, half),
        in_specs=[SMEM] + [VMEM] * 8,
        out_specs=(VMEM,) * 2,
        scratch_shapes=[
            tap_space(2),
            tap_space(10),
            plane_space(12, F32),
            plane_space(8),
            pltpu.VMEM((3 * channels, KDIM), F32),
            pltpu.VMEM((ROWS, 128), F32),
        ],
        compiler_params=vmem(20),
        cost_estimate=pl.CostEstimate(flops=2**32, bytes_accessed=2**22, transcendentals=0),
        name="backward",
    )(table, g_out, g_in, slope_out, slope_in, x_planes, outer, w2_back, masks)
    keep, send = pl.pallas_call(
        output_kernel,
        out_shape=(jax.ShapeDtypeStruct(bricks, BF16),) * 2,
        in_specs=[SMEM] + [VMEM] * 3,
        out_specs=(VMEM,) * 2,
        scratch_shapes=[plane_space(8), pltpu.VMEM(bricks, BF16)],
        compiler_params=vmem(8),
        cost_estimate=pl.CostEstimate(flops=2**28, bytes_accessed=2**21, transcendentals=0),
        name="output",
    )(table, out_out, out_in, jnp.asarray(move.T, BF16))
    output = (keep + lax.ppermute(send, "space", swap))[None]
    parts = shared_sum([keep_one, keep_two], [send_one, send_two], got_two)
    weight_shape = jax.ShapeDtypeStruct((channels, 27 * channels), F32)
    bias_shape = jax.ShapeDtypeStruct((1, channels), F32)
    total_w_one, total_w_two, total_b_one, total_b_two = pl.pallas_call(
        gather_kernel,
        out_shape=(weight_shape, weight_shape, bias_shape, bias_shape),
        in_specs=[SMEM] + [VMEM] * len(parts),
        out_specs=(VMEM,) * 4,
        scratch_shapes=[pltpu.VMEM((2, ROWS, 128), BF16)],
        compiler_params=vmem(8),
        name="gather",
    )(table, *parts)
    return (output, total_w_one, total_w_two, total_b_one[0], total_b_two[0])


def solution(mesh):
    in_specs = (
        P("dp", "space", None, None),
        P("dp", None, None),
        P("dp", None),
        P("dp", "space", None, None),
        P(),
        P(),
        P(),
        P(),
    )
    out_specs = (P("dp", "space", None, None), P(), P(), P(), P())
    return jax.shard_map(local, mesh=mesh, in_specs=in_specs, out_specs=out_specs, check_vma=False)
```

time: 75.7 us -> 68.1 us (0.90)
  local copies, waits for them, and re-layouts: 13.4 us -> 5.32 us
  waiting for transfers between devices: 23.8 us -> 20.2 us
  other arithmetic: 1.13 us -> 3.77 us
  Pallas kernels: 18.2 us -> 20.3 us
    reshape x3 -> x0, local copies, waits for them, and re-layouts: 4.12 us -> none  [the longest x1 2.47 us: local(): w2t = w2t.transpose(1, 4, 2, 3, 0).reshape(3 * channels, 9 * channels)]
    transpose x4 -> x0, local copies, waits for them, and re-layouts: 2.62 us -> none  [the longest x2 1.41 us: local(): w2t = w2t.transpose(1, 4, 2, 3, 0).reshape(3 * channels, 9 * channels)]
    ppermute x2, waiting for transfers between devices: 9.32 us -> 6.96 us  [shared_sum(): moved = lax.ppermute(total, 'dp', hop)]
    unnamed x24 -> x13, local copies, waits for them, and re-layouts: 6.43 us -> 4.58 us
    pallas_call x3 -> x5, Pallas kernels: 16.8 us -> 18.2 us  [the longest x1 5.47 us: local(): pl.pallas_call(backward_kernel, out_shape=(half, half), in_specs=[SMEM] +...]
    mul x0 -> x1, other arithmetic: none -> 1.24 us  [local(): cotangent * alive]
  transfers between devices with their start and end apart: 18 -> 18, of which waited for: 12 -> 11; matrix products, arithmetic and copies ran while one was open for 13% -> 7% of each run, Pallas kernels for 0% -> 10%
where the time goes in v1:
time: 68.1 us; the launch traced here: 67.7 us
  Pallas kernels  20.3 us (30%)
  waiting for transfers between devices  20.2 us (30%)
  starting transfers between devices  17.3 us (25%)
  local copies, waits for them, and re-layouts  5.32 us (8%)
  other arithmetic  3.77 us (6%)
  between operations  0.81 us (1%)
    ppermute x2, waiting for transfers between devices, shared_sum(): moved = lax.ppermute(total, 'dp', hop)  6.96 us
    ppermute x3, waiting for transfers between devices, shared_sum(): total = total + lax.ppermute(part, 'space', hop).astype(F32)  6.15 us
    pallas_call x1, Pallas kernels, local(): pl.pallas_call(backward_kernel, out_shape=(half, half), in_specs=[SMEM] +...  5.47 us
    pallas_call x1, Pallas kernels, local(): pl.pallas_call(inner_kernel, out_shape=(jax.ShapeDtypeStruct((9, KDIM, PL...  5.41 us
    pallas_call x1, Pallas kernels, local(): pl.pallas_call(outer_kernel, out_shape=(half, half, planes(1, F32), plane...  4.83 us
    unnamed x13, local copies, waits for them, and re-layouts  4.58 us
    ppermute x3, waiting for transfers between devices, shared_sum(): lax.ppermute(total, 'space', [(d, d ^ 2 * r) for d in range(count)])  4.42 us
    ppermute x1, starting transfers between devices, shared_sum(): halves = [keeps[0] + lax.ppermute(sends[0], 'space', swap)]  4.34 us
  transfers between devices with their start and end apart: 18, of which 11 were waited for; matrix products, arithmetic and copies ran while one was open for 7% of the time, Pallas kernels for 10%

profile of v1, /device:TPU:0, one launch (start us, length us, event | category | flops | bytes accessed | tf_op | source)
XLA Modules:
  0.0 67.7 jit_solution(13113465273953773978)
XLA Ops:
  4.0 1.2 %broadcast_multiply_fusion = (bf16[4,96,512]{2,1,0:T(8,128)(2,1)S(1)}, bf16[4,96,512]{2,1,0:T(8,128)(2,1)S(1)}) fusion(bf16[4]{0:T(256)(128)(2,1)S(1)} %convert_bitcast_fusion, bf16[1,4,96,512]{3,2,1,0:T(8,128)(2,1)} %param.14, bf16[1,4,96,512]{3,2,1,0:T(8,128)(2,1)} %param.11), kind=kLoop, calls=%fused_computation.7 | loop fusion | flops 393216 | bytes 1572872 | tf_op jit(solution)/shard_map/mul | solution.py:508
  6.2 1.5 %layout.1 = (bf16[12,96,256]{2,1,0:T(8,128)(2,1)S(1)}, bf16[9,96,256]{2,1,0:T(8,128)(2,1)S(1)}, bf16[4,96,256]{2,1,0:T(8,128)(2,1)S(1)}, f32[3,8,256]{2,1,0:T(8,128)S(1)}) custom-call(s32[6,32]{1,0:T(8,128)S(1)} %concatenate.3.table, bf16[4,96,512]{2,1,0:T(8,128)(2,1)S(1)} %get-tuple-element.72.own_ref, ...), custom_call_target="tpu_custom_call" | custom-call | tf_op jit(solution)/shard_map/layout/pallas_call | solution.py:497
  8.4 1.0 %copy-done.1 = bf16[96,2592]{1,0:T(8,128)(2,1)S(1)} copy-done((bf16[96,2592]{1,0:T(8,128)(2,1)S(1)}, bf16[96,2592]{1,0:T(8,128)(2,1)}, u32[]{:S(2)}) %copy-start.1) | copy-done | bytes 497688
  9.4 1.0 %copy-done.2 = bf16[96,2592]{1,0:T(8,128)(2,1)S(1)} copy-done((bf16[96,2592]{1,0:T(8,128)(2,1)S(1)}, bf16[96,2592]{1,0:T(8,128)(2,1)}, u32[]{:S(2)}) %copy-start.2) | copy-done | bytes 497688
  11.4 5.4 %inner.1 = (bf16[9,896,256]{2,1,0:T(8,128)(2,1)S(1)}, f32[2,96,256]{2,1,0:T(8,128)S(1)}, f32[2,96,256]{2,1,0:T(8,128)S(1)}, f32[7,96,256]{2,1,0:T(8,128)S(1)}, b...) custom-call(s32[6,32]{1,0:T(8,128)S(1)} %concatenate.3.table, ...), custom_call_target="tpu_custom_call" | custom-call | flops 8589934592 | bytes 8388608 | tf_op jit(solution)/shard_map/inner/pallas_call | solution.py:512
  16.8 4.8 %outer.1 = (f32[4,256,128]{2,1,0:T(8,128)S(1)}, f32[4,256,128]{2,1,0:T(8,128)S(1)}, f32[1,96,256]{2,1,0:T(8,128)S(1)}, bf16[3,96,256]{2,1,0:T(8,128)(2,1)S(1)}, bf16[2,96,256]{2,1,0:T(8,128)(2,1)S(1)}) custom-call(s32[6,32]{1,0:T(8,128)S(1)} %concatenate.3.table, bf16[4,96,256]{2,1,0:T(8,128)(2,1)S(1)} %collective-permute-done.2.edge_ref, ...), custom_call_target="tpu_custom_call" | custom-call | flops 4294967296 | bytes 8388608 | tf_op jit(solution)/shard_map/outer/pallas_call | solution.py:539
  21.6 5.5 %backward.1 = (f32[4,256,128]{2,1,0:T(8,128)S(1)}, f32[4,256,128]{2,1,0:T(8,128)S(1)}) custom-call(s32[6,32]{1,0:T(8,128)S(1)} %concatenate.3.table, bf16[3,96,256]{2,1,0:T(8,128)(2,1)S(1)} %get-tuple-element.45.g_out_ref, bf16[7,96,256]{2,1,0:T(8,128)(2,1)S(1)} %get-tuple-element.40.g_in_ref, f32[1,96,256]{2,1,0:T(8,128)S(1)} %get-tuple-element.46.slope_out_ref, ...), custom_call_target="tpu_custom_call" | custom-call | flops 4294967296 | bytes 4194304 | tf_op jit(solution)/shard_map/backward/pallas_call | solution.py:559
  27.1 4.3 %collective-permute-start.4 = (f32[4,256,128]{2,1,0:T(8,128)S(1)}, f32[4,256,128]{2,1,0:T(8,128)S(1)}, u32[]{:S(2)}, u32[]{:S(2)}) collective-permute-start(f32[4,256,128]{2,1,0:T(8,128)S(1)} %get-tuple-element.50), channel_id=1, source_target_pairs={{0,4},{4,0},{8,12},{12,8},{16,20},{20,16},{24,28},{28,24},{1,5},{5... | collective-permute-start | bytes 1572872 | tf_op jit(solution)/shard_map/ppermute | solution.py:447
  31.5 1.5 %collective-permute-done.4 = f32[4,256,128]{2,1,0:T(8,128)S(1)} collective-permute-done((f32[4,256,128]{2,1,0:T(8,128)S(1)}, f32[4,256,128]{2,1,0:T(8,128)S(1)}, u32[]{:S(2)}, u32[]{:S(2)}) %collective-permute-start.4) | collective-permute-done | bytes 524320 | tf_op jit(solution)/shard_map/ppermute | solution.py:447
  33.9 1.6 %collective-permute-start.7 = (bf16[2,256,128]{2,1,0:T(8,128)(2,1)S(1)}, bf16[2,256,128]{2,1,0:T(8,128)(2,1)S(1)}, u32[]{:S(2)}, u32[]{:S(2)}) collective-permute-start(bf16[2,256,128]{2,1,0:T(8,128)(2,1)S(1)} %pad_maximum_fusion.1), channel_id=1, source_target_pairs={{0,16},{4,20},{8,24},{12,28},{16,0},{20,4},{24,8},{28,12},{1,17},{... | collective-permute-start | bytes 393224 | tf_op jit(solution)/shard_map/ppermute | solution.py:453
  36.0 1.6 %collective-permute-start.6 = (bf16[2,256,128]{2,1,0:T(8,128)(2,1)S(1)}, bf16[2,256,128]{2,1,0:T(8,128)(2,1)S(1)}, u32[]{:S(2)}, u32[]{:S(2)}) collective-permute-start(bf16[2,256,128]{2,1,0:T(8,128)(2,1)S(1)} %pad_maximum_fusion), channel_id=1, source_target_pairs={{0,24},{4,28},{8,16},{12,20},{16,8},{20,12},{24,0},{28,4},{1,25},{... | collective-permute-start | bytes 393224 | tf_op jit(solution)/shard_map/ppermute | solution.py:453
  37.6 2.1 %collective-permute-done.7 = bf16[2,256,128]{2,1,0:T(8,128)(2,1)S(1)} collective-permute-done((bf16[2,256,128]{2,1,0:T(8,128)(2,1)S(1)}, bf16[2,256,128]{2,1,0:T(8,128)(2,1)S(1)}, u32[]{:S(2)}, u32[]{:S(2)}) %collective-permute-start.7) | collective-permute-done | bytes 131104 | tf_op jit(solution)/shard_map/ppermute | solution.py:453
  39.7 2.2 %collective-permute-done.8 = bf16[2,256,128]{2,1,0:T(8,128)(2,1)S(1)} collective-permute-done((bf16[2,256,128]{2,1,0:T(8,128)(2,1)S(1)}, bf16[2,256,128]{2,1,0:T(8,128)(2,1)S(1)}, u32[]{:S(2)}, u32[]{:S(2)}) %collective-permute-start.8) | collective-permute-done | bytes 131104 | tf_op jit(solution)/shard_map/ppermute | solution.py:453
  41.9 1.9 %collective-permute-done.6 = bf16[2,256,128]{2,1,0:T(8,128)(2,1)S(1)} collective-permute-done((bf16[2,256,128]{2,1,0:T(8,128)(2,1)S(1)}, bf16[2,256,128]{2,1,0:T(8,128)(2,1)S(1)}, u32[]{:S(2)}, u32[]{:S(2)}) %collective-permute-start.6) | collective-permute-done | bytes 131104 | tf_op jit(solution)/shard_map/ppermute | solution.py:453
  43.9 1.6 %collective-permute-start.9 = (bf16[2,256,128]{2,1,0:T(8,128)(2,1)S(1)}, bf16[2,256,128]{2,1,0:T(8,128)(2,1)S(1)}, u32[]{:S(2)}, u32[]{:S(2)}) collective-permute-start(bf16[2,256,128]{2,1,0:T(8,128)(2,1)S(1)} %fusion.2), channel_id=1, source_target_pairs={{0,1},{1,0},{2,3},{3,2},{4,5},{5,4},{6,7},{7,6},{8,9},{9,8},{10,11... | collective-permute-start | bytes 393224 | tf_op jit(solution)/shard_map/ppermute | solution.py:458
  45.5 3.4 %collective-permute-done.9 = bf16[2,256,128]{2,1,0:T(8,128)(2,1)S(1)} collective-permute-done((bf16[2,256,128]{2,1,0:T(8,128)(2,1)S(1)}, bf16[2,256,128]{2,1,0:T(8,128)(2,1)S(1)}, u32[]{:S(2)}, u32[]{:S(2)}) %collective-permute-start.9) | collective-permute-done | bytes 131104 | tf_op jit(solution)/shard_map/ppermute | solution.py:458
  48.9 2.6 %collective-permute-start.10 = (bf16[2,256,128]{2,1,0:T(8,128)(2,1)S(1)}, bf16[2,256,128]{2,1,0:T(8,128)(2,1)S(1)}, u32[]{:S(2)}, u32[]{:S(2)}) collective-permute-start(bf16[2,256,128]{2,1,0:T(8,128)(2,1)S(1)} %add_convert_fusion.1), channel_id=1, source_target_pairs={{0,2},{1,3},{2,0},{3,1},{4,6},{5,7},{6,4},{7,5},{8,10},{9,11},{10,... | collective-permute-start | bytes 393224 | tf_op jit(solution)/shard_map/ppermute | solution.py:458
  51.6 1.0 %output.1 = (bf16[4,96,512]{2,1,0:T(8,128)(2,1)S(1)}, bf16[4,96,512]{2,1,0:T(8,128)(2,1)S(1)}) custom-call(s32[6,32]{1,0:T(8,128)S(1)} %concatenate.3.table, bf16[2,96,256]{2,1,0:T(8,128)(2,1)S(1)} %get-tuple-element.41.first_ref, bf16[6,96,256]{2,1,0:T(8,128)(2,1)S(1)} %get-tuple-element.42.second_ref, bf16[256,256]{1,0:T(8,128)(2,1)S(1)} %copy-done.3), custom_call_target="tpu_custom_call" | custom-call | flops 268435456 | bytes 2097152 | tf_op jit(solution)/shard_map/output/pallas_call | solution.py:576
  52.7 3.6 %collective-permute-done.10 = bf16[2,256,128]{2,1,0:T(8,128)(2,1)S(1)} collective-permute-done((bf16[2,256,128]{2,1,0:T(8,128)(2,1)S(1)}, bf16[2,256,128]{2,1,0:T(8,128)(2,1)S(1)}, u32[]{:S(2)}, u32[]{:S(2)}) %collective-permute-start.10) | collective-permute-done | bytes 131104 | tf_op jit(solution)/shard_map/ppermute | solution.py:458
  56.3 1.3 %collective-permute-start.13 = (bf16[2,256,128]{2,1,0:T(8,128)(2,1)S(1)}, bf16[2,256,128]{2,1,0:T(8,128)(2,1)S(1)}, u32[]{:S(2)}, u32[]{:S(2)}) collective-permute-start(bf16[2,256,128]{2,1,0:T(8,128)(2,1)S(1)} %add_convert_fusion.refs_0_), channel_id=1, source_target_pairs={{0,24},{4,28},{8,16},{12,20},{16,8},{20,12},{24,0},{28,4},{1,25},{... | collective-permute-start | bytes 393224 | tf_op jit(solution)/shard_map/ppermute | solution.py:463
  57.6 1.7 %collective-permute-start.12 = (bf16[2,256,128]{2,1,0:T(8,128)(2,1)S(1)}, bf16[2,256,128]{2,1,0:T(8,128)(2,1)S(1)}, u32[]{:S(2)}, u32[]{:S(2)}) collective-permute-start(bf16[2,256,128]{2,1,0:T(8,128)(2,1)S(1)} %add_convert_fusion.refs_0_), channel_id=1, source_target_pairs={{0,16},{4,20},{8,24},{12,28},{16,0},{20,4},{24,8},{28,12},{1,17},{... | collective-permute-start | bytes 393224 | tf_op jit(solution)/shard_map/ppermute | solution.py:463
  59.9 2.5 %collective-permute-done.13.refs_3_ = bf16[2,256,128]{2,1,0:T(8,128)(2,1)S(1)} collective-permute-done((bf16[2,256,128]{2,1,0:T(8,128)(2,1)S(1)}, bf16[2,256,128]{2,1,0:T(8,128)(2,1)S(1)}, u32[]{:S(2)}, u32[]{:S(2)}) %collective-permute-start.13) | collective-permute-done | bytes 131104 | tf_op jit(solution)/shard_map/ppermute | solution.py:463
  62.4 1.3 %collective-permute-done.12.refs_2_ = bf16[2,256,128]{2,1,0:T(8,128)(2,1)S(1)} collective-permute-done((bf16[2,256,128]{2,1,0:T(8,128)(2,1)S(1)}, bf16[2,256,128]{2,1,0:T(8,128)(2,1)S(1)}, u32[]{:S(2)}, u32[]{:S(2)}) %collective-permute-start.12) | collective-permute-done | bytes 131104 | tf_op jit(solution)/shard_map/ppermute | solution.py:463
  65.7 2.1 %gather.1 = (f32[96,2592]{1,0:T(8,128)}, f32[96,2592]{1,0:T(8,128)}, f32[1,96]{1,0:T(1,128)}, f32[1,96]{1,0:T(1,128)}) custom-call(s32[6,32]{1,0:T(8,128)S(1)} %concatenate.3.table, bf16[2,256,128]{2,1,0:T(8,128)(2,1)S(1)} %add_convert_fusion.refs_0_, bf16[2,256,128]{2,1,0:T(8,128)(2,1)S(1)} %collective-permute-done.11.refs_1_, ...), custom_call_target="tpu_custom_call" | custom-call | tf_op jit(solution)/shard_map/gather/pallas_call | solution.py:590
  (49 shorter events, 10.2 us)
Async XLA Ops:
  0.6 4.6 %collective-permute-start.1 = (bf16[4,96,512]{2,1,0:T(8,128)(2,1)}, bf16[4,96,512]{2,1,0:T(8,128)(2,1)S(1)}, u32[]{:S(2)}, u32[]{:S(2)}) collective-permute-start(bf16[4,96,512]{2,1,0:T(8,128)(2,1)} %bitcast.17), channel_id=1, source_target_pairs={{0,4},{4,0},{8,12},{12,8},{16,20},{20,16},{24,28},{28,24},{1,5},{5... | collective-permute-start | bytes 1179656 | tf_op jit(solution)/shard_map/ppermute | solution.py:477
  1.1 4.1 %collective-permute-start = (bf16[4,96,512]{2,1,0:T(8,128)(2,1)}, bf16[4,96,512]{2,1,0:T(8,128)(2,1)S(1)}, u32[]{:S(2)}, u32[]{:S(2)}) collective-permute-start(bf16[4,96,512]{2,1,0:T(8,128)(2,1)} %bitcast.18), channel_id=1, source_target_pairs={{0,4},{4,0},{8,12},{12,8},{16,20},{20,16},{24,28},{28,24},{1,5},{5... | collective-permute-start | bytes 1179656 | tf_op jit(solution)/shard_map/ppermute | solution.py:476
  5.3 0.9 %copy-start = (bf16[256,256]{1,0:T(8,128)(2,1)S(1)}, bf16[256,256]{1,0:T(8,128)(2,1)}, u32[]{:S(2)}) copy-start(bf16[256,256]{1,0:T(8,128)(2,1)} %constant.20.clone.move_ref) | copy-start | bytes 393220
  7.7 9.1 %collective-permute-start.2 = (bf16[4,96,256]{2,1,0:T(8,128)(2,1)S(1)}, bf16[4,96,256]{2,1,0:T(8,128)(2,1)S(1)}, u32[]{:S(2)}, u32[]{:S(2)}) collective-permute-start(bf16[4,96,256]{2,1,0:T(8,128)(2,1)S(1)} %get-tuple-element.31), channel_id=1, source_target_pairs={{4,8},{12,16},{20,24},{8,4},{16,12},{24,20},{5,9},{13,17},{21,25},... | collective-permute-start | bytes 589832 | tf_op jit(solution)/shard_map/ppermute | solution.py:509
  8.4 1.0 %copy-start.1 = (bf16[96,2592]{1,0:T(8,128)(2,1)S(1)}, bf16[96,2592]{1,0:T(8,128)(2,1)}, u32[]{:S(2)}) copy-start(bf16[96,2592]{1,0:T(8,128)(2,1)} %w1_ref.1) | copy-start | bytes 1492996
  9.4 1.0 %copy-start.2 = (bf16[96,2592]{1,0:T(8,128)(2,1)S(1)}, bf16[96,2592]{1,0:T(8,128)(2,1)}, u32[]{:S(2)}) copy-start(bf16[96,2592]{1,0:T(8,128)(2,1)} %w2_ref.1) | copy-start | bytes 1492996
  10.5 0.9 %copy-start.4 = (bf16[9,16,256]{2,1,0:T(8,128)(2,1)S(1)}, bf16[9,16,256]{2,1,0:T(8,128)(2,1)}, u32[]{:S(2)}) copy-start(bf16[9,16,256]{2,1,0:T(8,128)(2,1)} %constant.19.clone.masks_ref) | copy-start | bytes 221188
  11.4 5.4 %copy-start.5 = (bf16[9,16,256]{2,1,0:T(8,128)(2,1)S(1)}, bf16[9,16,256]{2,1,0:T(8,128)(2,1)}, u32[]{:S(2)}) copy-start(bf16[9,16,256]{2,1,0:T(8,128)(2,1)} %constant.19.clone.masks_ref) | copy-start | bytes 221188
  27.1 24.5 %copy-start.3 = (bf16[256,256]{1,0:T(8,128)(2,1)S(1)}, bf16[256,256]{1,0:T(8,128)(2,1)}, u32[]{:S(2)}) copy-start(bf16[256,256]{1,0:T(8,128)(2,1)} %constant.21.clone.back_ref) | copy-start | bytes 393220
  27.1 5.9 %collective-permute-start.4 = (f32[4,256,128]{2,1,0:T(8,128)S(1)}, f32[4,256,128]{2,1,0:T(8,128)S(1)}, u32[]{:S(2)}, u32[]{:S(2)}) collective-permute-start(f32[4,256,128]{2,1,0:T(8,128)S(1)} %get-tuple-element.50), channel_id=1, source_target_pairs={{0,4},{4,0},{8,12},{12,8},{16,20},{20,16},{24,28},{28,24},{1,5},{5... | collective-permute-start | bytes 1572872 | tf_op jit(solution)/shard_map/ppermute | solution.py:447
  31.5 2.3 %collective-permute-start.5 = (f32[4,256,128]{2,1,0:T(8,128)S(1)}, f32[4,256,128]{2,1,0:T(8,128)S(1)}, u32[]{:S(2)}, u32[]{:S(2)}) collective-permute-start(f32[4,256,128]{2,1,0:T(8,128)S(1)} %get-tuple-element.52), channel_id=1, source_target_pairs={{0,4},{4,0},{8,12},{12,8},{16,20},{20,16},{24,28},{28,24},{1,5},{5... | collective-permute-start | bytes 1572872 | tf_op jit(solution)/shard_map/ppermute | solution.py:558
  33.9 5.8 %collective-permute-start.7 = (bf16[2,256,128]{2,1,0:T(8,128)(2,1)S(1)}, bf16[2,256,128]{2,1,0:T(8,128)(2,1)S(1)}, u32[]{:S(2)}, u32[]{:S(2)}) collective-permute-start(bf16[2,256,128]{2,1,0:T(8,128)(2,1)S(1)} %pad_maximum_fusion.1), channel_id=1, source_target_pairs={{0,16},{4,20},{8,24},{12,28},{16,0},{20,4},{24,8},{28,12},{1,17},{... | collective-permute-start | bytes 393224 | tf_op jit(solution)/shard_map/ppermute | solution.py:453
  35.5 6.4 %collective-permute-start.8 = (bf16[2,256,128]{2,1,0:T(8,128)(2,1)S(1)}, bf16[2,256,128]{2,1,0:T(8,128)(2,1)S(1)}, u32[]{:S(2)}, u32[]{:S(2)}) collective-permute-start(bf16[2,256,128]{2,1,0:T(8,128)(2,1)S(1)} %pad_maximum_fusion.2), channel_id=1, source_target_pairs={{0,8},{4,12},{8,0},{12,4},{16,24},{20,28},{24,16},{28,20},{1,9},{5... | collective-permute-start | bytes 393224 | tf_op jit(solution)/shard_map/ppermute | solution.py:453
  36.0 7.8 %collective-permute-start.6 = (bf16[2,256,128]{2,1,0:T(8,128)(2,1)S(1)}, bf16[2,256,128]{2,1,0:T(8,128)(2,1)S(1)}, u32[]{:S(2)}, u32[]{:S(2)}) collective-permute-start(bf16[2,256,128]{2,1,0:T(8,128)(2,1)S(1)} %pad_maximum_fusion), channel_id=1, source_target_pairs={{0,24},{4,28},{8,16},{12,20},{16,8},{20,12},{24,0},{28,4},{1,25},{... | collective-permute-start | bytes 393224 | tf_op jit(solution)/shard_map/ppermute | solution.py:453
  43.9 5.0 %collective-permute-start.9 = (bf16[2,256,128]{2,1,0:T(8,128)(2,1)S(1)}, bf16[2,256,128]{2,1,0:T(8,128)(2,1)S(1)}, u32[]{:S(2)}, u32[]{:S(2)}) collective-permute-start(bf16[2,256,128]{2,1,0:T(8,128)(2,1)S(1)} %fusion.2), channel_id=1, source_target_pairs={{0,1},{1,0},{2,3},{3,2},{4,5},{5,4},{6,7},{7,6},{8,9},{9,8},{10,11... | collective-permute-start | bytes 393224 | tf_op jit(solution)/shard_map/ppermute | solution.py:458
  48.9 7.3 %collective-permute-start.10 = (bf16[2,256,128]{2,1,0:T(8,128)(2,1)S(1)}, bf16[2,256,128]{2,1,0:T(8,128)(2,1)S(1)}, u32[]{:S(2)}, u32[]{:S(2)}) collective-permute-start(bf16[2,256,128]{2,1,0:T(8,128)(2,1)S(1)} %add_convert_fusion.1), channel_id=1, source_target_pairs={{0,2},{1,3},{2,0},{3,1},{4,6},{5,7},{6,4},{7,5},{8,10},{9,11},{10,... | collective-permute-start | bytes 393224 | tf_op jit(solution)/shard_map/ppermute | solution.py:458
  52.6 11.7 %collective-permute-start.3 = (bf16[4,96,512]{2,1,0:T(8,128)(2,1)S(1)}, bf16[4,96,512]{2,1,0:T(8,128)(2,1)S(1)}, u32[]{:S(2)}, u32[]{:S(2)}) collective-permute-start(bf16[4,96,512]{2,1,0:T(8,128)(2,1)S(1)} %get-tuple-element.44), channel_id=1, source_target_pairs={{0,4},{4,0},{8,12},{12,8},{16,20},{20,16},{24,28},{28,24},{1,5},{5... | collective-permute-start | bytes 1179656 | tf_op jit(solution)/shard_map/ppermute | solution.py:586
  56.3 6.0 %collective-permute-start.13 = (bf16[2,256,128]{2,1,0:T(8,128)(2,1)S(1)}, bf16[2,256,128]{2,1,0:T(8,128)(2,1)S(1)}, u32[]{:S(2)}, u32[]{:S(2)}) collective-permute-start(bf16[2,256,128]{2,1,0:T(8,128)(2,1)S(1)} %add_convert_fusion.refs_0_), channel_id=1, source_target_pairs={{0,24},{4,28},{8,16},{12,20},{16,8},{20,12},{24,0},{28,4},{1,25},{... | collective-permute-start | bytes 393224 | tf_op jit(solution)/shard_map/ppermute | solution.py:463
  57.6 6.0 %collective-permute-start.12 = (bf16[2,256,128]{2,1,0:T(8,128)(2,1)S(1)}, bf16[2,256,128]{2,1,0:T(8,128)(2,1)S(1)}, u32[]{:S(2)}, u32[]{:S(2)}) collective-permute-start(bf16[2,256,128]{2,1,0:T(8,128)(2,1)S(1)} %add_convert_fusion.refs_0_), channel_id=1, source_target_pairs={{0,16},{4,20},{8,24},{12,28},{16,0},{20,4},{24,8},{28,12},{1,17},{... | collective-permute-start | bytes 393224 | tf_op jit(solution)/shard_map/ppermute | solution.py:463
  59.3 5.0 %collective-permute-start.11 = (bf16[2,256,128]{2,1,0:T(8,128)(2,1)S(1)}, bf16[2,256,128]{2,1,0:T(8,128)(2,1)S(1)}, u32[]{:S(2)}, u32[]{:S(2)}) collective-permute-start(bf16[2,256,128]{2,1,0:T(8,128)(2,1)S(1)} %add_convert_fusion.refs_0_), channel_id=1, source_target_pairs={{0,8},{4,12},{8,0},{12,4},{16,24},{20,28},{24,16},{28,20},{1,9},{5... | collective-permute-start | bytes 393224 | tf_op jit(solution)/shard_map/ppermute | solution.py:463
  59.9 5.2 %collective-permute-start.14 = (bf16[2,256,128]{2,1,0:T(8,128)(2,1)S(1)}, bf16[2,256,128]{2,1,0:T(8,128)(2,1)S(1)}, u32[]{:S(2)}, u32[]{:S(2)}) collective-permute-start(bf16[2,256,128]{2,1,0:T(8,128)(2,1)S(1)} %add_convert_fusion.refs_0_), channel_id=1, source_target_pairs={{0,4},{4,0},{8,12},{12,8},{16,20},{20,16},{24,28},{28,24},{1,5},{5... | collective-permute-start | bytes 393224 | tf_op jit(solution)/shard_map/ppermute | solution.py:464
  62.4 2.8 %collective-permute-start.17 = (bf16[2,256,128]{2,1,0:T(8,128)(2,1)S(1)}, bf16[2,256,128]{2,1,0:T(8,128)(2,1)S(1)}, u32[]{:S(2)}, u32[]{:S(2)}) collective-permute-start(bf16[2,256,128]{2,1,0:T(8,128)(2,1)S(1)} %collective-permute-done.13.refs_3_), channel_id=1, source_target_pairs={{0,4},{4,0},{8,12},{12,8},{16,20},{20,16},{24,28},{28,24},{1,5},{5... | collective-permute-start | bytes 393224 | tf_op jit(solution)/shard_map/ppermute | solution.py:464
  63.7 1.5 %collective-permute-start.16 = (bf16[2,256,128]{2,1,0:T(8,128)(2,1)S(1)}, bf16[2,256,128]{2,1,0:T(8,128)(2,1)S(1)}, u32[]{:S(2)}, u32[]{:S(2)}) collective-permute-start(bf16[2,256,128]{2,1,0:T(8,128)(2,1)S(1)} %collective-permute-done.12.refs_2_), channel_id=1, source_target_pairs={{0,4},{4,0},{8,12},{12,8},{16,20},{20,16},{24,28},{28,24},{1,5},{5... | collective-permute-start | bytes 393224 | tf_op jit(solution)/shard_map/ppermute | solution.py:464
  64.3 1.3 %collective-permute-start.15 = (bf16[2,256,128]{2,1,0:T(8,128)(2,1)S(1)}, bf16[2,256,128]{2,1,0:T(8,128)(2,1)S(1)}, u32[]{:S(2)}, u32[]{:S(2)}) collective-permute-start(bf16[2,256,128]{2,1,0:T(8,128)(2,1)S(1)} %collective-permute-done.11.refs_1_), channel_id=1, source_target_pairs={{0,4},{4,0},{8,12},{12,8},{16,20},{20,16},{24,28},{28,24},{1,5},{5... | collective-permute-start | bytes 393224 | tf_op jit(solution)/shard_map/ppermute | solution.py:464

commit v2 on v1

--- a/solution.py
+++ b/solution.py
@@ -1,6 +1,5 @@
 import jax
 import jax.numpy as jnp
-import numpy as np
 from jax import lax
 from jax.experimental import pallas as pl
 from jax.experimental.pallas import tpu as pltpu
@@ -18,25 +17,19 @@
 BF16 = jnp.bfloat16
 
 
-def spread_matrix():
-    move = np.zeros((256, 256), np.float32)
-    for z in range(2):
-        for p in range(2):
-            for q in range(8):
-                for r in range(8):
-                    move[z * 128 + p * 64 + q * 8 + r, p * 128 + q * 16 + z * 8 + r] = 1.0
-    return move
-
-
-def tap_masks():
-    masks = np.zeros((9, 16, 256), np.float32)
-    for b in range(3):
-        for c in range(3):
-            for q in range(16):
-                for r in range(16):
-                    inside = 0 <= q + b - 1 < 16 and 0 <= r + c - 1 < 16
-                    masks[b * 3 + c, :, q * 16 + r] = float(inside)
-    return masks
+def spread_matrix(back=False):
+    near = lax.broadcasted_iota(jnp.int32, (256, 256), 1 if back else 0)
+    far = lax.broadcasted_iota(jnp.int32, (256, 256), 0 if back else 1)
+    source = ((far >> 3) & 1) * 128 + (far >> 7) * 64 + ((far >> 4) & 7) * 8 + (far & 7)
+    return jnp.where(near == source, 1.0, 0.0).astype(BF16)
+
+
+def fill_masks(masks):
+    lane = lax.broadcasted_iota(jnp.int32, (16, PLANE), 1)
+    for k in range(9):
+        q, r = (lane >> 4) + (k // 3 - 1), (lane & 15) + (k % 3 - 1)
+        inside = (q >= 0) & (q < 16) & (r >= 0) & (r < 16)
+        masks[k] = jnp.where(inside, 1.0, 0.0).astype(BF16)
 
 
 def write_taps(dst, plane, masks_ref):
@@ -52,6 +45,10 @@
         dst[k * channels : (k + 1) * channels, :] = moved
 
 
+def space_index(table, count):
+    return jnp.clip(table[DEVICE, 0] & 255, 0, count - 1)
+
+
 def slot_place(table, slot, pair_slots):
     shift = pair_slots.bit_length() - 1
     up = table[UP, slot]
@@ -124,43 +121,45 @@
     flat[TILES * channels :, :] = jnp.zeros((ROWS - TILES * channels, 128), F32)
 
 
-def split_tiles(keep_ref, send_ref, flat, me):
-    chips, rows = keep_ref.shape[0], keep_ref.shape[1]
-    core, chip = me & 1, me >> 1
-    for r in range(chips):
-        at = jnp.clip(chip ^ r, 0, chips - 1) * rows
-        here = at + jnp.where(core == 1, chips * rows, 0)
-        there = at + jnp.where(core == 1, 0, chips * rows)
+def chunk_place(table, r, chunks):
+    value = table[DEVICE, 0]
+    chips = chunks // 2
+    at = (((value >> 8) & 1) ^ (r // chips)) * chips + (((value & 255) >> 1) ^ (r % chips))
+    return jnp.clip(at, 0, chunks - 1)
+
+
+def split_tiles(keep_ref, send_ref, flat, table):
+    chunks, rows = keep_ref.shape[0], keep_ref.shape[1]
+    even = (table[DEVICE, 0] & 1) == 0
+    for r in range(chunks):
+        at = chunk_place(table, r, chunks) * rows
+        here = at + jnp.where(even, 0, chunks * rows)
+        there = at + jnp.where(even, chunks * rows, 0)
         keep_ref[r] = flat[pl.ds(pl.multiple_of(here, rows), rows), :]
-        send_ref[r] = flat[pl.ds(pl.multiple_of(there, rows), rows), :]
+        send_ref[r] = flat[pl.ds(pl.multiple_of(there, rows), rows), :].astype(BF16)
 
 
 def layout_kernel(
-    table, own_ref, pair_ref, cot_own_ref, cot_pair_ref, move_ref,
+    table, own_ref, pair_ref, cot_pair_ref,
     x_ref, cot_ref, edge_ref, mask_ref, bricks, cots,
 ):
     slots, channels = pair_ref.shape[0], pair_ref.shape[1]
     all_slots = table.shape[1]
-    me = jnp.clip(table[DEVICE, 0], 0, all_slots // slots - 1)
+    me = space_index(table, all_slots // slots)
     core = me & 1
     even = core == 0
 
     live = [[jnp.float32(0)] * 4 for _ in range(2)]
     beyond = [jnp.float32(0)] * 4
-    for device, source, cot_source in (
-        (me, own_ref, cot_own_ref), (me ^ 1, pair_ref, cot_pair_ref),
-    ):
+    for device in (me, me ^ 1):
         for s in range(slots):
             slot = jnp.clip(device * slots + s, 0, all_slots - 1)
             parity, place = slot_place(table, slot, 2 * slots)
             alive = table[LIVE, slot].astype(F32)
-            if source is own_ref:
-                bricks[parity, place] = source[s]
-                cots[parity, place] = cot_source[s]
-            else:
-                scale = jnp.full((channels, CELLS), alive, F32).astype(BF16)
-                bricks[parity, place] = source[s] * scale
-                cots[parity, place] = cot_source[s] * scale
+            scale = jnp.full((channels, CELLS), alive, F32).astype(BF16)
+            own = device is me
+            bricks[parity, place] = (own_ref[s] if own else pair_ref[s]) * scale
+            cots[parity, place] = (own_ref[slots + s] if own else cot_pair_ref[s]) * scale
             outer = jnp.where(even, table[DOWN, slot], table[UP, slot])
             alive_outer = table[LIVE, jnp.clip(outer, 0, all_slots - 1)].astype(F32)
             alive_outer = jnp.where(outer >= 0, alive_outer, 0.0)
@@ -174,7 +173,7 @@
     mask_ref[1] = lane_mask([jnp.where(even, live[0][k], live[1][k]) for k in range(4)])
     mask_ref[2] = lane_mask([jnp.where(even, live[1][k], live[0][k]) for k in range(4)])
 
-    move = move_ref[...]
+    move = spread_matrix()
     mine = jnp.where(even, 0, 1)
 
     def spread(left, right):
@@ -209,9 +208,9 @@
     edge_ref[3] = cot_ref[0]
 
 
-def tap_weights(out_ref, weight_ref, wide, even):
-    channels, width = weight_ref.shape
-    wide[:, :width] = weight_ref[...]
+def tap_weights(out_ref, weight, wide, even):
+    channels, width = weight.shape
+    wide[:, :width] = weight
     lane = lax.broadcasted_iota(jnp.int32, (channels, 128), 1)
     for a, (tile, moved) in enumerate(((0, 0), (6, 96), (13, 64))):
         span = wide[:, tile * 128 : (tile + 8) * 128].astype(F32)
@@ -262,13 +261,14 @@
 
 
 def inner_kernel(
-    table, x_ref, cot_ref, layer_mask, w1_ref, w2_ref, bias_ref, masks_ref,
+    table, x_ref, cot_ref, layer_mask, weight_ref, bias_ref,
     taps_ref, one_ref, two_ref, slope_ref, g_ref, out_ref, w1_taps, w2_taps, w2_back,
-    wide, xc, acc_one, acc_two,
+    wide, xc, acc_one, acc_two, masks_ref,
 ):
     channels = x_ref.shape[1]
     even = (table[DEVICE, 0] & 1) == 0
-    tap_weights(w1_taps, w1_ref, wide, even)
+    fill_masks(masks_ref)
+    tap_weights(w1_taps, weight_ref[:channels, :], wide, even)
     bias_one, bias_two = column(bias_ref[0:1]), column(bias_ref[1:2])
     ones = jnp.ones((KDIM - 9 * channels, PLANE), BF16)
     for k in range(2):
@@ -284,7 +284,7 @@
                 write_taps(xc.at[1 - (p & 1)], x_ref[p + 1], masks_ref)
             add_planes(acc_one, p + 1, product, fresh=(0, 1, 2) if p == 0 else (p + 2,))
         if p == 1:
-            tap_weights(w2_taps, w2_ref, wide, even)
+            tap_weights(w2_taps, weight_ref[channels:, :], wide, even)
         if p == 3:
             back_weights(w2_back, w2_taps)
         q = p - 2
@@ -309,13 +309,14 @@
 
 
 def outer_kernel(
-    table, edge_ref, cot_ref, layer_mask, w1_taps, w2_taps, bias_ref, masks_ref,
+    table, edge_ref, cot_ref, layer_mask, w1_taps, w2_taps, bias_ref,
     taps_ref, one_ref, two_ref, g_in_ref,
     keep_ref, send_ref, slope_ref, g_ref, out_ref,
-    xc, hc, acc_one, acc_two, total, flat,
+    xc, hc, acc_one, acc_two, total, flat, masks_ref,
 ):
     channels = cot_ref.shape[1]
-    me = jnp.clip(table[DEVICE, 0], 0, 2**15)
+    even = (table[DEVICE, 0] & 1) == 0
+    fill_masks(masks_ref)
     bias_one, bias_two = column(bias_ref[0:1]), column(bias_ref[1:2])
     ones = jnp.ones((KDIM - 9 * channels, PLANE), BF16)
     for k in range(3):
@@ -347,18 +348,18 @@
         return hc[q + 2] if q < 1 else taps_ref[q - 1]
 
     weight_products(total, grads, taps)
-    write_tiles(flat, total, channels, (me & 1) == 0)
-    split_tiles(keep_ref, send_ref, flat, me)
-
-
-def output_kernel(table, first_ref, second_ref, back_ref, keep_ref, send_ref, outs, bricks):
+    write_tiles(flat, total, channels, even)
+    split_tiles(keep_ref, send_ref, flat, table)
+
+
+def output_kernel(table, first_ref, second_ref, keep_ref, send_ref, outs, bricks):
     slots, channels = keep_ref.shape[0], keep_ref.shape[1]
-    me = jnp.clip(table[DEVICE, 0], 0, table.shape[1] // slots - 1)
+    me = space_index(table, table.shape[1] // slots)
     core = me & 1
     even = core == 0
     outs[:2] = first_ref[...]
     outs[2:] = second_ref[...]
-    back = back_ref[...]
+    back = spread_matrix(True)
     for y in range(2):
         row = slice(y * 128, (y + 1) * 128)
         for j in range(4):
@@ -378,11 +379,12 @@
 
 
 def backward_kernel(
-    table, g_out_ref, g_in_ref, slope_out_ref, slope_in_ref, x_ref, edge_ref, w2_back, masks_ref,
-    keep_ref, send_ref, gc, xc, acc, grad, total, flat,
+    table, g_out_ref, g_in_ref, slope_out_ref, slope_in_ref, x_ref, edge_ref, w2_back,
+    keep_ref, send_ref, gc, xc, acc, grad, total, flat, masks_ref,
 ):
     channels = x_ref.shape[1]
-    me = jnp.clip(table[DEVICE, 0], 0, 2**15)
+    even = (table[DEVICE, 0] & 1) == 0
+    fill_masks(masks_ref)
     ones = jnp.ones((KDIM - 9 * channels, PLANE), BF16)
     for k in range(2):
         gc[k, 9 * channels :, :] = ones
@@ -406,22 +408,21 @@
             slope = slope_out_ref[0] if q == 0 else slope_in_ref[q - 1]
             grad[q] = (acc[q + 2] * slope).astype(BF16)
     weight_products(total, lambda q: grad[q], lambda q: xc[q + 1])
-    write_tiles(flat, total, channels, (me & 1) == 0)
-    split_tiles(keep_ref, send_ref, flat, me)
+    write_tiles(flat, total, channels, even)
+    split_tiles(keep_ref, send_ref, flat, table)
 
 
 def gather_kernel(table, *refs):
-    chips = (len(refs) - 5) // 2
-    w_one_ref, w_two_ref, b_one_ref, b_two_ref, flat = refs[2 * chips :]
+    chunks = (len(refs) - 5) // 2
+    w_one_ref, w_two_ref, b_one_ref, b_two_ref, flat = refs[2 * chunks :]
     rows = refs[0].shape[1]
     channels = w_one_ref.shape[0]
-    me = jnp.clip(table[DEVICE, 0], 0, 2 * chips - 1)
-    core, chip = me & 1, me >> 1
+    core = table[DEVICE, 0] & 1
     for half in range(2):
-        base = jnp.where(core == half, 0, chips * rows)
-        for r in range(chips):
-            at = base + jnp.clip(chip ^ r, 0, chips - 1) * rows
-            flat[:, pl.ds(pl.multiple_of(at, rows), rows), :] = refs[half * chips + r][...]
+        base = jnp.where(core == half, 0, chunks * rows)
+        for r in range(chunks):
+            at = base + chunk_place(table, r, chunks) * rows
+            flat[:, pl.ds(pl.multiple_of(at, rows), rows), :] = refs[half * chunks + r][...]
     for n, (weight, bias) in enumerate(((w_one_ref, b_one_ref), (w_two_ref, b_two_ref))):
         for k in range(TILES - 1):
             tile = flat[n, k * channels : (k + 1) * channels, :]
@@ -439,28 +440,39 @@
     return pltpu.CompilerParams(vmem_limit_bytes=mebibytes * 2**20)
 
 
-def shared_sum(keeps, sends, send_two_done):
-    chips = keeps[0].shape[0]
-    count = 2 * chips
+def shared_sum(keeps, sends):
+    chunks = keeps[0].shape[0]
+    chips = chunks // 2
+    count = lax.axis_size("space")
     volumes = lax.axis_size("dp")
     swap = [(d, d ^ 1) for d in range(count)]
-    halves = [keeps[0] + lax.ppermute(sends[0], "space", swap)]
-    halves.append(keeps[1] + send_two_done)
+
+    def hop(r):
+        space, volume = 2 * (r % chips), r // chips
+        return [
+            (d * volumes + v, (d ^ space) * volumes + (v ^ volume))
+            for d in range(count)
+            for v in range(volumes)
+        ]
+
+    order = sorted(range(1, chunks), key=lambda r: -bin(r).count("1"))
+    halves = [
+        keep + lax.ppermute(send, "space", swap).astype(F32) for keep, send in zip(keeps, sends)
+    ]
     total = jnp.stack([half[0] for half in halves])
-    for r in range(chips - 1, 0, -1):
+    for r in order:
         part = jnp.stack([half[r] for half in halves]).astype(BF16)
-        hop = [(d, d ^ (2 * r)) for d in range(count)]
-        total = total + lax.ppermute(part, "space", hop).astype(F32)
+        total = total + lax.ppermute(part, ("space", "dp"), hop(r)).astype(F32)
     total = total.astype(BF16)
-    step = 1
+    step = 2
     while step < volumes:
-        hop = [(d, d ^ step) for d in range(volumes)]
-        moved = lax.ppermute(total, "dp", hop)
+        moved = lax.ppermute(total, "dp", [(v, v ^ step) for v in range(volumes)])
         total = (total.astype(F32) + moved.astype(F32)).astype(BF16)
         step *= 2
-    parts = [total]
-    for r in range(chips - 1, 0, -1):
-        parts.insert(1, lax.ppermute(total, "space", [(d, d ^ (2 * r)) for d in range(count)]))
+    parts = {0: total}
+    for r in order:
+        parts[r] = lax.ppermute(total, ("space", "dp"), hop(r))
+    parts = [parts[r] for r in range(chunks)]
     return parts + [lax.ppermute(part, "space", swap) for part in parts]
 
 
@@ -475,14 +487,12 @@
     hop = [(d, d + 1) for d in range(1, count - 1, 2)] + [(d, d - 1) for d in range(2, count, 2)]
     pair_volume = lax.ppermute(volume, "space", swap)
     pair_cot = lax.ppermute(cotangent, "space", swap)
-    move = spread_matrix()
-    masks = jnp.asarray(tap_masks(), BF16)
     biases = jnp.stack([bias_one, bias_two])
-    near = neighbours[0].T
-    table = [near[k : k + 1] for k in OFFSETS]
-    table = jnp.concatenate([*table, active, jnp.full_like(active, me)], axis=0)
-    alive = lax.dynamic_slice_in_dim(active[0], me * slots, slots, 0)
-    alive = alive.astype(BF16)[:, None, None]
+    weights = jnp.concatenate([weight_one, weight_two], axis=0)
+    own = jnp.concatenate([volume, cotangent], axis=0)
+    device = me + 256 * lax.axis_index("dp").astype(jnp.int32)
+    table = [neighbours[:, :, k] for k in OFFSETS]
+    table = jnp.concatenate([*table, active, jnp.full_like(active, device)], axis=0)
 
     def planes(number, dtype=BF16):
         return jax.ShapeDtypeStruct((number, channels, PLANE), dtype)
@@ -497,7 +507,7 @@
     x_planes, cot_planes, edge, layer_mask = pl.pallas_call(
         layout_kernel,
         out_shape=(planes(12), planes(9), planes(4), jax.ShapeDtypeStruct((3, 8, PLANE), F32)),
-        in_specs=[SMEM] + [VMEM] * 5,
+        in_specs=[SMEM] + [VMEM] * 3,
         out_specs=(VMEM,) * 4,
         scratch_shapes=[
             pltpu.VMEM((2, *bricks), BF16),
@@ -505,10 +515,10 @@
         ],
         compiler_params=vmem(8),
         name="layout",
-    )(table, volume * alive, pair_volume, cotangent * alive, pair_cot, jnp.asarray(move, BF16))
+    )(table, own, pair_volume, pair_cot)
     outer = lax.ppermute(edge, "space", hop)
 
-    weights = jax.ShapeDtypeStruct((3, channels, KDIM), BF16)
+    rearranged = jax.ShapeDtypeStruct((3, channels, KDIM), BF16)
     taps, one, two, slope_in, g_in, out_in, w1, w2, w2_back = pl.pallas_call(
         inner_kernel,
         out_shape=(
@@ -518,28 +528,30 @@
             planes(7, F32),
             planes(7),
             planes(6),
-            weights,
-            weights,
-            weights,
+            rearranged,
+            rearranged,
+            rearranged,
         ),
-        in_specs=[SMEM] + [VMEM] * 7,
+        in_specs=[SMEM] + [VMEM] * 5,
         out_specs=(VMEM,) * 9,
         scratch_shapes=[
             pltpu.VMEM((channels, 21 * 128), BF16),
             tap_space(2),
             plane_space(13, F32),
             plane_space(11, F32),
+            pltpu.VMEM((9, 16, PLANE), BF16),
         ],
         compiler_params=vmem(20),
         cost_estimate=pl.CostEstimate(flops=2**33, bytes_accessed=2**23, transcendentals=2**20),
         name="inner",
-    )(table, x_planes, cot_planes, layer_mask, weight_one, weight_two, biases, masks)
-
-    half = jax.ShapeDtypeStruct((chips, ROWS // count, 128), F32)
+    )(table, x_planes, cot_planes, layer_mask, weights, biases)
+
+    chunks = (2 * chips, ROWS // (4 * chips), 128)
+    kept, sent = jax.ShapeDtypeStruct(chunks, F32), jax.ShapeDtypeStruct(chunks, BF16)
     keep_two, send_two, slope_out, g_out, out_out = pl.pallas_call(
         outer_kernel,
-        out_shape=(half, half, planes(1, F32), planes(3), planes(2)),
-        in_specs=[SMEM] + [VMEM] * 11,
+        out_shape=(kept, sent, planes(1, F32), planes(3), planes(2)),
+        in_specs=[SMEM] + [VMEM] * 10,
         out_specs=(VMEM,) * 5,
         scratch_shapes=[
             tap_space(3),
@@ -548,18 +560,18 @@
             plane_space(3, F32),
             pltpu.VMEM((3 * channels, KDIM), F32),
             pltpu.VMEM((ROWS, 128), F32),
+            pltpu.VMEM((9, 16, PLANE), BF16),
         ],
         compiler_params=vmem(16),
         cost_estimate=pl.CostEstimate(flops=2**32, bytes_accessed=2**23, transcendentals=2**18),
         name="outer",
     )(
-        table, outer, cot_planes, layer_mask, w1, w2, biases, masks, taps, one, two, g_in,
+        table, outer, cot_planes, layer_mask, w1, w2, biases, taps, one, two, g_in,
     )
-    got_two = lax.ppermute(send_two, "space", swap)
     keep_one, send_one = pl.pallas_call(
         backward_kernel,
-        out_shape=(half, half),
-        in_specs=[SMEM] + [VMEM] * 8,
+        out_shape=(kept, sent),
+        in_specs=[SMEM] + [VMEM] * 7,
         out_specs=(VMEM,) * 2,
         scratch_shapes=[
             tap_space(2),
@@ -568,23 +580,24 @@
             plane_space(8),
             pltpu.VMEM((3 * channels, KDIM), F32),
             pltpu.VMEM((ROWS, 128), F32),
+            pltpu.VMEM((9, 16, PLANE), BF16),
         ],
         compiler_params=vmem(20),
         cost_estimate=pl.CostEstimate(flops=2**32, bytes_accessed=2**22, transcendentals=0),
         name="backward",
-    )(table, g_out, g_in, slope_out, slope_in, x_planes, outer, w2_back, masks)
+    )(table, g_out, g_in, slope_out, slope_in, x_planes, outer, w2_back)
     keep, send = pl.pallas_call(
         output_kernel,
         out_shape=(jax.ShapeDtypeStruct(bricks, BF16),) * 2,
-        in_specs=[SMEM] + [VMEM] * 3,
+        in_specs=[SMEM] + [VMEM] * 2,
         out_specs=(VMEM,) * 2,
         scratch_shapes=[plane_space(8), pltpu.VMEM(bricks, BF16)],
         compiler_params=vmem(8),
         cost_estimate=pl.CostEstimate(flops=2**28, bytes_accessed=2**21, transcendentals=0),
         name="output",
-    )(table, out_out, out_in, jnp.asarray(move.T, BF16))
+    )(table, out_out, out_in)
     output = (keep + lax.ppermute(send, "space", swap))[None]
-    parts = shared_sum([keep_one, keep_two], [send_one, send_two], got_two)
+    parts = shared_sum([keep_one, keep_two], [send_one, send_two])
     weight_shape = jax.ShapeDtypeStruct((channels, 27 * channels), F32)
     bias_shape = jax.ShapeDtypeStruct((1, channels), F32)
     total_w_one, total_w_two, total_b_one, total_b_two = pl.pallas_call(

time: 68.1 us -> 68.6 us (level)
  starting transfers between devices: 17.3 us -> 28.8 us
  waiting for transfers between devices: 20.2 us -> 12.9 us
  local copies, waits for them, and re-layouts: 5.32 us -> 1.44 us
    ppermute x10 -> x17, starting transfers between devices: 16 us -> 26.3 us  [the longest x7 10.5 us: shared_sum(): total = total + lax.ppermute(part, ('space', 'dp'), hop(r)).astype(F32)]
    ppermute x10 -> x17, waiting for transfers between devices: 19.7 us -> 12.5 us  [the longest x7 4.26 us: shared_sum(): total = total + lax.ppermute(part, ('space', 'dp'), hop(r)).astype(F32)]
    unnamed x13 -> x0, local copies, waits for them, and re-layouts: 4.58 us -> none
    concatenate x0 -> x2, other arithmetic: none -> 2.45 us  [the longest x1 1.27 us: local(): weights = jnp.concatenate([weight_one, weight_two], axis=0)]
    mul x1 -> x0, other arithmetic: 1.24 us -> none  [local(): cotangent * alive]
    ppermute x4 -> x8, starting transfers between devices: 0.01 us -> 1.17 us  [shared_sum(): return parts + [lax.ppermute(part, 'space', swap) for part in parts]]
    convert_element_type x1 -> x0, other arithmetic: 0.73 us -> none  [local(): alive = alive.astype(BF16)[:, None, None]]
    squeeze x0 -> x1, local copies, waits for them, and re-layouts: none -> 0.71 us  [local(): table = [neighbours[:, :, k] for k in OFFSETS]]
  transfers between devices with their start and end apart: 18 -> 29, of which waited for: 11 -> 10; matrix products, arithmetic and copies ran while one was open for 7% -> 8% of each run, Pallas kernels for 10% -> 9%
where the time goes in v2:
time: 68.6 us; the launch traced here: 68.4 us
  starting transfers between devices  28.8 us (42%)
  Pallas kernels  20.2 us (29%)
  waiting for transfers between devices  12.9 us (19%)
  other arithmetic  4.24 us (6%)
  local copies, waits for them, and re-layouts  1.44 us (2%)
  between operations  0.84 us (1%)
    ppermute x7, starting transfers between devices, shared_sum(): total = total + lax.ppermute(part, ('space', 'dp'), hop(r)).astype(F32)  10.5 us
    ppermute x7, starting transfers between devices, shared_sum(): parts[r] = lax.ppermute(total, ('space', 'dp'), hop(r))  8.74 us
    pallas_call x1, Pallas kernels, local(): pl.pallas_call(backward_kernel, out_shape=(kept, sent), in_specs=[SMEM] +...  5.38 us
    pallas_call x1, Pallas kernels, local(): pl.pallas_call(inner_kernel, out_shape=(jax.ShapeDtypeStruct((9, KDIM, PL...  5.34 us
    pallas_call x1, Pallas kernels, local(): pl.pallas_call(outer_kernel, out_shape=(kept, sent, planes(1, F32), plane...  4.84 us
    ppermute x2, starting transfers between devices, shared_sum(): lax.ppermute(send, 'space', swap).astype(F32)  4.42 us
    ppermute x7, waiting for transfers between devices, shared_sum(): total = total + lax.ppermute(part, ('space', 'dp'), hop(r)).astype(F32)  4.26 us
    ppermute x7, waiting for transfers between devices, shared_sum(): parts[r] = lax.ppermute(total, ('space', 'dp'), hop(r))  3.6 us
  transfers between devices with their start and end apart: 29, of which 10 were waited for; matrix products, arithmetic and copies ran while one was open for 8% of the time, Pallas kernels for 9%

profile of v2, /device:TPU:0, one launch (start us, length us, event | category | flops | bytes accessed | tf_op | source)
XLA Modules:
  0.0 68.4 jit_solution(7460050423159220727)
XLA Ops:
  1.2 1.2 %pad_maximum_fusion.1.own_ref = bf16[8,96,512]{2,1,0:T(8,128)(2,1)S(1)} fusion(bf16[4,96,512]{2,1,0:T(8,128)(2,1)} %bitcast.19, bf16[4,96,512]{2,1,0:T(8,128)(2,1)} %bitcast.17), kind=kLoop, calls=%fused_computation.1 | loop fusion | flops 393216 | bytes 1572864 | tf_op jit(solution)/shard_map/concatenate | solution.py:492
  4.5 1.3 %pad_maximum_fusion.weight_ref = bf16[192,2592]{1,0:T(8,128)(2,1)S(1)} fusion(bf16[96,2592]{1,0:T(8,128)(2,1)} %param.13, bf16[96,2592]{1,0:T(8,128)(2,1)} %param.12), kind=kLoop, calls=%fused_computation | loop fusion | flops 1990656 | bytes 1990656 | tf_op jit(solution)/shard_map/concatenate | solution.py:491
  5.8 1.5 %layout.1 = (bf16[12,96,256]{2,1,0:T(8,128)(2,1)S(1)}, bf16[9,96,256]{2,1,0:T(8,128)(2,1)S(1)}, bf16[4,96,256]{2,1,0:T(8,128)(2,1)S(1)}, f32[3,8,256]{2,1,0:T(8,128)S(1)}) custom-call(s32[6,32]{1,0:T(8,128)S(1)} %concatenate.9.table, bf16[8,96,512]{2,1,0:T(8,128)(2,1)S(1)} %pad_maximum_fusion.1.own_ref, ...), custom_call_target="tpu_custom_call" | custom-call | tf_op jit(solution)/shard_map/layout/pallas_call | solution.py:507
  8.0 5.3 %inner.1 = (bf16[9,896,256]{2,1,0:T(8,128)(2,1)S(1)}, f32[2,96,256]{2,1,0:T(8,128)S(1)}, f32[2,96,256]{2,1,0:T(8,128)S(1)}, f32[7,96,256]{2,1,0:T(8,128)S(1)}, b...) custom-call(s32[6,32]{1,0:T(8,128)S(1)} %concatenate.9.table, ...), custom_call_target="tpu_custom_call" | custom-call | flops 8589934592 | bytes 8388608 | tf_op jit(solution)/shard_map/inner/pallas_call | solution.py:522
  13.3 4.8 %outer.1 = (f32[8,128,128]{2,1,0:T(8,128)S(1)}, bf16[8,128,128]{2,1,0:T(8,128)(2,1)S(1)}, f32[1,96,256]{2,1,0:T(8,128)S(1)}, bf16[3,96,256]{2,1,0:T(8,128)(2,1)S(1)}, bf16[2,96,256]{2,1,0:T(8,128)(2,1)S(1)}) custom-call(s32[6,32]{1,0:T(8,128)S(1)} %concatenate.9.table, bf16[4,96,256]{2,1,0:T(8,128)(2,1)S(1)} %collective-permute-done.2.edge_ref, ...), custom_call_target="tpu_custom_call" | custom-call | flops 4294967296 | bytes 8388608 | tf_op jit(solution)/shard_map/outer/pallas_call | solution.py:551
  18.2 5.4 %backward.1 = (f32[8,128,128]{2,1,0:T(8,128)S(1)}, bf16[8,128,128]{2,1,0:T(8,128)(2,1)S(1)}) custom-call(s32[6,32]{1,0:T(8,128)S(1)} %concatenate.9.table, bf16[3,96,256]{2,1,0:T(8,128)(2,1)S(1)} %get-tuple-element.45.g_out_ref, bf16[7,96,256]{2,1,0:T(8,128)(2,1)S(1)} %get-tuple-element.40.g_in_ref, f32[1,96,256]{2,1,0:T(8,128)S(1)} %get-tuple-element.46.slope_out_ref, ...), custom_call_target="tpu_custom_call" | custom-call | flops 4294967296 | bytes 4194304 | tf_op jit(solution)/shard_map/backward/pallas_call | solution.py:571
  23.6 4.3 %collective-permute-start.4 = (bf16[8,128,128]{2,1,0:T(8,128)(2,1)S(1)}, bf16[8,128,128]{2,1,0:T(8,128)(2,1)S(1)}, u32[]{:S(2)}, u32[]{:S(2)}) collective-permute-start(bf16[8,128,128]{2,1,0:T(8,128)(2,1)S(1)} %get-tuple-element.50), channel_id=1, source_target_pairs={{0,4},{4,0},{8,12},{12,8},{16,20},{20,16},{24,28},{28,24},{1,5},{5... | collective-permute-start | bytes 786440 | tf_op jit(solution)/shard_map/ppermute | solution.py:460
  28.0 1.1 %collective-permute-done.4 = bf16[8,128,128]{2,1,0:T(8,128)(2,1)S(1)} collective-permute-done((bf16[8,128,128]{2,1,0:T(8,128)(2,1)S(1)}, bf16[8,128,128]{2,1,0:T(8,128)(2,1)S(1)}, u32[]{:S(2)}, u32[]{:S(2)}) %collective-permute-start.4) | collective-permute-done | bytes 262176 | tf_op jit(solution)/shard_map/ppermute | solution.py:460
  29.6 3.0 %collective-permute-start.7 = (bf16[2,128,128]{2,1,0:T(8,128)(2,1)S(1)}, bf16[2,128,128]{2,1,0:T(8,128)(2,1)S(1)}, u32[]{:S(2)}, u32[]{:S(2)}) collective-permute-start(bf16[2,128,128]{2,1,0:T(8,128)(2,1)S(1)} %pad_maximum_fusion.3), channel_id=1, source_target_pairs={{0,24},{1,25},{2,26},{3,27},{4,28},{5,29},{6,30},{7,31},{8,16},{9,... | collective-permute-start | bytes 196616 | tf_op jit(solution)/shard_map/ppermute | solution.py:465
  32.6 2.0 %collective-permute-start.8 = (bf16[2,128,128]{2,1,0:T(8,128)(2,1)S(1)}, bf16[2,128,128]{2,1,0:T(8,128)(2,1)S(1)}, u32[]{:S(2)}, u32[]{:S(2)}) collective-permute-start(bf16[2,128,128]{2,1,0:T(8,128)(2,1)S(1)} %pad_maximum_fusion.4), channel_id=1, source_target_pairs={{0,9},{1,8},{2,11},{3,10},{4,13},{5,12},{6,15},{7,14},{8,1},{9,0},... | collective-permute-start | bytes 196616 | tf_op jit(solution)/shard_map/ppermute | solution.py:465
  35.0 1.9 %collective-permute-start.10 = (bf16[2,128,128]{2,1,0:T(8,128)(2,1)S(1)}, bf16[2,128,128]{2,1,0:T(8,128)(2,1)S(1)}, u32[]{:S(2)}, u32[]{:S(2)}) collective-permute-start(bf16[2,128,128]{2,1,0:T(8,128)(2,1)S(1)} %pad_maximum_fusion.6), channel_id=1, source_target_pairs={{0,8},{1,9},{2,10},{3,11},{4,12},{5,13},{6,14},{7,15},{8,0},{9,1},... | collective-permute-start | bytes 196616 | tf_op jit(solution)/shard_map/ppermute | solution.py:465
  36.9 0.9 %collective-permute-start.11 = (bf16[2,128,128]{2,1,0:T(8,128)(2,1)S(1)}, bf16[2,128,128]{2,1,0:T(8,128)(2,1)S(1)}, u32[]{:S(2)}, u32[]{:S(2)}) collective-permute-start(bf16[2,128,128]{2,1,0:T(8,128)(2,1)S(1)} %pad_maximum_fusion.7), channel_id=1, source_target_pairs={{0,16},{1,17},{2,18},{3,19},{4,20},{5,21},{6,22},{7,23},{8,24},{9,... | collective-permute-start | bytes 196616 | tf_op jit(solution)/shard_map/ppermute | solution.py:465
  37.9 1.6 %collective-permute-start.12 = (bf16[2,128,128]{2,1,0:T(8,128)(2,1)S(1)}, bf16[2,128,128]{2,1,0:T(8,128)(2,1)S(1)}, u32[]{:S(2)}, u32[]{:S(2)}) collective-permute-start(bf16[2,128,128]{2,1,0:T(8,128)(2,1)S(1)} %pad_maximum_fusion.8), channel_id=1, source_target_pairs={{0,1},{1,0},{2,3},{3,2},{4,5},{5,4},{6,7},{7,6},{8,9},{9,8},{10,11... | collective-permute-start | bytes 196616 | tf_op jit(solution)/shard_map/ppermute | solution.py:465
  40.1 1.1 %output.1 = (bf16[4,96,512]{2,1,0:T(8,128)(2,1)S(1)}, bf16[4,96,512]{2,1,0:T(8,128)(2,1)S(1)}) custom-call(s32[6,32]{1,0:T(8,128)S(1)} %concatenate.9.table, bf16[2,96,256]{2,1,0:T(8,128)(2,1)S(1)} %get-tuple-element.41.first_ref, bf16[6,96,256]{2,1,0:T(8,128)(2,1)S(1)} %get-tuple-element.42.second_ref), custom_call_target="tpu_custom_call" | custom-call | flops 268435456 | bytes 2097152 | tf_op jit(solution)/shard_map/output/pallas_call | solution.py:589
  41.3 1.2 %collective-permute-done.12 = bf16[2,128,128]{2,1,0:T(8,128)(2,1)S(1)} collective-permute-done((bf16[2,128,128]{2,1,0:T(8,128)(2,1)S(1)}, bf16[2,128,128]{2,1,0:T(8,128)(2,1)S(1)}, u32[]{:S(2)}, u32[]{:S(2)}) %collective-permute-start.12) | collective-permute-done | bytes 65568 | tf_op jit(solution)/shard_map/ppermute | solution.py:465
  42.5 3.1 %collective-permute-done.6 = bf16[2,128,128]{2,1,0:T(8,128)(2,1)S(1)} collective-permute-done((bf16[2,128,128]{2,1,0:T(8,128)(2,1)S(1)}, bf16[2,128,128]{2,1,0:T(8,128)(2,1)S(1)}, u32[]{:S(2)}, u32[]{:S(2)}) %collective-permute-start.6) | collective-permute-done | bytes 65568 | tf_op jit(solution)/shard_map/ppermute | solution.py:465
  45.7 2.7 %collective-permute-start.13 = (bf16[2,128,128]{2,1,0:T(8,128)(2,1)S(1)}, bf16[2,128,128]{2,1,0:T(8,128)(2,1)S(1)}, u32[]{:S(2)}, u32[]{:S(2)}) collective-permute-start(bf16[2,128,128]{2,1,0:T(8,128)(2,1)S(1)} %fusion.6), channel_id=1, source_target_pairs={{0,2},{1,3},{2,0},{3,1},{4,6},{5,7},{6,4},{7,5},{8,10},{9,11},{10,... | collective-permute-start | bytes 196616 | tf_op jit(solution)/shard_map/ppermute | solution.py:469
  48.3 3.3 %collective-permute-done.13 = bf16[2,128,128]{2,1,0:T(8,128)(2,1)S(1)} collective-permute-done((bf16[2,128,128]{2,1,0:T(8,128)(2,1)S(1)}, bf16[2,128,128]{2,1,0:T(8,128)(2,1)S(1)}, u32[]{:S(2)}, u32[]{:S(2)}) %collective-permute-start.13) | collective-permute-done | bytes 65568 | tf_op jit(solution)/shard_map/ppermute | solution.py:469
  51.9 3.3 %collective-permute-start.19 = (bf16[2,128,128]{2,1,0:T(8,128)(2,1)S(1)}, bf16[2,128,128]{2,1,0:T(8,128)(2,1)S(1)}, u32[]{:S(2)}, u32[]{:S(2)}) collective-permute-start(bf16[2,128,128]{2,1,0:T(8,128)(2,1)S(1)} %add_convert_fusion.refs_0_), channel_id=1, source_target_pairs={{0,17},{1,16},{2,19},{3,18},{4,21},{5,20},{6,23},{7,22},{8,25},{9,... | collective-permute-start | bytes 196616 | tf_op jit(solution)/shard_map/ppermute | solution.py:474
  55.7 2.0 %collective-permute-start.17 = (bf16[2,128,128]{2,1,0:T(8,128)(2,1)S(1)}, bf16[2,128,128]{2,1,0:T(8,128)(2,1)S(1)}, u32[]{:S(2)}, u32[]{:S(2)}) collective-permute-start(bf16[2,128,128]{2,1,0:T(8,128)(2,1)S(1)} %add_convert_fusion.refs_0_), channel_id=1, source_target_pairs={{0,1},{1,0},{2,3},{3,2},{4,5},{5,4},{6,7},{7,6},{8,9},{9,8},{10,11... | collective-permute-start | bytes 196616 | tf_op jit(solution)/shard_map/ppermute | solution.py:474
  58.9 1.4 %collective-permute-start.15 = (bf16[2,128,128]{2,1,0:T(8,128)(2,1)S(1)}, bf16[2,128,128]{2,1,0:T(8,128)(2,1)S(1)}, u32[]{:S(2)}, u32[]{:S(2)}) collective-permute-start(bf16[2,128,128]{2,1,0:T(8,128)(2,1)S(1)} %add_convert_fusion.refs_0_), channel_id=1, source_target_pairs={{0,16},{1,17},{2,18},{3,19},{4,20},{5,21},{6,22},{7,23},{8,24},{9,... | collective-permute-start | bytes 196616 | tf_op jit(solution)/shard_map/ppermute | solution.py:474
  61.7 1.4 %collective-permute-done.16.refs_3_ = bf16[2,128,128]{2,1,0:T(8,128)(2,1)S(1)} collective-permute-done((bf16[2,128,128]{2,1,0:T(8,128)(2,1)S(1)}, bf16[2,128,128]{2,1,0:T(8,128)(2,1)S(1)}, u32[]{:S(2)}, u32[]{:S(2)}) %collective-permute-start.16) | collective-permute-done | bytes 65568 | tf_op jit(solution)/shard_map/ppermute | solution.py:474
  63.7 0.9 %collective-permute-done.14.refs_1_ = bf16[2,128,128]{2,1,0:T(8,128)(2,1)S(1)} collective-permute-done((bf16[2,128,128]{2,1,0:T(8,128)(2,1)S(1)}, bf16[2,128,128]{2,1,0:T(8,128)(2,1)S(1)}, u32[]{:S(2)}, u32[]{:S(2)}) %collective-permute-start.14) | collective-permute-done | bytes 65568 | tf_op jit(solution)/shard_map/ppermute | solution.py:474
  66.4 2.1 %gather.1 = (f32[96,2592]{1,0:T(8,128)}, f32[96,2592]{1,0:T(8,128)}, f32[1,96]{1,0:T(1,128)}, f32[1,96]{1,0:T(1,128)}) custom-call(s32[6,32]{1,0:T(8,128)S(1)} %concatenate.9.table, bf16[2,128,128]{2,1,0:T(8,128)(2,1)S(1)} %add_convert_fusion.refs_0_, bf16[2,128,128]{2,1,0:T(8,128)(2,1)S(1)} %collective-permute-done.14.refs_1_, ...), custom_call_target="tpu_custom_call" | custom-call | tf_op jit(solution)/shard_map/gather/pallas_call | solution.py:603
  (61 shorter events, 10.8 us)
Async XLA Ops:
  0.6 5.1 %collective-permute-start = (bf16[4,96,512]{2,1,0:T(8,128)(2,1)}, bf16[4,96,512]{2,1,0:T(8,128)(2,1)S(1)}, u32[]{:S(2)}, u32[]{:S(2)}) collective-permute-start(bf16[4,96,512]{2,1,0:T(8,128)(2,1)} %bitcast.16), channel_id=1, source_target_pairs={{0,4},{4,0},{8,12},{12,8},{16,20},{20,16},{24,28},{28,24},{1,5},{5... | collective-permute-start | bytes 1179656 | tf_op jit(solution)/shard_map/ppermute | solution.py:488
  1.1 4.6 %collective-permute-start.1 = (bf16[4,96,512]{2,1,0:T(8,128)(2,1)}, bf16[4,96,512]{2,1,0:T(8,128)(2,1)S(1)}, u32[]{:S(2)}, u32[]{:S(2)}) collective-permute-start(bf16[4,96,512]{2,1,0:T(8,128)(2,1)} %bitcast.18), channel_id=1, source_target_pairs={{0,4},{4,0},{8,12},{12,8},{16,20},{20,16},{24,28},{28,24},{1,5},{5... | collective-permute-start | bytes 1179656 | tf_op jit(solution)/shard_map/ppermute | solution.py:489
  7.3 6.0 %collective-permute-start.2 = (bf16[4,96,256]{2,1,0:T(8,128)(2,1)S(1)}, bf16[4,96,256]{2,1,0:T(8,128)(2,1)S(1)}, u32[]{:S(2)}, u32[]{:S(2)}) collective-permute-start(bf16[4,96,256]{2,1,0:T(8,128)(2,1)S(1)} %get-tuple-element.31), channel_id=1, source_target_pairs={{4,8},{12,16},{20,24},{8,4},{16,12},{24,20},{5,9},{13,17},{21,25},... | collective-permute-start | bytes 589832 | tf_op jit(solution)/shard_map/ppermute | solution.py:519
  23.6 5.5 %collective-permute-start.4 = (bf16[8,128,128]{2,1,0:T(8,128)(2,1)S(1)}, bf16[8,128,128]{2,1,0:T(8,128)(2,1)S(1)}, u32[]{:S(2)}, u32[]{:S(2)}) collective-permute-start(bf16[8,128,128]{2,1,0:T(8,128)(2,1)S(1)} %get-tuple-element.50), channel_id=1, source_target_pairs={{0,4},{4,0},{8,12},{12,8},{16,20},{20,16},{24,28},{28,24},{1,5},{5... | collective-permute-start | bytes 786440 | tf_op jit(solution)/shard_map/ppermute | solution.py:460
  29.6 8.3 %collective-permute-start.7 = (bf16[2,128,128]{2,1,0:T(8,128)(2,1)S(1)}, bf16[2,128,128]{2,1,0:T(8,128)(2,1)S(1)}, u32[]{:S(2)}, u32[]{:S(2)}) collective-permute-start(bf16[2,128,128]{2,1,0:T(8,128)(2,1)S(1)} %pad_maximum_fusion.3), channel_id=1, source_target_pairs={{0,24},{1,25},{2,26},{3,27},{4,28},{5,29},{6,30},{7,31},{8,16},{9,... | collective-permute-start | bytes 196616 | tf_op jit(solution)/shard_map/ppermute | solution.py:465
  32.6 6.9 %collective-permute-start.8 = (bf16[2,128,128]{2,1,0:T(8,128)(2,1)S(1)}, bf16[2,128,128]{2,1,0:T(8,128)(2,1)S(1)}, u32[]{:S(2)}, u32[]{:S(2)}) collective-permute-start(bf16[2,128,128]{2,1,0:T(8,128)(2,1)S(1)} %pad_maximum_fusion.4), channel_id=1, source_target_pairs={{0,9},{1,8},{2,11},{3,10},{4,13},{5,12},{6,15},{7,14},{8,1},{9,0},... | collective-permute-start | bytes 196616 | tf_op jit(solution)/shard_map/ppermute | solution.py:465
  34.7 6.6 %collective-permute-start.9 = (bf16[2,128,128]{2,1,0:T(8,128)(2,1)S(1)}, bf16[2,128,128]{2,1,0:T(8,128)(2,1)S(1)}, u32[]{:S(2)}, u32[]{:S(2)}) collective-permute-start(bf16[2,128,128]{2,1,0:T(8,128)(2,1)S(1)} %pad_maximum_fusion.5), channel_id=1, source_target_pairs={{0,17},{1,16},{2,19},{3,18},{4,21},{5,20},{6,23},{7,22},{8,25},{9,... | collective-permute-start | bytes 196616 | tf_op jit(solution)/shard_map/ppermute | solution.py:465
  35.0 6.4 %collective-permute-start.10 = (bf16[2,128,128]{2,1,0:T(8,128)(2,1)S(1)}, bf16[2,128,128]{2,1,0:T(8,128)(2,1)S(1)}, u32[]{:S(2)}, u32[]{:S(2)}) collective-permute-start(bf16[2,128,128]{2,1,0:T(8,128)(2,1)S(1)} %pad_maximum_fusion.6), channel_id=1, source_target_pairs={{0,8},{1,9},{2,10},{3,11},{4,12},{5,13},{6,14},{7,15},{8,0},{9,1},... | collective-permute-start | bytes 196616 | tf_op jit(solution)/shard_map/ppermute | solution.py:465
  36.9 4.4 %collective-permute-start.11 = (bf16[2,128,128]{2,1,0:T(8,128)(2,1)S(1)}, bf16[2,128,128]{2,1,0:T(8,128)(2,1)S(1)}, u32[]{:S(2)}, u32[]{:S(2)}) collective-permute-start(bf16[2,128,128]{2,1,0:T(8,128)(2,1)S(1)} %pad_maximum_fusion.7), channel_id=1, source_target_pairs={{0,16},{1,17},{2,18},{3,19},{4,20},{5,21},{6,22},{7,23},{8,24},{9,... | collective-permute-start | bytes 196616 | tf_op jit(solution)/shard_map/ppermute | solution.py:465
  37.9 4.7 %collective-permute-start.12 = (bf16[2,128,128]{2,1,0:T(8,128)(2,1)S(1)}, bf16[2,128,128]{2,1,0:T(8,128)(2,1)S(1)}, u32[]{:S(2)}, u32[]{:S(2)}) collective-permute-start(bf16[2,128,128]{2,1,0:T(8,128)(2,1)S(1)} %pad_maximum_fusion.8), channel_id=1, source_target_pairs={{0,1},{1,0},{2,3},{3,2},{4,5},{5,4},{6,7},{7,6},{8,9},{9,8},{10,11... | collective-permute-start | bytes 196616 | tf_op jit(solution)/shard_map/ppermute | solution.py:465
  39.5 6.1 %collective-permute-start.6 = (bf16[2,128,128]{2,1,0:T(8,128)(2,1)S(1)}, bf16[2,128,128]{2,1,0:T(8,128)(2,1)S(1)}, u32[]{:S(2)}, u32[]{:S(2)}) collective-permute-start(bf16[2,128,128]{2,1,0:T(8,128)(2,1)S(1)} %pad_maximum_fusion.2), channel_id=1, source_target_pairs={{0,25},{1,24},{2,27},{3,26},{4,29},{5,28},{6,31},{7,30},{8,17},{9,... | collective-permute-start | bytes 196616 | tf_op jit(solution)/shard_map/ppermute | solution.py:465
  41.2 14.4 %collective-permute-start.3 = (bf16[4,96,512]{2,1,0:T(8,128)(2,1)S(1)}, bf16[4,96,512]{2,1,0:T(8,128)(2,1)S(1)}, u32[]{:S(2)}, u32[]{:S(2)}) collective-permute-start(bf16[4,96,512]{2,1,0:T(8,128)(2,1)S(1)} %get-tuple-element.44), channel_id=1, source_target_pairs={{0,4},{4,0},{8,12},{12,8},{16,20},{20,16},{24,28},{28,24},{1,5},{5... | collective-permute-start | bytes 1179656 | tf_op jit(solution)/shard_map/ppermute | solution.py:599
  45.7 5.9 %collective-permute-start.13 = (bf16[2,128,128]{2,1,0:T(8,128)(2,1)S(1)}, bf16[2,128,128]{2,1,0:T(8,128)(2,1)S(1)}, u32[]{:S(2)}, u32[]{:S(2)}) collective-permute-start(bf16[2,128,128]{2,1,0:T(8,128)(2,1)S(1)} %fusion.6), channel_id=1, source_target_pairs={{0,2},{1,3},{2,0},{3,1},{4,6},{5,7},{6,4},{7,5},{8,10},{9,11},{10,... | collective-permute-start | bytes 196616 | tf_op jit(solution)/shard_map/ppermute | solution.py:469
  51.6 6.0 %collective-permute-start.21 = (bf16[2,128,128]{2,1,0:T(8,128)(2,1)S(1)}, bf16[2,128,128]{2,1,0:T(8,128)(2,1)S(1)}, u32[]{:S(2)}, u32[]{:S(2)}) collective-permute-start(bf16[2,128,128]{2,1,0:T(8,128)(2,1)S(1)} %add_convert_fusion.refs_0_), channel_id=1, source_target_pairs={{0,4},{4,0},{8,12},{12,8},{16,20},{20,16},{24,28},{28,24},{1,5},{5... | collective-permute-start | bytes 196616 | tf_op jit(solution)/shard_map/ppermute | solution.py:476
  51.7 7.2 %collective-permute-start.20 = (bf16[2,128,128]{2,1,0:T(8,128)(2,1)S(1)}, bf16[2,128,128]{2,1,0:T(8,128)(2,1)S(1)}, u32[]{:S(2)}, u32[]{:S(2)}) collective-permute-start(bf16[2,128,128]{2,1,0:T(8,128)(2,1)S(1)} %add_convert_fusion.refs_0_), channel_id=1, source_target_pairs={{0,25},{1,24},{2,27},{3,26},{4,29},{5,28},{6,31},{7,30},{8,17},{9,... | collective-permute-start | bytes 196616 | tf_op jit(solution)/shard_map/ppermute | solution.py:474
  51.9 8.4 %collective-permute-start.19 = (bf16[2,128,128]{2,1,0:T(8,128)(2,1)S(1)}, bf16[2,128,128]{2,1,0:T(8,128)(2,1)S(1)}, u32[]{:S(2)}, u32[]{:S(2)}) collective-permute-start(bf16[2,128,128]{2,1,0:T(8,128)(2,1)S(1)} %add_convert_fusion.refs_0_), channel_id=1, source_target_pairs={{0,17},{1,16},{2,19},{3,18},{4,21},{5,20},{6,23},{7,22},{8,25},{9,... | collective-permute-start | bytes 196616 | tf_op jit(solution)/shard_map/ppermute | solution.py:474
  55.2 6.0 %collective-permute-start.18 = (bf16[2,128,128]{2,1,0:T(8,128)(2,1)S(1)}, bf16[2,128,128]{2,1,0:T(8,128)(2,1)S(1)}, u32[]{:S(2)}, u32[]{:S(2)}) collective-permute-start(bf16[2,128,128]{2,1,0:T(8,128)(2,1)S(1)} %add_convert_fusion.refs_0_), channel_id=1, source_target_pairs={{0,9},{1,8},{2,11},{3,10},{4,13},{5,12},{6,15},{7,14},{8,1},{9,0},... | collective-permute-start | bytes 196616 | tf_op jit(solution)/shard_map/ppermute | solution.py:474
  55.7 5.5 %collective-permute-start.17 = (bf16[2,128,128]{2,1,0:T(8,128)(2,1)S(1)}, bf16[2,128,128]{2,1,0:T(8,128)(2,1)S(1)}, u32[]{:S(2)}, u32[]{:S(2)}) collective-permute-start(bf16[2,128,128]{2,1,0:T(8,128)(2,1)S(1)} %add_convert_fusion.refs_0_), channel_id=1, source_target_pairs={{0,1},{1,0},{2,3},{3,2},{4,5},{5,4},{6,7},{7,6},{8,9},{9,8},{10,11... | collective-permute-start | bytes 196616 | tf_op jit(solution)/shard_map/ppermute | solution.py:474
  57.6 5.4 %collective-permute-start.16 = (bf16[2,128,128]{2,1,0:T(8,128)(2,1)S(1)}, bf16[2,128,128]{2,1,0:T(8,128)(2,1)S(1)}, u32[]{:S(2)}, u32[]{:S(2)}) collective-permute-start(bf16[2,128,128]{2,1,0:T(8,128)(2,1)S(1)} %add_convert_fusion.refs_0_), channel_id=1, source_target_pairs={{0,24},{1,25},{2,26},{3,27},{4,28},{5,29},{6,30},{7,31},{8,16},{9,... | collective-permute-start | bytes 196616 | tf_op jit(solution)/shard_map/ppermute | solution.py:474
  58.9 4.8 %collective-permute-start.15 = (bf16[2,128,128]{2,1,0:T(8,128)(2,1)S(1)}, bf16[2,128,128]{2,1,0:T(8,128)(2,1)S(1)}, u32[]{:S(2)}, u32[]{:S(2)}) collective-permute-start(bf16[2,128,128]{2,1,0:T(8,128)(2,1)S(1)} %add_convert_fusion.refs_0_), channel_id=1, source_target_pairs={{0,16},{1,17},{2,18},{3,19},{4,20},{5,21},{6,22},{7,23},{8,24},{9,... | collective-permute-start | bytes 196616 | tf_op jit(solution)/shard_map/ppermute | solution.py:474
  60.3 4.3 %collective-permute-start.14 = (bf16[2,128,128]{2,1,0:T(8,128)(2,1)S(1)}, bf16[2,128,128]{2,1,0:T(8,128)(2,1)S(1)}, u32[]{:S(2)}, u32[]{:S(2)}) collective-permute-start(bf16[2,128,128]{2,1,0:T(8,128)(2,1)S(1)} %add_convert_fusion.refs_0_), channel_id=1, source_target_pairs={{0,8},{1,9},{2,10},{3,11},{4,12},{5,13},{6,14},{7,15},{8,0},{9,1},... | collective-permute-start | bytes 196616 | tf_op jit(solution)/shard_map/ppermute | solution.py:474
  61.1 3.5 %collective-permute-start.28 = (bf16[2,128,128]{2,1,0:T(8,128)(2,1)S(1)}, bf16[2,128,128]{2,1,0:T(8,128)(2,1)S(1)}, u32[]{:S(2)}, u32[]{:S(2)}) collective-permute-start(bf16[2,128,128]{2,1,0:T(8,128)(2,1)S(1)} %collective-permute-done.20.refs_7_), channel_id=1, source_target_pairs={{0,4},{4,0},{8,12},{12,8},{16,20},{20,16},{24,28},{28,24},{1,5},{5... | collective-permute-start | bytes 196616 | tf_op jit(solution)/shard_map/ppermute | solution.py:476
  61.1 4.0 %collective-permute-start.27 = (bf16[2,128,128]{2,1,0:T(8,128)(2,1)S(1)}, bf16[2,128,128]{2,1,0:T(8,128)(2,1)S(1)}, u32[]{:S(2)}, u32[]{:S(2)}) collective-permute-start(bf16[2,128,128]{2,1,0:T(8,128)(2,1)S(1)} %collective-permute-done.19.refs_6_), channel_id=1, source_target_pairs={{0,4},{4,0},{8,12},{12,8},{16,20},{20,16},{24,28},{28,24},{1,5},{5... | collective-permute-start | bytes 196616 | tf_op jit(solution)/shard_map/ppermute | solution.py:476
  63.0 2.9 %collective-permute-start.26 = (bf16[2,128,128]{2,1,0:T(8,128)(2,1)S(1)}, bf16[2,128,128]{2,1,0:T(8,128)(2,1)S(1)}, u32[]{:S(2)}, u32[]{:S(2)}) collective-permute-start(bf16[2,128,128]{2,1,0:T(8,128)(2,1)S(1)} %collective-permute-done.18.refs_5_), channel_id=1, source_target_pairs={{0,4},{4,0},{8,12},{12,8},{16,20},{20,16},{24,28},{28,24},{1,5},{5... | collective-permute-start | bytes 196616 | tf_op jit(solution)/shard_map/ppermute | solution.py:476
  (5 other events, 7.9 us)

commit v3 on v2

--- a/solution.py
+++ b/solution.py
@@ -121,22 +121,13 @@
     flat[TILES * channels :, :] = jnp.zeros((ROWS - TILES * channels, 128), F32)
 
 
-def chunk_place(table, r, chunks):
-    value = table[DEVICE, 0]
-    chips = chunks // 2
-    at = (((value >> 8) & 1) ^ (r // chips)) * chips + (((value & 255) >> 1) ^ (r % chips))
-    return jnp.clip(at, 0, chunks - 1)
-
-
 def split_tiles(keep_ref, send_ref, flat, table):
-    chunks, rows = keep_ref.shape[0], keep_ref.shape[1]
+    rows = keep_ref.shape[0]
     even = (table[DEVICE, 0] & 1) == 0
-    for r in range(chunks):
-        at = chunk_place(table, r, chunks) * rows
-        here = at + jnp.where(even, 0, chunks * rows)
-        there = at + jnp.where(even, chunks * rows, 0)
-        keep_ref[r] = flat[pl.ds(pl.multiple_of(here, rows), rows), :]
-        send_ref[r] = flat[pl.ds(pl.multiple_of(there, rows), rows), :].astype(BF16)
+    here = pl.multiple_of(jnp.where(even, 0, rows), rows)
+    there = pl.multiple_of(jnp.where(even, rows, 0), rows)
+    keep_ref[...] = flat[pl.ds(here, rows), :]
+    send_ref[...] = flat[pl.ds(there, rows), :].astype(BF16)
 
 
 def layout_kernel(
@@ -412,17 +403,17 @@
     split_tiles(keep_ref, send_ref, flat, table)
 
 
-def gather_kernel(table, *refs):
-    chunks = (len(refs) - 5) // 2
-    w_one_ref, w_two_ref, b_one_ref, b_two_ref, flat = refs[2 * chunks :]
-    rows = refs[0].shape[1]
+def gather_kernel(
+    table, own_ref, other_ref, w_one_ref, w_two_ref, b_one_ref, b_two_ref, flat
+):
+    chunks, _, rows, _ = own_ref.shape
     channels = w_one_ref.shape[0]
     core = table[DEVICE, 0] & 1
-    for half in range(2):
+    for half, source in enumerate((own_ref, other_ref)):
         base = jnp.where(core == half, 0, chunks * rows)
-        for r in range(chunks):
-            at = base + chunk_place(table, r, chunks) * rows
-            flat[:, pl.ds(pl.multiple_of(at, rows), rows), :] = refs[half * chunks + r][...]
+        for k in range(chunks):
+            at = pl.multiple_of(base + k * rows, rows)
+            flat[:, pl.ds(at, rows), :] = source[k]
     for n, (weight, bias) in enumerate(((w_one_ref, b_one_ref), (w_two_ref, b_two_ref))):
         for k in range(TILES - 1):
             tile = flat[n, k * channels : (k + 1) * channels, :]
@@ -441,46 +432,36 @@
 
 
 def shared_sum(keeps, sends):
-    chunks = keeps[0].shape[0]
-    chips = chunks // 2
     count = lax.axis_size("space")
     volumes = lax.axis_size("dp")
     swap = [(d, d ^ 1) for d in range(count)]
-
-    def hop(r):
-        space, volume = 2 * (r % chips), r // chips
-        return [
-            (d * volumes + v, (d ^ space) * volumes + (v ^ volume))
-            for d in range(count)
-            for v in range(volumes)
-        ]
-
-    order = sorted(range(1, chunks), key=lambda r: -bin(r).count("1"))
+    both = ("space", "dp")
+    groups = [
+        [(chip * 2 + core) * volumes + first + v for v in range(2) for chip in range(count // 2)]
+        for core in range(2)
+        for first in range(0, volumes, 2)
+    ]
     halves = [
         keep + lax.ppermute(send, "space", swap).astype(F32) for keep, send in zip(keeps, sends)
     ]
-    total = jnp.stack([half[0] for half in halves])
-    for r in order:
-        part = jnp.stack([half[r] for half in halves]).astype(BF16)
-        total = total + lax.ppermute(part, ("space", "dp"), hop(r)).astype(F32)
-    total = total.astype(BF16)
+    halves = [half.astype(BF16).reshape(count, -1, 128) for half in halves]
+    parts = jnp.stack(halves, axis=1)
+    parts = lax.all_to_all(parts, both, 0, 0, axis_index_groups=groups)
+    total = jnp.sum(parts.astype(F32), axis=0).astype(BF16)
     step = 2
     while step < volumes:
         moved = lax.ppermute(total, "dp", [(v, v ^ step) for v in range(volumes)])
         total = (total.astype(F32) + moved.astype(F32)).astype(BF16)
         step *= 2
-    parts = {0: total}
-    for r in order:
-        parts[r] = lax.ppermute(total, ("space", "dp"), hop(r))
-    parts = [parts[r] for r in range(chunks)]
-    return parts + [lax.ppermute(part, "space", swap) for part in parts]
+    copies = jnp.broadcast_to(total[None], parts.shape)
+    copies = lax.all_to_all(copies, both, 0, 0, axis_index_groups=groups)
+    return [copies, lax.ppermute(copies, "space", swap)]
 
 
 def local(volume, neighbours, active, cotangent, weight_one, weight_two, bias_one, bias_two):
     volume, cotangent = volume[0], cotangent[0]
     slots, channels = volume.shape[0], volume.shape[1]
     count = lax.axis_size("space")
-    chips = count // 2
     me = lax.axis_index("space").astype(jnp.int32)
 
     swap = [(d, d ^ 1) for d in range(count)]
@@ -546,8 +527,8 @@
         name="inner",
     )(table, x_planes, cot_planes, layer_mask, weights, biases)
 
-    chunks = (2 * chips, ROWS // (4 * chips), 128)
-    kept, sent = jax.ShapeDtypeStruct(chunks, F32), jax.ShapeDtypeStruct(chunks, BF16)
+    half = (ROWS // 2, 128)
+    kept, sent = jax.ShapeDtypeStruct(half, F32), jax.ShapeDtypeStruct(half, BF16)
     keep_two, send_two, slope_out, g_out, out_out = pl.pallas_call(
         outer_kernel,
         out_shape=(kept, sent, planes(1, F32), planes(3), planes(2)),

time: 68.6 us -> 66.6 us (0.971)
  starting transfers between devices: 28.8 us -> 11.9 us
  blocking collectives: 0 us -> 14.6 us
  local copies, waits for them, and re-layouts: 1.44 us -> 2.28 us
    ppermute x22 -> x1, starting transfers between devices: 20.4 us -> 0.01 us  [shared_sum(): return [copies, lax.ppermute(copies, 'space', swap)]]
    all_to_all x0 -> x1, blocking collectives: none -> 14.6 us  [shared_sum(): parts = lax.all_to_all(parts, both, 0, 0, axis_index_groups=groups)]
    ppermute x22 -> x1, waiting for transfers between devices: 8.26 us -> 1.1 us  [shared_sum(): return [copies, lax.ppermute(copies, 'space', swap)]]
    all_to_all x0 -> x1, waiting for transfers between devices: none -> 6.47 us  [shared_sum(): copies = lax.all_to_all(copies, both, 0, 0, axis_index_groups=groups)]
    all_to_all x0 -> x1, starting transfers between devices: none -> 3.49 us  [shared_sum(): copies = lax.all_to_all(copies, both, 0, 0, axis_index_groups=groups)]
    broadcast_in_dim x0 -> x1, local copies, waits for them, and re-layouts: none -> 0.9 us  [shared_sum(): copies = jnp.broadcast_to(total[None], parts.shape)]
  transfers between devices with their start and end apart: 29 -> 9, of which waited for: 10 -> 5; matrix products, arithmetic and copies ran while one was open for 8% -> 8% of each run, Pallas kernels for 9% -> 10%
where the time goes in v3:
time: 66.6 us; the launch traced here: 66.2 us
  Pallas kernels  20.2 us (30%)
  blocking collectives  14.6 us (22%)
  waiting for transfers between devices  12.3 us (18%)
  starting transfers between devices  11.9 us (18%)
  other arithmetic  4.22 us (6%)
  local copies, waits for them, and re-layouts  2.28 us (3%)
  between operations  0.74 us (1%)
    all_to_all x1, blocking collectives, shared_sum(): parts = lax.all_to_all(parts, both, 0, 0, axis_index_groups=groups)  14.6 us
    all_to_all x1, waiting for transfers between devices, shared_sum(): copies = lax.all_to_all(copies, both, 0, 0, axis_index_groups=groups)  6.47 us
    pallas_call x1, Pallas kernels, local(): pl.pallas_call(backward_kernel, out_shape=(kept, sent), in_specs=[SMEM] +...  5.39 us
    pallas_call x1, Pallas kernels, local(): pl.pallas_call(inner_kernel, out_shape=(jax.ShapeDtypeStruct((9, KDIM, PL...  5.34 us
    pallas_call x1, Pallas kernels, local(): pl.pallas_call(outer_kernel, out_shape=(kept, sent, planes(1, F32), plane...  4.85 us
    ppermute x2, starting transfers between devices, shared_sum(): lax.ppermute(send, 'space', swap).astype(F32)  4.44 us
    all_to_all x1, starting transfers between devices, shared_sum(): copies = lax.all_to_all(copies, both, 0, 0, axis_index_groups=groups)  3.49 us
    ppermute x1, waiting for transfers between devices, shared_sum(): moved = lax.ppermute(total, 'dp', [(v, v ^ step) for v in range(volumes)])  3.28 us
  transfers between devices with their start and end apart: 9, of which 5 were waited for; matrix products, arithmetic and copies ran while one was open for 8% of the time, Pallas kernels for 10%

profile of v3, /device:TPU:0, one launch (start us, length us, event | category | flops | bytes accessed | tf_op | source)
XLA Modules:
  0.0 66.2 jit_solution(12704963308842807321)
XLA Ops:
  0.6 0.5 collective-permute-start
  1.2 1.2 %pad_maximum_fusion.1.own_ref = bf16[8,96,512]{2,1,0:T(8,128)(2,1)S(1)} fusion(bf16[4,96,512]{2,1,0:T(8,128)(2,1)} %bitcast.27, bf16[4,96,512]{2,1,0:T(8,128)(2,1)} %bitcast.25), kind=kLoop, calls=%fused_computation.1 | loop fusion | flops 393216 | bytes 1572864 | tf_op jit(solution)/shard_map/concatenate | solution.py:473
  2.4 0.7 %slice_bitcast_fusion = (s32[1,32]{1,0:T(1,128)S(1)}, s32[1,32]{1,0:T(1,128)S(1)}, s32[1,32]{1,0:T(1,128)S(1)}, s32[1,32]{1,0:T(1,128)S(1)}) fusion(s32[1,32,26]{1,0,2:T(1,128)} %param.9), kind=kLoop, calls=%fused_computation.8 | loop fusion | bytes 1024 | tf_op jit(solution)/shard_map/squeeze | solution.py:475
  3.1 0.7 %pad_maximum_fusion.3.bias_ref = f32[2,96]{1,0:T(2,128)S(1)} fusion(f32[1,96]{1,0:T(1,128)} %bitcast.28, f32[1,96]{1,0:T(1,128)} %bitcast.29), kind=kLoop, calls=%fused_computation.7 | loop fusion | flops 192 | bytes 1536 | tf_op jit(solution)/shard_map/stack | solution.py:471
  3.8 0.7 %concatenate.9.table = s32[6,32]{1,0:T(8,128)S(1)} concatenate(s32[1,32]{1,0:T(1,128)S(1)} %get-tuple-element.59, s32[1,32]{1,0:T(1,128)S(1)} %get-tuple-element.58, s32[1,32]{1,0:T(1,128)S(1)} %get-tuple-element.60, s32[1,32]{1,0:T(1,128)S(1)} %get-tuple-element.57, s32[1,32]{1,0:T(1,128)} %param.10, s32[1,32]{1,0:T(1,128)S(1)} %broadcast_in_dim.12), dimensions={0} | concatenate | bytes 1536 | tf_op jit(solution)/shard_map/concatenate | solution.py:476
  4.5 1.3 %pad_maximum_fusion.weight_ref = bf16[192,2592]{1,0:T(8,128)(2,1)S(1)} fusion(bf16[96,2592]{1,0:T(8,128)(2,1)} %param.13, bf16[96,2592]{1,0:T(8,128)(2,1)} %param.12), kind=kLoop, calls=%fused_computation | loop fusion | flops 1990656 | bytes 1990656 | tf_op jit(solution)/shard_map/concatenate | solution.py:472
  5.8 1.5 %layout.1 = (bf16[12,96,256]{2,1,0:T(8,128)(2,1)S(1)}, bf16[9,96,256]{2,1,0:T(8,128)(2,1)S(1)}, bf16[4,96,256]{2,1,0:T(8,128)(2,1)S(1)}, f32[3,8,256]{2,1,0:T(8,128)S(1)}) custom-call(s32[6,32]{1,0:T(8,128)S(1)} %concatenate.9.table, bf16[8,96,512]{2,1,0:T(8,128)(2,1)S(1)} %pad_maximum_fusion.1.own_ref, ...), custom_call_target="tpu_custom_call" | custom-call | tf_op jit(solution)/shard_map/layout/pallas_call | solution.py:488
  7.3 0.7 %collective-permute-start.2 = (bf16[4,96,256]{2,1,0:T(8,128)(2,1)S(1)}, bf16[4,96,256]{2,1,0:T(8,128)(2,1)S(1)}, u32[]{:S(2)}, u32[]{:S(2)}) collective-permute-start(bf16[4,96,256]{2,1,0:T(8,128)(2,1)S(1)} %get-tuple-element.31), channel_id=1, source_target_pairs={{4,8},{12,16},{20,24},{8,4},{16,12},{24,20},{5,9},{13,17},{21,25},... | collective-permute-start | bytes 589832 | tf_op jit(solution)/shard_map/ppermute | solution.py:500
  8.0 5.3 %inner.1 = (bf16[9,896,256]{2,1,0:T(8,128)(2,1)S(1)}, f32[2,96,256]{2,1,0:T(8,128)S(1)}, f32[2,96,256]{2,1,0:T(8,128)S(1)}, f32[7,96,256]{2,1,0:T(8,128)S(1)}, b...) custom-call(s32[6,32]{1,0:T(8,128)S(1)} %concatenate.9.table, ...), custom_call_target="tpu_custom_call" | custom-call | flops 8589934592 | bytes 8388608 | tf_op jit(solution)/shard_map/inner/pallas_call | solution.py:503
  13.3 4.9 %outer.1 = (f32[1024,128]{1,0:T(8,128)S(1)}, bf16[1024,128]{1,0:T(8,128)(2,1)S(1)}, f32[1,96,256]{2,1,0:T(8,128)S(1)}, bf16[3,96,256]{2,1,0:T(8,128)(2,1)S(1)}, bf16[2,96,256]{2,1,0:T(8,128)(2,1)S(1)}) custom-call(s32[6,32]{1,0:T(8,128)S(1)} %concatenate.9.table, bf16[4,96,256]{2,1,0:T(8,128)(2,1)S(1)} %collective-permute-done.2.edge_ref, ...), custom_call_target="tpu_custom_call" | custom-call | flops 4294967296 | bytes 8388608 | tf_op jit(solution)/shard_map/outer/pallas_call | solution.py:532
  18.2 5.4 %backward.1 = (f32[1024,128]{1,0:T(8,128)S(1)}, bf16[1024,128]{1,0:T(8,128)(2,1)S(1)}) custom-call(s32[6,32]{1,0:T(8,128)S(1)} %concatenate.9.table, bf16[3,96,256]{2,1,0:T(8,128)(2,1)S(1)} %get-tuple-element.45.g_out_ref, bf16[7,96,256]{2,1,0:T(8,128)(2,1)S(1)} %get-tuple-element.40.g_in_ref, f32[1,96,256]{2,1,0:T(8,128)S(1)} %get-tuple-element.46.slope_out_ref, ...), custom_call_target="tpu_custom_call" | custom-call | flops 4294967296 | bytes 4194304 | tf_op jit(solution)/shard_map/backward/pallas_call | solution.py:552
  23.6 4.4 %collective-permute-start.4 = (bf16[1024,128]{1,0:T(8,128)(2,1)S(1)}, bf16[1024,128]{1,0:T(8,128)(2,1)S(1)}, u32[]{:S(2)}, u32[]{:S(2)}) collective-permute-start(bf16[1024,128]{1,0:T(8,128)(2,1)S(1)} %get-tuple-element.50), channel_id=1, source_target_pairs={{0,4},{4,0},{8,12},{12,8},{16,20},{20,16},{24,28},{28,24},{1,5},{5... | collective-permute-start | bytes 786440 | tf_op jit(solution)/shard_map/ppermute | solution.py:445
  28.0 1.1 %collective-permute-done.4 = bf16[1024,128]{1,0:T(8,128)(2,1)S(1)} collective-permute-done((bf16[1024,128]{1,0:T(8,128)(2,1)S(1)}, bf16[1024,128]{1,0:T(8,128)(2,1)S(1)}, u32[]{:S(2)}, u32[]{:S(2)}) %collective-permute-start.4) | collective-permute-done | bytes 262176 | tf_op jit(solution)/shard_map/ppermute | solution.py:445
  29.2 0.3 collective-permute-done.5
  29.6 14.6 %all_to_all.10 = bf16[8,2,128,128]{3,2,1,0:T(8,128)(2,1)S(1)} all-to-all(bf16[8,2,128,128]{3,2,1,0:T(8,128)(2,1)S(1)} %pad_maximum_fusion.2), channel_id=1, replica_groups={{0,8,16,24,1,9,17,25},{2,10,18,26,3,11,19,27},{4,12,20,28,5,13,21,29},{..., dimensions={0} | all-to-all | bytes 1048576 | tf_op jit(solution)/shard_map/all_to_all | solution.py:449
  44.3 2.6 %collective-permute-start.6 = (bf16[2,128,128]{2,1,0:T(8,128)(2,1)S(1)}, bf16[2,128,128]{2,1,0:T(8,128)(2,1)S(1)}, u32[]{:S(2)}, u32[]{:S(2)}) collective-permute-start(bf16[2,128,128]{2,1,0:T(8,128)(2,1)S(1)} %reduce_sum.12), channel_id=1, source_target_pairs={{0,2},{1,3},{2,0},{3,1},{4,6},{5,7},{6,4},{7,5},{8,10},{9,11},{10,... | collective-permute-start | bytes 196616 | tf_op jit(solution)/shard_map/ppermute | solution.py:453
  46.9 3.3 %collective-permute-done.6 = bf16[2,128,128]{2,1,0:T(8,128)(2,1)S(1)} collective-permute-done((bf16[2,128,128]{2,1,0:T(8,128)(2,1)S(1)}, bf16[2,128,128]{2,1,0:T(8,128)(2,1)S(1)}, u32[]{:S(2)}, u32[]{:S(2)}) %collective-permute-start.6) | collective-permute-done | bytes 65568 | tf_op jit(solution)/shard_map/ppermute | solution.py:453
  50.2 0.9 %broadcast_in_dim.14 = bf16[8,2,128,128]{3,2,1,0:T(8,128)(2,1)} broadcast(bf16[2,128,128]{2,1,0:T(8,128)(2,1)S(1)} %add_convert_fusion.2), dimensions={1,2,3} | broadcast | bytes 589824 | tf_op jit(solution)/shard_map/broadcast_in_dim | solution.py:456
  51.1 3.5 %all-to-all-start.1 = ((bf16[8,2,128,128]{3,2,1,0:T(8,128)(2,1)}), bf16[8,2,128,128]{3,2,1,0:T(8,128)(2,1)S(1)}, u32[]{:S(2)}, u32[]{:S(2)}) async-start(bf16[8,2,128,128]{3,2,1,0:T(8,128)(2,1)} %broadcast_in_dim.14), calls=%async_computation.1 | async-start | bytes 1048576 | tf_op jit(solution)/shard_map/all_to_all | solution.py:457
  54.6 1.1 %output.1 = (bf16[4,96,512]{2,1,0:T(8,128)(2,1)S(1)}, bf16[4,96,512]{2,1,0:T(8,128)(2,1)S(1)}) custom-call(s32[6,32]{1,0:T(8,128)S(1)} %concatenate.9.table, bf16[2,96,256]{2,1,0:T(8,128)(2,1)S(1)} %get-tuple-element.41.first_ref, bf16[6,96,256]{2,1,0:T(8,128)(2,1)S(1)} %get-tuple-element.42.second_ref), custom_call_target="tpu_custom_call" | custom-call | flops 268435456 | bytes 2097152 | tf_op jit(solution)/shard_map/output/pallas_call | solution.py:570
  55.8 6.5 %all-to-all-done.1.own_ref = bf16[8,2,128,128]{3,2,1,0:T(8,128)(2,1)S(1)} async-done(((bf16[8,2,128,128]{3,2,1,0:T(8,128)(2,1)}), bf16[8,2,128,128]{3,2,1,0:T(8,128)(2,1)S(1)}, u32[]{:S(2)}, u32[]{:S(2)}) %all-to-all-start.1) | async-done | bytes 524320 | tf_op jit(solution)/shard_map/all_to_all | solution.py:457
  62.3 0.8 %add_bitcast_fusion = bf16[1,4,96,512]{3,2,1,0:T(8,128)(2,1)} fusion(bf16[4,96,512]{2,1,0:T(8,128)(2,1)S(1)} %get-tuple-element.43, bf16[4,96,512]{2,1,0:T(8,128)(2,1)S(1)} %collective-permute-done.3), kind=kLoop, calls=%fused_computation.5 | loop fusion | flops 196608 | bytes 1179648 | tf_op jit(solution)/shard_map/broadcast_in_dim | solution.py:580
  63.1 1.1 %collective-permute-done.7.other_ref = bf16[8,2,128,128]{3,2,1,0:T(8,128)(2,1)S(1)} collective-permute-done((bf16[8,2,128,128]{3,2,1,0:T(8,128)(2,1)S(1)}, bf16[8,2,128,128]{3,2,1,0:T(8,128)(2,1)S(1)}, u32[]{:S(2)}, u32[]{:S(2)}) %collective-permute-start.7) | collective-permute-done | bytes 524320 | tf_op jit(solution)/shard_map/ppermute | solution.py:458
  64.2 2.1 %gather.1 = (f32[96,2592]{1,0:T(8,128)}, f32[96,2592]{1,0:T(8,128)}, f32[1,96]{1,0:T(1,128)}, f32[1,96]{1,0:T(1,128)}) custom-call(s32[6,32]{1,0:T(8,128)S(1)} %concatenate.9.table, bf16[8,2,128,128]{3,2,1,0:T(8,128)(2,1)S(1)} %all-to-all-done.1.own_ref, bf16[8,2,128,128]{3,2,1,0:T(8,128)(2,1)S(1)} %collective-permute-done.7.other_ref), custom_call_target="tpu_custom_call" | custom-call | tf_op jit(solution)/shard_map/gather/pallas_call | solution.py:584
  (14 shorter events, 0.5 us)
Async XLA Ops:
  0.6 5.1 %collective-permute-start = (bf16[4,96,512]{2,1,0:T(8,128)(2,1)}, bf16[4,96,512]{2,1,0:T(8,128)(2,1)S(1)}, u32[]{:S(2)}, u32[]{:S(2)}) collective-permute-start(bf16[4,96,512]{2,1,0:T(8,128)(2,1)} %bitcast.24), channel_id=1, source_target_pairs={{0,4},{4,0},{8,12},{12,8},{16,20},{20,16},{24,28},{28,24},{1,5},{5... | collective-permute-start | bytes 1179656 | tf_op jit(solution)/shard_map/ppermute | solution.py:469
  1.1 4.6 %collective-permute-start.1 = (bf16[4,96,512]{2,1,0:T(8,128)(2,1)}, bf16[4,96,512]{2,1,0:T(8,128)(2,1)S(1)}, u32[]{:S(2)}, u32[]{:S(2)}) collective-permute-start(bf16[4,96,512]{2,1,0:T(8,128)(2,1)} %bitcast.26), channel_id=1, source_target_pairs={{0,4},{4,0},{8,12},{12,8},{16,20},{20,16},{24,28},{28,24},{1,5},{5... | collective-permute-start | bytes 1179656 | tf_op jit(solution)/shard_map/ppermute | solution.py:470
  7.3 6.0 %collective-permute-start.2 = (bf16[4,96,256]{2,1,0:T(8,128)(2,1)S(1)}, bf16[4,96,256]{2,1,0:T(8,128)(2,1)S(1)}, u32[]{:S(2)}, u32[]{:S(2)}) collective-permute-start(bf16[4,96,256]{2,1,0:T(8,128)(2,1)S(1)} %get-tuple-element.31), channel_id=1, source_target_pairs={{4,8},{12,16},{20,24},{8,4},{16,12},{24,20},{5,9},{13,17},{21,25},... | collective-permute-start | bytes 589832 | tf_op jit(solution)/shard_map/ppermute | solution.py:500
  23.6 5.5 %collective-permute-start.4 = (bf16[1024,128]{1,0:T(8,128)(2,1)S(1)}, bf16[1024,128]{1,0:T(8,128)(2,1)S(1)}, u32[]{:S(2)}, u32[]{:S(2)}) collective-permute-start(bf16[1024,128]{1,0:T(8,128)(2,1)S(1)} %get-tuple-element.50), channel_id=1, source_target_pairs={{0,4},{4,0},{8,12},{12,8},{16,20},{20,16},{24,28},{28,24},{1,5},{5... | collective-permute-start | bytes 786440 | tf_op jit(solution)/shard_map/ppermute | solution.py:445
  27.9 1.5 %collective-permute-start.5 = (bf16[1024,128]{1,0:T(8,128)(2,1)S(1)}, bf16[1024,128]{1,0:T(8,128)(2,1)S(1)}, u32[]{:S(2)}, u32[]{:S(2)}) collective-permute-start(bf16[1024,128]{1,0:T(8,128)(2,1)S(1)} %get-tuple-element.52), channel_id=1, source_target_pairs={{0,4},{4,0},{8,12},{12,8},{16,20},{20,16},{24,28},{28,24},{1,5},{5... | collective-permute-start | bytes 786440 | tf_op jit(solution)/shard_map/ppermute | solution.py:445
  44.3 5.9 %collective-permute-start.6 = (bf16[2,128,128]{2,1,0:T(8,128)(2,1)S(1)}, bf16[2,128,128]{2,1,0:T(8,128)(2,1)S(1)}, u32[]{:S(2)}, u32[]{:S(2)}) collective-permute-start(bf16[2,128,128]{2,1,0:T(8,128)(2,1)S(1)} %reduce_sum.12), channel_id=1, source_target_pairs={{0,2},{1,3},{2,0},{3,1},{4,6},{5,7},{6,4},{7,5},{8,10},{9,11},{10,... | collective-permute-start | bytes 196616 | tf_op jit(solution)/shard_map/ppermute | solution.py:453
  51.1 11.1 %all-to-all-start.1 = ((bf16[8,2,128,128]{3,2,1,0:T(8,128)(2,1)}), bf16[8,2,128,128]{3,2,1,0:T(8,128)(2,1)S(1)}, u32[]{:S(2)}, u32[]{:S(2)}) async-start(bf16[8,2,128,128]{3,2,1,0:T(8,128)(2,1)} %broadcast_in_dim.14), calls=%async_computation.1 | async-start | bytes 1048576 | tf_op jit(solution)/shard_map/all_to_all | solution.py:457
  55.7 6.6 %collective-permute-start.3 = (bf16[4,96,512]{2,1,0:T(8,128)(2,1)S(1)}, bf16[4,96,512]{2,1,0:T(8,128)(2,1)S(1)}, u32[]{:S(2)}, u32[]{:S(2)}) collective-permute-start(bf16[4,96,512]{2,1,0:T(8,128)(2,1)S(1)} %get-tuple-element.44), channel_id=1, source_target_pairs={{0,4},{4,0},{8,12},{12,8},{16,20},{20,16},{24,28},{28,24},{1,5},{5... | collective-permute-start | bytes 1179656 | tf_op jit(solution)/shard_map/ppermute | solution.py:580
  62.3 1.9 %collective-permute-start.7 = (bf16[8,2,128,128]{3,2,1,0:T(8,128)(2,1)S(1)}, bf16[8,2,128,128]{3,2,1,0:T(8,128)(2,1)S(1)}, u32[]{:S(2)}, u32[]{:S(2)}) collective-permute-start(bf16[8,2,128,128]{3,2,1,0:T(8,128)(2,1)S(1)} %all-to-all-done.1.own_ref), channel_id=1, source_target_pairs={{0,4},{4,0},{8,12},{12,8},{16,20},{20,16},{24,28},{28,24},{1,5},{5... | collective-permute-start | bytes 1572872 | tf_op jit(solution)/shard_map/ppermute | solution.py:458

commit v4 on v3

--- a/solution.py
+++ b/solution.py
@@ -34,13 +34,12 @@
 
 def write_taps(dst, plane, masks_ref):
     channels = plane.shape[0]
-    wide = plane.astype(F32)
     for k in range(9):
         step = (k // 3 - 1) * 16 + (k % 3 - 1)
         if step == 0:
             moved = plane
         else:
-            moved = pltpu.roll(wide, (-step) % PLANE, 1).astype(BF16)
+            moved = pltpu.roll(plane, (-step) % PLANE, 1)
             moved = moved * jnp.concatenate([masks_ref[k]] * (channels // 16), axis=0)
         dst[k * channels : (k + 1) * channels, :] = moved
 
@@ -137,8 +136,8 @@
     slots, channels = pair_ref.shape[0], pair_ref.shape[1]
     all_slots = table.shape[1]
     me = space_index(table, all_slots // slots)
-    core = me & 1
-    even = core == 0
+    layer = table[DEVICE, 0] >> 16
+    even = layer == 0
 
     live = [[jnp.float32(0)] * 4 for _ in range(2)]
     beyond = [jnp.float32(0)] * 4
@@ -158,7 +157,7 @@
                 for p in range(2):
                     here = jnp.logical_and(parity == p, place == k)
                     live[p][k] = jnp.where(here, alive, live[p][k])
-                here = jnp.logical_and(parity == core, place == k)
+                here = jnp.logical_and(parity == layer, place == k)
                 beyond[k] = jnp.where(here, alive_outer, beyond[k])
     mask_ref[0] = lane_mask(beyond)
     mask_ref[1] = lane_mask([jnp.where(even, live[0][k], live[1][k]) for k in range(4)])
@@ -257,7 +256,7 @@
     wide, xc, acc_one, acc_two, masks_ref,
 ):
     channels = x_ref.shape[1]
-    even = (table[DEVICE, 0] & 1) == 0
+    even = (table[DEVICE, 0] >> 16) == 0
     fill_masks(masks_ref)
     tap_weights(w1_taps, weight_ref[:channels, :], wide, even)
     bias_one, bias_two = column(bias_ref[0:1]), column(bias_ref[1:2])
@@ -306,7 +305,7 @@
     xc, hc, acc_one, acc_two, total, flat, masks_ref,
 ):
     channels = cot_ref.shape[1]
-    even = (table[DEVICE, 0] & 1) == 0
+    even = (table[DEVICE, 0] >> 16) == 0
     fill_masks(masks_ref)
     bias_one, bias_two = column(bias_ref[0:1]), column(bias_ref[1:2])
     ones = jnp.ones((KDIM - 9 * channels, PLANE), BF16)
@@ -346,8 +345,8 @@
 def output_kernel(table, first_ref, second_ref, keep_ref, send_ref, outs, bricks):
     slots, channels = keep_ref.shape[0], keep_ref.shape[1]
     me = space_index(table, table.shape[1] // slots)
-    core = me & 1
-    even = core == 0
+    layer = table[DEVICE, 0] >> 16
+    even = layer == 0
     outs[:2] = first_ref[...]
     outs[2:] = second_ref[...]
     back = spread_matrix(True)
@@ -365,7 +364,7 @@
         for s in range(slots):
             slot = jnp.clip(device * slots + s, 0, table.shape[1] - 1)
             parity, place = slot_place(table, slot, 2 * slots)
-            scale = jnp.where(parity == core, 1.0, 0.0)
+            scale = jnp.where(parity == layer, 1.0, 0.0)
             target[s] = bricks[place] * jnp.full((channels, CELLS), scale, F32).astype(BF16)
 
 
@@ -374,7 +373,7 @@
     keep_ref, send_ref, gc, xc, acc, grad, total, flat, masks_ref,
 ):
     channels = x_ref.shape[1]
-    even = (table[DEVICE, 0] & 1) == 0
+    even = (table[DEVICE, 0] >> 16) == 0
     fill_masks(masks_ref)
     ones = jnp.ones((KDIM - 9 * channels, PLANE), BF16)
     for k in range(2):
@@ -403,8 +402,14 @@
     split_tiles(keep_ref, send_ref, flat, table)
 
 
+def copies_kernel(first_ref, second_ref, out_ref):
+    total = (first_ref[...].astype(F32) + second_ref[...].astype(F32)).astype(BF16)
+    for k in range(out_ref.shape[0]):
+        out_ref[k] = total
+
+
 def gather_kernel(
-    table, own_ref, other_ref, w_one_ref, w_two_ref, b_one_ref, b_two_ref, flat
+    table, own_ref, other_ref, w_one_ref, w_two_ref, b_one_ref, b_two_ref, flat, wide, sems
 ):
     chunks, _, rows, _ = own_ref.shape
     channels = w_one_ref.shape[0]
@@ -414,17 +419,23 @@
         for k in range(chunks):
             at = pl.multiple_of(base + k * rows, rows)
             flat[:, pl.ds(at, rows), :] = source[k]
+    copies = []
     for n, (weight, bias) in enumerate(((w_one_ref, b_one_ref), (w_two_ref, b_two_ref))):
         for k in range(TILES - 1):
             tile = flat[n, k * channels : (k + 1) * channels, :]
-            weight[:, k * 128 : (k + 1) * 128] = tile.astype(F32)
+            wide[n, :, k * 128 : (k + 1) * 128] = tile.astype(F32)
         last = flat[n, (TILES - 1) * channels : TILES * channels, :].astype(F32)
-        weight[:, 2560:2592] = last[:, :32]
+        wide[n, :, 2560:2592] = last[:, :32]
+        copies.append(pltpu.make_async_copy(wide.at[n], weight, sems.at[n]))
+        copies[n].start()
         bias[...] = last.T[32:33, :]
+    for copy in copies:
+        copy.wait()
 
 
 VMEM = pl.BlockSpec(memory_space=pltpu.VMEM)
 SMEM = pl.BlockSpec(memory_space=pltpu.SMEM)
+ANY = pl.BlockSpec(memory_space=pl.ANY)
 
 
 def vmem(mebibytes):
@@ -448,12 +459,20 @@
     parts = jnp.stack(halves, axis=1)
     parts = lax.all_to_all(parts, both, 0, 0, axis_index_groups=groups)
     total = jnp.sum(parts.astype(F32), axis=0).astype(BF16)
-    step = 2
+    moved, step = jnp.zeros_like(total), 2
     while step < volumes:
         moved = lax.ppermute(total, "dp", [(v, v ^ step) for v in range(volumes)])
-        total = (total.astype(F32) + moved.astype(F32)).astype(BF16)
+        if step * 2 < volumes:
+            total = (total.astype(F32) + moved.astype(F32)).astype(BF16)
         step *= 2
-    copies = jnp.broadcast_to(total[None], parts.shape)
+    copies = pl.pallas_call(
+        copies_kernel,
+        out_shape=jax.ShapeDtypeStruct(parts.shape, BF16),
+        in_specs=[VMEM] * 2,
+        out_specs=VMEM,
+        compiler_params=vmem(8),
+        name="copies",
+    )(total, moved)
     copies = lax.all_to_all(copies, both, 0, 0, axis_index_groups=groups)
     return [copies, lax.ppermute(copies, "space", swap)]
 
@@ -465,13 +484,16 @@
     me = lax.axis_index("space").astype(jnp.int32)
 
     swap = [(d, d ^ 1) for d in range(count)]
-    hop = [(d, d + 1) for d in range(1, count - 1, 2)] + [(d, d - 1) for d in range(2, count, 2)]
+    at = [2 * (n // 2) + (n & 1 ^ n // 2 & 1) for n in range(count)]
+    hop = [(at[n], at[n + 1]) for n in range(1, count - 1, 2)]
+    hop += [(there, here) for here, there in hop]
     pair_volume = lax.ppermute(volume, "space", swap)
     pair_cot = lax.ppermute(cotangent, "space", swap)
     biases = jnp.stack([bias_one, bias_two])
     weights = jnp.concatenate([weight_one, weight_two], axis=0)
     own = jnp.concatenate([volume, cotangent], axis=0)
     device = me + 256 * lax.axis_index("dp").astype(jnp.int32)
+    device = device + 65536 * ((me ^ (me >> 1)) & 1)
     table = [neighbours[:, :, k] for k in OFFSETS]
     table = jnp.concatenate([*table, active, jnp.full_like(active, device)], axis=0)
 
@@ -585,8 +607,12 @@
         gather_kernel,
         out_shape=(weight_shape, weight_shape, bias_shape, bias_shape),
         in_specs=[SMEM] + [VMEM] * len(parts),
-        out_specs=(VMEM,) * 4,
-        scratch_shapes=[pltpu.VMEM((2, ROWS, 128), BF16)],
+        out_specs=(ANY, ANY, VMEM, VMEM),
+        scratch_shapes=[
+            pltpu.VMEM((2, ROWS, 128), BF16),
+            pltpu.VMEM((2, channels, 27 * channels), F32),
+            pltpu.SemaphoreType.DMA((2,)),
+        ],
         compiler_params=vmem(8),
         name="gather",
     )(table, *parts)

time: 66.6 us -> 66.9 us (level)
  Pallas kernels: 20.2 us -> 21.4 us
  local copies, waits for them, and re-layouts: 2.28 us -> 1.39 us
    broadcast_in_dim x1 -> x0, local copies, waits for them, and re-layouts: 0.9 us -> none  [shared_sum(): copies = jnp.broadcast_to(total[None], parts.shape)]
    pallas_call x0 -> x1, Pallas kernels: none -> 0.84 us  [shared_sum(): pl.pallas_call(copies_kernel, out_shape=jax.ShapeDtypeStruct(parts.shape,...]
  transfers between devices with their start and end apart: 9 -> 9, of which waited for: 5 -> 5; matrix products, arithmetic and copies ran while one was open for 8% -> 8% of each run, Pallas kernels for 10% -> 9%
where the time goes in v4:
time: 66.9 us; the launch traced here: 66.5 us
  Pallas kernels  21.4 us (32%)
  blocking collectives  15 us (22%)
  waiting for transfers between devices  12.3 us (18%)
  starting transfers between devices  11.6 us (17%)
  other arithmetic  4.19 us (6%)
  local copies, waits for them, and re-layouts  1.39 us (2%)
  between operations  0.74 us (1%)
    all_to_all x1, blocking collectives, shared_sum(): parts = lax.all_to_all(parts, both, 0, 0, axis_index_groups=groups)  15 us
    all_to_all x1, waiting for transfers between devices, shared_sum(): copies = lax.all_to_all(copies, both, 0, 0, axis_index_groups=groups)  6.46 us
    pallas_call x1, Pallas kernels, local(): pl.pallas_call(backward_kernel, out_shape=(kept, sent), in_specs=[SMEM] +...  5.4 us
    pallas_call x1, Pallas kernels, local(): pl.pallas_call(inner_kernel, out_shape=(jax.ShapeDtypeStruct((9, KDIM, PL...  5.16 us
    pallas_call x1, Pallas kernels, local(): pl.pallas_call(outer_kernel, out_shape=(kept, sent, planes(1, F32), plane...  4.82 us
    ppermute x2, starting transfers between devices, shared_sum(): lax.ppermute(send, 'space', swap).astype(F32)  4.13 us
    all_to_all x1, starting transfers between devices, shared_sum(): copies = lax.all_to_all(copies, both, 0, 0, axis_index_groups=groups)  3.49 us
    ppermute x1, waiting for transfers between devices, shared_sum(): moved = lax.ppermute(total, 'dp', [(v, v ^ step) for v in range(volumes)])  3.28 us
  transfers between devices with their start and end apart: 9, of which 5 were waited for; matrix products, arithmetic and copies ran while one was open for 8% of the time, Pallas kernels for 9%

profile of v4, /device:TPU:0, one launch (start us, length us, event | category | flops | bytes accessed | tf_op | source)
XLA Modules:
  0.0 66.5 jit_solution(14585080273738595668)
XLA Ops:
  0.6 0.5 collective-permute-start
  1.2 1.2 %pad_maximum_fusion.1.own_ref = bf16[8,96,512]{2,1,0:T(8,128)(2,1)S(1)} fusion(bf16[4,96,512]{2,1,0:T(8,128)(2,1)} %bitcast.27, bf16[4,96,512]{2,1,0:T(8,128)(2,1)} %bitcast.25), kind=kLoop, calls=%fused_computation.1 | loop fusion | flops 393216 | bytes 1572864 | tf_op jit(solution)/shard_map/concatenate | solution.py:494
  2.4 0.7 %slice_bitcast_fusion = (s32[1,32]{1,0:T(1,128)S(1)}, s32[1,32]{1,0:T(1,128)S(1)}, s32[1,32]{1,0:T(1,128)S(1)}, s32[1,32]{1,0:T(1,128)S(1)}) fusion(s32[1,32,26]{1,0,2:T(1,128)} %param.9), kind=kLoop, calls=%fused_computation.7 | loop fusion | bytes 1024 | tf_op jit(solution)/shard_map/squeeze | solution.py:497
  3.1 0.7 %pad_maximum_fusion.3.bias_ref = f32[2,96]{1,0:T(2,128)S(1)} fusion(f32[1,96]{1,0:T(1,128)} %bitcast.28, f32[1,96]{1,0:T(1,128)} %bitcast.29), kind=kLoop, calls=%fused_computation.6 | loop fusion | flops 192 | bytes 1536 | tf_op jit(solution)/shard_map/stack | solution.py:492
  3.8 0.7 %concatenate.9.table = s32[6,32]{1,0:T(8,128)S(1)} concatenate(s32[1,32]{1,0:T(1,128)S(1)} %get-tuple-element.59, s32[1,32]{1,0:T(1,128)S(1)} %get-tuple-element.58, s32[1,32]{1,0:T(1,128)S(1)} %get-tuple-element.60, s32[1,32]{1,0:T(1,128)S(1)} %get-tuple-element.57, s32[1,32]{1,0:T(1,128)} %param.10, s32[1,32]{1,0:T(1,128)S(1)} %broadcast_in_dim.6), dimensions={0} | concatenate | bytes 1536 | tf_op jit(solution)/shard_map/concatenate | solution.py:498
  4.5 1.3 %pad_maximum_fusion.weight_ref = bf16[192,2592]{1,0:T(8,128)(2,1)S(1)} fusion(bf16[96,2592]{1,0:T(8,128)(2,1)} %param.13, bf16[96,2592]{1,0:T(8,128)(2,1)} %param.12), kind=kLoop, calls=%fused_computation | loop fusion | flops 1990656 | bytes 1990656 | tf_op jit(solution)/shard_map/concatenate | solution.py:493
  5.8 1.5 %layout.1 = (bf16[12,96,256]{2,1,0:T(8,128)(2,1)S(1)}, bf16[9,96,256]{2,1,0:T(8,128)(2,1)S(1)}, bf16[4,96,256]{2,1,0:T(8,128)(2,1)S(1)}, f32[3,8,256]{2,1,0:T(8,128)S(1)}) custom-call(s32[6,32]{1,0:T(8,128)S(1)} %concatenate.9.table, bf16[8,96,512]{2,1,0:T(8,128)(2,1)S(1)} %pad_maximum_fusion.1.own_ref, ...), custom_call_target="tpu_custom_call" | custom-call | tf_op jit(solution)/shard_map/layout/pallas_call | solution.py:510
  7.3 0.7 %collective-permute-start.2 = (bf16[4,96,256]{2,1,0:T(8,128)(2,1)S(1)}, bf16[4,96,256]{2,1,0:T(8,128)(2,1)S(1)}, u32[]{:S(2)}, u32[]{:S(2)}) collective-permute-start(bf16[4,96,256]{2,1,0:T(8,128)(2,1)S(1)} %get-tuple-element.31), channel_id=1, source_target_pairs={{4,12},{8,16},{20,28},{12,4},{16,8},{28,20},{5,13},{9,17},{21,29},... | collective-permute-start | bytes 589832 | tf_op jit(solution)/shard_map/ppermute | solution.py:522
  8.0 5.2 %inner.1 = (bf16[9,896,256]{2,1,0:T(8,128)(2,1)S(1)}, f32[2,96,256]{2,1,0:T(8,128)S(1)}, f32[2,96,256]{2,1,0:T(8,128)S(1)}, f32[7,96,256]{2,1,0:T(8,128)S(1)}, b...) custom-call(s32[6,32]{1,0:T(8,128)S(1)} %concatenate.9.table, ...), custom_call_target="tpu_custom_call" | custom-call | flops 8589934592 | bytes 8388608 | tf_op jit(solution)/shard_map/inner/pallas_call | solution.py:525
  13.1 4.8 %outer.1 = (f32[1024,128]{1,0:T(8,128)S(1)}, bf16[1024,128]{1,0:T(8,128)(2,1)S(1)}, f32[1,96,256]{2,1,0:T(8,128)S(1)}, bf16[3,96,256]{2,1,0:T(8,128)(2,1)S(1)}, bf16[2,96,256]{2,1,0:T(8,128)(2,1)S(1)}) custom-call(s32[6,32]{1,0:T(8,128)S(1)} %concatenate.9.table, bf16[4,96,256]{2,1,0:T(8,128)(2,1)S(1)} %collective-permute-done.2.edge_ref, ...), custom_call_target="tpu_custom_call" | custom-call | flops 4294967296 | bytes 8388608 | tf_op jit(solution)/shard_map/outer/pallas_call | solution.py:554
  18.0 5.4 %backward.1 = (f32[1024,128]{1,0:T(8,128)S(1)}, bf16[1024,128]{1,0:T(8,128)(2,1)S(1)}) custom-call(s32[6,32]{1,0:T(8,128)S(1)} %concatenate.9.table, bf16[3,96,256]{2,1,0:T(8,128)(2,1)S(1)} %get-tuple-element.45.g_out_ref, bf16[7,96,256]{2,1,0:T(8,128)(2,1)S(1)} %get-tuple-element.40.g_in_ref, f32[1,96,256]{2,1,0:T(8,128)S(1)} %get-tuple-element.46.slope_out_ref, ...), custom_call_target="tpu_custom_call" | custom-call | flops 4294967296 | bytes 4194304 | tf_op jit(solution)/shard_map/backward/pallas_call | solution.py:574
  23.4 4.0 %collective-permute-start.4 = (bf16[1024,128]{1,0:T(8,128)(2,1)S(1)}, bf16[1024,128]{1,0:T(8,128)(2,1)S(1)}, u32[]{:S(2)}, u32[]{:S(2)}) collective-permute-start(bf16[1024,128]{1,0:T(8,128)(2,1)S(1)} %get-tuple-element.50), channel_id=1, source_target_pairs={{0,4},{4,0},{8,12},{12,8},{16,20},{20,16},{24,28},{28,24},{1,5},{5... | collective-permute-start | bytes 786440 | tf_op jit(solution)/shard_map/ppermute | solution.py:456
  27.5 1.1 %collective-permute-done.4 = bf16[1024,128]{1,0:T(8,128)(2,1)S(1)} collective-permute-done((bf16[1024,128]{1,0:T(8,128)(2,1)S(1)}, bf16[1024,128]{1,0:T(8,128)(2,1)S(1)}, u32[]{:S(2)}, u32[]{:S(2)}) %collective-permute-start.4) | collective-permute-done | bytes 262176 | tf_op jit(solution)/shard_map/ppermute | solution.py:456
  28.6 0.3 collective-permute-done.5
  29.1 15.0 %all_to_all.10 = bf16[8,2,128,128]{3,2,1,0:T(8,128)(2,1)S(1)} all-to-all(bf16[8,2,128,128]{3,2,1,0:T(8,128)(2,1)S(1)} %pad_maximum_fusion.2), channel_id=1, replica_groups={{0,8,16,24,1,9,17,25},{2,10,18,26,3,11,19,27},{4,12,20,28,5,13,21,29},{..., dimensions={0} | all-to-all | bytes 1048576 | tf_op jit(solution)/shard_map/all_to_all | solution.py:460
  44.2 2.6 %collective-permute-start.6 = (bf16[2,128,128]{2,1,0:T(8,128)(2,1)S(1)}, bf16[2,128,128]{2,1,0:T(8,128)(2,1)S(1)}, u32[]{:S(2)}, u32[]{:S(2)}) collective-permute-start(bf16[2,128,128]{2,1,0:T(8,128)(2,1)S(1)} %reduce_sum.12.first_ref), channel_id=1, source_target_pairs={{0,2},{1,3},{2,0},{3,1},{4,6},{5,7},{6,4},{7,5},{8,10},{9,11},{10,... | collective-permute-start | bytes 196616 | tf_op jit(solution)/shard_map/ppermute | solution.py:464
  46.8 3.3 %collective-permute-done.6.second_ref = bf16[2,128,128]{2,1,0:T(8,128)(2,1)S(1)} collective-permute-done((bf16[2,128,128]{2,1,0:T(8,128)(2,1)S(1)}, bf16[2,128,128]{2,1,0:T(8,128)(2,1)S(1)}, u32[]{:S(2)}, u32[]{:S(2)}) %collective-permute-start.6) | collective-permute-done | bytes 65568 | tf_op jit(solution)/shard_map/ppermute | solution.py:464
  50.1 0.8 %copies.1 = bf16[8,2,128,128]{3,2,1,0:T(8,128)(2,1)} custom-call(bf16[2,128,128]{2,1,0:T(8,128)(2,1)S(1)} %reduce_sum.12.first_ref, bf16[2,128,128]{2,1,0:T(8,128)(2,1)S(1)} %collective-permute-done.6.second_ref), custom_call_target="tpu_custom_call" | custom-call | tf_op jit(solution)/shard_map/copies/pallas_call | solution.py:468
  50.9 3.5 %all-to-all-start.1 = ((bf16[8,2,128,128]{3,2,1,0:T(8,128)(2,1)}), bf16[8,2,128,128]{3,2,1,0:T(8,128)(2,1)S(1)}, u32[]{:S(2)}, u32[]{:S(2)}) async-start(bf16[8,2,128,128]{3,2,1,0:T(8,128)(2,1)} %copies.1), calls=%async_computation.1 | async-start | bytes 1048576 | tf_op jit(solution)/shard_map/all_to_all | solution.py:476
  54.4 1.1 %output.1 = (bf16[4,96,512]{2,1,0:T(8,128)(2,1)S(1)}, bf16[4,96,512]{2,1,0:T(8,128)(2,1)S(1)}) custom-call(s32[6,32]{1,0:T(8,128)S(1)} %concatenate.9.table, bf16[2,96,256]{2,1,0:T(8,128)(2,1)S(1)} %get-tuple-element.41.first_ref, bf16[6,96,256]{2,1,0:T(8,128)(2,1)S(1)} %get-tuple-element.42.second_ref), custom_call_target="tpu_custom_call" | custom-call | flops 268435456 | bytes 2097152 | tf_op jit(solution)/shard_map/output/pallas_call | solution.py:592
  55.6 6.5 %all-to-all-done.1.own_ref = bf16[8,2,128,128]{3,2,1,0:T(8,128)(2,1)S(1)} async-done(((bf16[8,2,128,128]{3,2,1,0:T(8,128)(2,1)}), bf16[8,2,128,128]{3,2,1,0:T(8,128)(2,1)S(1)}, u32[]{:S(2)}, u32[]{:S(2)}) %all-to-all-start.1) | async-done | bytes 524320 | tf_op jit(solution)/shard_map/all_to_all | solution.py:476
  62.0 0.8 %add_bitcast_fusion = bf16[1,4,96,512]{3,2,1,0:T(8,128)(2,1)} fusion(bf16[4,96,512]{2,1,0:T(8,128)(2,1)S(1)} %get-tuple-element.43, bf16[4,96,512]{2,1,0:T(8,128)(2,1)S(1)} %collective-permute-done.3), kind=kLoop, calls=%fused_computation.5 | loop fusion | flops 196608 | bytes 1179648 | tf_op jit(solution)/shard_map/broadcast_in_dim | solution.py:602
  62.8 1.1 %collective-permute-done.7.other_ref = bf16[8,2,128,128]{3,2,1,0:T(8,128)(2,1)S(1)} collective-permute-done((bf16[8,2,128,128]{3,2,1,0:T(8,128)(2,1)S(1)}, bf16[8,2,128,128]{3,2,1,0:T(8,128)(2,1)S(1)}, u32[]{:S(2)}, u32[]{:S(2)}) %collective-permute-start.7) | collective-permute-done | bytes 524320 | tf_op jit(solution)/shard_map/ppermute | solution.py:477
  63.9 2.6 %gather.1 = (f32[96,2592]{1,0:T(8,128)}, f32[96,2592]{1,0:T(8,128)}, f32[1,96]{1,0:T(1,128)}, f32[1,96]{1,0:T(1,128)}) custom-call(s32[6,32]{1,0:T(8,128)S(1)} %concatenate.9.table, bf16[8,2,128,128]{3,2,1,0:T(8,128)(2,1)S(1)} %all-to-all-done.1.own_ref, bf16[8,2,128,128]{3,2,1,0:T(8,128)(2,1)S(1)} %collective-permute-done.7.other_ref), custom_call_target="tpu_custom_call" | custom-call | tf_op jit(solution)/shard_map/gather/pallas_call | solution.py:606
  (13 shorter events, 0.5 us)
Async XLA Ops:
  0.6 5.1 %collective-permute-start = (bf16[4,96,512]{2,1,0:T(8,128)(2,1)}, bf16[4,96,512]{2,1,0:T(8,128)(2,1)S(1)}, u32[]{:S(2)}, u32[]{:S(2)}) collective-permute-start(bf16[4,96,512]{2,1,0:T(8,128)(2,1)} %bitcast.24), channel_id=1, source_target_pairs={{0,4},{4,0},{8,12},{12,8},{16,20},{20,16},{24,28},{28,24},{1,5},{5... | collective-permute-start | bytes 1179656 | tf_op jit(solution)/shard_map/ppermute | solution.py:490
  1.1 4.6 %collective-permute-start.1 = (bf16[4,96,512]{2,1,0:T(8,128)(2,1)}, bf16[4,96,512]{2,1,0:T(8,128)(2,1)S(1)}, u32[]{:S(2)}, u32[]{:S(2)}) collective-permute-start(bf16[4,96,512]{2,1,0:T(8,128)(2,1)} %bitcast.26), channel_id=1, source_target_pairs={{0,4},{4,0},{8,12},{12,8},{16,20},{20,16},{24,28},{28,24},{1,5},{5... | collective-permute-start | bytes 1179656 | tf_op jit(solution)/shard_map/ppermute | solution.py:491
  7.3 5.9 %collective-permute-start.2 = (bf16[4,96,256]{2,1,0:T(8,128)(2,1)S(1)}, bf16[4,96,256]{2,1,0:T(8,128)(2,1)S(1)}, u32[]{:S(2)}, u32[]{:S(2)}) collective-permute-start(bf16[4,96,256]{2,1,0:T(8,128)(2,1)S(1)} %get-tuple-element.31), channel_id=1, source_target_pairs={{4,12},{8,16},{20,28},{12,4},{16,8},{28,20},{5,13},{9,17},{21,29},... | collective-permute-start | bytes 589832 | tf_op jit(solution)/shard_map/ppermute | solution.py:522
  23.4 5.2 %collective-permute-start.4 = (bf16[1024,128]{1,0:T(8,128)(2,1)S(1)}, bf16[1024,128]{1,0:T(8,128)(2,1)S(1)}, u32[]{:S(2)}, u32[]{:S(2)}) collective-permute-start(bf16[1024,128]{1,0:T(8,128)(2,1)S(1)} %get-tuple-element.50), channel_id=1, source_target_pairs={{0,4},{4,0},{8,12},{12,8},{16,20},{20,16},{24,28},{28,24},{1,5},{5... | collective-permute-start | bytes 786440 | tf_op jit(solution)/shard_map/ppermute | solution.py:456
  27.4 1.5 %collective-permute-start.5 = (bf16[1024,128]{1,0:T(8,128)(2,1)S(1)}, bf16[1024,128]{1,0:T(8,128)(2,1)S(1)}, u32[]{:S(2)}, u32[]{:S(2)}) collective-permute-start(bf16[1024,128]{1,0:T(8,128)(2,1)S(1)} %get-tuple-element.52), channel_id=1, source_target_pairs={{0,4},{4,0},{8,12},{12,8},{16,20},{20,16},{24,28},{28,24},{1,5},{5... | collective-permute-start | bytes 786440 | tf_op jit(solution)/shard_map/ppermute | solution.py:456
  44.2 5.9 %collective-permute-start.6 = (bf16[2,128,128]{2,1,0:T(8,128)(2,1)S(1)}, bf16[2,128,128]{2,1,0:T(8,128)(2,1)S(1)}, u32[]{:S(2)}, u32[]{:S(2)}) collective-permute-start(bf16[2,128,128]{2,1,0:T(8,128)(2,1)S(1)} %reduce_sum.12.first_ref), channel_id=1, source_target_pairs={{0,2},{1,3},{2,0},{3,1},{4,6},{5,7},{6,4},{7,5},{8,10},{9,11},{10,... | collective-permute-start | bytes 196616 | tf_op jit(solution)/shard_map/ppermute | solution.py:464
  50.9 11.1 %all-to-all-start.1 = ((bf16[8,2,128,128]{3,2,1,0:T(8,128)(2,1)}), bf16[8,2,128,128]{3,2,1,0:T(8,128)(2,1)S(1)}, u32[]{:S(2)}, u32[]{:S(2)}) async-start(bf16[8,2,128,128]{3,2,1,0:T(8,128)(2,1)} %copies.1), calls=%async_computation.1 | async-start | bytes 1048576 | tf_op jit(solution)/shard_map/all_to_all | solution.py:476
  55.5 6.5 %collective-permute-start.3 = (bf16[4,96,512]{2,1,0:T(8,128)(2,1)S(1)}, bf16[4,96,512]{2,1,0:T(8,128)(2,1)S(1)}, u32[]{:S(2)}, u32[]{:S(2)}) collective-permute-start(bf16[4,96,512]{2,1,0:T(8,128)(2,1)S(1)} %get-tuple-element.44), channel_id=1, source_target_pairs={{0,4},{4,0},{8,12},{12,8},{16,20},{20,16},{24,28},{28,24},{1,5},{5... | collective-permute-start | bytes 1179656 | tf_op jit(solution)/shard_map/ppermute | solution.py:602
  62.0 1.9 %collective-permute-start.7 = (bf16[8,2,128,128]{3,2,1,0:T(8,128)(2,1)S(1)}, bf16[8,2,128,128]{3,2,1,0:T(8,128)(2,1)S(1)}, u32[]{:S(2)}, u32[]{:S(2)}) collective-permute-start(bf16[8,2,128,128]{3,2,1,0:T(8,128)(2,1)S(1)} %all-to-all-done.1.own_ref), channel_id=1, source_target_pairs={{0,4},{4,0},{8,12},{12,8},{16,20},{20,16},{24,28},{28,24},{1,5},{5... | collective-permute-start | bytes 1572872 | tf_op jit(solution)/shard_map/ppermute | solution.py:477

commit v5 on v4

--- a/solution.py
+++ b/solution.py
@@ -65,20 +65,30 @@
     return jnp.where(high_y, jnp.where(high_z, s[3], s[2]), jnp.where(high_z, s[1], s[0]))
 
 
-def plane_product(weight_ref, taps):
-    blocks, channels = weight_ref.shape[0], weight_ref.shape[1]
-    left = weight_ref[...].reshape(blocks * channels, KDIM)
+def product(weight_ref, taps, plane_taps=slice(0, 3)):
+    left = weight_ref[plane_taps]
+    left = left.reshape(left.shape[0] * left.shape[1], KDIM)
     return jnp.dot(left, taps, preferred_element_type=F32)
 
 
-def add_planes(acc, at, product, fresh=()):
-    channels = acc.shape[1]
-    for a in range(3):
-        k = at + 1 - a
-        if not 0 <= k < acc.shape[0]:
-            continue
-        part = product[a * channels : (a + 1) * channels]
-        acc[k] = part if k in fresh else acc[k] + part
+def pair_sums(full, low, weight_ref, taps, first):
+    channels = low.shape[1]
+    both = product(weight_ref, taps)
+    left, right = both[:, :PLANE], both[:, PLANE:]
+
+    def part(value, a):
+        return value[a * channels : (a + 1) * channels]
+
+    before = part(left, 2)
+    here = part(left, 1) + part(right, 2)
+    full[0] = before if first else low[0] + before
+    full[1] = here if first else low[1] + here
+    low[0] = part(left, 0) + part(right, 1)
+    low[1] = part(right, 0)
+
+
+def half(k):
+    return pl.ds((k & 1) * PLANE, PLANE)
 
 
 def weight_products(total, grads, taps):
@@ -90,9 +100,8 @@
 
     for p in range(-1, EDGE + 1, 2):
         both_left = jnp.concatenate([left(p), left(p + 1)], axis=1)
-        both_right = jnp.concatenate([taps(p), taps(p + 1)], axis=1)
         part = lax.dot_general(
-            both_left, both_right, (((1,), (1,)), ((), ())), preferred_element_type=F32
+            both_left, taps(p), (((1,), (1,)), ((), ())), preferred_element_type=F32
         )
         total[...] = part if p == -1 else total[...] + part
 
@@ -253,80 +262,108 @@
 def inner_kernel(
     table, x_ref, cot_ref, layer_mask, weight_ref, bias_ref,
     taps_ref, one_ref, two_ref, slope_ref, g_ref, out_ref, w1_taps, w2_taps, w2_back,
-    wide, xc, acc_one, acc_two, masks_ref,
+    wide, xc, hc, full_one, low_one, full_two, low_two, masks_ref,
 ):
     channels = x_ref.shape[1]
     even = (table[DEVICE, 0] >> 16) == 0
     fill_masks(masks_ref)
     tap_weights(w1_taps, weight_ref[:channels, :], wide, even)
     bias_one, bias_two = column(bias_ref[0:1]), column(bias_ref[1:2])
-    ones = jnp.ones((KDIM - 9 * channels, PLANE), BF16)
+    ones = jnp.ones((KDIM - 9 * channels, 2 * PLANE), BF16)
     for k in range(2):
         xc[k, 9 * channels :, :] = ones
-    for k in range(9):
+    for k in range(4):
         taps_ref[k, 9 * channels :, :] = ones
-    write_taps(xc.at[0], x_ref[0], masks_ref)
-
-    for p in range(15):
-        if p <= 10:
-            product = plane_product(w1_taps, xc[p & 1])
-            if p < 10:
-                write_taps(xc.at[1 - (p & 1)], x_ref[p + 1], masks_ref)
-            add_planes(acc_one, p + 1, product, fresh=(0, 1, 2) if p == 0 else (p + 2,))
-        if p == 1:
+    hc[9 * channels :, :] = ones[:, :PLANE]
+
+    def write_x(p):
+        write_taps(xc.at[(p >> 1) & 1, :, half(p)], x_ref[p], masks_ref)
+
+    def finish_one(q, pre):
+        hidden, slope = hidden_plane(pre + bias_one, layer_mask[layer_of(q)][:1])
+        dst = taps_ref.at[(q - 1) // 2, :, half(q - 1)] if q < 9 else hc
+        write_taps(dst, hidden, masks_ref)
+        if q < EDGE:
+            slope_ref[q - 1] = slope
+
+    def finish_two(q, pre):
+        out, grad = out_plane(pre + bias_two, layer_mask[layer_of(q)][:1], cot_ref[q])
+        g_ref[q - 2] = grad
+        if q < EDGE:
+            out_ref[q - 2] = out
+
+    write_x(0)
+    write_x(1)
+    for j in range(8):
+        now, last = j & 1, (j + 1) & 1
+        if j < 5:
+            pair_sums(full_one.at[now], low_one, w1_taps, xc[now], j == 0)
+            for p in (2 * j + 2, 2 * j + 3):
+                if p <= 10:
+                    write_x(p)
+        if j == 5:
+            third = product(w1_taps, xc[1, :, :PLANE], slice(2, 3))
+            full_one[now, 0] = low_one[0] + third
+        if j == 0:
             tap_weights(w2_taps, weight_ref[channels:, :], wide, even)
-        if p == 3:
+        if j == 1:
+            one_ref[...] = full_one[0]
             back_weights(w2_back, w2_taps)
-        q = p - 2
-        if 1 <= q <= 9:
-            hidden, slope = hidden_plane(acc_one[q + 1] + bias_one, layer_mask[layer_of(q)][:1])
-            write_taps(taps_ref.at[q - 1], hidden, masks_ref)
-            if q < EDGE:
-                slope_ref[q - 1] = slope
-        q = p - 4
-        if 1 <= q <= 9:
-            product = plane_product(w2_taps, taps_ref[q - 1])
-            add_planes(acc_two, q, product, fresh=(0, 1, 2) if q == 1 else (q + 1,))
-        q = p - 6
-        if 2 <= q <= 8:
-            mask = layer_mask[layer_of(q)][:1]
-            out, grad = out_plane(acc_two[q] + bias_two, mask, cot_ref[q])
-            g_ref[q - 2] = grad
-            if q < EDGE:
-                out_ref[q - 2] = out
-    one_ref[...] = acc_one[:2]
-    two_ref[...] = acc_two[:2]
+        if 2 <= j <= 5:
+            finish_one(2 * j - 3, full_one[last, 0])
+            finish_one(2 * j - 2, full_one[last, 1])
+        if j == 6:
+            finish_one(9, full_one[last, 0])
+        if 3 <= j <= 6:
+            pair_sums(full_two.at[now], low_two, w2_taps, taps_ref[j - 3], j == 3)
+        if j == 7:
+            third = product(w2_taps, hc[...], slice(2, 3))
+            finish_two(8, low_two[0] + third)
+        if j == 4:
+            two_ref[...] = full_two[last]
+        if 5 <= j:
+            finish_two(2 * j - 8, full_two[last, 0])
+            finish_two(2 * j - 7, full_two[last, 1])
 
 
 def outer_kernel(
     table, edge_ref, cot_ref, layer_mask, w1_taps, w2_taps, bias_ref,
     taps_ref, one_ref, two_ref, g_in_ref,
     keep_ref, send_ref, slope_ref, g_ref, out_ref,
-    xc, hc, acc_one, acc_two, total, flat, masks_ref,
+    xc, hc, x_pair, h_pair, total, flat, masks_ref,
 ):
     channels = cot_ref.shape[1]
     even = (table[DEVICE, 0] >> 16) == 0
     fill_masks(masks_ref)
     bias_one, bias_two = column(bias_ref[0:1]), column(bias_ref[1:2])
-    ones = jnp.ones((KDIM - 9 * channels, PLANE), BF16)
-    for k in range(3):
-        xc[k, 9 * channels :, :] = ones
-        hc[k, 9 * channels :, :] = ones
-        write_taps(xc.at[k], edge_ref[2 - k], masks_ref)
-    acc_one[1:] = one_ref[...]
-    acc_two[1:] = two_ref[...]
-    for p in range(-3, 0):
-        add_planes(acc_one, p + 2, plane_product(w1_taps, xc[p + 3]), fresh=(0,) if p == -3 else ())
-    for q in range(-2, 1):
-        hidden, slope = hidden_plane(acc_one[q + 2] + bias_one, layer_mask[layer_of(q)][:1])
-        write_taps(hc.at[q + 2], hidden, masks_ref)
+    ones = jnp.ones((KDIM - 9 * channels, 2 * PLANE), BF16)
+    for single in (xc, hc):
+        single[9 * channels :, :] = ones[:, :PLANE]
+    for pair in (x_pair, h_pair):
+        pair[9 * channels :, :] = ones
+    write_taps(xc, edge_ref[2], masks_ref)
+    write_taps(x_pair.at[:, half(0)], edge_ref[1], masks_ref)
+    write_taps(x_pair.at[:, half(1)], edge_ref[0], masks_ref)
+
+    def three_planes(weights, single, pair, parts):
+        first = product(weights, single[...], slice(0, 1))
+        both = product(weights, pair[...])
+        left, right = both[:, :PLANE], both[:, PLANE:]
+        one, two = slice(channels, 2 * channels), slice(2 * channels, 3 * channels)
+        return (
+            first + left[one] + right[two],
+            left[:channels] + right[one] + parts[0],
+            right[:channels] + parts[1],
+        )
+
+    for q, pre in zip(range(-2, 1), three_planes(w1_taps, xc, x_pair, one_ref)):
+        hidden, slope = hidden_plane(pre + bias_one, layer_mask[layer_of(q)][:1])
+        write_taps(hc if q == -2 else h_pair.at[:, half(q + 1)], hidden, masks_ref)
         if q == 0:
             slope_ref[0] = slope
-    for q in range(-2, 1):
-        add_planes(acc_two, q + 1, plane_product(w2_taps, hc[q + 2]), fresh=(0,) if q == -2 else ())
-    for q in range(-1, 2):
+    for q, pre in zip(range(-1, 2), three_planes(w2_taps, hc, h_pair, two_ref)):
         cot = edge_ref[3] if q < 0 else cot_ref[q]
-        out, grad = out_plane(acc_two[q + 1] + bias_two, layer_mask[layer_of(q)][:1], cot)
+        out, grad = out_plane(pre + bias_two, layer_mask[layer_of(q)][:1], cot)
         g_ref[q + 1] = grad
         if q >= 0:
             out_ref[q] = out
@@ -334,8 +371,8 @@
     def grads(q):
         return g_ref[q + 1] if q < 2 else g_in_ref[q - 2]
 
-    def taps(q):
-        return hc[q + 2] if q < 1 else taps_ref[q - 1]
+    def taps(p):
+        return h_pair[...] if p < 0 else taps_ref[p // 2]
 
     weight_products(total, grads, taps)
     write_tiles(flat, total, channels, even)
@@ -370,34 +407,38 @@
 
 def backward_kernel(
     table, g_out_ref, g_in_ref, slope_out_ref, slope_in_ref, x_ref, edge_ref, w2_back,
-    keep_ref, send_ref, gc, xc, acc, grad, total, flat, masks_ref,
+    keep_ref, send_ref, gc, xc, full, low, grad, total, flat, masks_ref,
 ):
     channels = x_ref.shape[1]
     even = (table[DEVICE, 0] >> 16) == 0
     fill_masks(masks_ref)
-    ones = jnp.ones((KDIM - 9 * channels, PLANE), BF16)
+    ones = jnp.ones((KDIM - 9 * channels, 2 * PLANE), BF16)
     for k in range(2):
         gc[k, 9 * channels :, :] = ones
-    for k in range(10):
+    for k in range(5):
         xc[k, 9 * channels :, :] = ones
 
-    def g_plane(q):
-        return g_out_ref[q + 1] if q < 2 else g_in_ref[q - 2]
-
-    write_taps(gc.at[0], g_plane(-1), masks_ref)
-    for p in range(-1, 10):
-        if p <= 8:
-            now = (p + 1) & 1
-            product = plane_product(w2_back, gc[now])
-            if p < 8:
-                write_taps(gc.at[1 - now], g_plane(p + 1), masks_ref)
-            write_taps(xc.at[p + 1], edge_ref[0] if p < 0 else x_ref[p], masks_ref)
-            add_planes(acc, p + 2, product, fresh=(0, 1, 2) if p == -1 else (p + 3,))
-        q = p - 2
-        if 0 <= q < EDGE:
-            slope = slope_out_ref[0] if q == 0 else slope_in_ref[q - 1]
-            grad[q] = (acc[q + 2] * slope).astype(BF16)
-    weight_products(total, lambda q: grad[q], lambda q: xc[q + 1])
+    def write_g(q):
+        plane = g_out_ref[q + 1] if q < 2 else g_in_ref[q - 2]
+        write_taps(gc.at[((q + 1) >> 1) & 1, :, half(q + 1)], plane, masks_ref)
+
+    write_g(-1)
+    write_g(0)
+    for j in range(6):
+        now, last = j & 1, (j + 1) & 1
+        if j < 5:
+            pair_sums(full.at[now], low, w2_back, gc[now], j == 0)
+            for q in (2 * j + 1, 2 * j + 2):
+                if q <= 8:
+                    write_g(q)
+            for q in (2 * j - 1, 2 * j):
+                plane = edge_ref[0] if q < 0 else x_ref[q]
+                write_taps(xc.at[j, :, half(q + 1)], plane, masks_ref)
+        if j >= 2:
+            for k, q in enumerate((2 * j - 4, 2 * j - 3)):
+                slope = slope_out_ref[0] if q == 0 else slope_in_ref[q - 1]
+                grad[q] = (full[last, k] * slope).astype(BF16)
+    weight_products(total, lambda q: grad[q], lambda p: xc[(p + 1) // 2])
     write_tiles(flat, total, channels, even)
     split_tiles(keep_ref, send_ref, flat, table)
 
@@ -409,7 +450,7 @@
 
 
 def gather_kernel(
-    table, own_ref, other_ref, w_one_ref, w_two_ref, b_one_ref, b_two_ref, flat, wide, sems
+    table, own_ref, other_ref, w_one_ref, w_two_ref, b_one_ref, b_two_ref, flat
 ):
     chunks, _, rows, _ = own_ref.shape
     channels = w_one_ref.shape[0]
@@ -419,23 +460,17 @@
         for k in range(chunks):
             at = pl.multiple_of(base + k * rows, rows)
             flat[:, pl.ds(at, rows), :] = source[k]
-    copies = []
     for n, (weight, bias) in enumerate(((w_one_ref, b_one_ref), (w_two_ref, b_two_ref))):
         for k in range(TILES - 1):
             tile = flat[n, k * channels : (k + 1) * channels, :]
-            wide[n, :, k * 128 : (k + 1) * 128] = tile.astype(F32)
+            weight[:, k * 128 : (k + 1) * 128] = tile.astype(F32)
         last = flat[n, (TILES - 1) * channels : TILES * channels, :].astype(F32)
-        wide[n, :, 2560:2592] = last[:, :32]
-        copies.append(pltpu.make_async_copy(wide.at[n], weight, sems.at[n]))
-        copies[n].start()
+        weight[:, 2560:2592] = last[:, :32]
         bias[...] = last.T[32:33, :]
-    for copy in copies:
-        copy.wait()
 
 
 VMEM = pl.BlockSpec(memory_space=pltpu.VMEM)
 SMEM = pl.BlockSpec(memory_space=pltpu.SMEM)
-ANY = pl.BlockSpec(memory_space=pl.ANY)
 
 
 def vmem(mebibytes):
@@ -500,11 +535,14 @@
     def planes(number, dtype=BF16):
         return jax.ShapeDtypeStruct((number, channels, PLANE), dtype)
 
-    def plane_space(number, dtype=BF16):
-        return pltpu.VMEM((number, channels, PLANE), dtype)
-
-    def tap_space(number):
-        return pltpu.VMEM((number, KDIM, PLANE), BF16)
+    def plane_space(number):
+        return pltpu.VMEM((number, channels, PLANE), BF16)
+
+    def tap_space(*extent):
+        return pltpu.VMEM(extent, BF16)
+
+    def sum_space(*extent):
+        return pltpu.VMEM((*extent, channels, PLANE), F32)
 
     bricks = (slots, channels, CELLS)
     x_planes, cot_planes, edge, layer_mask = pl.pallas_call(
@@ -525,7 +563,7 @@
     taps, one, two, slope_in, g_in, out_in, w1, w2, w2_back = pl.pallas_call(
         inner_kernel,
         out_shape=(
-            jax.ShapeDtypeStruct((9, KDIM, PLANE), BF16),
+            jax.ShapeDtypeStruct((4, KDIM, 2 * PLANE), BF16),
             planes(2, F32),
             planes(2, F32),
             planes(7, F32),
@@ -539,9 +577,12 @@
         out_specs=(VMEM,) * 9,
         scratch_shapes=[
             pltpu.VMEM((channels, 21 * 128), BF16),
-            tap_space(2),
-            plane_space(13, F32),
-            plane_space(11, F32),
+            tap_space(2, KDIM, 2 * PLANE),
+            tap_space(KDIM, PLANE),
+            sum_space(2, 2),
+            sum_space(2),
+            sum_space(2, 2),
+            sum_space(2),
             pltpu.VMEM((9, 16, PLANE), BF16),
         ],
         compiler_params=vmem(20),
@@ -549,18 +590,18 @@
         name="inner",
     )(table, x_planes, cot_planes, layer_mask, weights, biases)
 
-    half = (ROWS // 2, 128)
-    kept, sent = jax.ShapeDtypeStruct(half, F32), jax.ShapeDtypeStruct(half, BF16)
+    rows = (ROWS // 2, 128)
+    kept, sent = jax.ShapeDtypeStruct(rows, F32), jax.ShapeDtypeStruct(rows, BF16)
     keep_two, send_two, slope_out, g_out, out_out = pl.pallas_call(
         outer_kernel,
         out_shape=(kept, sent, planes(1, F32), planes(3), planes(2)),
         in_specs=[SMEM] + [VMEM] * 10,
         out_specs=(VMEM,) * 5,
         scratch_shapes=[
-            tap_space(3),
-            tap_space(3),
-            plane_space(3, F32),
-            plane_space(3, F32),
+            tap_space(KDIM, PLANE),
+            tap_space(KDIM, PLANE),
+            tap_space(KDIM, 2 * PLANE),
+            tap_space(KDIM, 2 * PLANE),
             pltpu.VMEM((3 * channels, KDIM), F32),
             pltpu.VMEM((ROWS, 128), F32),
             pltpu.VMEM((9, 16, PLANE), BF16),
@@ -577,9 +618,10 @@
         in_specs=[SMEM] + [VMEM] * 7,
         out_specs=(VMEM,) * 2,
         scratch_shapes=[
-            tap_space(2),
-            tap_space(10),
-            plane_space(12, F32),
+            tap_space(2, KDIM, 2 * PLANE),
+            tap_space(5, KDIM, 2 * PLANE),
+            sum_space(2, 2),
+            sum_space(2),
             plane_space(8),
             pltpu.VMEM((3 * channels, KDIM), F32),
             pltpu.VMEM((ROWS, 128), F32),
@@ -607,12 +649,8 @@
         gather_kernel,
         out_shape=(weight_shape, weight_shape, bias_shape, bias_shape),
         in_specs=[SMEM] + [VMEM] * len(parts),
-        out_specs=(ANY, ANY, VMEM, VMEM),
-        scratch_shapes=[
-            pltpu.VMEM((2, ROWS, 128), BF16),
-            pltpu.VMEM((2, channels, 27 * channels), F32),
-            pltpu.SemaphoreType.DMA((2,)),
-        ],
+        out_specs=(VMEM,) * 4,
+        scratch_shapes=[pltpu.VMEM((2, ROWS, 128), BF16)],
         compiler_params=vmem(8),
         name="gather",
     )(table, *parts)

time: 66.9 us -> 65.8 us (0.984)
  Pallas kernels: 21.4 us -> 20.2 us
where the time goes in v5:
time: 65.8 us; the launch traced here: 65.5 us
  Pallas kernels  20.2 us (31%)
  blocking collectives  15.1 us (23%)
  waiting for transfers between devices  12.3 us (19%)
  starting transfers between devices  11.6 us (18%)
  other arithmetic  4.19 us (6%)
  local copies, waits for them, and re-layouts  1.39 us (2%)
  between operations  0.74 us (1%)
    all_to_all x1, blocking collectives, shared_sum(): parts = lax.all_to_all(parts, both, 0, 0, axis_index_groups=groups)  15.1 us
    all_to_all x1, waiting for transfers between devices, shared_sum(): copies = lax.all_to_all(copies, both, 0, 0, axis_index_groups=groups)  6.47 us
    pallas_call x1, Pallas kernels, local(): pl.pallas_call(backward_kernel, out_shape=(kept, sent), in_specs=[SMEM] +...  5.4 us
    pallas_call x1, Pallas kernels, local(): pl.pallas_call(inner_kernel, out_shape=(jax.ShapeDtypeStruct((4, KDIM, 2...  5.07 us
    pallas_call x1, Pallas kernels, local(): pl.pallas_call(outer_kernel, out_shape=(kept, sent, planes(1, F32), plane...  4.28 us
    ppermute x2, starting transfers between devices, shared_sum(): lax.ppermute(send, 'space', swap).astype(F32)  4.13 us
    all_to_all x1, starting transfers between devices, shared_sum(): copies = lax.all_to_all(copies, both, 0, 0, axis_index_groups=groups)  3.49 us
    ppermute x1, waiting for transfers between devices, shared_sum(): moved = lax.ppermute(total, 'dp', [(v, v ^ step) for v in range(volumes)])  3.28 us
  transfers between devices with their start and end apart: 9, of which 5 were waited for; matrix products, arithmetic and copies ran while one was open for 8% of the time, Pallas kernels for 9%

profile of v5, /device:TPU:0, one launch (start us, length us, event | category | flops | bytes accessed | tf_op | source)
XLA Modules:
  0.0 65.5 jit_solution(6852422471547769215)
XLA Ops:
  0.6 0.5 collective-permute-start
  1.2 1.2 %pad_maximum_fusion.1.own_ref = bf16[8,96,512]{2,1,0:T(8,128)(2,1)S(1)} fusion(bf16[4,96,512]{2,1,0:T(8,128)(2,1)} %bitcast.27, bf16[4,96,512]{2,1,0:T(8,128)(2,1)} %bitcast.25), kind=kLoop, calls=%fused_computation.1 | loop fusion | flops 393216 | bytes 1572864 | tf_op jit(solution)/shard_map/concatenate | solution.py:529
  2.4 0.7 %slice_bitcast_fusion = (s32[1,32]{1,0:T(1,128)S(1)}, s32[1,32]{1,0:T(1,128)S(1)}, s32[1,32]{1,0:T(1,128)S(1)}, s32[1,32]{1,0:T(1,128)S(1)}) fusion(s32[1,32,26]{1,0,2:T(1,128)} %param.9), kind=kLoop, calls=%fused_computation.7 | loop fusion | bytes 1024 | tf_op jit(solution)/shard_map/squeeze | solution.py:532
  3.1 0.7 %pad_maximum_fusion.3.bias_ref = f32[2,96]{1,0:T(2,128)S(1)} fusion(f32[1,96]{1,0:T(1,128)} %bitcast.28, f32[1,96]{1,0:T(1,128)} %bitcast.29), kind=kLoop, calls=%fused_computation.6 | loop fusion | flops 192 | bytes 1536 | tf_op jit(solution)/shard_map/stack | solution.py:527
  3.8 0.7 %concatenate.9.table = s32[6,32]{1,0:T(8,128)S(1)} concatenate(s32[1,32]{1,0:T(1,128)S(1)} %get-tuple-element.59, s32[1,32]{1,0:T(1,128)S(1)} %get-tuple-element.58, s32[1,32]{1,0:T(1,128)S(1)} %get-tuple-element.60, s32[1,32]{1,0:T(1,128)S(1)} %get-tuple-element.57, s32[1,32]{1,0:T(1,128)} %param.10, s32[1,32]{1,0:T(1,128)S(1)} %broadcast_in_dim.6), dimensions={0} | concatenate | bytes 1536 | tf_op jit(solution)/shard_map/concatenate | solution.py:533
  4.5 1.3 %pad_maximum_fusion.weight_ref = bf16[192,2592]{1,0:T(8,128)(2,1)S(1)} fusion(bf16[96,2592]{1,0:T(8,128)(2,1)} %param.13, bf16[96,2592]{1,0:T(8,128)(2,1)} %param.12), kind=kLoop, calls=%fused_computation | loop fusion | flops 1990656 | bytes 1990656 | tf_op jit(solution)/shard_map/concatenate | solution.py:528
  5.8 1.5 %layout.1 = (bf16[12,96,256]{2,1,0:T(8,128)(2,1)S(1)}, bf16[9,96,256]{2,1,0:T(8,128)(2,1)S(1)}, bf16[4,96,256]{2,1,0:T(8,128)(2,1)S(1)}, f32[3,8,256]{2,1,0:T(8,128)S(1)}) custom-call(s32[6,32]{1,0:T(8,128)S(1)} %concatenate.9.table, bf16[8,96,512]{2,1,0:T(8,128)(2,1)S(1)} %pad_maximum_fusion.1.own_ref, ...), custom_call_target="tpu_custom_call" | custom-call | tf_op jit(solution)/shard_map/layout/pallas_call | solution.py:548
  7.3 0.7 %collective-permute-start.2 = (bf16[4,96,256]{2,1,0:T(8,128)(2,1)S(1)}, bf16[4,96,256]{2,1,0:T(8,128)(2,1)S(1)}, u32[]{:S(2)}, u32[]{:S(2)}) collective-permute-start(bf16[4,96,256]{2,1,0:T(8,128)(2,1)S(1)} %get-tuple-element.31), channel_id=1, source_target_pairs={{4,12},{8,16},{20,28},{12,4},{16,8},{28,20},{5,13},{9,17},{21,29},... | collective-permute-start | bytes 589832 | tf_op jit(solution)/shard_map/ppermute | solution.py:560
  8.0 5.1 %inner.1 = (bf16[4,896,512]{2,1,0:T(8,128)(2,1)S(1)}, f32[2,96,256]{2,1,0:T(8,128)S(1)}, f32[2,96,256]{2,1,0:T(8,128)S(1)}, f32[7,96,256]{2,1,0:T(8,128)S(1)}, b...) custom-call(s32[6,32]{1,0:T(8,128)S(1)} %concatenate.9.table, ...), custom_call_target="tpu_custom_call" | custom-call | flops 8589934592 | bytes 8388608 | tf_op jit(solution)/shard_map/inner/pallas_call | solution.py:563
  13.0 4.3 %outer.1 = (f32[1024,128]{1,0:T(8,128)S(1)}, bf16[1024,128]{1,0:T(8,128)(2,1)S(1)}, f32[1,96,256]{2,1,0:T(8,128)S(1)}, bf16[3,96,256]{2,1,0:T(8,128)(2,1)S(1)}, bf16[2,96,256]{2,1,0:T(8,128)(2,1)S(1)}) custom-call(s32[6,32]{1,0:T(8,128)S(1)} %concatenate.9.table, bf16[4,96,256]{2,1,0:T(8,128)(2,1)S(1)} %collective-permute-done.2.edge_ref, ...), custom_call_target="tpu_custom_call" | custom-call | flops 4294967296 | bytes 8388608 | tf_op jit(solution)/shard_map/outer/pallas_call | solution.py:595
  17.3 5.4 %backward.1 = (f32[1024,128]{1,0:T(8,128)S(1)}, bf16[1024,128]{1,0:T(8,128)(2,1)S(1)}) custom-call(s32[6,32]{1,0:T(8,128)S(1)} %concatenate.9.table, bf16[3,96,256]{2,1,0:T(8,128)(2,1)S(1)} %get-tuple-element.45.g_out_ref, bf16[7,96,256]{2,1,0:T(8,128)(2,1)S(1)} %get-tuple-element.40.g_in_ref, f32[1,96,256]{2,1,0:T(8,128)S(1)} %get-tuple-element.46.slope_out_ref, ...), custom_call_target="tpu_custom_call" | custom-call | flops 4294967296 | bytes 4194304 | tf_op jit(solution)/shard_map/backward/pallas_call | solution.py:615
  22.7 4.0 %collective-permute-start.4 = (bf16[1024,128]{1,0:T(8,128)(2,1)S(1)}, bf16[1024,128]{1,0:T(8,128)(2,1)S(1)}, u32[]{:S(2)}, u32[]{:S(2)}) collective-permute-start(bf16[1024,128]{1,0:T(8,128)(2,1)S(1)} %get-tuple-element.50), channel_id=1, source_target_pairs={{0,4},{4,0},{8,12},{12,8},{16,20},{20,16},{24,28},{28,24},{1,5},{5... | collective-permute-start | bytes 786440 | tf_op jit(solution)/shard_map/ppermute | solution.py:491
  26.9 1.1 %collective-permute-done.4 = bf16[1024,128]{1,0:T(8,128)(2,1)S(1)} collective-permute-done((bf16[1024,128]{1,0:T(8,128)(2,1)S(1)}, bf16[1024,128]{1,0:T(8,128)(2,1)S(1)}, u32[]{:S(2)}, u32[]{:S(2)}) %collective-permute-start.4) | collective-permute-done | bytes 262176 | tf_op jit(solution)/shard_map/ppermute | solution.py:491
  28.0 0.3 collective-permute-done.5
  28.4 15.1 %all_to_all.10 = bf16[8,2,128,128]{3,2,1,0:T(8,128)(2,1)S(1)} all-to-all(bf16[8,2,128,128]{3,2,1,0:T(8,128)(2,1)S(1)} %pad_maximum_fusion.2), channel_id=1, replica_groups={{0,8,16,24,1,9,17,25},{2,10,18,26,3,11,19,27},{4,12,20,28,5,13,21,29},{..., dimensions={0} | all-to-all | bytes 1048576 | tf_op jit(solution)/shard_map/all_to_all | solution.py:495
  43.6 2.7 %collective-permute-start.6 = (bf16[2,128,128]{2,1,0:T(8,128)(2,1)S(1)}, bf16[2,128,128]{2,1,0:T(8,128)(2,1)S(1)}, u32[]{:S(2)}, u32[]{:S(2)}) collective-permute-start(bf16[2,128,128]{2,1,0:T(8,128)(2,1)S(1)} %reduce_sum.12.first_ref), channel_id=1, source_target_pairs={{0,2},{1,3},{2,0},{3,1},{4,6},{5,7},{6,4},{7,5},{8,10},{9,11},{10,... | collective-permute-start | bytes 196616 | tf_op jit(solution)/shard_map/ppermute | solution.py:499
  46.2 3.3 %collective-permute-done.6.second_ref = bf16[2,128,128]{2,1,0:T(8,128)(2,1)S(1)} collective-permute-done((bf16[2,128,128]{2,1,0:T(8,128)(2,1)S(1)}, bf16[2,128,128]{2,1,0:T(8,128)(2,1)S(1)}, u32[]{:S(2)}, u32[]{:S(2)}) %collective-permute-start.6) | collective-permute-done | bytes 65568 | tf_op jit(solution)/shard_map/ppermute | solution.py:499
  49.5 0.8 %copies.1 = bf16[8,2,128,128]{3,2,1,0:T(8,128)(2,1)} custom-call(bf16[2,128,128]{2,1,0:T(8,128)(2,1)S(1)} %reduce_sum.12.first_ref, bf16[2,128,128]{2,1,0:T(8,128)(2,1)S(1)} %collective-permute-done.6.second_ref), custom_call_target="tpu_custom_call" | custom-call | tf_op jit(solution)/shard_map/copies/pallas_call | solution.py:503
  50.4 3.5 %all-to-all-start.1 = ((bf16[8,2,128,128]{3,2,1,0:T(8,128)(2,1)}), bf16[8,2,128,128]{3,2,1,0:T(8,128)(2,1)S(1)}, u32[]{:S(2)}, u32[]{:S(2)}) async-start(bf16[8,2,128,128]{3,2,1,0:T(8,128)(2,1)} %copies.1), calls=%async_computation.1 | async-start | bytes 1048576 | tf_op jit(solution)/shard_map/all_to_all | solution.py:511
  53.9 1.1 %output.1 = (bf16[4,96,512]{2,1,0:T(8,128)(2,1)S(1)}, bf16[4,96,512]{2,1,0:T(8,128)(2,1)S(1)}) custom-call(s32[6,32]{1,0:T(8,128)S(1)} %concatenate.9.table, bf16[2,96,256]{2,1,0:T(8,128)(2,1)S(1)} %get-tuple-element.41.first_ref, bf16[6,96,256]{2,1,0:T(8,128)(2,1)S(1)} %get-tuple-element.42.second_ref), custom_call_target="tpu_custom_call" | custom-call | flops 268435456 | bytes 2097152 | tf_op jit(solution)/shard_map/output/pallas_call | solution.py:634
  55.0 6.5 %all-to-all-done.1.own_ref = bf16[8,2,128,128]{3,2,1,0:T(8,128)(2,1)S(1)} async-done(((bf16[8,2,128,128]{3,2,1,0:T(8,128)(2,1)}), bf16[8,2,128,128]{3,2,1,0:T(8,128)(2,1)S(1)}, u32[]{:S(2)}, u32[]{:S(2)}) %all-to-all-start.1) | async-done | bytes 524320 | tf_op jit(solution)/shard_map/all_to_all | solution.py:511
  61.5 0.8 %add_bitcast_fusion = bf16[1,4,96,512]{3,2,1,0:T(8,128)(2,1)} fusion(bf16[4,96,512]{2,1,0:T(8,128)(2,1)S(1)} %get-tuple-element.43, bf16[4,96,512]{2,1,0:T(8,128)(2,1)S(1)} %collective-permute-done.3), kind=kLoop, calls=%fused_computation.5 | loop fusion | flops 196608 | bytes 1179648 | tf_op jit(solution)/shard_map/broadcast_in_dim | solution.py:644
  62.3 1.1 %collective-permute-done.7.other_ref = bf16[8,2,128,128]{3,2,1,0:T(8,128)(2,1)S(1)} collective-permute-done((bf16[8,2,128,128]{3,2,1,0:T(8,128)(2,1)S(1)}, bf16[8,2,128,128]{3,2,1,0:T(8,128)(2,1)S(1)}, u32[]{:S(2)}, u32[]{:S(2)}) %collective-permute-start.7) | collective-permute-done | bytes 524320 | tf_op jit(solution)/shard_map/ppermute | solution.py:512
  63.4 2.1 %gather.1 = (f32[96,2592]{1,0:T(8,128)}, f32[96,2592]{1,0:T(8,128)}, f32[1,96]{1,0:T(1,128)}, f32[1,96]{1,0:T(1,128)}) custom-call(s32[6,32]{1,0:T(8,128)S(1)} %concatenate.9.table, bf16[8,2,128,128]{3,2,1,0:T(8,128)(2,1)S(1)} %all-to-all-done.1.own_ref, bf16[8,2,128,128]{3,2,1,0:T(8,128)(2,1)S(1)} %collective-permute-done.7.other_ref), custom_call_target="tpu_custom_call" | custom-call | tf_op jit(solution)/shard_map/gather/pallas_call | solution.py:648
  (13 shorter events, 0.5 us)
Async XLA Ops:
  0.6 5.1 %collective-permute-start = (bf16[4,96,512]{2,1,0:T(8,128)(2,1)}, bf16[4,96,512]{2,1,0:T(8,128)(2,1)S(1)}, u32[]{:S(2)}, u32[]{:S(2)}) collective-permute-start(bf16[4,96,512]{2,1,0:T(8,128)(2,1)} %bitcast.24), channel_id=1, source_target_pairs={{0,4},{4,0},{8,12},{12,8},{16,20},{20,16},{24,28},{28,24},{1,5},{5... | collective-permute-start | bytes 1179656 | tf_op jit(solution)/shard_map/ppermute | solution.py:525
  1.1 4.6 %collective-permute-start.1 = (bf16[4,96,512]{2,1,0:T(8,128)(2,1)}, bf16[4,96,512]{2,1,0:T(8,128)(2,1)S(1)}, u32[]{:S(2)}, u32[]{:S(2)}) collective-permute-start(bf16[4,96,512]{2,1,0:T(8,128)(2,1)} %bitcast.26), channel_id=1, source_target_pairs={{0,4},{4,0},{8,12},{12,8},{16,20},{20,16},{24,28},{28,24},{1,5},{5... | collective-permute-start | bytes 1179656 | tf_op jit(solution)/shard_map/ppermute | solution.py:526
  7.3 5.8 %collective-permute-start.2 = (bf16[4,96,256]{2,1,0:T(8,128)(2,1)S(1)}, bf16[4,96,256]{2,1,0:T(8,128)(2,1)S(1)}, u32[]{:S(2)}, u32[]{:S(2)}) collective-permute-start(bf16[4,96,256]{2,1,0:T(8,128)(2,1)S(1)} %get-tuple-element.31), channel_id=1, source_target_pairs={{4,12},{8,16},{20,28},{12,4},{16,8},{28,20},{5,13},{9,17},{21,29},... | collective-permute-start | bytes 589832 | tf_op jit(solution)/shard_map/ppermute | solution.py:560
  22.7 5.2 %collective-permute-start.4 = (bf16[1024,128]{1,0:T(8,128)(2,1)S(1)}, bf16[1024,128]{1,0:T(8,128)(2,1)S(1)}, u32[]{:S(2)}, u32[]{:S(2)}) collective-permute-start(bf16[1024,128]{1,0:T(8,128)(2,1)S(1)} %get-tuple-element.50), channel_id=1, source_target_pairs={{0,4},{4,0},{8,12},{12,8},{16,20},{20,16},{24,28},{28,24},{1,5},{5... | collective-permute-start | bytes 786440 | tf_op jit(solution)/shard_map/ppermute | solution.py:491
  26.8 1.5 %collective-permute-start.5 = (bf16[1024,128]{1,0:T(8,128)(2,1)S(1)}, bf16[1024,128]{1,0:T(8,128)(2,1)S(1)}, u32[]{:S(2)}, u32[]{:S(2)}) collective-permute-start(bf16[1024,128]{1,0:T(8,128)(2,1)S(1)} %get-tuple-element.52), channel_id=1, source_target_pairs={{0,4},{4,0},{8,12},{12,8},{16,20},{20,16},{24,28},{28,24},{1,5},{5... | collective-permute-start | bytes 786440 | tf_op jit(solution)/shard_map/ppermute | solution.py:491
  43.6 5.9 %collective-permute-start.6 = (bf16[2,128,128]{2,1,0:T(8,128)(2,1)S(1)}, bf16[2,128,128]{2,1,0:T(8,128)(2,1)S(1)}, u32[]{:S(2)}, u32[]{:S(2)}) collective-permute-start(bf16[2,128,128]{2,1,0:T(8,128)(2,1)S(1)} %reduce_sum.12.first_ref), channel_id=1, source_target_pairs={{0,2},{1,3},{2,0},{3,1},{4,6},{5,7},{6,4},{7,5},{8,10},{9,11},{10,... | collective-permute-start | bytes 196616 | tf_op jit(solution)/shard_map/ppermute | solution.py:499
  50.4 11.1 %all-to-all-start.1 = ((bf16[8,2,128,128]{3,2,1,0:T(8,128)(2,1)}), bf16[8,2,128,128]{3,2,1,0:T(8,128)(2,1)S(1)}, u32[]{:S(2)}, u32[]{:S(2)}) async-start(bf16[8,2,128,128]{3,2,1,0:T(8,128)(2,1)} %copies.1), calls=%async_computation.1 | async-start | bytes 1048576 | tf_op jit(solution)/shard_map/all_to_all | solution.py:511
  54.9 6.6 %collective-permute-start.3 = (bf16[4,96,512]{2,1,0:T(8,128)(2,1)S(1)}, bf16[4,96,512]{2,1,0:T(8,128)(2,1)S(1)}, u32[]{:S(2)}, u32[]{:S(2)}) collective-permute-start(bf16[4,96,512]{2,1,0:T(8,128)(2,1)S(1)} %get-tuple-element.44), channel_id=1, source_target_pairs={{0,4},{4,0},{8,12},{12,8},{16,20},{20,16},{24,28},{28,24},{1,5},{5... | collective-permute-start | bytes 1179656 | tf_op jit(solution)/shard_map/ppermute | solution.py:644
  61.5 1.9 %collective-permute-start.7 = (bf16[8,2,128,128]{3,2,1,0:T(8,128)(2,1)S(1)}, bf16[8,2,128,128]{3,2,1,0:T(8,128)(2,1)S(1)}, u32[]{:S(2)}, u32[]{:S(2)}) collective-permute-start(bf16[8,2,128,128]{3,2,1,0:T(8,128)(2,1)S(1)} %all-to-all-done.1.own_ref), channel_id=1, source_target_pairs={{0,4},{4,0},{8,12},{12,8},{16,20},{20,16},{24,28},{28,24},{1,5},{5... | collective-permute-start | bytes 1572872 | tf_op jit(solution)/shard_map/ppermute | solution.py:512

commit v6 on v5

--- a/solution.py
+++ b/solution.py
@@ -11,8 +11,7 @@
 KDIM = 896
 TILES = 21
 ROWS = 2048
-OFFSETS = (4, 10, 12, 21)
-DOWN, NEAR_Y, NEAR_Z, UP, LIVE, DEVICE = range(6)
+DOWN, NEAR_Y, NEAR_Z, UP, LIVE, DEVICE = 4, 10, 12, 21, 26, 27
 F32 = jnp.float32
 BF16 = jnp.bfloat16
 
@@ -45,15 +44,15 @@
 
 
 def space_index(table, count):
-    return jnp.clip(table[DEVICE, 0] & 255, 0, count - 1)
+    return jnp.clip(table[DEVICE, 0, 0] & 255, 0, count - 1)
 
 
 def slot_place(table, slot, pair_slots):
     shift = pair_slots.bit_length() - 1
-    up = table[UP, slot]
+    up = table[UP, 0, slot]
     inside = jnp.logical_and(up >= 0, up >> shift == slot >> shift)
     parity = jnp.where(inside, 0, 1)
-    place = jnp.where(table[NEAR_Y, slot] >= 0, 2, 0) + jnp.where(table[NEAR_Z, slot] >= 0, 1, 0)
+    place = jnp.where(table[NEAR_Y, 0, slot] >= 0, 2, 0) + jnp.where(table[NEAR_Z, 0, slot] >= 0, 1, 0)
     return parity, place
 
 
@@ -87,30 +86,26 @@
     low[1] = part(right, 0)
 
 
-def half(k):
-    return pl.ds((k & 1) * PLANE, PLANE)
-
-
-def weight_products(total, grads, taps):
-    blank = jnp.zeros((total.shape[0] // 3, PLANE), BF16)
+def place(k):
+    return pl.ds(k * PLANE, PLANE)
+
+
+def weight_products(grads, planes, taps):
+    blank = jnp.zeros_like(grads(3))
 
     def left(p):
         inside = [grads(p + 1 - a) if 0 <= p + 1 - a < EDGE else blank for a in range(3)]
         return jnp.concatenate(inside, axis=0)
 
-    for p in range(-1, EDGE + 1, 2):
-        both_left = jnp.concatenate([left(p), left(p + 1)], axis=1)
-        part = lax.dot_general(
-            both_left, taps(p), (((1,), (1,)), ((), ())), preferred_element_type=F32
-        )
-        total[...] = part if p == -1 else total[...] + part
+    lefts = jnp.concatenate([left(p) for p in planes], axis=1)
+    return lax.dot_general(lefts, taps, (((1,), (1,)), ((), ())), preferred_element_type=F32)
 
 
 def write_tiles(flat, total, channels, even):
     lane = lax.broadcasted_iota(jnp.int32, (channels, 128), 1)
     blank = jnp.zeros((channels, 128), F32)
-    low = total[pl.ds(pl.multiple_of(jnp.where(even, 0, 2 * channels), channels), channels), :]
-    high = total[pl.ds(pl.multiple_of(jnp.where(even, 2 * channels, 0), channels), channels), :]
+    first, last = total[:channels, :], total[2 * channels :, :]
+    low, high = jnp.where(even, first, last), jnp.where(even, last, first)
     second = jnp.concatenate([total[channels : 2 * channels, :], blank], axis=1)
     third = jnp.concatenate([high, blank], axis=1)
     second = pltpu.roll(second, 96, 1)
@@ -131,7 +126,7 @@
 
 def split_tiles(keep_ref, send_ref, flat, table):
     rows = keep_ref.shape[0]
-    even = (table[DEVICE, 0] & 1) == 0
+    even = (table[DEVICE, 0, 0] & 1) == 0
     here = pl.multiple_of(jnp.where(even, 0, rows), rows)
     there = pl.multiple_of(jnp.where(even, rows, 0), rows)
     keep_ref[...] = flat[pl.ds(here, rows), :]
@@ -143,9 +138,9 @@
     x_ref, cot_ref, edge_ref, mask_ref, bricks, cots,
 ):
     slots, channels = pair_ref.shape[0], pair_ref.shape[1]
-    all_slots = table.shape[1]
+    all_slots = table.shape[2]
     me = space_index(table, all_slots // slots)
-    layer = table[DEVICE, 0] >> 16
+    layer = table[DEVICE, 0, 0] >> 16
     even = layer == 0
 
     live = [[jnp.float32(0)] * 4 for _ in range(2)]
@@ -153,20 +148,20 @@
     for device in (me, me ^ 1):
         for s in range(slots):
             slot = jnp.clip(device * slots + s, 0, all_slots - 1)
-            parity, place = slot_place(table, slot, 2 * slots)
-            alive = table[LIVE, slot].astype(F32)
+            parity, spot = slot_place(table, slot, 2 * slots)
+            alive = table[LIVE, 0, slot].astype(F32)
             scale = jnp.full((channels, CELLS), alive, F32).astype(BF16)
             own = device is me
-            bricks[parity, place] = (own_ref[s] if own else pair_ref[s]) * scale
-            cots[parity, place] = (own_ref[slots + s] if own else cot_pair_ref[s]) * scale
-            outer = jnp.where(even, table[DOWN, slot], table[UP, slot])
-            alive_outer = table[LIVE, jnp.clip(outer, 0, all_slots - 1)].astype(F32)
+            bricks[parity, spot] = (own_ref[s] if own else pair_ref[s]) * scale
+            cots[parity, spot] = (own_ref[slots + s] if own else cot_pair_ref[s]) * scale
+            outer = jnp.where(even, table[DOWN, 0, slot], table[UP, 0, slot])
+            alive_outer = table[LIVE, 0, jnp.clip(outer, 0, all_slots - 1)].astype(F32)
             alive_outer = jnp.where(outer >= 0, alive_outer, 0.0)
             for k in range(4):
                 for p in range(2):
-                    here = jnp.logical_and(parity == p, place == k)
+                    here = jnp.logical_and(parity == p, spot == k)
                     live[p][k] = jnp.where(here, alive, live[p][k])
-                here = jnp.logical_and(parity == layer, place == k)
+                here = jnp.logical_and(parity == layer, spot == k)
                 beyond[k] = jnp.where(here, alive_outer, beyond[k])
     mask_ref[0] = lane_mask(beyond)
     mask_ref[1] = lane_mask([jnp.where(even, live[0][k], live[1][k]) for k in range(4)])
@@ -261,11 +256,11 @@
 
 def inner_kernel(
     table, x_ref, cot_ref, layer_mask, weight_ref, bias_ref,
-    taps_ref, one_ref, two_ref, slope_ref, g_ref, out_ref, w1_taps, w2_taps, w2_back,
+    taps_ref, one_ref, two_ref, slope_ref, g_ref, out_ref, total_ref, w1_taps, w2_taps, w2_back,
     wide, xc, hc, full_one, low_one, full_two, low_two, masks_ref,
 ):
     channels = x_ref.shape[1]
-    even = (table[DEVICE, 0] >> 16) == 0
+    even = (table[DEVICE, 0, 0] >> 16) == 0
     fill_masks(masks_ref)
     tap_weights(w1_taps, weight_ref[:channels, :], wide, even)
     bias_one, bias_two = column(bias_ref[0:1]), column(bias_ref[1:2])
@@ -273,15 +268,15 @@
     for k in range(2):
         xc[k, 9 * channels :, :] = ones
     for k in range(4):
-        taps_ref[k, 9 * channels :, :] = ones
+        taps_ref[9 * channels :, 2 * k * PLANE : (2 * k + 2) * PLANE] = ones
     hc[9 * channels :, :] = ones[:, :PLANE]
 
     def write_x(p):
-        write_taps(xc.at[(p >> 1) & 1, :, half(p)], x_ref[p], masks_ref)
+        write_taps(xc.at[(p >> 1) & 1, :, place(p & 1)], x_ref[p], masks_ref)
 
     def finish_one(q, pre):
         hidden, slope = hidden_plane(pre + bias_one, layer_mask[layer_of(q)][:1])
-        dst = taps_ref.at[(q - 1) // 2, :, half(q - 1)] if q < 9 else hc
+        dst = taps_ref.at[:, place(q - 1)] if q < 9 else hc
         write_taps(dst, hidden, masks_ref)
         if q < EDGE:
             slope_ref[q - 1] = slope
@@ -315,7 +310,8 @@
         if j == 6:
             finish_one(9, full_one[last, 0])
         if 3 <= j <= 6:
-            pair_sums(full_two.at[now], low_two, w2_taps, taps_ref[j - 3], j == 3)
+            hidden = taps_ref[:, (2 * j - 6) * PLANE : (2 * j - 4) * PLANE]
+            pair_sums(full_two.at[now], low_two, w2_taps, hidden, j == 3)
         if j == 7:
             third = product(w2_taps, hc[...], slice(2, 3))
             finish_two(8, low_two[0] + third)
@@ -324,16 +320,18 @@
         if 5 <= j:
             finish_two(2 * j - 8, full_two[last, 0])
             finish_two(2 * j - 7, full_two[last, 1])
+    hidden = taps_ref[:, 2 * PLANE : 6 * PLANE]
+    total_ref[...] = weight_products(lambda q: g_ref[q - 2], range(3, 7), hidden)
 
 
 def outer_kernel(
     table, edge_ref, cot_ref, layer_mask, w1_taps, w2_taps, bias_ref,
-    taps_ref, one_ref, two_ref, g_in_ref,
+    taps_ref, one_ref, two_ref, g_in_ref, total_ref,
     keep_ref, send_ref, slope_ref, g_ref, out_ref,
-    xc, hc, x_pair, h_pair, total, flat, masks_ref,
+    xc, hc, x_pair, h_pair, flat, masks_ref,
 ):
     channels = cot_ref.shape[1]
-    even = (table[DEVICE, 0] >> 16) == 0
+    even = (table[DEVICE, 0, 0] >> 16) == 0
     fill_masks(masks_ref)
     bias_one, bias_two = column(bias_ref[0:1]), column(bias_ref[1:2])
     ones = jnp.ones((KDIM - 9 * channels, 2 * PLANE), BF16)
@@ -342,8 +340,8 @@
     for pair in (x_pair, h_pair):
         pair[9 * channels :, :] = ones
     write_taps(xc, edge_ref[2], masks_ref)
-    write_taps(x_pair.at[:, half(0)], edge_ref[1], masks_ref)
-    write_taps(x_pair.at[:, half(1)], edge_ref[0], masks_ref)
+    write_taps(x_pair.at[:, place(0)], edge_ref[1], masks_ref)
+    write_taps(x_pair.at[:, place(1)], edge_ref[0], masks_ref)
 
     def three_planes(weights, single, pair, parts):
         first = product(weights, single[...], slice(0, 1))
@@ -358,7 +356,7 @@
 
     for q, pre in zip(range(-2, 1), three_planes(w1_taps, xc, x_pair, one_ref)):
         hidden, slope = hidden_plane(pre + bias_one, layer_mask[layer_of(q)][:1])
-        write_taps(hc if q == -2 else h_pair.at[:, half(q + 1)], hidden, masks_ref)
+        write_taps(hc if q == -2 else h_pair.at[:, place(q + 1)], hidden, masks_ref)
         if q == 0:
             slope_ref[0] = slope
     for q, pre in zip(range(-1, 2), three_planes(w2_taps, hc, h_pair, two_ref)):
@@ -371,18 +369,17 @@
     def grads(q):
         return g_ref[q + 1] if q < 2 else g_in_ref[q - 2]
 
-    def taps(p):
-        return h_pair[...] if p < 0 else taps_ref[p // 2]
-
-    weight_products(total, grads, taps)
+    planes = (-1, 0, 1, 2, 7, 8)
+    taps = [h_pair[...], taps_ref[:, : 2 * PLANE], taps_ref[:, 6 * PLANE :]]
+    total = total_ref[...] + weight_products(grads, planes, jnp.concatenate(taps, axis=1))
     write_tiles(flat, total, channels, even)
     split_tiles(keep_ref, send_ref, flat, table)
 
 
 def output_kernel(table, first_ref, second_ref, keep_ref, send_ref, outs, bricks):
     slots, channels = keep_ref.shape[0], keep_ref.shape[1]
-    me = space_index(table, table.shape[1] // slots)
-    layer = table[DEVICE, 0] >> 16
+    me = space_index(table, table.shape[2] // slots)
+    layer = table[DEVICE, 0, 0] >> 16
     even = layer == 0
     outs[:2] = first_ref[...]
     outs[2:] = second_ref[...]
@@ -399,28 +396,28 @@
             bricks[2 * y + 1, :, pair] = both[:, 128:]
     for target, device in ((keep_ref, me), (send_ref, me ^ 1)):
         for s in range(slots):
-            slot = jnp.clip(device * slots + s, 0, table.shape[1] - 1)
-            parity, place = slot_place(table, slot, 2 * slots)
+            slot = jnp.clip(device * slots + s, 0, table.shape[2] - 1)
+            parity, spot = slot_place(table, slot, 2 * slots)
             scale = jnp.where(parity == layer, 1.0, 0.0)
-            target[s] = bricks[place] * jnp.full((channels, CELLS), scale, F32).astype(BF16)
+            target[s] = bricks[spot] * jnp.full((channels, CELLS), scale, F32).astype(BF16)
 
 
 def backward_kernel(
     table, g_out_ref, g_in_ref, slope_out_ref, slope_in_ref, x_ref, edge_ref, w2_back,
-    keep_ref, send_ref, gc, xc, full, low, grad, total, flat, masks_ref,
+    keep_ref, send_ref, gc, xc, full, low, grad, flat, masks_ref,
 ):
     channels = x_ref.shape[1]
-    even = (table[DEVICE, 0] >> 16) == 0
+    even = (table[DEVICE, 0, 0] >> 16) == 0
     fill_masks(masks_ref)
     ones = jnp.ones((KDIM - 9 * channels, 2 * PLANE), BF16)
     for k in range(2):
         gc[k, 9 * channels :, :] = ones
     for k in range(5):
-        xc[k, 9 * channels :, :] = ones
+        xc[9 * channels :, 2 * k * PLANE : (2 * k + 2) * PLANE] = ones
 
     def write_g(q):
         plane = g_out_ref[q + 1] if q < 2 else g_in_ref[q - 2]
-        write_taps(gc.at[((q + 1) >> 1) & 1, :, half(q + 1)], plane, masks_ref)
+        write_taps(gc.at[((q + 1) >> 1) & 1, :, place((q + 1) & 1)], plane, masks_ref)
 
     write_g(-1)
     write_g(0)
@@ -433,12 +430,12 @@
                     write_g(q)
             for q in (2 * j - 1, 2 * j):
                 plane = edge_ref[0] if q < 0 else x_ref[q]
-                write_taps(xc.at[j, :, half(q + 1)], plane, masks_ref)
+                write_taps(xc.at[:, place(q + 1)], plane, masks_ref)
         if j >= 2:
             for k, q in enumerate((2 * j - 4, 2 * j - 3)):
                 slope = slope_out_ref[0] if q == 0 else slope_in_ref[q - 1]
                 grad[q] = (full[last, k] * slope).astype(BF16)
-    weight_products(total, lambda q: grad[q], lambda p: xc[(p + 1) // 2])
+    total = weight_products(lambda q: grad[q], range(-1, EDGE + 1), xc[...])
     write_tiles(flat, total, channels, even)
     split_tiles(keep_ref, send_ref, flat, table)
 
@@ -454,7 +451,7 @@
 ):
     chunks, _, rows, _ = own_ref.shape
     channels = w_one_ref.shape[0]
-    core = table[DEVICE, 0] & 1
+    core = table[DEVICE, 0, 0] & 1
     for half, source in enumerate((own_ref, other_ref)):
         base = jnp.where(core == half, 0, chunks * rows)
         for k in range(chunks):
@@ -529,8 +526,8 @@
     own = jnp.concatenate([volume, cotangent], axis=0)
     device = me + 256 * lax.axis_index("dp").astype(jnp.int32)
     device = device + 65536 * ((me ^ (me >> 1)) & 1)
-    table = [neighbours[:, :, k] for k in OFFSETS]
-    table = jnp.concatenate([*table, active, jnp.full_like(active, device)], axis=0)
+    rows = [neighbours.transpose(2, 0, 1), active[None], jnp.full_like(active, device)[None]]
+    table = jnp.concatenate(rows, axis=0)
 
     def planes(number, dtype=BF16):
         return jax.ShapeDtypeStruct((number, channels, PLANE), dtype)
@@ -560,21 +557,22 @@
     outer = lax.ppermute(edge, "space", hop)
 
     rearranged = jax.ShapeDtypeStruct((3, channels, KDIM), BF16)
-    taps, one, two, slope_in, g_in, out_in, w1, w2, w2_back = pl.pallas_call(
+    taps, one, two, slope_in, g_in, out_in, part_two, w1, w2, w2_back = pl.pallas_call(
         inner_kernel,
         out_shape=(
-            jax.ShapeDtypeStruct((4, KDIM, 2 * PLANE), BF16),
+            jax.ShapeDtypeStruct((KDIM, EDGE * PLANE), BF16),
             planes(2, F32),
             planes(2, F32),
             planes(7, F32),
             planes(7),
             planes(6),
+            jax.ShapeDtypeStruct((3 * channels, KDIM), F32),
             rearranged,
             rearranged,
             rearranged,
         ),
         in_specs=[SMEM] + [VMEM] * 5,
-        out_specs=(VMEM,) * 9,
+        out_specs=(VMEM,) * 10,
         scratch_shapes=[
             pltpu.VMEM((channels, 21 * 128), BF16),
             tap_space(2, KDIM, 2 * PLANE),
@@ -595,14 +593,13 @@
     keep_two, send_two, slope_out, g_out, out_out = pl.pallas_call(
         outer_kernel,
         out_shape=(kept, sent, planes(1, F32), planes(3), planes(2)),
-        in_specs=[SMEM] + [VMEM] * 10,
+        in_specs=[SMEM] + [VMEM] * 11,
         out_specs=(VMEM,) * 5,
         scratch_shapes=[
             tap_space(KDIM, PLANE),
             tap_space(KDIM, PLANE),
             tap_space(KDIM, 2 * PLANE),
             tap_space(KDIM, 2 * PLANE),
-            pltpu.VMEM((3 * channels, KDIM), F32),
             pltpu.VMEM((ROWS, 128), F32),
             pltpu.VMEM((9, 16, PLANE), BF16),
         ],
@@ -611,6 +608,7 @@
         name="outer",
     )(
         table, outer, cot_planes, layer_mask, w1, w2, biases, taps, one, two, g_in,
+        part_two,
     )
     keep_one, send_one = pl.pallas_call(
         backward_kernel,
@@ -619,11 +617,10 @@
         out_specs=(VMEM,) * 2,
         scratch_shapes=[
             tap_space(2, KDIM, 2 * PLANE),
-            tap_space(5, KDIM, 2 * PLANE),
+            tap_space(KDIM, (EDGE + 2) * PLANE),
             sum_space(2, 2),
             sum_space(2),
             plane_space(8),
-            pltpu.VMEM((3 * channels, KDIM), F32),
             pltpu.VMEM((ROWS, 128), F32),
             pltpu.VMEM((9, 16, PLANE), BF16),
         ],

time: 65.8 us -> 66.7 us (1.014)
  Pallas kernels: 20.2 us -> 22.9 us
  local copies, waits for them, and re-layouts: 1.39 us -> 0.07 us
  blocking collectives: 15.1 us -> 13.9 us
  other arithmetic: 4.19 us -> 5.02 us
    pallas_call x1, Pallas kernels: 5.4 us -> 6.88 us  [local(): pl.pallas_call(backward_kernel, out_shape=(kept, sent), in_specs=[SMEM] +...]
    pallas_call x1, Pallas kernels: 5.07 us -> 6.26 us  [local(): pl.pallas_call(inner_kernel, out_shape=(jax.ShapeDtypeStruct((KDIM, EDGE...]
    all_to_all x1, blocking collectives: 15.1 us -> 13.9 us  [shared_sum(): parts = lax.all_to_all(parts, both, 0, 0, axis_index_groups=groups)]
    concatenate x0 -> x1, other arithmetic: none -> 0.82 us  [local(): table = jnp.concatenate(rows, axis=0)]
    squeeze x1 -> x0, local copies, waits for them, and re-layouts: 0.71 us -> none  [local(): table = [neighbours[:, :, k] for k in OFFSETS]]
  transfers between devices with their start and end apart: 9 -> 9, of which waited for: 5 -> 5; matrix products, arithmetic and copies ran while one was open for 8% -> 7% of each run, Pallas kernels for 9% -> 11%
where the time goes in v6:
time: 66.7 us; the launch traced here: 66.3 us
  Pallas kernels  22.9 us (34%)
  blocking collectives  13.9 us (21%)
  waiting for transfers between devices  12.1 us (18%)
  starting transfers between devices  11.6 us (17%)
  other arithmetic  5.02 us (8%)
  between operations  0.75 us (1%)
    all_to_all x1, blocking collectives, shared_sum(): parts = lax.all_to_all(parts, both, 0, 0, axis_index_groups=groups)  13.9 us
    pallas_call x1, Pallas kernels, local(): pl.pallas_call(backward_kernel, out_shape=(kept, sent), in_specs=[SMEM] +...  6.88 us
    all_to_all x1, waiting for transfers between devices, shared_sum(): copies = lax.all_to_all(copies, both, 0, 0, axis_index_groups=groups)  6.3 us
    pallas_call x1, Pallas kernels, local(): pl.pallas_call(inner_kernel, out_shape=(jax.ShapeDtypeStruct((KDIM, EDGE...  6.26 us
    ppermute x2, starting transfers between devices, shared_sum(): lax.ppermute(send, 'space', swap).astype(F32)  4.11 us
    pallas_call x1, Pallas kernels, local(): pl.pallas_call(outer_kernel, out_shape=(kept, sent, planes(1, F32), plane...  3.8 us
    all_to_all x1, starting transfers between devices, shared_sum(): copies = lax.all_to_all(copies, both, 0, 0, axis_index_groups=groups)  3.49 us
    ppermute x1, waiting for transfers between devices, shared_sum(): moved = lax.ppermute(total, 'dp', [(v, v ^ step) for v in range(volumes)])  3.28 us
  transfers between devices with their start and end apart: 9, of which 5 were waited for; matrix products, arithmetic and copies ran while one was open for 7% of the time, Pallas kernels for 11%

profile of v6, /device:TPU:0, one launch (start us, length us, event | category | flops | bytes accessed | tf_op | source)
XLA Modules:
  0.0 66.3 jit_solution(16078409223728258750)
XLA Ops:
  0.6 0.5 collective-permute-start
  1.2 1.2 %pad_maximum_fusion.1.own_ref = bf16[8,96,512]{2,1,0:T(8,128)(2,1)S(1)} fusion(bf16[4,96,512]{2,1,0:T(8,128)(2,1)} %bitcast.22, bf16[4,96,512]{2,1,0:T(8,128)(2,1)} %bitcast.20), kind=kLoop, calls=%fused_computation.1 | loop fusion | flops 393216 | bytes 1572864 | tf_op jit(solution)/shard_map/concatenate | solution.py:526
  2.5 0.8 %add_add_fusion.table = s32[28,1,32]{2,1,0:T(1,128)S(1)} fusion(s32[1,1,32]{2,1,0:T(1,128)} %bitcast.24, s32[26,1,32]{2,1,0:T(1,128)} %bitcast.23, s32[28]{0:T(128)S(1)} %pad.10.clone), kind=kLoop, calls=%fused_computation.6 | loop fusion | flops 1792 | bytes 7152 | tf_op jit(solution)/shard_map/concatenate | solution.py:530
  3.3 0.7 %pad_maximum_fusion.3.bias_ref = f32[2,96]{1,0:T(2,128)S(1)} fusion(f32[1,96]{1,0:T(1,128)} %bitcast.25, f32[1,96]{1,0:T(1,128)} %bitcast.26), kind=kLoop, calls=%fused_computation.7 | loop fusion | flops 192 | bytes 1536 | tf_op jit(solution)/shard_map/stack | solution.py:524
  4.0 1.3 %pad_maximum_fusion.weight_ref = bf16[192,2592]{1,0:T(8,128)(2,1)S(1)} fusion(bf16[96,2592]{1,0:T(8,128)(2,1)} %param.13, bf16[96,2592]{1,0:T(8,128)(2,1)} %param.12), kind=kLoop, calls=%fused_computation | loop fusion | flops 1990656 | bytes 1990656 | tf_op jit(solution)/shard_map/concatenate | solution.py:525
  5.3 1.7 %layout.1 = (bf16[12,96,256]{2,1,0:T(8,128)(2,1)S(1)}, bf16[9,96,256]{2,1,0:T(8,128)(2,1)S(1)}, bf16[4,96,256]{2,1,0:T(8,128)(2,1)S(1)}, f32[3,8,256]{2,1,0:T(8,128)S(1)}) custom-call(s32[28,1,32]{2,1,0:T(1,128)S(1)} %add_add_fusion.table, bf16[8,96,512]{2,1,0:T(8,128)(2,1)S(1)} %pad_maximum_fusion.1.own_ref, ...), custom_call_target="tpu_custom_call" | custom-call | tf_op jit(solution)/shard_map/layout/pallas_call | solution.py:545
  7.0 0.7 %collective-permute-start.2 = (bf16[4,96,256]{2,1,0:T(8,128)(2,1)S(1)}, bf16[4,96,256]{2,1,0:T(8,128)(2,1)S(1)}, u32[]{:S(2)}, u32[]{:S(2)}) collective-permute-start(bf16[4,96,256]{2,1,0:T(8,128)(2,1)S(1)} %get-tuple-element.32), channel_id=1, source_target_pairs={{4,12},{8,16},{20,28},{12,4},{16,8},{28,20},{5,13},{9,17},{21,29},... | collective-permute-start | bytes 589832 | tf_op jit(solution)/shard_map/ppermute | solution.py:557
  7.6 6.3 %inner.1 = (bf16[896,2048]{1,0:T(8,128)(2,1)S(1)}, f32[2,96,256]{2,1,0:T(8,128)S(1)}, f32[2,96,256]{2,1,0:T(8,128)S(1)}, f32[7,96,256]{2,1,0:T(8,128)S(1)}, bf16...) custom-call(s32[28,1,32]{2,1,0:T(1,128)S(1)} %add_add_fusion.table, ...), custom_call_target="tpu_custom_call" | custom-call | flops 8589934592 | bytes 8388608 | tf_op jit(solution)/shard_map/inner/pallas_call | solution.py:560
  13.9 3.8 %outer.1 = (f32[1024,128]{1,0:T(8,128)S(1)}, bf16[1024,128]{1,0:T(8,128)(2,1)S(1)}, f32[1,96,256]{2,1,0:T(8,128)S(1)}, bf16[3,96,256]{2,1,0:T(8,128)(2,1)S(1)}, bf16[2,96,256]{2,1,0:T(8,128)(2,1)S(1)}) custom-call(s32[28,1,32]{2,1,0:T(1,128)S(1)} %add_add_fusion.table, bf16[4,96,256]{2,1,0:T(8,128)(2,1)S(1)} %collective-permute-done.2.edge_ref, ...), custom_call_target="tpu_custom_call" | custom-call | flops 4294967296 | bytes 8388608 | tf_op jit(solution)/shard_map/outer/pallas_call | solution.py:593
  17.7 6.9 %backward.1 = (f32[1024,128]{1,0:T(8,128)S(1)}, bf16[1024,128]{1,0:T(8,128)(2,1)S(1)}) custom-call(s32[28,1,32]{2,1,0:T(1,128)S(1)} %add_add_fusion.table, bf16[3,96,256]{2,1,0:T(8,128)(2,1)S(1)} %get-tuple-element.47.g_out_ref, bf16[7,96,256]{2,1,0:T(8,128)(2,1)S(1)} %get-tuple-element.41.g_in_ref, f32[1,96,256]{2,1,0:T(8,128)S(1)} %get-tuple-element.48.slope_out_ref, ...), custom_call_target="tpu_custom_call" | custom-call | flops 4294967296 | bytes 4194304 | tf_op jit(solution)/shard_map/backward/pallas_call | solution.py:613
  24.6 4.0 %collective-permute-start.4 = (bf16[1024,128]{1,0:T(8,128)(2,1)S(1)}, bf16[1024,128]{1,0:T(8,128)(2,1)S(1)}, u32[]{:S(2)}, u32[]{:S(2)}) collective-permute-start(bf16[1024,128]{1,0:T(8,128)(2,1)S(1)} %get-tuple-element.52), channel_id=1, source_target_pairs={{0,4},{4,0},{8,12},{12,8},{16,20},{20,16},{24,28},{28,24},{1,5},{5... | collective-permute-start | bytes 786440 | tf_op jit(solution)/shard_map/ppermute | solution.py:488
  28.7 0.1 collective-permute-start.5
  28.7 1.1 %collective-permute-done.4 = bf16[1024,128]{1,0:T(8,128)(2,1)S(1)} collective-permute-done((bf16[1024,128]{1,0:T(8,128)(2,1)S(1)}, bf16[1024,128]{1,0:T(8,128)(2,1)S(1)}, u32[]{:S(2)}, u32[]{:S(2)}) %collective-permute-start.4) | collective-permute-done | bytes 262176 | tf_op jit(solution)/shard_map/ppermute | solution.py:488
  29.9 0.3 collective-permute-done.5
  30.3 13.9 %all_to_all.10 = bf16[8,2,128,128]{3,2,1,0:T(8,128)(2,1)S(1)} all-to-all(bf16[8,2,128,128]{3,2,1,0:T(8,128)(2,1)S(1)} %pad_maximum_fusion.2), channel_id=1, replica_groups={{0,8,16,24,1,9,17,25},{2,10,18,26,3,11,19,27},{4,12,20,28,5,13,21,29},{..., dimensions={0} | all-to-all | bytes 1048576 | tf_op jit(solution)/shard_map/all_to_all | solution.py:492
  44.3 2.7 %collective-permute-start.6 = (bf16[2,128,128]{2,1,0:T(8,128)(2,1)S(1)}, bf16[2,128,128]{2,1,0:T(8,128)(2,1)S(1)}, u32[]{:S(2)}, u32[]{:S(2)}) collective-permute-start(bf16[2,128,128]{2,1,0:T(8,128)(2,1)S(1)} %reduce_sum.12.first_ref), channel_id=1, source_target_pairs={{0,2},{1,3},{2,0},{3,1},{4,6},{5,7},{6,4},{7,5},{8,10},{9,11},{10,... | collective-permute-start | bytes 196616 | tf_op jit(solution)/shard_map/ppermute | solution.py:496
  47.0 3.3 %collective-permute-done.6.second_ref = bf16[2,128,128]{2,1,0:T(8,128)(2,1)S(1)} collective-permute-done((bf16[2,128,128]{2,1,0:T(8,128)(2,1)S(1)}, bf16[2,128,128]{2,1,0:T(8,128)(2,1)S(1)}, u32[]{:S(2)}, u32[]{:S(2)}) %collective-permute-start.6) | collective-permute-done | bytes 65568 | tf_op jit(solution)/shard_map/ppermute | solution.py:496
  50.2 0.8 %copies.1 = bf16[8,2,128,128]{3,2,1,0:T(8,128)(2,1)} custom-call(bf16[2,128,128]{2,1,0:T(8,128)(2,1)S(1)} %reduce_sum.12.first_ref, bf16[2,128,128]{2,1,0:T(8,128)(2,1)S(1)} %collective-permute-done.6.second_ref), custom_call_target="tpu_custom_call" | custom-call | tf_op jit(solution)/shard_map/copies/pallas_call | solution.py:500
  51.1 3.5 %all-to-all-start.1 = ((bf16[8,2,128,128]{3,2,1,0:T(8,128)(2,1)}), bf16[8,2,128,128]{3,2,1,0:T(8,128)(2,1)S(1)}, u32[]{:S(2)}, u32[]{:S(2)}) async-start(bf16[8,2,128,128]{3,2,1,0:T(8,128)(2,1)} %copies.1), calls=%async_computation.1 | async-start | bytes 1048576 | tf_op jit(solution)/shard_map/all_to_all | solution.py:508
  54.6 1.2 %output.1 = (bf16[4,96,512]{2,1,0:T(8,128)(2,1)S(1)}, bf16[4,96,512]{2,1,0:T(8,128)(2,1)S(1)}) custom-call(s32[28,1,32]{2,1,0:T(1,128)S(1)} %add_add_fusion.table, bf16[2,96,256]{2,1,0:T(8,128)(2,1)S(1)} %get-tuple-element.43.first_ref, bf16[6,96,256]{2,1,0:T(8,128)(2,1)S(1)} %get-tuple-element.44.second_ref), custom_call_target="tpu_custom_call" | custom-call | flops 268435456 | bytes 2097152 | tf_op jit(solution)/shard_map/output/pallas_call | solution.py:631
  55.9 6.3 %all-to-all-done.1.own_ref = bf16[8,2,128,128]{3,2,1,0:T(8,128)(2,1)S(1)} async-done(((bf16[8,2,128,128]{3,2,1,0:T(8,128)(2,1)}), bf16[8,2,128,128]{3,2,1,0:T(8,128)(2,1)S(1)}, u32[]{:S(2)}, u32[]{:S(2)}) %all-to-all-start.1) | async-done | bytes 524320 | tf_op jit(solution)/shard_map/all_to_all | solution.py:508
  62.2 0.8 %add_bitcast_fusion = bf16[1,4,96,512]{3,2,1,0:T(8,128)(2,1)} fusion(bf16[4,96,512]{2,1,0:T(8,128)(2,1)S(1)} %get-tuple-element.45, bf16[4,96,512]{2,1,0:T(8,128)(2,1)S(1)} %collective-permute-done.3), kind=kLoop, calls=%fused_computation.5 | loop fusion | flops 196608 | bytes 1179648 | tf_op jit(solution)/shard_map/broadcast_in_dim | solution.py:641
  63.0 1.1 %collective-permute-done.7.other_ref = bf16[8,2,128,128]{3,2,1,0:T(8,128)(2,1)S(1)} collective-permute-done((bf16[8,2,128,128]{3,2,1,0:T(8,128)(2,1)S(1)}, bf16[8,2,128,128]{3,2,1,0:T(8,128)(2,1)S(1)}, u32[]{:S(2)}, u32[]{:S(2)}) %collective-permute-start.7) | collective-permute-done | bytes 524320 | tf_op jit(solution)/shard_map/ppermute | solution.py:509
  64.1 2.2 %gather.1 = (f32[96,2592]{1,0:T(8,128)}, f32[96,2592]{1,0:T(8,128)}, f32[1,96]{1,0:T(1,128)}, f32[1,96]{1,0:T(1,128)}) custom-call(s32[28,1,32]{2,1,0:T(1,128)S(1)} %add_add_fusion.table, bf16[8,2,128,128]{3,2,1,0:T(8,128)(2,1)S(1)} %all-to-all-done.1.own_ref, bf16[8,2,128,128]{3,2,1,0:T(8,128)(2,1)S(1)} %collective-permute-done.7.other_ref), custom_call_target="tpu_custom_call" | custom-call | tf_op jit(solution)/shard_map/gather/pallas_call | solution.py:645
  (12 shorter events, 0.5 us)
Async XLA Ops:
  0.6 4.6 %collective-permute-start = (bf16[4,96,512]{2,1,0:T(8,128)(2,1)}, bf16[4,96,512]{2,1,0:T(8,128)(2,1)S(1)}, u32[]{:S(2)}, u32[]{:S(2)}) collective-permute-start(bf16[4,96,512]{2,1,0:T(8,128)(2,1)} %bitcast.19), channel_id=1, source_target_pairs={{0,4},{4,0},{8,12},{12,8},{16,20},{20,16},{24,28},{28,24},{1,5},{5... | collective-permute-start | bytes 1179656 | tf_op jit(solution)/shard_map/ppermute | solution.py:522
  1.1 4.1 %collective-permute-start.1 = (bf16[4,96,512]{2,1,0:T(8,128)(2,1)}, bf16[4,96,512]{2,1,0:T(8,128)(2,1)S(1)}, u32[]{:S(2)}, u32[]{:S(2)}) collective-permute-start(bf16[4,96,512]{2,1,0:T(8,128)(2,1)} %bitcast.21), channel_id=1, source_target_pairs={{0,4},{4,0},{8,12},{12,8},{16,20},{20,16},{24,28},{28,24},{1,5},{5... | collective-permute-start | bytes 1179656 | tf_op jit(solution)/shard_map/ppermute | solution.py:523
  7.0 7.0 %collective-permute-start.2 = (bf16[4,96,256]{2,1,0:T(8,128)(2,1)S(1)}, bf16[4,96,256]{2,1,0:T(8,128)(2,1)S(1)}, u32[]{:S(2)}, u32[]{:S(2)}) collective-permute-start(bf16[4,96,256]{2,1,0:T(8,128)(2,1)S(1)} %get-tuple-element.32), channel_id=1, source_target_pairs={{4,12},{8,16},{20,28},{12,4},{16,8},{28,20},{5,13},{9,17},{21,29},... | collective-permute-start | bytes 589832 | tf_op jit(solution)/shard_map/ppermute | solution.py:557
  24.6 5.2 %collective-permute-start.4 = (bf16[1024,128]{1,0:T(8,128)(2,1)S(1)}, bf16[1024,128]{1,0:T(8,128)(2,1)S(1)}, u32[]{:S(2)}, u32[]{:S(2)}) collective-permute-start(bf16[1024,128]{1,0:T(8,128)(2,1)S(1)} %get-tuple-element.52), channel_id=1, source_target_pairs={{0,4},{4,0},{8,12},{12,8},{16,20},{20,16},{24,28},{28,24},{1,5},{5... | collective-permute-start | bytes 786440 | tf_op jit(solution)/shard_map/ppermute | solution.py:488
  28.7 1.5 %collective-permute-start.5 = (bf16[1024,128]{1,0:T(8,128)(2,1)S(1)}, bf16[1024,128]{1,0:T(8,128)(2,1)S(1)}, u32[]{:S(2)}, u32[]{:S(2)}) collective-permute-start(bf16[1024,128]{1,0:T(8,128)(2,1)S(1)} %get-tuple-element.54), channel_id=1, source_target_pairs={{0,4},{4,0},{8,12},{12,8},{16,20},{20,16},{24,28},{28,24},{1,5},{5... | collective-permute-start | bytes 786440 | tf_op jit(solution)/shard_map/ppermute | solution.py:488
  44.3 5.9 %collective-permute-start.6 = (bf16[2,128,128]{2,1,0:T(8,128)(2,1)S(1)}, bf16[2,128,128]{2,1,0:T(8,128)(2,1)S(1)}, u32[]{:S(2)}, u32[]{:S(2)}) collective-permute-start(bf16[2,128,128]{2,1,0:T(8,128)(2,1)S(1)} %reduce_sum.12.first_ref), channel_id=1, source_target_pairs={{0,2},{1,3},{2,0},{3,1},{4,6},{5,7},{6,4},{7,5},{8,10},{9,11},{10,... | collective-permute-start | bytes 196616 | tf_op jit(solution)/shard_map/ppermute | solution.py:496
  51.1 11.1 %all-to-all-start.1 = ((bf16[8,2,128,128]{3,2,1,0:T(8,128)(2,1)}), bf16[8,2,128,128]{3,2,1,0:T(8,128)(2,1)S(1)}, u32[]{:S(2)}, u32[]{:S(2)}) async-start(bf16[8,2,128,128]{3,2,1,0:T(8,128)(2,1)} %copies.1), calls=%async_computation.1 | async-start | bytes 1048576 | tf_op jit(solution)/shard_map/all_to_all | solution.py:508
  55.8 6.4 %collective-permute-start.3 = (bf16[4,96,512]{2,1,0:T(8,128)(2,1)S(1)}, bf16[4,96,512]{2,1,0:T(8,128)(2,1)S(1)}, u32[]{:S(2)}, u32[]{:S(2)}) collective-permute-start(bf16[4,96,512]{2,1,0:T(8,128)(2,1)S(1)} %get-tuple-element.46), channel_id=1, source_target_pairs={{0,4},{4,0},{8,12},{12,8},{16,20},{20,16},{24,28},{28,24},{1,5},{5... | collective-permute-start | bytes 1179656 | tf_op jit(solution)/shard_map/ppermute | solution.py:641
  62.2 1.9 %collective-permute-start.7 = (bf16[8,2,128,128]{3,2,1,0:T(8,128)(2,1)S(1)}, bf16[8,2,128,128]{3,2,1,0:T(8,128)(2,1)S(1)}, u32[]{:S(2)}, u32[]{:S(2)}) collective-permute-start(bf16[8,2,128,128]{3,2,1,0:T(8,128)(2,1)S(1)} %all-to-all-done.1.own_ref), channel_id=1, source_target_pairs={{0,4},{4,0},{8,12},{12,8},{16,20},{20,16},{24,28},{28,24},{1,5},{5... | collective-permute-start | bytes 1572872 | tf_op jit(solution)/shard_map/ppermute | solution.py:509

commit v7 on v6

--- a/solution.py
+++ b/solution.py
@@ -90,15 +90,23 @@
     return pl.ds(k * PLANE, PLANE)
 
 
-def weight_products(grads, planes, taps):
+def weight_products(total, grads, planes, taps, start=None):
     blank = jnp.zeros_like(grads(3))
 
     def left(p):
         inside = [grads(p + 1 - a) if 0 <= p + 1 - a < EDGE else blank for a in range(3)]
         return jnp.concatenate(inside, axis=0)
 
-    lefts = jnp.concatenate([left(p) for p in planes], axis=1)
-    return lax.dot_general(lefts, taps, (((1,), (1,)), ((), ())), preferred_element_type=F32)
+    for first in range(0, KDIM, 256):
+        rows = slice(first, min(first + 256, KDIM))
+        block = None if start is None else start[:, rows]
+        for p in planes:
+            both = jnp.concatenate([left(p), left(p + 1)], axis=1)
+            part = lax.dot_general(
+                both, taps(p, rows), (((1,), (1,)), ((), ())), preferred_element_type=F32
+            )
+            block = part if block is None else block + part
+        total[:, rows] = block
 
 
 def write_tiles(flat, total, channels, even):
@@ -320,15 +328,18 @@
         if 5 <= j:
             finish_two(2 * j - 8, full_two[last, 0])
             finish_two(2 * j - 7, full_two[last, 1])
-    hidden = taps_ref[:, 2 * PLANE : 6 * PLANE]
-    total_ref[...] = weight_products(lambda q: g_ref[q - 2], range(3, 7), hidden)
+
+    def taps(p, rows):
+        return taps_ref[rows, (p - 1) * PLANE : (p + 1) * PLANE]
+
+    weight_products(total_ref, lambda q: g_ref[q - 2], (3, 5), taps)
 
 
 def outer_kernel(
     table, edge_ref, cot_ref, layer_mask, w1_taps, w2_taps, bias_ref,
     taps_ref, one_ref, two_ref, g_in_ref, total_ref,
     keep_ref, send_ref, slope_ref, g_ref, out_ref,
-    xc, hc, x_pair, h_pair, flat, masks_ref,
+    xc, hc, x_pair, h_pair, total, flat, masks_ref,
 ):
     channels = cot_ref.shape[1]
     even = (table[DEVICE, 0, 0] >> 16) == 0
@@ -369,9 +380,10 @@
     def grads(q):
         return g_ref[q + 1] if q < 2 else g_in_ref[q - 2]
 
-    planes = (-1, 0, 1, 2, 7, 8)
-    taps = [h_pair[...], taps_ref[:, : 2 * PLANE], taps_ref[:, 6 * PLANE :]]
-    total = total_ref[...] + weight_products(grads, planes, jnp.concatenate(taps, axis=1))
+    def taps(p, rows):
+        return h_pair[rows] if p < 0 else taps_ref[rows, (p - 1) * PLANE : (p + 1) * PLANE]
+
+    weight_products(total, grads, (-1, 1, 7), taps, total_ref)
     write_tiles(flat, total, channels, even)
     split_tiles(keep_ref, send_ref, flat, table)
 
@@ -404,7 +416,7 @@
 
 def backward_kernel(
     table, g_out_ref, g_in_ref, slope_out_ref, slope_in_ref, x_ref, edge_ref, w2_back,
-    keep_ref, send_ref, gc, xc, full, low, grad, flat, masks_ref,
+    keep_ref, send_ref, gc, xc, full, low, grad, total, flat, masks_ref,
 ):
     channels = x_ref.shape[1]
     even = (table[DEVICE, 0, 0] >> 16) == 0
@@ -435,7 +447,11 @@
             for k, q in enumerate((2 * j - 4, 2 * j - 3)):
                 slope = slope_out_ref[0] if q == 0 else slope_in_ref[q - 1]
                 grad[q] = (full[last, k] * slope).astype(BF16)
-    total = weight_products(lambda q: grad[q], range(-1, EDGE + 1), xc[...])
+
+    def taps(p, rows):
+        return xc[rows, (p + 1) * PLANE : (p + 3) * PLANE]
+
+    weight_products(total, lambda q: grad[q], range(-1, EDGE, 2), taps)
     write_tiles(flat, total, channels, even)
     split_tiles(keep_ref, send_ref, flat, table)
 
@@ -600,6 +616,7 @@
             tap_space(KDIM, PLANE),
             tap_space(KDIM, 2 * PLANE),
             tap_space(KDIM, 2 * PLANE),
+            pltpu.VMEM((3 * channels, KDIM), F32),
             pltpu.VMEM((ROWS, 128), F32),
             pltpu.VMEM((9, 16, PLANE), BF16),
         ],
@@ -621,6 +638,7 @@
             sum_space(2, 2),
             sum_space(2),
             plane_space(8),
+            pltpu.VMEM((3 * channels, KDIM), F32),
             pltpu.VMEM((ROWS, 128), F32),
             pltpu.VMEM((9, 16, PLANE), BF16),
         ],

time: 66.7 us -> 66.7 us (level)
  no operation moved by 1% of the time
where the time goes in v7:
time: 66.7 us; the launch traced here: 66.3 us
  Pallas kernels  22.9 us (34%)
  blocking collectives  13.9 us (21%)
  waiting for transfers between devices  12.1 us (18%)
  starting transfers between devices  11.6 us (17%)
  other arithmetic  5.02 us (8%)
  between operations  0.75 us (1%)
    all_to_all x1, blocking collectives, shared_sum(): parts = lax.all_to_all(parts, both, 0, 0, axis_index_groups=groups)  13.9 us
    pallas_call x1, Pallas kernels, local(): pl.pallas_call(backward_kernel, out_shape=(kept, sent), in_specs=[SMEM] +...  6.88 us
    all_to_all x1, waiting for transfers between devices, shared_sum(): copies = lax.all_to_all(copies, both, 0, 0, axis_index_groups=groups)  6.29 us
    pallas_call x1, Pallas kernels, local(): pl.pallas_call(inner_kernel, out_shape=(jax.ShapeDtypeStruct((KDIM, EDGE...  6.22 us
    ppermute x2, starting transfers between devices, shared_sum(): lax.ppermute(send, 'space', swap).astype(F32)  4.12 us
    pallas_call x1, Pallas kernels, local(): pl.pallas_call(outer_kernel, out_shape=(kept, sent, planes(1, F32), plane...  3.8 us
    all_to_all x1, starting transfers between devices, shared_sum(): copies = lax.all_to_all(copies, both, 0, 0, axis_index_groups=groups)  3.49 us
    ppermute x1, waiting for transfers between devices, shared_sum(): moved = lax.ppermute(total, 'dp', [(v, v ^ step) for v in range(volumes)])  3.28 us
  transfers between devices with their start and end apart: 9, of which 5 were waited for; matrix products, arithmetic and copies ran while one was open for 7% of the time, Pallas kernels for 11%

profile of v7, /device:TPU:0, one launch (start us, length us, event | category | flops | bytes accessed | tf_op | source)
XLA Modules:
  0.0 66.3 jit_solution(510011649903565295)
XLA Ops:
  0.6 0.5 collective-permute-start
  1.2 1.2 %pad_maximum_fusion.1.own_ref = bf16[8,96,512]{2,1,0:T(8,128)(2,1)S(1)} fusion(bf16[4,96,512]{2,1,0:T(8,128)(2,1)} %bitcast.22, bf16[4,96,512]{2,1,0:T(8,128)(2,1)} %bitcast.20), kind=kLoop, calls=%fused_computation.1 | loop fusion | flops 393216 | bytes 1572864 | tf_op jit(solution)/shard_map/concatenate | solution.py:542
  2.5 0.8 %add_add_fusion.table = s32[28,1,32]{2,1,0:T(1,128)S(1)} fusion(s32[1,1,32]{2,1,0:T(1,128)} %bitcast.24, s32[26,1,32]{2,1,0:T(1,128)} %bitcast.23, s32[28]{0:T(128)S(1)} %pad.10.clone), kind=kLoop, calls=%fused_computation.6 | loop fusion | flops 1792 | bytes 7152 | tf_op jit(solution)/shard_map/concatenate | solution.py:546
  3.3 0.7 %pad_maximum_fusion.3.bias_ref = f32[2,96]{1,0:T(2,128)S(1)} fusion(f32[1,96]{1,0:T(1,128)} %bitcast.25, f32[1,96]{1,0:T(1,128)} %bitcast.26), kind=kLoop, calls=%fused_computation.7 | loop fusion | flops 192 | bytes 1536 | tf_op jit(solution)/shard_map/stack | solution.py:540
  4.0 1.3 %pad_maximum_fusion.weight_ref = bf16[192,2592]{1,0:T(8,128)(2,1)S(1)} fusion(bf16[96,2592]{1,0:T(8,128)(2,1)} %param.13, bf16[96,2592]{1,0:T(8,128)(2,1)} %param.12), kind=kLoop, calls=%fused_computation | loop fusion | flops 1990656 | bytes 1990656 | tf_op jit(solution)/shard_map/concatenate | solution.py:541
  5.3 1.6 %layout.1 = (bf16[12,96,256]{2,1,0:T(8,128)(2,1)S(1)}, bf16[9,96,256]{2,1,0:T(8,128)(2,1)S(1)}, bf16[4,96,256]{2,1,0:T(8,128)(2,1)S(1)}, f32[3,8,256]{2,1,0:T(8,128)S(1)}) custom-call(s32[28,1,32]{2,1,0:T(1,128)S(1)} %add_add_fusion.table, bf16[8,96,512]{2,1,0:T(8,128)(2,1)S(1)} %pad_maximum_fusion.1.own_ref, ...), custom_call_target="tpu_custom_call" | custom-call | tf_op jit(solution)/shard_map/layout/pallas_call | solution.py:561
  7.0 0.7 %collective-permute-start.2 = (bf16[4,96,256]{2,1,0:T(8,128)(2,1)S(1)}, bf16[4,96,256]{2,1,0:T(8,128)(2,1)S(1)}, u32[]{:S(2)}, u32[]{:S(2)}) collective-permute-start(bf16[4,96,256]{2,1,0:T(8,128)(2,1)S(1)} %get-tuple-element.32), channel_id=1, source_target_pairs={{4,12},{8,16},{20,28},{12,4},{16,8},{28,20},{5,13},{9,17},{21,29},... | collective-permute-start | bytes 589832 | tf_op jit(solution)/shard_map/ppermute | solution.py:573
  7.6 6.2 %inner.1 = (bf16[896,2048]{1,0:T(8,128)(2,1)S(1)}, f32[2,96,256]{2,1,0:T(8,128)S(1)}, f32[2,96,256]{2,1,0:T(8,128)S(1)}, f32[7,96,256]{2,1,0:T(8,128)S(1)}, bf16...) custom-call(s32[28,1,32]{2,1,0:T(1,128)S(1)} %add_add_fusion.table, ...), custom_call_target="tpu_custom_call" | custom-call | flops 8589934592 | bytes 8388608 | tf_op jit(solution)/shard_map/inner/pallas_call | solution.py:576
  13.9 3.8 %outer.1 = (f32[1024,128]{1,0:T(8,128)S(1)}, bf16[1024,128]{1,0:T(8,128)(2,1)S(1)}, f32[1,96,256]{2,1,0:T(8,128)S(1)}, bf16[3,96,256]{2,1,0:T(8,128)(2,1)S(1)}, bf16[2,96,256]{2,1,0:T(8,128)(2,1)S(1)}) custom-call(s32[28,1,32]{2,1,0:T(1,128)S(1)} %add_add_fusion.table, bf16[4,96,256]{2,1,0:T(8,128)(2,1)S(1)} %collective-permute-done.2.edge_ref, ...), custom_call_target="tpu_custom_call" | custom-call | flops 4294967296 | bytes 8388608 | tf_op jit(solution)/shard_map/outer/pallas_call | solution.py:609
  17.7 6.9 %backward.1 = (f32[1024,128]{1,0:T(8,128)S(1)}, bf16[1024,128]{1,0:T(8,128)(2,1)S(1)}) custom-call(s32[28,1,32]{2,1,0:T(1,128)S(1)} %add_add_fusion.table, bf16[3,96,256]{2,1,0:T(8,128)(2,1)S(1)} %get-tuple-element.47.g_out_ref, bf16[7,96,256]{2,1,0:T(8,128)(2,1)S(1)} %get-tuple-element.41.g_in_ref, f32[1,96,256]{2,1,0:T(8,128)S(1)} %get-tuple-element.48.slope_out_ref, ...), custom_call_target="tpu_custom_call" | custom-call | flops 4294967296 | bytes 4194304 | tf_op jit(solution)/shard_map/backward/pallas_call | solution.py:630
  24.6 4.0 %collective-permute-start.4 = (bf16[1024,128]{1,0:T(8,128)(2,1)S(1)}, bf16[1024,128]{1,0:T(8,128)(2,1)S(1)}, u32[]{:S(2)}, u32[]{:S(2)}) collective-permute-start(bf16[1024,128]{1,0:T(8,128)(2,1)S(1)} %get-tuple-element.52), channel_id=1, source_target_pairs={{0,4},{4,0},{8,12},{12,8},{16,20},{20,16},{24,28},{28,24},{1,5},{5... | collective-permute-start | bytes 786440 | tf_op jit(solution)/shard_map/ppermute | solution.py:504
  28.6 0.1 collective-permute-start.5
  28.7 1.1 %collective-permute-done.4 = bf16[1024,128]{1,0:T(8,128)(2,1)S(1)} collective-permute-done((bf16[1024,128]{1,0:T(8,128)(2,1)S(1)}, bf16[1024,128]{1,0:T(8,128)(2,1)S(1)}, u32[]{:S(2)}, u32[]{:S(2)}) %collective-permute-start.4) | collective-permute-done | bytes 262176 | tf_op jit(solution)/shard_map/ppermute | solution.py:504
  29.8 0.3 collective-permute-done.5
  30.3 13.9 %all_to_all.10 = bf16[8,2,128,128]{3,2,1,0:T(8,128)(2,1)S(1)} all-to-all(bf16[8,2,128,128]{3,2,1,0:T(8,128)(2,1)S(1)} %pad_maximum_fusion.2), channel_id=1, replica_groups={{0,8,16,24,1,9,17,25},{2,10,18,26,3,11,19,27},{4,12,20,28,5,13,21,29},{..., dimensions={0} | all-to-all | bytes 1048576 | tf_op jit(solution)/shard_map/all_to_all | solution.py:508
  44.3 2.7 %collective-permute-start.6 = (bf16[2,128,128]{2,1,0:T(8,128)(2,1)S(1)}, bf16[2,128,128]{2,1,0:T(8,128)(2,1)S(1)}, u32[]{:S(2)}, u32[]{:S(2)}) collective-permute-start(bf16[2,128,128]{2,1,0:T(8,128)(2,1)S(1)} %reduce_sum.12.first_ref), channel_id=1, source_target_pairs={{0,2},{1,3},{2,0},{3,1},{4,6},{5,7},{6,4},{7,5},{8,10},{9,11},{10,... | collective-permute-start | bytes 196616 | tf_op jit(solution)/shard_map/ppermute | solution.py:512
  46.9 3.3 %collective-permute-done.6.second_ref = bf16[2,128,128]{2,1,0:T(8,128)(2,1)S(1)} collective-permute-done((bf16[2,128,128]{2,1,0:T(8,128)(2,1)S(1)}, bf16[2,128,128]{2,1,0:T(8,128)(2,1)S(1)}, u32[]{:S(2)}, u32[]{:S(2)}) %collective-permute-start.6) | collective-permute-done | bytes 65568 | tf_op jit(solution)/shard_map/ppermute | solution.py:512
  50.2 0.8 %copies.1 = bf16[8,2,128,128]{3,2,1,0:T(8,128)(2,1)} custom-call(bf16[2,128,128]{2,1,0:T(8,128)(2,1)S(1)} %reduce_sum.12.first_ref, bf16[2,128,128]{2,1,0:T(8,128)(2,1)S(1)} %collective-permute-done.6.second_ref), custom_call_target="tpu_custom_call" | custom-call | tf_op jit(solution)/shard_map/copies/pallas_call | solution.py:516
  51.1 3.5 %all-to-all-start.1 = ((bf16[8,2,128,128]{3,2,1,0:T(8,128)(2,1)}), bf16[8,2,128,128]{3,2,1,0:T(8,128)(2,1)S(1)}, u32[]{:S(2)}, u32[]{:S(2)}) async-start(bf16[8,2,128,128]{3,2,1,0:T(8,128)(2,1)} %copies.1), calls=%async_computation.1 | async-start | bytes 1048576 | tf_op jit(solution)/shard_map/all_to_all | solution.py:524
  54.6 1.2 %output.1 = (bf16[4,96,512]{2,1,0:T(8,128)(2,1)S(1)}, bf16[4,96,512]{2,1,0:T(8,128)(2,1)S(1)}) custom-call(s32[28,1,32]{2,1,0:T(1,128)S(1)} %add_add_fusion.table, bf16[2,96,256]{2,1,0:T(8,128)(2,1)S(1)} %get-tuple-element.43.first_ref, bf16[6,96,256]{2,1,0:T(8,128)(2,1)S(1)} %get-tuple-element.44.second_ref), custom_call_target="tpu_custom_call" | custom-call | flops 268435456 | bytes 2097152 | tf_op jit(solution)/shard_map/output/pallas_call | solution.py:649
  55.9 6.3 %all-to-all-done.1.own_ref = bf16[8,2,128,128]{3,2,1,0:T(8,128)(2,1)S(1)} async-done(((bf16[8,2,128,128]{3,2,1,0:T(8,128)(2,1)}), bf16[8,2,128,128]{3,2,1,0:T(8,128)(2,1)S(1)}, u32[]{:S(2)}, u32[]{:S(2)}) %all-to-all-start.1) | async-done | bytes 524320 | tf_op jit(solution)/shard_map/all_to_all | solution.py:524
  62.2 0.8 %add_bitcast_fusion = bf16[1,4,96,512]{3,2,1,0:T(8,128)(2,1)} fusion(bf16[4,96,512]{2,1,0:T(8,128)(2,1)S(1)} %get-tuple-element.45, bf16[4,96,512]{2,1,0:T(8,128)(2,1)S(1)} %collective-permute-done.3), kind=kLoop, calls=%fused_computation.5 | loop fusion | flops 196608 | bytes 1179648 | tf_op jit(solution)/shard_map/broadcast_in_dim | solution.py:659
  63.0 1.1 %collective-permute-done.7.other_ref = bf16[8,2,128,128]{3,2,1,0:T(8,128)(2,1)S(1)} collective-permute-done((bf16[8,2,128,128]{3,2,1,0:T(8,128)(2,1)S(1)}, bf16[8,2,128,128]{3,2,1,0:T(8,128)(2,1)S(1)}, u32[]{:S(2)}, u32[]{:S(2)}) %collective-permute-start.7) | collective-permute-done | bytes 524320 | tf_op jit(solution)/shard_map/ppermute | solution.py:525
  64.1 2.2 %gather.1 = (f32[96,2592]{1,0:T(8,128)}, f32[96,2592]{1,0:T(8,128)}, f32[1,96]{1,0:T(1,128)}, f32[1,96]{1,0:T(1,128)}) custom-call(s32[28,1,32]{2,1,0:T(1,128)S(1)} %add_add_fusion.table, bf16[8,2,128,128]{3,2,1,0:T(8,128)(2,1)S(1)} %all-to-all-done.1.own_ref, bf16[8,2,128,128]{3,2,1,0:T(8,128)(2,1)S(1)} %collective-permute-done.7.other_ref), custom_call_target="tpu_custom_call" | custom-call | tf_op jit(solution)/shard_map/gather/pallas_call | solution.py:663
  (12 shorter events, 0.5 us)
Async XLA Ops:
  0.6 4.6 %collective-permute-start = (bf16[4,96,512]{2,1,0:T(8,128)(2,1)}, bf16[4,96,512]{2,1,0:T(8,128)(2,1)S(1)}, u32[]{:S(2)}, u32[]{:S(2)}) collective-permute-start(bf16[4,96,512]{2,1,0:T(8,128)(2,1)} %bitcast.19), channel_id=1, source_target_pairs={{0,4},{4,0},{8,12},{12,8},{16,20},{20,16},{24,28},{28,24},{1,5},{5... | collective-permute-start | bytes 1179656 | tf_op jit(solution)/shard_map/ppermute | solution.py:538
  1.1 4.1 %collective-permute-start.1 = (bf16[4,96,512]{2,1,0:T(8,128)(2,1)}, bf16[4,96,512]{2,1,0:T(8,128)(2,1)S(1)}, u32[]{:S(2)}, u32[]{:S(2)}) collective-permute-start(bf16[4,96,512]{2,1,0:T(8,128)(2,1)} %bitcast.21), channel_id=1, source_target_pairs={{0,4},{4,0},{8,12},{12,8},{16,20},{20,16},{24,28},{28,24},{1,5},{5... | collective-permute-start | bytes 1179656 | tf_op jit(solution)/shard_map/ppermute | solution.py:539
  7.0 6.9 %collective-permute-start.2 = (bf16[4,96,256]{2,1,0:T(8,128)(2,1)S(1)}, bf16[4,96,256]{2,1,0:T(8,128)(2,1)S(1)}, u32[]{:S(2)}, u32[]{:S(2)}) collective-permute-start(bf16[4,96,256]{2,1,0:T(8,128)(2,1)S(1)} %get-tuple-element.32), channel_id=1, source_target_pairs={{4,12},{8,16},{20,28},{12,4},{16,8},{28,20},{5,13},{9,17},{21,29},... | collective-permute-start | bytes 589832 | tf_op jit(solution)/shard_map/ppermute | solution.py:573
  24.6 5.2 %collective-permute-start.4 = (bf16[1024,128]{1,0:T(8,128)(2,1)S(1)}, bf16[1024,128]{1,0:T(8,128)(2,1)S(1)}, u32[]{:S(2)}, u32[]{:S(2)}) collective-permute-start(bf16[1024,128]{1,0:T(8,128)(2,1)S(1)} %get-tuple-element.52), channel_id=1, source_target_pairs={{0,4},{4,0},{8,12},{12,8},{16,20},{20,16},{24,28},{28,24},{1,5},{5... | collective-permute-start | bytes 786440 | tf_op jit(solution)/shard_map/ppermute | solution.py:504
  28.6 1.5 %collective-permute-start.5 = (bf16[1024,128]{1,0:T(8,128)(2,1)S(1)}, bf16[1024,128]{1,0:T(8,128)(2,1)S(1)}, u32[]{:S(2)}, u32[]{:S(2)}) collective-permute-start(bf16[1024,128]{1,0:T(8,128)(2,1)S(1)} %get-tuple-element.54), channel_id=1, source_target_pairs={{0,4},{4,0},{8,12},{12,8},{16,20},{20,16},{24,28},{28,24},{1,5},{5... | collective-permute-start | bytes 786440 | tf_op jit(solution)/shard_map/ppermute | solution.py:504
  44.3 5.9 %collective-permute-start.6 = (bf16[2,128,128]{2,1,0:T(8,128)(2,1)S(1)}, bf16[2,128,128]{2,1,0:T(8,128)(2,1)S(1)}, u32[]{:S(2)}, u32[]{:S(2)}) collective-permute-start(bf16[2,128,128]{2,1,0:T(8,128)(2,1)S(1)} %reduce_sum.12.first_ref), channel_id=1, source_target_pairs={{0,2},{1,3},{2,0},{3,1},{4,6},{5,7},{6,4},{7,5},{8,10},{9,11},{10,... | collective-permute-start | bytes 196616 | tf_op jit(solution)/shard_map/ppermute | solution.py:512
  51.1 11.1 %all-to-all-start.1 = ((bf16[8,2,128,128]{3,2,1,0:T(8,128)(2,1)}), bf16[8,2,128,128]{3,2,1,0:T(8,128)(2,1)S(1)}, u32[]{:S(2)}, u32[]{:S(2)}) async-start(bf16[8,2,128,128]{3,2,1,0:T(8,128)(2,1)} %copies.1), calls=%async_computation.1 | async-start | bytes 1048576 | tf_op jit(solution)/shard_map/all_to_all | solution.py:524
  55.8 6.4 %collective-permute-start.3 = (bf16[4,96,512]{2,1,0:T(8,128)(2,1)S(1)}, bf16[4,96,512]{2,1,0:T(8,128)(2,1)S(1)}, u32[]{:S(2)}, u32[]{:S(2)}) collective-permute-start(bf16[4,96,512]{2,1,0:T(8,128)(2,1)S(1)} %get-tuple-element.46), channel_id=1, source_target_pairs={{0,4},{4,0},{8,12},{12,8},{16,20},{20,16},{24,28},{28,24},{1,5},{5... | collective-permute-start | bytes 1179656 | tf_op jit(solution)/shard_map/ppermute | solution.py:659
  62.2 1.9 %collective-permute-start.7 = (bf16[8,2,128,128]{3,2,1,0:T(8,128)(2,1)S(1)}, bf16[8,2,128,128]{3,2,1,0:T(8,128)(2,1)S(1)}, u32[]{:S(2)}, u32[]{:S(2)}) collective-permute-start(bf16[8,2,128,128]{3,2,1,0:T(8,128)(2,1)S(1)} %all-to-all-done.1.own_ref), channel_id=1, source_target_pairs={{0,4},{4,0},{8,12},{12,8},{16,20},{20,16},{24,28},{28,24},{1,5},{5... | collective-permute-start | bytes 1572872 | tf_op jit(solution)/shard_map/ppermute | solution.py:525

commit v8 on v7

--- a/solution.py
+++ b/solution.py
@@ -11,7 +11,7 @@
 KDIM = 896
 TILES = 21
 ROWS = 2048
-DOWN, NEAR_Y, NEAR_Z, UP, LIVE, DEVICE = 4, 10, 12, 21, 26, 27
+DOWN, NEAR_Y, NEAR_Z, UP, LIVE = 4, 10, 12, 21, 26
 F32 = jnp.float32
 BF16 = jnp.bfloat16
 
@@ -43,8 +43,16 @@
         dst[k * channels : (k + 1) * channels, :] = moved
 
 
-def space_index(table, count):
-    return jnp.clip(table[DEVICE, 0, 0] & 255, 0, count - 1)
+def space_index(device, count):
+    return jnp.clip(device[0] >> 1, 0, count - 1)
+
+
+def layer_side(device):
+    return device[0] & 1
+
+
+def core_of(device):
+    return (device[0] >> 1) & 1
 
 
 def slot_place(table, slot, pair_slots):
@@ -132,9 +140,9 @@
     flat[TILES * channels :, :] = jnp.zeros((ROWS - TILES * channels, 128), F32)
 
 
-def split_tiles(keep_ref, send_ref, flat, table):
+def split_tiles(keep_ref, send_ref, flat, device):
     rows = keep_ref.shape[0]
-    even = (table[DEVICE, 0, 0] & 1) == 0
+    even = core_of(device) == 0
     here = pl.multiple_of(jnp.where(even, 0, rows), rows)
     there = pl.multiple_of(jnp.where(even, rows, 0), rows)
     keep_ref[...] = flat[pl.ds(here, rows), :]
@@ -142,24 +150,24 @@
 
 
 def layout_kernel(
-    table, own_ref, pair_ref, cot_pair_ref,
+    device, table, own_ref, pair_ref, cot_pair_ref,
     x_ref, cot_ref, edge_ref, mask_ref, bricks, cots,
 ):
     slots, channels = pair_ref.shape[0], pair_ref.shape[1]
     all_slots = table.shape[2]
-    me = space_index(table, all_slots // slots)
-    layer = table[DEVICE, 0, 0] >> 16
+    me = space_index(device, all_slots // slots)
+    layer = layer_side(device)
     even = layer == 0
 
     live = [[jnp.float32(0)] * 4 for _ in range(2)]
     beyond = [jnp.float32(0)] * 4
-    for device in (me, me ^ 1):
+    for index in (me, me ^ 1):
         for s in range(slots):
-            slot = jnp.clip(device * slots + s, 0, all_slots - 1)
+            slot = jnp.clip(index * slots + s, 0, all_slots - 1)
             parity, spot = slot_place(table, slot, 2 * slots)
             alive = table[LIVE, 0, slot].astype(F32)
             scale = jnp.full((channels, CELLS), alive, F32).astype(BF16)
-            own = device is me
+            own = index is me
             bricks[parity, spot] = (own_ref[s] if own else pair_ref[s]) * scale
             cots[parity, spot] = (own_ref[slots + s] if own else cot_pair_ref[s]) * scale
             outer = jnp.where(even, table[DOWN, 0, slot], table[UP, 0, slot])
@@ -263,12 +271,12 @@
 
 
 def inner_kernel(
-    table, x_ref, cot_ref, layer_mask, weight_ref, bias_ref,
+    device, x_ref, cot_ref, layer_mask, weight_ref, bias_ref,
     taps_ref, one_ref, two_ref, slope_ref, g_ref, out_ref, total_ref, w1_taps, w2_taps, w2_back,
     wide, xc, hc, full_one, low_one, full_two, low_two, masks_ref,
 ):
     channels = x_ref.shape[1]
-    even = (table[DEVICE, 0, 0] >> 16) == 0
+    even = layer_side(device) == 0
     fill_masks(masks_ref)
     tap_weights(w1_taps, weight_ref[:channels, :], wide, even)
     bias_one, bias_two = column(bias_ref[0:1]), column(bias_ref[1:2])
@@ -276,7 +284,7 @@
     for k in range(2):
         xc[k, 9 * channels :, :] = ones
     for k in range(4):
-        taps_ref[9 * channels :, 2 * k * PLANE : (2 * k + 2) * PLANE] = ones
+        taps_ref[k, 9 * channels :, :] = ones
     hc[9 * channels :, :] = ones[:, :PLANE]
 
     def write_x(p):
@@ -284,7 +292,7 @@
 
     def finish_one(q, pre):
         hidden, slope = hidden_plane(pre + bias_one, layer_mask[layer_of(q)][:1])
-        dst = taps_ref.at[:, place(q - 1)] if q < 9 else hc
+        dst = taps_ref.at[(q - 1) // 2, :, place((q - 1) & 1)] if q < 9 else hc
         write_taps(dst, hidden, masks_ref)
         if q < EDGE:
             slope_ref[q - 1] = slope
@@ -318,8 +326,7 @@
         if j == 6:
             finish_one(9, full_one[last, 0])
         if 3 <= j <= 6:
-            hidden = taps_ref[:, (2 * j - 6) * PLANE : (2 * j - 4) * PLANE]
-            pair_sums(full_two.at[now], low_two, w2_taps, hidden, j == 3)
+            pair_sums(full_two.at[now], low_two, w2_taps, taps_ref[j - 3], j == 3)
         if j == 7:
             third = product(w2_taps, hc[...], slice(2, 3))
             finish_two(8, low_two[0] + third)
@@ -330,19 +337,19 @@
             finish_two(2 * j - 7, full_two[last, 1])
 
     def taps(p, rows):
-        return taps_ref[rows, (p - 1) * PLANE : (p + 1) * PLANE]
+        return taps_ref[p // 2, rows]
 
     weight_products(total_ref, lambda q: g_ref[q - 2], (3, 5), taps)
 
 
 def outer_kernel(
-    table, edge_ref, cot_ref, layer_mask, w1_taps, w2_taps, bias_ref,
+    device, edge_ref, cot_ref, layer_mask, w1_taps, w2_taps, bias_ref,
     taps_ref, one_ref, two_ref, g_in_ref, total_ref,
     keep_ref, send_ref, slope_ref, g_ref, out_ref,
     xc, hc, x_pair, h_pair, total, flat, masks_ref,
 ):
     channels = cot_ref.shape[1]
-    even = (table[DEVICE, 0, 0] >> 16) == 0
+    even = layer_side(device) == 0
     fill_masks(masks_ref)
     bias_one, bias_two = column(bias_ref[0:1]), column(bias_ref[1:2])
     ones = jnp.ones((KDIM - 9 * channels, 2 * PLANE), BF16)
@@ -381,17 +388,17 @@
         return g_ref[q + 1] if q < 2 else g_in_ref[q - 2]
 
     def taps(p, rows):
-        return h_pair[rows] if p < 0 else taps_ref[rows, (p - 1) * PLANE : (p + 1) * PLANE]
+        return h_pair[rows] if p < 0 else taps_ref[p // 2, rows]
 
     weight_products(total, grads, (-1, 1, 7), taps, total_ref)
     write_tiles(flat, total, channels, even)
-    split_tiles(keep_ref, send_ref, flat, table)
-
-
-def output_kernel(table, first_ref, second_ref, keep_ref, send_ref, outs, bricks):
+    split_tiles(keep_ref, send_ref, flat, device)
+
+
+def output_kernel(device, table, first_ref, second_ref, keep_ref, send_ref, outs, bricks):
     slots, channels = keep_ref.shape[0], keep_ref.shape[1]
-    me = space_index(table, table.shape[2] // slots)
-    layer = table[DEVICE, 0, 0] >> 16
+    me = space_index(device, table.shape[2] // slots)
+    layer = layer_side(device)
     even = layer == 0
     outs[:2] = first_ref[...]
     outs[2:] = second_ref[...]
@@ -406,26 +413,26 @@
             pair = slice(j * 128, (j + 1) * 128)
             bricks[2 * y, :, pair] = both[:, :128]
             bricks[2 * y + 1, :, pair] = both[:, 128:]
-    for target, device in ((keep_ref, me), (send_ref, me ^ 1)):
+    for target, index in ((keep_ref, me), (send_ref, me ^ 1)):
         for s in range(slots):
-            slot = jnp.clip(device * slots + s, 0, table.shape[2] - 1)
+            slot = jnp.clip(index * slots + s, 0, table.shape[2] - 1)
             parity, spot = slot_place(table, slot, 2 * slots)
             scale = jnp.where(parity == layer, 1.0, 0.0)
             target[s] = bricks[spot] * jnp.full((channels, CELLS), scale, F32).astype(BF16)
 
 
 def backward_kernel(
-    table, g_out_ref, g_in_ref, slope_out_ref, slope_in_ref, x_ref, edge_ref, w2_back,
+    device, g_out_ref, g_in_ref, slope_out_ref, slope_in_ref, x_ref, edge_ref, w2_back,
     keep_ref, send_ref, gc, xc, full, low, grad, total, flat, masks_ref,
 ):
     channels = x_ref.shape[1]
-    even = (table[DEVICE, 0, 0] >> 16) == 0
+    even = layer_side(device) == 0
     fill_masks(masks_ref)
     ones = jnp.ones((KDIM - 9 * channels, 2 * PLANE), BF16)
     for k in range(2):
         gc[k, 9 * channels :, :] = ones
     for k in range(5):
-        xc[9 * channels :, 2 * k * PLANE : (2 * k + 2) * PLANE] = ones
+        xc[k, 9 * channels :, :] = ones
 
     def write_g(q):
         plane = g_out_ref[q + 1] if q < 2 else g_in_ref[q - 2]
@@ -442,18 +449,18 @@
                     write_g(q)
             for q in (2 * j - 1, 2 * j):
                 plane = edge_ref[0] if q < 0 else x_ref[q]
-                write_taps(xc.at[:, place(q + 1)], plane, masks_ref)
+                write_taps(xc.at[j, :, place((q + 1) & 1)], plane, masks_ref)
         if j >= 2:
             for k, q in enumerate((2 * j - 4, 2 * j - 3)):
                 slope = slope_out_ref[0] if q == 0 else slope_in_ref[q - 1]
                 grad[q] = (full[last, k] * slope).astype(BF16)
 
     def taps(p, rows):
-        return xc[rows, (p + 1) * PLANE : (p + 3) * PLANE]
+        return xc[(p + 1) // 2, rows]
 
     weight_products(total, lambda q: grad[q], range(-1, EDGE, 2), taps)
     write_tiles(flat, total, channels, even)
-    split_tiles(keep_ref, send_ref, flat, table)
+    split_tiles(keep_ref, send_ref, flat, device)
 
 
 def copies_kernel(first_ref, second_ref, out_ref):
@@ -463,11 +470,11 @@
 
 
 def gather_kernel(
-    table, own_ref, other_ref, w_one_ref, w_two_ref, b_one_ref, b_two_ref, flat
+    device, own_ref, other_ref, w_one_ref, w_two_ref, b_one_ref, b_two_ref, flat
 ):
     chunks, _, rows, _ = own_ref.shape
     channels = w_one_ref.shape[0]
-    core = table[DEVICE, 0, 0] & 1
+    core = core_of(device)
     for half, source in enumerate((own_ref, other_ref)):
         base = jnp.where(core == half, 0, chunks * rows)
         for k in range(chunks):
@@ -540,10 +547,8 @@
     biases = jnp.stack([bias_one, bias_two])
     weights = jnp.concatenate([weight_one, weight_two], axis=0)
     own = jnp.concatenate([volume, cotangent], axis=0)
-    device = me + 256 * lax.axis_index("dp").astype(jnp.int32)
-    device = device + 65536 * ((me ^ (me >> 1)) & 1)
-    rows = [neighbours.transpose(2, 0, 1), active[None], jnp.full_like(active, device)[None]]
-    table = jnp.concatenate(rows, axis=0)
+    device = (2 * me + ((me ^ (me >> 1)) & 1))[None]
+    table = jnp.concatenate([neighbours.transpose(2, 0, 1), active[None]], axis=0)
 
     def planes(number, dtype=BF16):
         return jax.ShapeDtypeStruct((number, channels, PLANE), dtype)
@@ -561,7 +566,7 @@
     x_planes, cot_planes, edge, layer_mask = pl.pallas_call(
         layout_kernel,
         out_shape=(planes(12), planes(9), planes(4), jax.ShapeDtypeStruct((3, 8, PLANE), F32)),
-        in_specs=[SMEM] + [VMEM] * 3,
+        in_specs=[SMEM] * 2 + [VMEM] * 3,
         out_specs=(VMEM,) * 4,
         scratch_shapes=[
             pltpu.VMEM((2, *bricks), BF16),
@@ -569,14 +574,14 @@
         ],
         compiler_params=vmem(8),
         name="layout",
-    )(table, own, pair_volume, pair_cot)
+    )(device, table, own, pair_volume, pair_cot)
     outer = lax.ppermute(edge, "space", hop)
 
     rearranged = jax.ShapeDtypeStruct((3, channels, KDIM), BF16)
     taps, one, two, slope_in, g_in, out_in, part_two, w1, w2, w2_back = pl.pallas_call(
         inner_kernel,
         out_shape=(
-            jax.ShapeDtypeStruct((KDIM, EDGE * PLANE), BF16),
+            jax.ShapeDtypeStruct((4, KDIM, 2 * PLANE), BF16),
             planes(2, F32),
             planes(2, F32),
             planes(7, F32),
@@ -602,7 +607,7 @@
         compiler_params=vmem(20),
         cost_estimate=pl.CostEstimate(flops=2**33, bytes_accessed=2**23, transcendentals=2**20),
         name="inner",
-    )(table, x_planes, cot_planes, layer_mask, weights, biases)
+    )(device, x_planes, cot_planes, layer_mask, weights, biases)
 
     rows = (ROWS // 2, 128)
     kept, sent = jax.ShapeDtypeStruct(rows, F32), jax.ShapeDtypeStruct(rows, BF16)
@@ -624,7 +629,7 @@
         cost_estimate=pl.CostEstimate(flops=2**32, bytes_accessed=2**23, transcendentals=2**18),
         name="outer",
     )(
-        table, outer, cot_planes, layer_mask, w1, w2, biases, taps, one, two, g_in,
+        device, outer, cot_planes, layer_mask, w1, w2, biases, taps, one, two, g_in,
         part_two,
     )
     keep_one, send_one = pl.pallas_call(
@@ -634,7 +639,7 @@
         out_specs=(VMEM,) * 2,
         scratch_shapes=[
             tap_space(2, KDIM, 2 * PLANE),
-            tap_space(KDIM, (EDGE + 2) * PLANE),
+            tap_space(5, KDIM, 2 * PLANE),
             sum_space(2, 2),
             sum_space(2),
             plane_space(8),
@@ -645,17 +650,17 @@
         compiler_params=vmem(20),
         cost_estimate=pl.CostEstimate(flops=2**32, bytes_accessed=2**22, transcendentals=0),
         name="backward",
-    )(table, g_out, g_in, slope_out, slope_in, x_planes, outer, w2_back)
+    )(device, g_out, g_in, slope_out, slope_in, x_planes, outer, w2_back)
     keep, send = pl.pallas_call(
         output_kernel,
         out_shape=(jax.ShapeDtypeStruct(bricks, BF16),) * 2,
-        in_specs=[SMEM] + [VMEM] * 2,
+        in_specs=[SMEM] * 2 + [VMEM] * 2,
         out_specs=(VMEM,) * 2,
         scratch_shapes=[plane_space(8), pltpu.VMEM(bricks, BF16)],
         compiler_params=vmem(8),
         cost_estimate=pl.CostEstimate(flops=2**28, bytes_accessed=2**21, transcendentals=0),
         name="output",
-    )(table, out_out, out_in)
+    )(device, table, out_out, out_in)
     output = (keep + lax.ppermute(send, "space", swap))[None]
     parts = shared_sum([keep_one, keep_two], [send_one, send_two])
     weight_shape = jax.ShapeDtypeStruct((channels, 27 * channels), F32)
@@ -668,7 +673,7 @@
         scratch_shapes=[pltpu.VMEM((2, ROWS, 128), BF16)],
         compiler_params=vmem(8),
         name="gather",
-    )(table, *parts)
+    )(device, *parts)
     return (output, total_w_one, total_w_two, total_b_one[0], total_b_two[0])
 
 

time: 66.7 us -> 64.2 us (0.963)
  Pallas kernels: 22.9 us -> 19.7 us
  blocking collectives: 13.9 us -> 14.7 us
    all_to_all x1, blocking collectives: 13.9 us -> 14.7 us  [shared_sum(): parts = lax.all_to_all(parts, both, 0, 0, axis_index_groups=groups)]
    pallas_call x1, Pallas kernels: 6.22 us -> 5.42 us  [local(): pl.pallas_call(inner_kernel, out_shape=(jax.ShapeDtypeStruct((4, KDIM, 2...]
    pallas_call x1, Pallas kernels: 3.8 us -> 3.01 us  [local(): pl.pallas_call(outer_kernel, out_shape=(kept, sent, planes(1, F32), plane...]
    pallas_call x1, Pallas kernels: 6.88 us -> 6.1 us  [local(): pl.pallas_call(backward_kernel, out_shape=(kept, sent), in_specs=[SMEM] +...]
    pallas_call x1, Pallas kernels: 2.23 us -> 1.46 us  [local(): pl.pallas_call(gather_kernel, out_shape=(weight_shape, weight_shape, bias...]
  transfers between devices with their start and end apart: 9 -> 9, of which waited for: 5 -> 5; matrix products, arithmetic and copies ran while one was open for 7% -> 7% of each run, Pallas kernels for 11% -> 10%
where the time goes in v8:
time: 64.2 us; the launch traced here: 63.8 us
  Pallas kernels  19.7 us (31%)
  blocking collectives  14.7 us (23%)
  waiting for transfers between devices  12.1 us (19%)
  starting transfers between devices  11.6 us (18%)
  other arithmetic  4.93 us (8%)
  between operations  0.74 us (1%)
    all_to_all x1, blocking collectives, shared_sum(): parts = lax.all_to_all(parts, both, 0, 0, axis_index_groups=groups)  14.7 us
    all_to_all x1, waiting for transfers between devices, shared_sum(): copies = lax.all_to_all(copies, both, 0, 0, axis_index_groups=groups)  6.3 us
    pallas_call x1, Pallas kernels, local(): pl.pallas_call(backward_kernel, out_shape=(kept, sent), in_specs=[SMEM] +...  6.1 us
    pallas_call x1, Pallas kernels, local(): pl.pallas_call(inner_kernel, out_shape=(jax.ShapeDtypeStruct((4, KDIM, 2...  5.42 us
    ppermute x2, starting transfers between devices, shared_sum(): lax.ppermute(send, 'space', swap).astype(F32)  4.12 us
    all_to_all x1, starting transfers between devices, shared_sum(): copies = lax.all_to_all(copies, both, 0, 0, axis_index_groups=groups)  3.49 us
    ppermute x1, waiting for transfers between devices, shared_sum(): moved = lax.ppermute(total, 'dp', [(v, v ^ step) for v in range(volumes)])  3.28 us
    pallas_call x1, Pallas kernels, local(): pl.pallas_call(outer_kernel, out_shape=(kept, sent, planes(1, F32), plane...  3.01 us
  transfers between devices with their start and end apart: 9, of which 5 were waited for; matrix products, arithmetic and copies ran while one was open for 7% of the time, Pallas kernels for 10%

profile of v8, /device:TPU:0, one launch (start us, length us, event | category | flops | bytes accessed | tf_op | source)
XLA Modules:
  0.0 63.8 jit_solution(14368150974207071622)
XLA Ops:
  0.6 0.5 collective-permute-start
  1.2 1.2 %pad_maximum_fusion.1.own_ref = bf16[8,96,512]{2,1,0:T(8,128)(2,1)S(1)} fusion(bf16[4,96,512]{2,1,0:T(8,128)(2,1)} %bitcast.22, bf16[4,96,512]{2,1,0:T(8,128)(2,1)} %bitcast.20), kind=kLoop, calls=%fused_computation.1 | loop fusion | flops 393216 | bytes 1572864 | tf_op jit(solution)/shard_map/concatenate | solution.py:549
  2.4 0.7 %pad_add_fusion.table = s32[27,1,32]{2,1,0:T(1,128)S(1)} fusion(s32[1,1,32]{2,1,0:T(1,128)} %bitcast.24, s32[26,1,32]{2,1,0:T(1,128)} %bitcast.23), kind=kLoop, calls=%fused_computation.6 | loop fusion | flops 864 | bytes 6912 | tf_op jit(solution)/shard_map/concatenate | solution.py:551
  3.2 0.7 %pad_maximum_fusion.3.bias_ref = f32[2,96]{1,0:T(2,128)S(1)} fusion(f32[1,96]{1,0:T(1,128)} %bitcast.25, f32[1,96]{1,0:T(1,128)} %bitcast.26), kind=kLoop, calls=%fused_computation.7 | loop fusion | flops 192 | bytes 1536 | tf_op jit(solution)/shard_map/stack | solution.py:547
  3.8 1.3 %pad_maximum_fusion.weight_ref = bf16[192,2592]{1,0:T(8,128)(2,1)S(1)} fusion(bf16[96,2592]{1,0:T(8,128)(2,1)} %param.13, bf16[96,2592]{1,0:T(8,128)(2,1)} %param.12), kind=kLoop, calls=%fused_computation | loop fusion | flops 1990656 | bytes 1990656 | tf_op jit(solution)/shard_map/concatenate | solution.py:548
  5.1 1.7 %layout.1 = (bf16[12,96,256]{2,1,0:T(8,128)(2,1)S(1)}, bf16[9,96,256]{2,1,0:T(8,128)(2,1)S(1)}, bf16[4,96,256]{2,1,0:T(8,128)(2,1)S(1)}, f32[3,8,256]{2,1,0:T(8,128)S(1)}) custom-call(s32[1]{0:T(128)} %bitcast.device, s32[27,1,32]{2,1,0:T(1,128)S(1)} %pad_add_fusion.table, bf16[8,96,512]{2,1,0:T(8,128)(2,1)S(1)} %pad_maximum_fusion.1.own_ref, ...), custom_call_target="tpu_custom_call" | custom-call | tf_op jit(solution)/shard_map/layout/pallas_call | solution.py:566
  6.8 0.7 %collective-permute-start.2 = (bf16[4,96,256]{2,1,0:T(8,128)(2,1)S(1)}, bf16[4,96,256]{2,1,0:T(8,128)(2,1)S(1)}, u32[]{:S(2)}, u32[]{:S(2)}) collective-permute-start(bf16[4,96,256]{2,1,0:T(8,128)(2,1)S(1)} %get-tuple-element.32), channel_id=1, source_target_pairs={{4,12},{8,16},{20,28},{12,4},{16,8},{28,20},{5,13},{9,17},{21,29},... | collective-permute-start | bytes 589832 | tf_op jit(solution)/shard_map/ppermute | solution.py:578
  7.5 5.4 %inner.1 = (bf16[4,896,512]{2,1,0:T(8,128)(2,1)S(1)}, f32[2,96,256]{2,1,0:T(8,128)S(1)}, f32[2,96,256]{2,1,0:T(8,128)S(1)}, f32[7,96,256]{2,1,0:T(8,128)S(1)}, b...) custom-call(s32[1]{0:T(128)} %bitcast.device, ...), custom_call_target="tpu_custom_call" | custom-call | flops 8589934592 | bytes 8388608 | tf_op jit(solution)/shard_map/inner/pallas_call | solution.py:581
  12.9 3.0 %outer.1 = (f32[1024,128]{1,0:T(8,128)S(1)}, bf16[1024,128]{1,0:T(8,128)(2,1)S(1)}, f32[1,96,256]{2,1,0:T(8,128)S(1)}, bf16[3,96,256]{2,1,0:T(8,128)(2,1)S(1)}, bf16[2,96,256]{2,1,0:T(8,128)(2,1)S(1)}) custom-call(s32[1]{0:T(128)} %bitcast.device, bf16[4,96,256]{2,1,0:T(8,128)(2,1)S(1)} %collective-permute-done.2.edge_ref, ...), custom_call_target="tpu_custom_call" | custom-call | flops 4294967296 | bytes 8388608 | tf_op jit(solution)/shard_map/outer/pallas_call | solution.py:614
  15.9 6.1 %backward.1 = (f32[1024,128]{1,0:T(8,128)S(1)}, bf16[1024,128]{1,0:T(8,128)(2,1)S(1)}) custom-call(s32[1]{0:T(128)} %bitcast.device, bf16[3,96,256]{2,1,0:T(8,128)(2,1)S(1)} %get-tuple-element.47.g_out_ref, bf16[7,96,256]{2,1,0:T(8,128)(2,1)S(1)} %get-tuple-element.41.g_in_ref, f32[1,96,256]{2,1,0:T(8,128)S(1)} %get-tuple-element.48.slope_out_ref, ...), custom_call_target="tpu_custom_call" | custom-call | flops 4294967296 | bytes 4194304 | tf_op jit(solution)/shard_map/backward/pallas_call | solution.py:635
  22.0 4.0 %collective-permute-start.4 = (bf16[1024,128]{1,0:T(8,128)(2,1)S(1)}, bf16[1024,128]{1,0:T(8,128)(2,1)S(1)}, u32[]{:S(2)}, u32[]{:S(2)}) collective-permute-start(bf16[1024,128]{1,0:T(8,128)(2,1)S(1)} %get-tuple-element.52), channel_id=1, source_target_pairs={{0,4},{4,0},{8,12},{12,8},{16,20},{20,16},{24,28},{28,24},{1,5},{5... | collective-permute-start | bytes 786440 | tf_op jit(solution)/shard_map/ppermute | solution.py:511
  26.1 0.1 collective-permute-start.5
  26.2 1.1 %collective-permute-done.4 = bf16[1024,128]{1,0:T(8,128)(2,1)S(1)} collective-permute-done((bf16[1024,128]{1,0:T(8,128)(2,1)S(1)}, bf16[1024,128]{1,0:T(8,128)(2,1)S(1)}, u32[]{:S(2)}, u32[]{:S(2)}) %collective-permute-start.4) | collective-permute-done | bytes 262176 | tf_op jit(solution)/shard_map/ppermute | solution.py:511
  27.3 0.3 collective-permute-done.5
  27.8 14.7 %all_to_all.10 = bf16[8,2,128,128]{3,2,1,0:T(8,128)(2,1)S(1)} all-to-all(bf16[8,2,128,128]{3,2,1,0:T(8,128)(2,1)S(1)} %pad_maximum_fusion.2), channel_id=1, replica_groups={{0,8,16,24,1,9,17,25},{2,10,18,26,3,11,19,27},{4,12,20,28,5,13,21,29},{..., dimensions={0} | all-to-all | bytes 1048576 | tf_op jit(solution)/shard_map/all_to_all | solution.py:515
  42.6 2.6 %collective-permute-start.6 = (bf16[2,128,128]{2,1,0:T(8,128)(2,1)S(1)}, bf16[2,128,128]{2,1,0:T(8,128)(2,1)S(1)}, u32[]{:S(2)}, u32[]{:S(2)}) collective-permute-start(bf16[2,128,128]{2,1,0:T(8,128)(2,1)S(1)} %reduce_sum.12.first_ref), channel_id=1, source_target_pairs={{0,2},{1,3},{2,0},{3,1},{4,6},{5,7},{6,4},{7,5},{8,10},{9,11},{10,... | collective-permute-start | bytes 196616 | tf_op jit(solution)/shard_map/ppermute | solution.py:519
  45.2 3.3 %collective-permute-done.6.second_ref = bf16[2,128,128]{2,1,0:T(8,128)(2,1)S(1)} collective-permute-done((bf16[2,128,128]{2,1,0:T(8,128)(2,1)S(1)}, bf16[2,128,128]{2,1,0:T(8,128)(2,1)S(1)}, u32[]{:S(2)}, u32[]{:S(2)}) %collective-permute-start.6) | collective-permute-done | bytes 65568 | tf_op jit(solution)/shard_map/ppermute | solution.py:519
  48.5 0.8 %copies.1 = bf16[8,2,128,128]{3,2,1,0:T(8,128)(2,1)} custom-call(bf16[2,128,128]{2,1,0:T(8,128)(2,1)S(1)} %reduce_sum.12.first_ref, bf16[2,128,128]{2,1,0:T(8,128)(2,1)S(1)} %collective-permute-done.6.second_ref), custom_call_target="tpu_custom_call" | custom-call | tf_op jit(solution)/shard_map/copies/pallas_call | solution.py:523
  49.3 3.5 %all-to-all-start.1 = ((bf16[8,2,128,128]{3,2,1,0:T(8,128)(2,1)}), bf16[8,2,128,128]{3,2,1,0:T(8,128)(2,1)S(1)}, u32[]{:S(2)}, u32[]{:S(2)}) async-start(bf16[8,2,128,128]{3,2,1,0:T(8,128)(2,1)} %copies.1), calls=%async_computation.1 | async-start | bytes 1048576 | tf_op jit(solution)/shard_map/all_to_all | solution.py:531
  52.8 1.2 %output.1 = (bf16[4,96,512]{2,1,0:T(8,128)(2,1)S(1)}, bf16[4,96,512]{2,1,0:T(8,128)(2,1)S(1)}) custom-call(s32[1]{0:T(128)} %bitcast.device, s32[27,1,32]{2,1,0:T(1,128)S(1)} %pad_add_fusion.table, bf16[2,96,256]{2,1,0:T(8,128)(2,1)S(1)} %get-tuple-element.43.first_ref, bf16[6,96,256]{2,1,0:T(8,128)(2,1)S(1)} %get-tuple-element.44.second_ref), custom_call_target="tpu_custom_call" | custom-call | flops 268435456 | bytes 2097152 | tf_op jit(solution)/shard_map/output/pallas_call | solution.py:654
  54.2 6.3 %all-to-all-done.1.own_ref = bf16[8,2,128,128]{3,2,1,0:T(8,128)(2,1)S(1)} async-done(((bf16[8,2,128,128]{3,2,1,0:T(8,128)(2,1)}), bf16[8,2,128,128]{3,2,1,0:T(8,128)(2,1)S(1)}, u32[]{:S(2)}, u32[]{:S(2)}) %all-to-all-start.1) | async-done | bytes 524320 | tf_op jit(solution)/shard_map/all_to_all | solution.py:531
  60.5 0.8 %add_bitcast_fusion = bf16[1,4,96,512]{3,2,1,0:T(8,128)(2,1)} fusion(bf16[4,96,512]{2,1,0:T(8,128)(2,1)S(1)} %get-tuple-element.45, bf16[4,96,512]{2,1,0:T(8,128)(2,1)S(1)} %collective-permute-done.3), kind=kLoop, calls=%fused_computation.5 | loop fusion | flops 196608 | bytes 1179648 | tf_op jit(solution)/shard_map/broadcast_in_dim | solution.py:664
  61.3 1.1 %collective-permute-done.7.other_ref = bf16[8,2,128,128]{3,2,1,0:T(8,128)(2,1)S(1)} collective-permute-done((bf16[8,2,128,128]{3,2,1,0:T(8,128)(2,1)S(1)}, bf16[8,2,128,128]{3,2,1,0:T(8,128)(2,1)S(1)}, u32[]{:S(2)}, u32[]{:S(2)}) %collective-permute-start.7) | collective-permute-done | bytes 524320 | tf_op jit(solution)/shard_map/ppermute | solution.py:532
  62.4 1.5 %gather.1 = (f32[96,2592]{1,0:T(8,128)}, f32[96,2592]{1,0:T(8,128)}, f32[1,96]{1,0:T(1,128)}, f32[1,96]{1,0:T(1,128)}) custom-call(s32[1]{0:T(128)} %bitcast.device, bf16[8,2,128,128]{3,2,1,0:T(8,128)(2,1)S(1)} %all-to-all-done.1.own_ref, bf16[8,2,128,128]{3,2,1,0:T(8,128)(2,1)S(1)} %collective-permute-done.7.other_ref), custom_call_target="tpu_custom_call" | custom-call | tf_op jit(solution)/shard_map/gather/pallas_call | solution.py:668
  (11 shorter events, 0.4 us)
Async XLA Ops:
  0.6 4.5 %collective-permute-start = (bf16[4,96,512]{2,1,0:T(8,128)(2,1)}, bf16[4,96,512]{2,1,0:T(8,128)(2,1)S(1)}, u32[]{:S(2)}, u32[]{:S(2)}) collective-permute-start(bf16[4,96,512]{2,1,0:T(8,128)(2,1)} %bitcast.19), channel_id=1, source_target_pairs={{0,4},{4,0},{8,12},{12,8},{16,20},{20,16},{24,28},{28,24},{1,5},{5... | collective-permute-start | bytes 1179656 | tf_op jit(solution)/shard_map/ppermute | solution.py:545
  1.1 4.0 %collective-permute-start.1 = (bf16[4,96,512]{2,1,0:T(8,128)(2,1)}, bf16[4,96,512]{2,1,0:T(8,128)(2,1)S(1)}, u32[]{:S(2)}, u32[]{:S(2)}) collective-permute-start(bf16[4,96,512]{2,1,0:T(8,128)(2,1)} %bitcast.21), channel_id=1, source_target_pairs={{0,4},{4,0},{8,12},{12,8},{16,20},{20,16},{24,28},{28,24},{1,5},{5... | collective-permute-start | bytes 1179656 | tf_op jit(solution)/shard_map/ppermute | solution.py:546
  6.8 6.1 %collective-permute-start.2 = (bf16[4,96,256]{2,1,0:T(8,128)(2,1)S(1)}, bf16[4,96,256]{2,1,0:T(8,128)(2,1)S(1)}, u32[]{:S(2)}, u32[]{:S(2)}) collective-permute-start(bf16[4,96,256]{2,1,0:T(8,128)(2,1)S(1)} %get-tuple-element.32), channel_id=1, source_target_pairs={{4,12},{8,16},{20,28},{12,4},{16,8},{28,20},{5,13},{9,17},{21,29},... | collective-permute-start | bytes 589832 | tf_op jit(solution)/shard_map/ppermute | solution.py:578
  22.0 5.2 %collective-permute-start.4 = (bf16[1024,128]{1,0:T(8,128)(2,1)S(1)}, bf16[1024,128]{1,0:T(8,128)(2,1)S(1)}, u32[]{:S(2)}, u32[]{:S(2)}) collective-permute-start(bf16[1024,128]{1,0:T(8,128)(2,1)S(1)} %get-tuple-element.52), channel_id=1, source_target_pairs={{0,4},{4,0},{8,12},{12,8},{16,20},{20,16},{24,28},{28,24},{1,5},{5... | collective-permute-start | bytes 786440 | tf_op jit(solution)/shard_map/ppermute | solution.py:511
  26.1 1.5 %collective-permute-start.5 = (bf16[1024,128]{1,0:T(8,128)(2,1)S(1)}, bf16[1024,128]{1,0:T(8,128)(2,1)S(1)}, u32[]{:S(2)}, u32[]{:S(2)}) collective-permute-start(bf16[1024,128]{1,0:T(8,128)(2,1)S(1)} %get-tuple-element.54), channel_id=1, source_target_pairs={{0,4},{4,0},{8,12},{12,8},{16,20},{20,16},{24,28},{28,24},{1,5},{5... | collective-permute-start | bytes 786440 | tf_op jit(solution)/shard_map/ppermute | solution.py:511
  42.6 5.9 %collective-permute-start.6 = (bf16[2,128,128]{2,1,0:T(8,128)(2,1)S(1)}, bf16[2,128,128]{2,1,0:T(8,128)(2,1)S(1)}, u32[]{:S(2)}, u32[]{:S(2)}) collective-permute-start(bf16[2,128,128]{2,1,0:T(8,128)(2,1)S(1)} %reduce_sum.12.first_ref), channel_id=1, source_target_pairs={{0,2},{1,3},{2,0},{3,1},{4,6},{5,7},{6,4},{7,5},{8,10},{9,11},{10,... | collective-permute-start | bytes 196616 | tf_op jit(solution)/shard_map/ppermute | solution.py:519
  49.3 11.1 %all-to-all-start.1 = ((bf16[8,2,128,128]{3,2,1,0:T(8,128)(2,1)}), bf16[8,2,128,128]{3,2,1,0:T(8,128)(2,1)S(1)}, u32[]{:S(2)}, u32[]{:S(2)}) async-start(bf16[8,2,128,128]{3,2,1,0:T(8,128)(2,1)} %copies.1), calls=%async_computation.1 | async-start | bytes 1048576 | tf_op jit(solution)/shard_map/all_to_all | solution.py:531
  54.1 6.4 %collective-permute-start.3 = (bf16[4,96,512]{2,1,0:T(8,128)(2,1)S(1)}, bf16[4,96,512]{2,1,0:T(8,128)(2,1)S(1)}, u32[]{:S(2)}, u32[]{:S(2)}) collective-permute-start(bf16[4,96,512]{2,1,0:T(8,128)(2,1)S(1)} %get-tuple-element.46), channel_id=1, source_target_pairs={{0,4},{4,0},{8,12},{12,8},{16,20},{20,16},{24,28},{28,24},{1,5},{5... | collective-permute-start | bytes 1179656 | tf_op jit(solution)/shard_map/ppermute | solution.py:664
  60.5 1.9 %collective-permute-start.7 = (bf16[8,2,128,128]{3,2,1,0:T(8,128)(2,1)S(1)}, bf16[8,2,128,128]{3,2,1,0:T(8,128)(2,1)S(1)}, u32[]{:S(2)}, u32[]{:S(2)}) collective-permute-start(bf16[8,2,128,128]{3,2,1,0:T(8,128)(2,1)S(1)} %all-to-all-done.1.own_ref), channel_id=1, source_target_pairs={{0,4},{4,0},{8,12},{12,8},{16,20},{20,16},{24,28},{28,24},{1,5},{5... | collective-permute-start | bytes 1572872 | tf_op jit(solution)/shard_map/ppermute | solution.py:532

commit v9 on v8

--- a/solution.py
+++ b/solution.py
@@ -98,21 +98,26 @@
     return pl.ds(k * PLANE, PLANE)
 
 
-def weight_products(total, grads, planes, taps, start=None):
+def pair_grads(grads, p):
     blank = jnp.zeros_like(grads(3))
 
     def left(p):
         inside = [grads(p + 1 - a) if 0 <= p + 1 - a < EDGE else blank for a in range(3)]
         return jnp.concatenate(inside, axis=0)
 
+    return jnp.concatenate([left(p), left(p + 1)], axis=1)
+
+
+def weight_part(left, taps):
+    return lax.dot_general(left, taps, (((1,), (1,)), ((), ())), preferred_element_type=F32)
+
+
+def weight_products(total, grads, planes, taps, start=None):
     for first in range(0, KDIM, 256):
         rows = slice(first, min(first + 256, KDIM))
         block = None if start is None else start[:, rows]
         for p in planes:
-            both = jnp.concatenate([left(p), left(p + 1)], axis=1)
-            part = lax.dot_general(
-                both, taps(p, rows), (((1,), (1,)), ((), ())), preferred_element_type=F32
-            )
+            part = weight_part(pair_grads(grads, p), taps(p, rows))
             block = part if block is None else block + part
         total[:, rows] = block
 
@@ -272,7 +277,7 @@
 
 def inner_kernel(
     device, x_ref, cot_ref, layer_mask, weight_ref, bias_ref,
-    taps_ref, one_ref, two_ref, slope_ref, g_ref, out_ref, total_ref, w1_taps, w2_taps, w2_back,
+    taps_ref, x_taps, one_ref, two_ref, slope_ref, g_ref, out_ref, total_ref, w1_taps, w2_taps, w2_back,
     wide, xc, hc, full_one, low_one, full_two, low_two, masks_ref,
 ):
     channels = x_ref.shape[1]
@@ -281,14 +286,15 @@
     tap_weights(w1_taps, weight_ref[:channels, :], wide, even)
     bias_one, bias_two = column(bias_ref[0:1]), column(bias_ref[1:2])
     ones = jnp.ones((KDIM - 9 * channels, 2 * PLANE), BF16)
-    for k in range(2):
-        xc[k, 9 * channels :, :] = ones
+    for k in range(5):
+        x_taps[k, 9 * channels :, :] = ones
     for k in range(4):
         taps_ref[k, 9 * channels :, :] = ones
-    hc[9 * channels :, :] = ones[:, :PLANE]
+    for single in (xc, hc):
+        single[9 * channels :, :] = ones[:, :PLANE]
 
     def write_x(p):
-        write_taps(xc.at[(p >> 1) & 1, :, place(p & 1)], x_ref[p], masks_ref)
+        write_taps(x_taps.at[p // 2, :, place(p & 1)] if p < 10 else xc, x_ref[p], masks_ref)
 
     def finish_one(q, pre):
         hidden, slope = hidden_plane(pre + bias_one, layer_mask[layer_of(q)][:1])
@@ -308,12 +314,12 @@
     for j in range(8):
         now, last = j & 1, (j + 1) & 1
         if j < 5:
-            pair_sums(full_one.at[now], low_one, w1_taps, xc[now], j == 0)
+            pair_sums(full_one.at[now], low_one, w1_taps, x_taps[j], j == 0)
             for p in (2 * j + 2, 2 * j + 3):
                 if p <= 10:
                     write_x(p)
         if j == 5:
-            third = product(w1_taps, xc[1, :, :PLANE], slice(2, 3))
+            third = product(w1_taps, xc[...], slice(2, 3))
             full_one[now, 0] = low_one[0] + third
         if j == 0:
             tap_weights(w2_taps, weight_ref[channels:, :], wide, even)
@@ -339,14 +345,14 @@
     def taps(p, rows):
         return taps_ref[p // 2, rows]
 
-    weight_products(total_ref, lambda q: g_ref[q - 2], (3, 5), taps)
+    weight_products(total_ref, lambda q: g_ref[q - 2], (3, 5, 7), taps)
 
 
 def outer_kernel(
     device, edge_ref, cot_ref, layer_mask, w1_taps, w2_taps, bias_ref,
     taps_ref, one_ref, two_ref, g_in_ref, total_ref,
-    keep_ref, send_ref, slope_ref, g_ref, out_ref,
-    xc, hc, x_pair, h_pair, total, flat, masks_ref,
+    keep_ref, send_ref, slope_ref, g_ref, out_ref, x_pair,
+    xc, hc, h_pair, total, flat, masks_ref,
 ):
     channels = cot_ref.shape[1]
     even = layer_side(device) == 0
@@ -390,7 +396,7 @@
     def taps(p, rows):
         return h_pair[rows] if p < 0 else taps_ref[p // 2, rows]
 
-    weight_products(total, grads, (-1, 1, 7), taps, total_ref)
+    weight_products(total, grads, (-1, 1), taps, total_ref)
     write_tiles(flat, total, channels, even)
     split_tiles(keep_ref, send_ref, flat, device)
 
@@ -422,17 +428,15 @@
 
 
 def backward_kernel(
-    device, g_out_ref, g_in_ref, slope_out_ref, slope_in_ref, x_ref, edge_ref, w2_back,
-    keep_ref, send_ref, gc, xc, full, low, grad, total, flat, masks_ref,
+    device, g_out_ref, g_in_ref, slope_out_ref, slope_in_ref, x_taps, x_pair, w2_back,
+    keep_ref, send_ref, gc, full, low, grad, total, flat, masks_ref,
 ):
-    channels = x_ref.shape[1]
+    channels = g_in_ref.shape[1]
     even = layer_side(device) == 0
     fill_masks(masks_ref)
     ones = jnp.ones((KDIM - 9 * channels, 2 * PLANE), BF16)
     for k in range(2):
         gc[k, 9 * channels :, :] = ones
-    for k in range(5):
-        xc[k, 9 * channels :, :] = ones
 
     def write_g(q):
         plane = g_out_ref[q + 1] if q < 2 else g_in_ref[q - 2]
@@ -447,18 +451,17 @@
             for q in (2 * j + 1, 2 * j + 2):
                 if q <= 8:
                     write_g(q)
-            for q in (2 * j - 1, 2 * j):
-                plane = edge_ref[0] if q < 0 else x_ref[q]
-                write_taps(xc.at[j, :, place((q + 1) & 1)], plane, masks_ref)
         if j >= 2:
             for k, q in enumerate((2 * j - 4, 2 * j - 3)):
                 slope = slope_out_ref[0] if q == 0 else slope_in_ref[q - 1]
                 grad[q] = (full[last, k] * slope).astype(BF16)
-
-    def taps(p, rows):
-        return xc[(p + 1) // 2, rows]
-
-    weight_products(total, lambda q: grad[q], range(-1, EDGE, 2), taps)
+        if j >= 3:
+            for p in (2 * j - 6,) if j < 5 else (4, 6):
+                part = weight_part(pair_grads(lambda q: grad[q], p), x_taps[p // 2])
+                total[...] = part if p == 0 else total[...] + part
+    low_rows, high_rows = slice(0, channels), slice(2 * channels, 3 * channels)
+    total[low_rows] = total[low_rows] + weight_part(grad[0], x_pair[:, PLANE:])
+    total[high_rows] = total[high_rows] + weight_part(grad[EDGE - 1], x_taps[4, :, :PLANE])
     write_tiles(flat, total, channels, even)
     split_tiles(keep_ref, send_ref, flat, device)
 
@@ -578,10 +581,11 @@
     outer = lax.ppermute(edge, "space", hop)
 
     rearranged = jax.ShapeDtypeStruct((3, channels, KDIM), BF16)
-    taps, one, two, slope_in, g_in, out_in, part_two, w1, w2, w2_back = pl.pallas_call(
+    taps, x_taps, one, two, slope_in, g_in, out_in, part_two, w1, w2, w2_back = pl.pallas_call(
         inner_kernel,
         out_shape=(
             jax.ShapeDtypeStruct((4, KDIM, 2 * PLANE), BF16),
+            jax.ShapeDtypeStruct((5, KDIM, 2 * PLANE), BF16),
             planes(2, F32),
             planes(2, F32),
             planes(7, F32),
@@ -593,10 +597,10 @@
             rearranged,
         ),
         in_specs=[SMEM] + [VMEM] * 5,
-        out_specs=(VMEM,) * 10,
+        out_specs=(VMEM,) * 11,
         scratch_shapes=[
             pltpu.VMEM((channels, 21 * 128), BF16),
-            tap_space(2, KDIM, 2 * PLANE),
+            tap_space(KDIM, PLANE),
             tap_space(KDIM, PLANE),
             sum_space(2, 2),
             sum_space(2),
@@ -611,15 +615,21 @@
 
     rows = (ROWS // 2, 128)
     kept, sent = jax.ShapeDtypeStruct(rows, F32), jax.ShapeDtypeStruct(rows, BF16)
-    keep_two, send_two, slope_out, g_out, out_out = pl.pallas_call(
+    keep_two, send_two, slope_out, g_out, out_out, x_pair = pl.pallas_call(
         outer_kernel,
-        out_shape=(kept, sent, planes(1, F32), planes(3), planes(2)),
+        out_shape=(
+            kept,
+            sent,
+            planes(1, F32),
+            planes(3),
+            planes(2),
+            jax.ShapeDtypeStruct((KDIM, 2 * PLANE), BF16),
+        ),
         in_specs=[SMEM] + [VMEM] * 11,
-        out_specs=(VMEM,) * 5,
+        out_specs=(VMEM,) * 6,
         scratch_shapes=[
             tap_space(KDIM, PLANE),
             tap_space(KDIM, PLANE),
-            tap_space(KDIM, 2 * PLANE),
             tap_space(KDIM, 2 * PLANE),
             pltpu.VMEM((3 * channels, KDIM), F32),
             pltpu.VMEM((ROWS, 128), F32),
@@ -639,7 +649,6 @@
         out_specs=(VMEM,) * 2,
         scratch_shapes=[
             tap_space(2, KDIM, 2 * PLANE),
-            tap_space(5, KDIM, 2 * PLANE),
             sum_space(2, 2),
             sum_space(2),
             plane_space(8),
@@ -650,7 +659,7 @@
         compiler_params=vmem(20),
         cost_estimate=pl.CostEstimate(flops=2**32, bytes_accessed=2**22, transcendentals=0),
         name="backward",
-    )(device, g_out, g_in, slope_out, slope_in, x_planes, outer, w2_back)
+    )(device, g_out, g_in, slope_out, slope_in, x_taps, x_pair, w2_back)
     keep, send = pl.pallas_call(
         output_kernel,
         out_shape=(jax.ShapeDtypeStruct(bricks, BF16),) * 2,

time: 64.2 us -> 62.6 us (0.975)
  Pallas kernels: 19.7 us -> 18.6 us
    pallas_call x1, Pallas kernels: 6.1 us -> 4.8 us  [local(): pl.pallas_call(backward_kernel, out_shape=(kept, sent), in_specs=[SMEM] +...]
  transfers between devices with their start and end apart: 9 -> 9, of which waited for: 5 -> 5; matrix products, arithmetic and copies ran while one was open for 7% -> 8% of each run, Pallas kernels for 10% -> 12%
where the time goes in v9:
time: 62.6 us; the launch traced here: 62.2 us
  Pallas kernels  18.6 us (30%)
  blocking collectives  14.2 us (23%)
  waiting for transfers between devices  12.1 us (19%)
  starting transfers between devices  11.6 us (19%)
  other arithmetic  4.92 us (8%)
  between operations  0.74 us (1%)
    all_to_all x1, blocking collectives, shared_sum(): parts = lax.all_to_all(parts, both, 0, 0, axis_index_groups=groups)  14.2 us
    all_to_all x1, waiting for transfers between devices, shared_sum(): copies = lax.all_to_all(copies, both, 0, 0, axis_index_groups=groups)  6.3 us
    pallas_call x1, Pallas kernels, local(): pl.pallas_call(inner_kernel, out_shape=(jax.ShapeDtypeStruct((4, KDIM, 2...  5.93 us
    pallas_call x1, Pallas kernels, local(): pl.pallas_call(backward_kernel, out_shape=(kept, sent), in_specs=[SMEM] +...  4.8 us
    ppermute x2, starting transfers between devices, shared_sum(): lax.ppermute(send, 'space', swap).astype(F32)  4.12 us
    all_to_all x1, starting transfers between devices, shared_sum(): copies = lax.all_to_all(copies, both, 0, 0, axis_index_groups=groups)  3.49 us
    ppermute x1, waiting for transfers between devices, shared_sum(): moved = lax.ppermute(total, 'dp', [(v, v ^ step) for v in range(volumes)])  3.28 us
    pallas_call x1, Pallas kernels, local(): pl.pallas_call(outer_kernel, out_shape=(kept, sent, planes(1, F32), plane...  2.7 us
  transfers between devices with their start and end apart: 9, of which 5 were waited for; matrix products, arithmetic and copies ran while one was open for 8% of the time, Pallas kernels for 12%

profile of v9, /device:TPU:0, one launch (start us, length us, event | category | flops | bytes accessed | tf_op | source)
XLA Modules:
  0.0 62.2 jit_solution(9404386829612359120)
XLA Ops:
  0.6 0.5 collective-permute-start
  1.2 1.2 %pad_maximum_fusion.1.own_ref = bf16[8,96,512]{2,1,0:T(8,128)(2,1)S(1)} fusion(bf16[4,96,512]{2,1,0:T(8,128)(2,1)} %bitcast.22, bf16[4,96,512]{2,1,0:T(8,128)(2,1)} %bitcast.20), kind=kLoop, calls=%fused_computation.1 | loop fusion | flops 393216 | bytes 1572864 | tf_op jit(solution)/shard_map/concatenate | solution.py:552
  2.4 0.7 %pad_add_fusion.table = s32[27,1,32]{2,1,0:T(1,128)S(1)} fusion(s32[1,1,32]{2,1,0:T(1,128)} %bitcast.24, s32[26,1,32]{2,1,0:T(1,128)} %bitcast.23), kind=kLoop, calls=%fused_computation.6 | loop fusion | flops 864 | bytes 6912 | tf_op jit(solution)/shard_map/concatenate | solution.py:554
  3.2 0.7 %pad_maximum_fusion.3.bias_ref = f32[2,96]{1,0:T(2,128)S(1)} fusion(f32[1,96]{1,0:T(1,128)} %bitcast.25, f32[1,96]{1,0:T(1,128)} %bitcast.26), kind=kLoop, calls=%fused_computation.7 | loop fusion | flops 192 | bytes 1536 | tf_op jit(solution)/shard_map/stack | solution.py:550
  3.8 1.3 %pad_maximum_fusion.weight_ref = bf16[192,2592]{1,0:T(8,128)(2,1)S(1)} fusion(bf16[96,2592]{1,0:T(8,128)(2,1)} %param.13, bf16[96,2592]{1,0:T(8,128)(2,1)} %param.12), kind=kLoop, calls=%fused_computation | loop fusion | flops 1990656 | bytes 1990656 | tf_op jit(solution)/shard_map/concatenate | solution.py:551
  5.1 1.7 %layout.1 = (bf16[12,96,256]{2,1,0:T(8,128)(2,1)S(1)}, bf16[9,96,256]{2,1,0:T(8,128)(2,1)S(1)}, bf16[4,96,256]{2,1,0:T(8,128)(2,1)S(1)}, f32[3,8,256]{2,1,0:T(8,128)S(1)}) custom-call(s32[1]{0:T(128)} %bitcast.device, s32[27,1,32]{2,1,0:T(1,128)S(1)} %pad_add_fusion.table, bf16[8,96,512]{2,1,0:T(8,128)(2,1)S(1)} %pad_maximum_fusion.1.own_ref, ...), custom_call_target="tpu_custom_call" | custom-call | tf_op jit(solution)/shard_map/layout/pallas_call | solution.py:569
  6.8 0.7 %collective-permute-start.2 = (bf16[4,96,256]{2,1,0:T(8,128)(2,1)S(1)}, bf16[4,96,256]{2,1,0:T(8,128)(2,1)S(1)}, u32[]{:S(2)}, u32[]{:S(2)}) collective-permute-start(bf16[4,96,256]{2,1,0:T(8,128)(2,1)S(1)} %get-tuple-element.34), channel_id=1, source_target_pairs={{4,12},{8,16},{20,28},{12,4},{16,8},{28,20},{5,13},{9,17},{21,29},... | collective-permute-start | bytes 589832 | tf_op jit(solution)/shard_map/ppermute | solution.py:581
  7.5 5.9 %inner.1 = (bf16[4,896,512]{2,1,0:T(8,128)(2,1)S(1)}, bf16[5,896,512]{2,1,0:T(8,128)(2,1)S(1)}, f32[2,96,256]{2,1,0:T(8,128)S(1)}, f32[2,96,256]{2,1,0:T(8,128)S...) custom-call(s32[1]{0:T(128)} %bitcast.device, ...), custom_call_target="tpu_custom_call" | custom-call | flops 8589934592 | bytes 8388608 | tf_op jit(solution)/shard_map/inner/pallas_call | solution.py:584
  13.4 2.7 %outer.1 = (f32[1024,128]{1,0:T(8,128)S(1)}, bf16[1024,128]{1,0:T(8,128)(2,1)S(1)}, f32[1,96,256]{2,1,0:T(8,128)S(1)}, bf16[3,96,256]{2,1,0:T(8,128)(2,1)S(1)}, ...) custom-call(s32[1]{0:T(128)} %bitcast.device, bf16[4,96,256]{2,1,0:T(8,128)(2,1)S(1)} %collective-permute-done.2.edge_ref, ...), custom_call_target="tpu_custom_call" | custom-call | flops 4294967296 | bytes 8388608 | tf_op jit(solution)/shard_map/outer/pallas_call | solution.py:618
  16.1 4.8 %backward.1 = (f32[1024,128]{1,0:T(8,128)S(1)}, bf16[1024,128]{1,0:T(8,128)(2,1)S(1)}) custom-call(s32[1]{0:T(128)} %bitcast.device, bf16[3,96,256]{2,1,0:T(8,128)(2,1)S(1)} %get-tuple-element.49.g_out_ref, bf16[7,96,256]{2,1,0:T(8,128)(2,1)S(1)} %get-tuple-element.43.g_in_ref, f32[1,96,256]{2,1,0:T(8,128)S(1)} %get-tuple-element.50.slope_out_ref, ...), custom_call_target="tpu_custom_call" | custom-call | flops 4294967296 | bytes 4194304 | tf_op jit(solution)/shard_map/backward/pallas_call | solution.py:645
  20.9 4.0 %collective-permute-start.4 = (bf16[1024,128]{1,0:T(8,128)(2,1)S(1)}, bf16[1024,128]{1,0:T(8,128)(2,1)S(1)}, u32[]{:S(2)}, u32[]{:S(2)}) collective-permute-start(bf16[1024,128]{1,0:T(8,128)(2,1)S(1)} %get-tuple-element.56), channel_id=1, source_target_pairs={{0,4},{4,0},{8,12},{12,8},{16,20},{20,16},{24,28},{28,24},{1,5},{5... | collective-permute-start | bytes 786440 | tf_op jit(solution)/shard_map/ppermute | solution.py:514
  25.0 0.1 collective-permute-start.5
  25.1 1.1 %collective-permute-done.4 = bf16[1024,128]{1,0:T(8,128)(2,1)S(1)} collective-permute-done((bf16[1024,128]{1,0:T(8,128)(2,1)S(1)}, bf16[1024,128]{1,0:T(8,128)(2,1)S(1)}, u32[]{:S(2)}, u32[]{:S(2)}) %collective-permute-start.4) | collective-permute-done | bytes 262176 | tf_op jit(solution)/shard_map/ppermute | solution.py:514
  26.2 0.3 collective-permute-done.5
  26.6 14.2 %all_to_all.10 = bf16[8,2,128,128]{3,2,1,0:T(8,128)(2,1)S(1)} all-to-all(bf16[8,2,128,128]{3,2,1,0:T(8,128)(2,1)S(1)} %pad_maximum_fusion.2), channel_id=1, replica_groups={{0,8,16,24,1,9,17,25},{2,10,18,26,3,11,19,27},{4,12,20,28,5,13,21,29},{..., dimensions={0} | all-to-all | bytes 1048576 | tf_op jit(solution)/shard_map/all_to_all | solution.py:518
  41.0 2.6 %collective-permute-start.6 = (bf16[2,128,128]{2,1,0:T(8,128)(2,1)S(1)}, bf16[2,128,128]{2,1,0:T(8,128)(2,1)S(1)}, u32[]{:S(2)}, u32[]{:S(2)}) collective-permute-start(bf16[2,128,128]{2,1,0:T(8,128)(2,1)S(1)} %reduce_sum.12.first_ref), channel_id=1, source_target_pairs={{0,2},{1,3},{2,0},{3,1},{4,6},{5,7},{6,4},{7,5},{8,10},{9,11},{10,... | collective-permute-start | bytes 196616 | tf_op jit(solution)/shard_map/ppermute | solution.py:522
  43.6 3.3 %collective-permute-done.6.second_ref = bf16[2,128,128]{2,1,0:T(8,128)(2,1)S(1)} collective-permute-done((bf16[2,128,128]{2,1,0:T(8,128)(2,1)S(1)}, bf16[2,128,128]{2,1,0:T(8,128)(2,1)S(1)}, u32[]{:S(2)}, u32[]{:S(2)}) %collective-permute-start.6) | collective-permute-done | bytes 65568 | tf_op jit(solution)/shard_map/ppermute | solution.py:522
  46.9 0.8 %copies.1 = bf16[8,2,128,128]{3,2,1,0:T(8,128)(2,1)} custom-call(bf16[2,128,128]{2,1,0:T(8,128)(2,1)S(1)} %reduce_sum.12.first_ref, bf16[2,128,128]{2,1,0:T(8,128)(2,1)S(1)} %collective-permute-done.6.second_ref), custom_call_target="tpu_custom_call" | custom-call | tf_op jit(solution)/shard_map/copies/pallas_call | solution.py:526
  47.7 3.5 %all-to-all-start.1 = ((bf16[8,2,128,128]{3,2,1,0:T(8,128)(2,1)}), bf16[8,2,128,128]{3,2,1,0:T(8,128)(2,1)S(1)}, u32[]{:S(2)}, u32[]{:S(2)}) async-start(bf16[8,2,128,128]{3,2,1,0:T(8,128)(2,1)} %copies.1), calls=%async_computation.1 | async-start | bytes 1048576 | tf_op jit(solution)/shard_map/all_to_all | solution.py:534
  51.2 1.2 %output.1 = (bf16[4,96,512]{2,1,0:T(8,128)(2,1)S(1)}, bf16[4,96,512]{2,1,0:T(8,128)(2,1)S(1)}) custom-call(s32[1]{0:T(128)} %bitcast.device, s32[27,1,32]{2,1,0:T(1,128)S(1)} %pad_add_fusion.table, bf16[2,96,256]{2,1,0:T(8,128)(2,1)S(1)} %get-tuple-element.45.first_ref, bf16[6,96,256]{2,1,0:T(8,128)(2,1)S(1)} %get-tuple-element.46.second_ref), custom_call_target="tpu_custom_call" | custom-call | flops 268435456 | bytes 2097152 | tf_op jit(solution)/shard_map/output/pallas_call | solution.py:663
  52.5 6.3 %all-to-all-done.1.own_ref = bf16[8,2,128,128]{3,2,1,0:T(8,128)(2,1)S(1)} async-done(((bf16[8,2,128,128]{3,2,1,0:T(8,128)(2,1)}), bf16[8,2,128,128]{3,2,1,0:T(8,128)(2,1)S(1)}, u32[]{:S(2)}, u32[]{:S(2)}) %all-to-all-start.1) | async-done | bytes 524320 | tf_op jit(solution)/shard_map/all_to_all | solution.py:534
  58.8 0.8 %add_bitcast_fusion = bf16[1,4,96,512]{3,2,1,0:T(8,128)(2,1)} fusion(bf16[4,96,512]{2,1,0:T(8,128)(2,1)S(1)} %get-tuple-element.47, bf16[4,96,512]{2,1,0:T(8,128)(2,1)S(1)} %collective-permute-done.3), kind=kLoop, calls=%fused_computation.5 | loop fusion | flops 196608 | bytes 1179648 | tf_op jit(solution)/shard_map/broadcast_in_dim | solution.py:673
  59.6 1.1 %collective-permute-done.7.other_ref = bf16[8,2,128,128]{3,2,1,0:T(8,128)(2,1)S(1)} collective-permute-done((bf16[8,2,128,128]{3,2,1,0:T(8,128)(2,1)S(1)}, bf16[8,2,128,128]{3,2,1,0:T(8,128)(2,1)S(1)}, u32[]{:S(2)}, u32[]{:S(2)}) %collective-permute-start.7) | collective-permute-done | bytes 524320 | tf_op jit(solution)/shard_map/ppermute | solution.py:535
  60.8 1.5 %gather.1 = (f32[96,2592]{1,0:T(8,128)}, f32[96,2592]{1,0:T(8,128)}, f32[1,96]{1,0:T(1,128)}, f32[1,96]{1,0:T(1,128)}) custom-call(s32[1]{0:T(128)} %bitcast.device, bf16[8,2,128,128]{3,2,1,0:T(8,128)(2,1)S(1)} %all-to-all-done.1.own_ref, bf16[8,2,128,128]{3,2,1,0:T(8,128)(2,1)S(1)} %collective-permute-done.7.other_ref), custom_call_target="tpu_custom_call" | custom-call | tf_op jit(solution)/shard_map/gather/pallas_call | solution.py:677
  (11 shorter events, 0.4 us)
Async XLA Ops:
  0.6 4.5 %collective-permute-start = (bf16[4,96,512]{2,1,0:T(8,128)(2,1)}, bf16[4,96,512]{2,1,0:T(8,128)(2,1)S(1)}, u32[]{:S(2)}, u32[]{:S(2)}) collective-permute-start(bf16[4,96,512]{2,1,0:T(8,128)(2,1)} %bitcast.19), channel_id=1, source_target_pairs={{0,4},{4,0},{8,12},{12,8},{16,20},{20,16},{24,28},{28,24},{1,5},{5... | collective-permute-start | bytes 1179656 | tf_op jit(solution)/shard_map/ppermute | solution.py:548
  1.1 4.0 %collective-permute-start.1 = (bf16[4,96,512]{2,1,0:T(8,128)(2,1)}, bf16[4,96,512]{2,1,0:T(8,128)(2,1)S(1)}, u32[]{:S(2)}, u32[]{:S(2)}) collective-permute-start(bf16[4,96,512]{2,1,0:T(8,128)(2,1)} %bitcast.21), channel_id=1, source_target_pairs={{0,4},{4,0},{8,12},{12,8},{16,20},{20,16},{24,28},{28,24},{1,5},{5... | collective-permute-start | bytes 1179656 | tf_op jit(solution)/shard_map/ppermute | solution.py:549
  6.8 6.6 %collective-permute-start.2 = (bf16[4,96,256]{2,1,0:T(8,128)(2,1)S(1)}, bf16[4,96,256]{2,1,0:T(8,128)(2,1)S(1)}, u32[]{:S(2)}, u32[]{:S(2)}) collective-permute-start(bf16[4,96,256]{2,1,0:T(8,128)(2,1)S(1)} %get-tuple-element.34), channel_id=1, source_target_pairs={{4,12},{8,16},{20,28},{12,4},{16,8},{28,20},{5,13},{9,17},{21,29},... | collective-permute-start | bytes 589832 | tf_op jit(solution)/shard_map/ppermute | solution.py:581
  20.9 5.2 %collective-permute-start.4 = (bf16[1024,128]{1,0:T(8,128)(2,1)S(1)}, bf16[1024,128]{1,0:T(8,128)(2,1)S(1)}, u32[]{:S(2)}, u32[]{:S(2)}) collective-permute-start(bf16[1024,128]{1,0:T(8,128)(2,1)S(1)} %get-tuple-element.56), channel_id=1, source_target_pairs={{0,4},{4,0},{8,12},{12,8},{16,20},{20,16},{24,28},{28,24},{1,5},{5... | collective-permute-start | bytes 786440 | tf_op jit(solution)/shard_map/ppermute | solution.py:514
  25.0 1.5 %collective-permute-start.5 = (bf16[1024,128]{1,0:T(8,128)(2,1)S(1)}, bf16[1024,128]{1,0:T(8,128)(2,1)S(1)}, u32[]{:S(2)}, u32[]{:S(2)}) collective-permute-start(bf16[1024,128]{1,0:T(8,128)(2,1)S(1)} %get-tuple-element.58), channel_id=1, source_target_pairs={{0,4},{4,0},{8,12},{12,8},{16,20},{20,16},{24,28},{28,24},{1,5},{5... | collective-permute-start | bytes 786440 | tf_op jit(solution)/shard_map/ppermute | solution.py:514
  41.0 5.9 %collective-permute-start.6 = (bf16[2,128,128]{2,1,0:T(8,128)(2,1)S(1)}, bf16[2,128,128]{2,1,0:T(8,128)(2,1)S(1)}, u32[]{:S(2)}, u32[]{:S(2)}) collective-permute-start(bf16[2,128,128]{2,1,0:T(8,128)(2,1)S(1)} %reduce_sum.12.first_ref), channel_id=1, source_target_pairs={{0,2},{1,3},{2,0},{3,1},{4,6},{5,7},{6,4},{7,5},{8,10},{9,11},{10,... | collective-permute-start | bytes 196616 | tf_op jit(solution)/shard_map/ppermute | solution.py:522
  47.7 11.1 %all-to-all-start.1 = ((bf16[8,2,128,128]{3,2,1,0:T(8,128)(2,1)}), bf16[8,2,128,128]{3,2,1,0:T(8,128)(2,1)S(1)}, u32[]{:S(2)}, u32[]{:S(2)}) async-start(bf16[8,2,128,128]{3,2,1,0:T(8,128)(2,1)} %copies.1), calls=%async_computation.1 | async-start | bytes 1048576 | tf_op jit(solution)/shard_map/all_to_all | solution.py:534
  52.5 6.4 %collective-permute-start.3 = (bf16[4,96,512]{2,1,0:T(8,128)(2,1)S(1)}, bf16[4,96,512]{2,1,0:T(8,128)(2,1)S(1)}, u32[]{:S(2)}, u32[]{:S(2)}) collective-permute-start(bf16[4,96,512]{2,1,0:T(8,128)(2,1)S(1)} %get-tuple-element.48), channel_id=1, source_target_pairs={{0,4},{4,0},{8,12},{12,8},{16,20},{20,16},{24,28},{28,24},{1,5},{5... | collective-permute-start | bytes 1179656 | tf_op jit(solution)/shard_map/ppermute | solution.py:673
  58.8 1.9 %collective-permute-start.7 = (bf16[8,2,128,128]{3,2,1,0:T(8,128)(2,1)S(1)}, bf16[8,2,128,128]{3,2,1,0:T(8,128)(2,1)S(1)}, u32[]{:S(2)}, u32[]{:S(2)}) collective-permute-start(bf16[8,2,128,128]{3,2,1,0:T(8,128)(2,1)S(1)} %all-to-all-done.1.own_ref), channel_id=1, source_target_pairs={{0,4},{4,0},{8,12},{12,8},{16,20},{20,16},{24,28},{28,24},{1,5},{5... | collective-permute-start | bytes 1572872 | tf_op jit(solution)/shard_map/ppermute | solution.py:535

commit v10 on v9

--- a/solution.py
+++ b/solution.py
@@ -146,12 +146,15 @@
 
 
 def split_tiles(keep_ref, send_ref, flat, device):
-    rows = keep_ref.shape[0]
+    chunks, rows = keep_ref.shape[0], keep_ref.shape[1]
     even = core_of(device) == 0
-    here = pl.multiple_of(jnp.where(even, 0, rows), rows)
-    there = pl.multiple_of(jnp.where(even, rows, 0), rows)
-    keep_ref[...] = flat[pl.ds(here, rows), :]
-    send_ref[...] = flat[pl.ds(there, rows), :].astype(BF16)
+    here = jnp.where(even, 0, chunks * rows)
+    there = jnp.where(even, chunks * rows, 0)
+    for k in range(chunks):
+        at = pl.multiple_of(here + k * rows, rows)
+        keep_ref[k] = flat[pl.ds(at, rows), :]
+        at = pl.multiple_of(there + k * rows, rows)
+        send_ref[k] = flat[pl.ds(at, rows), :].astype(BF16)
 
 
 def layout_kernel(
@@ -276,7 +279,7 @@
 
 
 def inner_kernel(
-    device, x_ref, cot_ref, layer_mask, weight_ref, bias_ref,
+    device, x_ref, cot_ref, layer_mask, weight_ref, b1_ref, b2_ref,
     taps_ref, x_taps, one_ref, two_ref, slope_ref, g_ref, out_ref, total_ref, w1_taps, w2_taps, w2_back,
     wide, xc, hc, full_one, low_one, full_two, low_two, masks_ref,
 ):
@@ -284,7 +287,7 @@
     even = layer_side(device) == 0
     fill_masks(masks_ref)
     tap_weights(w1_taps, weight_ref[:channels, :], wide, even)
-    bias_one, bias_two = column(bias_ref[0:1]), column(bias_ref[1:2])
+    bias_one, bias_two = column(b1_ref[...]), column(b2_ref[...])
     ones = jnp.ones((KDIM - 9 * channels, 2 * PLANE), BF16)
     for k in range(5):
         x_taps[k, 9 * channels :, :] = ones
@@ -349,7 +352,7 @@
 
 
 def outer_kernel(
-    device, edge_ref, cot_ref, layer_mask, w1_taps, w2_taps, bias_ref,
+    device, edge_ref, cot_ref, layer_mask, w1_taps, w2_taps, b1_ref, b2_ref,
     taps_ref, one_ref, two_ref, g_in_ref, total_ref,
     keep_ref, send_ref, slope_ref, g_ref, out_ref, x_pair,
     xc, hc, h_pair, total, flat, masks_ref,
@@ -357,7 +360,7 @@
     channels = cot_ref.shape[1]
     even = layer_side(device) == 0
     fill_masks(masks_ref)
-    bias_one, bias_two = column(bias_ref[0:1]), column(bias_ref[1:2])
+    bias_one, bias_two = column(b1_ref[...]), column(b2_ref[...])
     ones = jnp.ones((KDIM - 9 * channels, 2 * PLANE), BF16)
     for single in (xc, hc):
         single[9 * channels :, :] = ones[:, :PLANE]
@@ -428,8 +431,8 @@
 
 
 def backward_kernel(
-    device, g_out_ref, g_in_ref, slope_out_ref, slope_in_ref, x_taps, x_pair, w2_back,
-    keep_ref, send_ref, gc, full, low, grad, total, flat, masks_ref,
+    device, g_out_ref, g_in_ref, slope_out_ref, slope_in_ref, x_taps, x_pair, w2_back, keep_two,
+    send_two, keep_ref, send_ref, gc, full, low, grad, total, flat, masks_ref,
 ):
     channels = g_in_ref.shape[1]
     even = layer_side(device) == 0
@@ -463,7 +466,9 @@
     total[low_rows] = total[low_rows] + weight_part(grad[0], x_pair[:, PLANE:])
     total[high_rows] = total[high_rows] + weight_part(grad[EDGE - 1], x_taps[4, :, :PLANE])
     write_tiles(flat, total, channels, even)
-    split_tiles(keep_ref, send_ref, flat, device)
+    split_tiles(keep_ref.at[:, 0], send_ref.at[:, 0], flat, device)
+    keep_ref[:, 1] = keep_two[...]
+    send_ref[:, 1] = send_two[...]
 
 
 def copies_kernel(first_ref, second_ref, out_ref):
@@ -500,7 +505,7 @@
     return pltpu.CompilerParams(vmem_limit_bytes=mebibytes * 2**20)
 
 
-def shared_sum(keeps, sends):
+def shared_sum(keep, send):
     count = lax.axis_size("space")
     volumes = lax.axis_size("dp")
     swap = [(d, d ^ 1) for d in range(count)]
@@ -510,11 +515,7 @@
         for core in range(2)
         for first in range(0, volumes, 2)
     ]
-    halves = [
-        keep + lax.ppermute(send, "space", swap).astype(F32) for keep, send in zip(keeps, sends)
-    ]
-    halves = [half.astype(BF16).reshape(count, -1, 128) for half in halves]
-    parts = jnp.stack(halves, axis=1)
+    parts = (keep + lax.ppermute(send, "space", swap).astype(F32)).astype(BF16)
     parts = lax.all_to_all(parts, both, 0, 0, axis_index_groups=groups)
     total = jnp.sum(parts.astype(F32), axis=0).astype(BF16)
     moved, step = jnp.zeros_like(total), 2
@@ -547,7 +548,7 @@
     hop += [(there, here) for here, there in hop]
     pair_volume = lax.ppermute(volume, "space", swap)
     pair_cot = lax.ppermute(cotangent, "space", swap)
-    biases = jnp.stack([bias_one, bias_two])
+    biases = (bias_one[None], bias_two[None])
     weights = jnp.concatenate([weight_one, weight_two], axis=0)
     own = jnp.concatenate([volume, cotangent], axis=0)
     device = (2 * me + ((me ^ (me >> 1)) & 1))[None]
@@ -596,7 +597,7 @@
             rearranged,
             rearranged,
         ),
-        in_specs=[SMEM] + [VMEM] * 5,
+        in_specs=[SMEM] + [VMEM] * 6,
         out_specs=(VMEM,) * 11,
         scratch_shapes=[
             pltpu.VMEM((channels, 21 * 128), BF16),
@@ -611,10 +612,10 @@
         compiler_params=vmem(20),
         cost_estimate=pl.CostEstimate(flops=2**33, bytes_accessed=2**23, transcendentals=2**20),
         name="inner",
-    )(device, x_planes, cot_planes, layer_mask, weights, biases)
-
-    rows = (ROWS // 2, 128)
-    kept, sent = jax.ShapeDtypeStruct(rows, F32), jax.ShapeDtypeStruct(rows, BF16)
+    )(device, x_planes, cot_planes, layer_mask, weights, *biases)
+
+    chunks = (count, ROWS // (2 * count), 128)
+    kept, sent = jax.ShapeDtypeStruct(chunks, F32), jax.ShapeDtypeStruct(chunks, BF16)
     keep_two, send_two, slope_out, g_out, out_out, x_pair = pl.pallas_call(
         outer_kernel,
         out_shape=(
@@ -625,7 +626,7 @@
             planes(2),
             jax.ShapeDtypeStruct((KDIM, 2 * PLANE), BF16),
         ),
-        in_specs=[SMEM] + [VMEM] * 11,
+        in_specs=[SMEM] + [VMEM] * 12,
         out_specs=(VMEM,) * 6,
         scratch_shapes=[
             tap_space(KDIM, PLANE),
@@ -639,13 +640,16 @@
         cost_estimate=pl.CostEstimate(flops=2**32, bytes_accessed=2**23, transcendentals=2**18),
         name="outer",
     )(
-        device, outer, cot_planes, layer_mask, w1, w2, biases, taps, one, two, g_in,
+        device, outer, cot_planes, layer_mask, w1, w2, *biases, taps, one, two, g_in,
         part_two,
     )
-    keep_one, send_one = pl.pallas_call(
+    gradient_keep, gradient_send = pl.pallas_call(
         backward_kernel,
-        out_shape=(kept, sent),
-        in_specs=[SMEM] + [VMEM] * 7,
+        out_shape=(
+            jax.ShapeDtypeStruct((count, 2, *chunks[1:]), F32),
+            jax.ShapeDtypeStruct((count, 2, *chunks[1:]), BF16),
+        ),
+        in_specs=[SMEM] + [VMEM] * 9,
         out_specs=(VMEM,) * 2,
         scratch_shapes=[
             tap_space(2, KDIM, 2 * PLANE),
@@ -659,7 +663,9 @@
         compiler_params=vmem(20),
         cost_estimate=pl.CostEstimate(flops=2**32, bytes_accessed=2**22, transcendentals=0),
         name="backward",
-    )(device, g_out, g_in, slope_out, slope_in, x_taps, x_pair, w2_back)
+    )(
+        device, g_out, g_in, slope_out, slope_in, x_taps, x_pair, w2_back, keep_two, send_two,
+    )
     keep, send = pl.pallas_call(
         output_kernel,
         out_shape=(jax.ShapeDtypeStruct(bricks, BF16),) * 2,
@@ -671,7 +677,7 @@
         name="output",
     )(device, table, out_out, out_in)
     output = (keep + lax.ppermute(send, "space", swap))[None]
-    parts = shared_sum([keep_one, keep_two], [send_one, send_two])
+    parts = shared_sum(gradient_keep, gradient_send)
     weight_shape = jax.ShapeDtypeStruct((channels, 27 * channels), F32)
     bias_shape = jax.ShapeDtypeStruct((1, channels), F32)
     total_w_one, total_w_two, total_b_one, total_b_two = pl.pallas_call(

time: 62.6 us -> 62 us (level)
  other arithmetic: 4.92 us -> 4.21 us
    another operation x2 -> x0, other arithmetic: 0.74 us -> none  [the longest x1 0.68 us: local(): biases = jnp.stack([bias_one, bias_two])]
    ppermute x2 -> x1, waiting for transfers between devices: 1.39 us -> 1.54 us  [shared_sum(): parts = (keep + lax.ppermute(send, 'space', swap).astype(F32)).astype(BF16)]
    ppermute x2 -> x1, starting transfers between devices: 4.12 us -> 4.03 us  [shared_sum(): parts = (keep + lax.ppermute(send, 'space', swap).astype(F32)).astype(BF16)]
  transfers between devices with their start and end apart: 9 -> 8, of which waited for: 5 -> 4; matrix products, arithmetic and copies ran while one was open for 8% -> 6% of each run, Pallas kernels for 12% -> 12%
where the time goes in v10:
time: 62 us; the launch traced here: 61.6 us
  Pallas kernels  18.7 us (30%)
  blocking collectives  14.2 us (23%)
  waiting for transfers between devices  12.2 us (20%)
  starting transfers between devices  11.5 us (19%)
  other arithmetic  4.21 us (7%)
  between operations  0.77 us (1%)
    all_to_all x1, blocking collectives, shared_sum(): parts = lax.all_to_all(parts, both, 0, 0, axis_index_groups=groups)  14.2 us
    all_to_all x1, waiting for transfers between devices, shared_sum(): copies = lax.all_to_all(copies, both, 0, 0, axis_index_groups=groups)  6.3 us
    pallas_call x1, Pallas kernels, local(): pl.pallas_call(inner_kernel, out_shape=(jax.ShapeDtypeStruct((4, KDIM, 2...  5.96 us
    pallas_call x1, Pallas kernels, local(): pl.pallas_call(backward_kernel, out_shape=(jax.ShapeDtypeStruct((count, 2...  4.81 us
    ppermute x1, starting transfers between devices, shared_sum(): parts = (keep + lax.ppermute(send, 'space', swap).astype(F32)).astype(BF16)  4.03 us
    all_to_all x1, starting transfers between devices, shared_sum(): copies = lax.all_to_all(copies, both, 0, 0, axis_index_groups=groups)  3.49 us
    ppermute x1, waiting for transfers between devices, shared_sum(): moved = lax.ppermute(total, 'dp', [(v, v ^ step) for v in range(volumes)])  3.28 us
    pallas_call x1, Pallas kernels, local(): pl.pallas_call(outer_kernel, out_shape=(kept, sent, planes(1, F32), plane...  2.71 us
  transfers between devices with their start and end apart: 8, of which 4 were waited for; matrix products, arithmetic and copies ran while one was open for 6% of the time, Pallas kernels for 12%

profile of v10, /device:TPU:0, one launch (start us, length us, event | category | flops | bytes accessed | tf_op | source)
XLA Modules:
  0.0 61.6 jit_solution(9191790876782009874)
XLA Ops:
  0.6 0.5 collective-permute-start
  1.1 0.1 collective-permute-start.1
  1.2 1.2 %pad_maximum_fusion.1.own_ref = bf16[8,96,512]{2,1,0:T(8,128)(2,1)S(1)} fusion(bf16[4,96,512]{2,1,0:T(8,128)(2,1)} %bitcast.18, bf16[4,96,512]{2,1,0:T(8,128)(2,1)} %bitcast.16), kind=kLoop, calls=%fused_computation.2 | loop fusion | flops 393216 | bytes 1572864 | tf_op jit(solution)/shard_map/concatenate | solution.py:553
  2.4 0.7 %pad_add_fusion.table = s32[27,1,32]{2,1,0:T(1,128)S(1)} fusion(s32[1,1,32]{2,1,0:T(1,128)} %bitcast.20, s32[26,1,32]{2,1,0:T(1,128)} %bitcast.19), kind=kLoop, calls=%fused_computation.4 | loop fusion | flops 864 | bytes 6912 | tf_op jit(solution)/shard_map/concatenate | solution.py:555
  3.2 1.3 %pad_maximum_fusion.weight_ref = bf16[192,2592]{1,0:T(8,128)(2,1)S(1)} fusion(bf16[96,2592]{1,0:T(8,128)(2,1)} %param.13, bf16[96,2592]{1,0:T(8,128)(2,1)} %param.12), kind=kLoop, calls=%fused_computation.1 | loop fusion | flops 1990656 | bytes 1990656 | tf_op jit(solution)/shard_map/concatenate | solution.py:552
  4.5 1.7 %layout.1 = (bf16[12,96,256]{2,1,0:T(8,128)(2,1)S(1)}, bf16[9,96,256]{2,1,0:T(8,128)(2,1)S(1)}, bf16[4,96,256]{2,1,0:T(8,128)(2,1)S(1)}, f32[3,8,256]{2,1,0:T(8,128)S(1)}) custom-call(s32[1]{0:T(128)} %bitcast.device, s32[27,1,32]{2,1,0:T(1,128)S(1)} %pad_add_fusion.table, bf16[8,96,512]{2,1,0:T(8,128)(2,1)S(1)} %pad_maximum_fusion.1.own_ref, ...), custom_call_target="tpu_custom_call" | custom-call | tf_op jit(solution)/shard_map/layout/pallas_call | solution.py:570
  6.2 0.7 %collective-permute-start.2 = (bf16[4,96,256]{2,1,0:T(8,128)(2,1)S(1)}, bf16[4,96,256]{2,1,0:T(8,128)(2,1)S(1)}, u32[]{:S(2)}, u32[]{:S(2)}) collective-permute-start(bf16[4,96,256]{2,1,0:T(8,128)(2,1)S(1)} %get-tuple-element.34), channel_id=1, source_target_pairs={{4,12},{8,16},{20,28},{12,4},{16,8},{28,20},{5,13},{9,17},{21,29},... | collective-permute-start | bytes 589832 | tf_op jit(solution)/shard_map/ppermute | solution.py:582
  6.9 6.0 %inner.1 = (bf16[4,896,512]{2,1,0:T(8,128)(2,1)S(1)}, bf16[5,896,512]{2,1,0:T(8,128)(2,1)S(1)}, f32[2,96,256]{2,1,0:T(8,128)S(1)}, f32[2,96,256]{2,1,0:T(8,128)S...) custom-call(s32[1]{0:T(128)} %bitcast.device, ...), custom_call_target="tpu_custom_call" | custom-call | flops 8589934592 | bytes 8388608 | tf_op jit(solution)/shard_map/inner/pallas_call | solution.py:585
  12.8 2.7 %outer.1 = (f32[8,128,128]{2,1,0:T(8,128)S(1)}, bf16[8,128,128]{2,1,0:T(8,128)(2,1)S(1)}, f32[1,96,256]{2,1,0:T(8,128)S(1)}, bf16[3,96,256]{2,1,0:T(8,128)(2,1)S...) custom-call(s32[1]{0:T(128)} %bitcast.device, ...), custom_call_target="tpu_custom_call" | custom-call | flops 4294967296 | bytes 8388608 | tf_op jit(solution)/shard_map/outer/pallas_call | solution.py:619
  15.6 4.8 %backward.1 = (f32[8,2,128,128]{3,2,1,0:T(8,128)S(1)}, bf16[8,2,128,128]{3,2,1,0:T(8,128)(2,1)S(1)}) custom-call(s32[1]{0:T(128)} %bitcast.device, bf16[3,96,256]{2,1,0:T(8,128)(2,1)S(1)} %get-tuple-element.49.g_out_ref, bf16[7,96,256]{2,1,0:T(8,128)(2,1)S(1)} %get-tuple-element.43.g_in_ref, f32[1,96,256]{2,1,0:T(8,128)S(1)} %get-tuple-element.50.slope_out_ref, ...), custom_call_target="tpu_custom_call" | custom-call | flops 4294967296 | bytes 4194304 | tf_op jit(solution)/shard_map/backward/pallas_call | solution.py:646
  20.4 4.0 %collective-permute-start.4 = (bf16[8,2,128,128]{3,2,1,0:T(8,128)(2,1)S(1)}, bf16[8,2,128,128]{3,2,1,0:T(8,128)(2,1)S(1)}, u32[]{:S(2)}, u32[]{:S(2)}) collective-permute-start(bf16[8,2,128,128]{3,2,1,0:T(8,128)(2,1)S(1)} %get-tuple-element.58), channel_id=1, source_target_pairs={{0,4},{4,0},{8,12},{12,8},{16,20},{20,16},{24,28},{28,24},{1,5},{5... | collective-permute-start | bytes 1572872 | tf_op jit(solution)/shard_map/ppermute | solution.py:518
  24.4 1.5 %collective-permute-done.4 = bf16[8,2,128,128]{3,2,1,0:T(8,128)(2,1)S(1)} collective-permute-done((bf16[8,2,128,128]{3,2,1,0:T(8,128)(2,1)S(1)}, bf16[8,2,128,128]{3,2,1,0:T(8,128)(2,1)S(1)}, u32[]{:S(2)}, u32[]{:S(2)}) %collective-permute-start.4) | collective-permute-done | bytes 524320 | tf_op jit(solution)/shard_map/ppermute | solution.py:518
  25.9 0.1 add_convert_fusion
  26.1 14.2 %all_to_all.10 = bf16[8,2,128,128]{3,2,1,0:T(8,128)(2,1)S(1)} all-to-all(bf16[8,2,128,128]{3,2,1,0:T(8,128)(2,1)S(1)} %add_convert_fusion), channel_id=1, replica_groups={{0,8,16,24,1,9,17,25},{2,10,18,26,3,11,19,27},{4,12,20,28,5,13,21,29},{..., dimensions={0} | all-to-all | bytes 1048576 | tf_op jit(solution)/shard_map/all_to_all | solution.py:519
  40.3 0.1 reduce_sum.12.first_ref
  40.4 2.7 %collective-permute-start.5 = (bf16[2,128,128]{2,1,0:T(8,128)(2,1)S(1)}, bf16[2,128,128]{2,1,0:T(8,128)(2,1)S(1)}, u32[]{:S(2)}, u32[]{:S(2)}) collective-permute-start(bf16[2,128,128]{2,1,0:T(8,128)(2,1)S(1)} %reduce_sum.12.first_ref), channel_id=1, source_target_pairs={{0,2},{1,3},{2,0},{3,1},{4,6},{5,7},{6,4},{7,5},{8,10},{9,11},{10,... | collective-permute-start | bytes 196616 | tf_op jit(solution)/shard_map/ppermute | solution.py:523
  43.0 3.3 %collective-permute-done.5.second_ref = bf16[2,128,128]{2,1,0:T(8,128)(2,1)S(1)} collective-permute-done((bf16[2,128,128]{2,1,0:T(8,128)(2,1)S(1)}, bf16[2,128,128]{2,1,0:T(8,128)(2,1)S(1)}, u32[]{:S(2)}, u32[]{:S(2)}) %collective-permute-start.5) | collective-permute-done | bytes 65568 | tf_op jit(solution)/shard_map/ppermute | solution.py:523
  46.3 0.8 %copies.1 = bf16[8,2,128,128]{3,2,1,0:T(8,128)(2,1)} custom-call(bf16[2,128,128]{2,1,0:T(8,128)(2,1)S(1)} %reduce_sum.12.first_ref, bf16[2,128,128]{2,1,0:T(8,128)(2,1)S(1)} %collective-permute-done.5.second_ref), custom_call_target="tpu_custom_call" | custom-call | tf_op jit(solution)/shard_map/copies/pallas_call | solution.py:527
  47.1 3.5 %all-to-all-start.1 = ((bf16[8,2,128,128]{3,2,1,0:T(8,128)(2,1)}), bf16[8,2,128,128]{3,2,1,0:T(8,128)(2,1)S(1)}, u32[]{:S(2)}, u32[]{:S(2)}) async-start(bf16[8,2,128,128]{3,2,1,0:T(8,128)(2,1)} %copies.1), calls=%async_computation.1 | async-start | bytes 1048576 | tf_op jit(solution)/shard_map/all_to_all | solution.py:535
  50.6 1.2 %output.1 = (bf16[4,96,512]{2,1,0:T(8,128)(2,1)S(1)}, bf16[4,96,512]{2,1,0:T(8,128)(2,1)S(1)}) custom-call(s32[1]{0:T(128)} %bitcast.device, s32[27,1,32]{2,1,0:T(1,128)S(1)} %pad_add_fusion.table, bf16[2,96,256]{2,1,0:T(8,128)(2,1)S(1)} %get-tuple-element.45.first_ref, bf16[6,96,256]{2,1,0:T(8,128)(2,1)S(1)} %get-tuple-element.46.second_ref), custom_call_target="tpu_custom_call" | custom-call | flops 268435456 | bytes 2097152 | tf_op jit(solution)/shard_map/output/pallas_call | solution.py:669
  51.9 6.3 %all-to-all-done.1.own_ref = bf16[8,2,128,128]{3,2,1,0:T(8,128)(2,1)S(1)} async-done(((bf16[8,2,128,128]{3,2,1,0:T(8,128)(2,1)}), bf16[8,2,128,128]{3,2,1,0:T(8,128)(2,1)S(1)}, u32[]{:S(2)}, u32[]{:S(2)}) %all-to-all-start.1) | async-done | bytes 524320 | tf_op jit(solution)/shard_map/all_to_all | solution.py:535
  58.2 0.8 %add_bitcast_fusion = bf16[1,4,96,512]{3,2,1,0:T(8,128)(2,1)} fusion(bf16[4,96,512]{2,1,0:T(8,128)(2,1)S(1)} %get-tuple-element.47, bf16[4,96,512]{2,1,0:T(8,128)(2,1)S(1)} %collective-permute-done.3), kind=kLoop, calls=%fused_computation.3 | loop fusion | flops 196608 | bytes 1179648 | tf_op jit(solution)/shard_map/broadcast_in_dim | solution.py:679
  59.0 1.1 %collective-permute-done.6.other_ref = bf16[8,2,128,128]{3,2,1,0:T(8,128)(2,1)S(1)} collective-permute-done((bf16[8,2,128,128]{3,2,1,0:T(8,128)(2,1)S(1)}, bf16[8,2,128,128]{3,2,1,0:T(8,128)(2,1)S(1)}, u32[]{:S(2)}, u32[]{:S(2)}) %collective-permute-start.6) | collective-permute-done | bytes 524320 | tf_op jit(solution)/shard_map/ppermute | solution.py:536
  60.1 1.5 %gather.1 = (f32[96,2592]{1,0:T(8,128)}, f32[96,2592]{1,0:T(8,128)}, f32[1,96]{1,0:T(1,128)}, f32[1,96]{1,0:T(1,128)}) custom-call(s32[1]{0:T(128)} %bitcast.device, bf16[8,2,128,128]{3,2,1,0:T(8,128)(2,1)S(1)} %all-to-all-done.1.own_ref, bf16[8,2,128,128]{3,2,1,0:T(8,128)(2,1)S(1)} %collective-permute-done.6.other_ref), custom_call_target="tpu_custom_call" | custom-call | tf_op jit(solution)/shard_map/gather/pallas_call | solution.py:683
  (10 shorter events, 0.1 us)
Async XLA Ops:
  0.6 3.8 %collective-permute-start = (bf16[4,96,512]{2,1,0:T(8,128)(2,1)}, bf16[4,96,512]{2,1,0:T(8,128)(2,1)S(1)}, u32[]{:S(2)}, u32[]{:S(2)}) collective-permute-start(bf16[4,96,512]{2,1,0:T(8,128)(2,1)} %bitcast.15), channel_id=1, source_target_pairs={{0,4},{4,0},{8,12},{12,8},{16,20},{20,16},{24,28},{28,24},{1,5},{5... | collective-permute-start | bytes 1179656 | tf_op jit(solution)/shard_map/ppermute | solution.py:549
  1.1 3.3 %collective-permute-start.1 = (bf16[4,96,512]{2,1,0:T(8,128)(2,1)}, bf16[4,96,512]{2,1,0:T(8,128)(2,1)S(1)}, u32[]{:S(2)}, u32[]{:S(2)}) collective-permute-start(bf16[4,96,512]{2,1,0:T(8,128)(2,1)} %bitcast.17), channel_id=1, source_target_pairs={{0,4},{4,0},{8,12},{12,8},{16,20},{20,16},{24,28},{28,24},{1,5},{5... | collective-permute-start | bytes 1179656 | tf_op jit(solution)/shard_map/ppermute | solution.py:550
  2.4 4.4 %copy-start = (f32[96]{0:T(128)S(1)}, f32[96]{0:T(128)}, u32[]{:S(2)}) copy-start(f32[96]{0:T(128)} %param.14) | copy-start | bytes 1156
  2.4 4.4 %copy-start.1 = (f32[96]{0:T(128)S(1)}, f32[96]{0:T(128)}, u32[]{:S(2)}) copy-start(f32[96]{0:T(128)} %param.15) | copy-start | bytes 1156
  6.2 6.7 %collective-permute-start.2 = (bf16[4,96,256]{2,1,0:T(8,128)(2,1)S(1)}, bf16[4,96,256]{2,1,0:T(8,128)(2,1)S(1)}, u32[]{:S(2)}, u32[]{:S(2)}) collective-permute-start(bf16[4,96,256]{2,1,0:T(8,128)(2,1)S(1)} %get-tuple-element.34), channel_id=1, source_target_pairs={{4,12},{8,16},{20,28},{12,4},{16,8},{28,20},{5,13},{9,17},{21,29},... | collective-permute-start | bytes 589832 | tf_op jit(solution)/shard_map/ppermute | solution.py:582
  20.4 5.6 %collective-permute-start.4 = (bf16[8,2,128,128]{3,2,1,0:T(8,128)(2,1)S(1)}, bf16[8,2,128,128]{3,2,1,0:T(8,128)(2,1)S(1)}, u32[]{:S(2)}, u32[]{:S(2)}) collective-permute-start(bf16[8,2,128,128]{3,2,1,0:T(8,128)(2,1)S(1)} %get-tuple-element.58), channel_id=1, source_target_pairs={{0,4},{4,0},{8,12},{12,8},{16,20},{20,16},{24,28},{28,24},{1,5},{5... | collective-permute-start | bytes 1572872 | tf_op jit(solution)/shard_map/ppermute | solution.py:518
  40.4 5.9 %collective-permute-start.5 = (bf16[2,128,128]{2,1,0:T(8,128)(2,1)S(1)}, bf16[2,128,128]{2,1,0:T(8,128)(2,1)S(1)}, u32[]{:S(2)}, u32[]{:S(2)}) collective-permute-start(bf16[2,128,128]{2,1,0:T(8,128)(2,1)S(1)} %reduce_sum.12.first_ref), channel_id=1, source_target_pairs={{0,2},{1,3},{2,0},{3,1},{4,6},{5,7},{6,4},{7,5},{8,10},{9,11},{10,... | collective-permute-start | bytes 196616 | tf_op jit(solution)/shard_map/ppermute | solution.py:523
  47.1 11.1 %all-to-all-start.1 = ((bf16[8,2,128,128]{3,2,1,0:T(8,128)(2,1)}), bf16[8,2,128,128]{3,2,1,0:T(8,128)(2,1)S(1)}, u32[]{:S(2)}, u32[]{:S(2)}) async-start(bf16[8,2,128,128]{3,2,1,0:T(8,128)(2,1)} %copies.1), calls=%async_computation.1 | async-start | bytes 1048576 | tf_op jit(solution)/shard_map/all_to_all | solution.py:535
  51.9 6.4 %collective-permute-start.3 = (bf16[4,96,512]{2,1,0:T(8,128)(2,1)S(1)}, bf16[4,96,512]{2,1,0:T(8,128)(2,1)S(1)}, u32[]{:S(2)}, u32[]{:S(2)}) collective-permute-start(bf16[4,96,512]{2,1,0:T(8,128)(2,1)S(1)} %get-tuple-element.48), channel_id=1, source_target_pairs={{0,4},{4,0},{8,12},{12,8},{16,20},{20,16},{24,28},{28,24},{1,5},{5... | collective-permute-start | bytes 1179656 | tf_op jit(solution)/shard_map/ppermute | solution.py:679
  58.2 1.9 %collective-permute-start.6 = (bf16[8,2,128,128]{3,2,1,0:T(8,128)(2,1)S(1)}, bf16[8,2,128,128]{3,2,1,0:T(8,128)(2,1)S(1)}, u32[]{:S(2)}, u32[]{:S(2)}) collective-permute-start(bf16[8,2,128,128]{3,2,1,0:T(8,128)(2,1)S(1)} %all-to-all-done.1.own_ref), channel_id=1, source_target_pairs={{0,4},{4,0},{8,12},{12,8},{16,20},{20,16},{24,28},{28,24},{1,5},{5... | collective-permute-start | bytes 1572872 | tf_op jit(solution)/shard_map/ppermute | solution.py:536

commit v11 on v10

--- a/solution.py
+++ b/solution.py
@@ -352,10 +352,10 @@
 
 
 def outer_kernel(
-    device, edge_ref, cot_ref, layer_mask, w1_taps, w2_taps, b1_ref, b2_ref,
-    taps_ref, one_ref, two_ref, g_in_ref, total_ref,
-    keep_ref, send_ref, slope_ref, g_ref, out_ref, x_pair,
-    xc, hc, h_pair, total, flat, masks_ref,
+    device, edge_ref, cot_ref, layer_mask, w1_taps, w2_taps, w2_back, b1_ref, b2_ref,
+    taps_ref, x_taps, one_ref, two_ref, slope_in_ref, g_in_ref, total_ref,
+    keep_ref, send_ref, out_ref,
+    xc, hc, x_pair, h_pair, gc, slope_out_ref, g_out_ref, full, low, grad, total, flat, masks_ref,
 ):
     channels = cot_ref.shape[1]
     even = layer_side(device) == 0
@@ -385,23 +385,53 @@
         hidden, slope = hidden_plane(pre + bias_one, layer_mask[layer_of(q)][:1])
         write_taps(hc if q == -2 else h_pair.at[:, place(q + 1)], hidden, masks_ref)
         if q == 0:
-            slope_ref[0] = slope
+            slope_out_ref[0] = slope
     for q, pre in zip(range(-1, 2), three_planes(w2_taps, hc, h_pair, two_ref)):
         cot = edge_ref[3] if q < 0 else cot_ref[q]
-        out, grad = out_plane(pre + bias_two, layer_mask[layer_of(q)][:1], cot)
-        g_ref[q + 1] = grad
+        out, g_out_ref[q + 1] = out_plane(pre + bias_two, layer_mask[layer_of(q)][:1], cot)
         if q >= 0:
             out_ref[q] = out
 
     def grads(q):
-        return g_ref[q + 1] if q < 2 else g_in_ref[q - 2]
-
-    def taps(p, rows):
-        return h_pair[rows] if p < 0 else taps_ref[p // 2, rows]
-
-    weight_products(total, grads, (-1, 1), taps, total_ref)
+        return g_out_ref[q + 1] if q < 2 else g_in_ref[q - 2]
+
+    for k in range(2):
+        gc[k, 9 * channels :, :] = ones
+
+    def write_g(q):
+        plane = g_out_ref[q + 1] if q < 2 else g_in_ref[q - 2]
+        write_taps(gc.at[((q + 1) >> 1) & 1, :, place((q + 1) & 1)], plane, masks_ref)
+
+    write_g(-1)
+    write_g(0)
+    for j in range(6):
+        now, last = j & 1, (j + 1) & 1
+        if j < 5:
+            pair_sums(full.at[now], low, w2_back, gc[now], j == 0)
+            for q in (2 * j + 1, 2 * j + 2):
+                if q <= 8:
+                    write_g(q)
+        if j == 0:
+            part = weight_part(pair_grads(grads, -1), h_pair[...])
+            total[...] = total_ref[...] + part
+        if j == 1:
+            total[...] = total[...] + weight_part(pair_grads(grads, 1), taps_ref[0])
+        if j == 2:
+            write_tiles(flat, total, channels, even)
+            split_tiles(keep_ref.at[:, 1], send_ref.at[:, 1], flat, device)
+        if j >= 2:
+            for k, q in enumerate((2 * j - 4, 2 * j - 3)):
+                slope = slope_out_ref[0] if q == 0 else slope_in_ref[q - 1]
+                grad[q] = (full[last, k] * slope).astype(BF16)
+        if j >= 3:
+            for p in (2 * j - 6,) if j < 5 else (4, 6):
+                part = weight_part(pair_grads(lambda q: grad[q], p), x_taps[p // 2])
+                total[...] = part if p == 0 else total[...] + part
+    low_rows, high_rows = slice(0, channels), slice(2 * channels, 3 * channels)
+    total[low_rows] = total[low_rows] + weight_part(grad[0], x_pair[:, PLANE:])
+    total[high_rows] = total[high_rows] + weight_part(grad[EDGE - 1], x_taps[4, :, :PLANE])
     write_tiles(flat, total, channels, even)
-    split_tiles(keep_ref, send_ref, flat, device)
+    split_tiles(keep_ref.at[:, 0], send_ref.at[:, 0], flat, device)
 
 
 def output_kernel(device, table, first_ref, second_ref, keep_ref, send_ref, outs, bricks):
@@ -428,47 +458,6 @@
             parity, spot = slot_place(table, slot, 2 * slots)
             scale = jnp.where(parity == layer, 1.0, 0.0)
             target[s] = bricks[spot] * jnp.full((channels, CELLS), scale, F32).astype(BF16)
-
-
-def backward_kernel(
-    device, g_out_ref, g_in_ref, slope_out_ref, slope_in_ref, x_taps, x_pair, w2_back, keep_two,
-    send_two, keep_ref, send_ref, gc, full, low, grad, total, flat, masks_ref,
-):
-    channels = g_in_ref.shape[1]
-    even = layer_side(device) == 0
-    fill_masks(masks_ref)
-    ones = jnp.ones((KDIM - 9 * channels, 2 * PLANE), BF16)
-    for k in range(2):
-        gc[k, 9 * channels :, :] = ones
-
-    def write_g(q):
-        plane = g_out_ref[q + 1] if q < 2 else g_in_ref[q - 2]
-        write_taps(gc.at[((q + 1) >> 1) & 1, :, place((q + 1) & 1)], plane, masks_ref)
-
-    write_g(-1)
-    write_g(0)
-    for j in range(6):
-        now, last = j & 1, (j + 1) & 1
-        if j < 5:
-            pair_sums(full.at[now], low, w2_back, gc[now], j == 0)
-            for q in (2 * j + 1, 2 * j + 2):
-                if q <= 8:
-                    write_g(q)
-        if j >= 2:
-            for k, q in enumerate((2 * j - 4, 2 * j - 3)):
-                slope = slope_out_ref[0] if q == 0 else slope_in_ref[q - 1]
-                grad[q] = (full[last, k] * slope).astype(BF16)
-        if j >= 3:
-            for p in (2 * j - 6,) if j < 5 else (4, 6):
-                part = weight_part(pair_grads(lambda q: grad[q], p), x_taps[p // 2])
-                total[...] = part if p == 0 else total[...] + part
-    low_rows, high_rows = slice(0, channels), slice(2 * channels, 3 * channels)
-    total[low_rows] = total[low_rows] + weight_part(grad[0], x_pair[:, PLANE:])
-    total[high_rows] = total[high_rows] + weight_part(grad[EDGE - 1], x_taps[4, :, :PLANE])
-    write_tiles(flat, total, channels, even)
-    split_tiles(keep_ref.at[:, 0], send_ref.at[:, 0], flat, device)
-    keep_ref[:, 1] = keep_two[...]
-    send_ref[:, 1] = send_two[...]
 
 
 def copies_kernel(first_ref, second_ref, out_ref):
@@ -614,45 +603,24 @@
         name="inner",
     )(device, x_planes, cot_planes, layer_mask, weights, *biases)
 
-    chunks = (count, ROWS // (2 * count), 128)
-    kept, sent = jax.ShapeDtypeStruct(chunks, F32), jax.ShapeDtypeStruct(chunks, BF16)
-    keep_two, send_two, slope_out, g_out, out_out, x_pair = pl.pallas_call(
+    halves = (count, 2, ROWS // (2 * count), 128)
+    gradient_keep, gradient_send, out_out = pl.pallas_call(
         outer_kernel,
         out_shape=(
-            kept,
-            sent,
-            planes(1, F32),
-            planes(3),
+            jax.ShapeDtypeStruct(halves, F32),
+            jax.ShapeDtypeStruct(halves, BF16),
             planes(2),
-            jax.ShapeDtypeStruct((KDIM, 2 * PLANE), BF16),
         ),
-        in_specs=[SMEM] + [VMEM] * 12,
-        out_specs=(VMEM,) * 6,
+        in_specs=[SMEM] + [VMEM] * 15,
+        out_specs=(VMEM,) * 3,
         scratch_shapes=[
             tap_space(KDIM, PLANE),
             tap_space(KDIM, PLANE),
             tap_space(KDIM, 2 * PLANE),
-            pltpu.VMEM((3 * channels, KDIM), F32),
-            pltpu.VMEM((ROWS, 128), F32),
-            pltpu.VMEM((9, 16, PLANE), BF16),
-        ],
-        compiler_params=vmem(16),
-        cost_estimate=pl.CostEstimate(flops=2**32, bytes_accessed=2**23, transcendentals=2**18),
-        name="outer",
-    )(
-        device, outer, cot_planes, layer_mask, w1, w2, *biases, taps, one, two, g_in,
-        part_two,
-    )
-    gradient_keep, gradient_send = pl.pallas_call(
-        backward_kernel,
-        out_shape=(
-            jax.ShapeDtypeStruct((count, 2, *chunks[1:]), F32),
-            jax.ShapeDtypeStruct((count, 2, *chunks[1:]), BF16),
-        ),
-        in_specs=[SMEM] + [VMEM] * 9,
-        out_specs=(VMEM,) * 2,
-        scratch_shapes=[
+            tap_space(KDIM, 2 * PLANE),
             tap_space(2, KDIM, 2 * PLANE),
+            sum_space(1),
+            plane_space(3),
             sum_space(2, 2),
             sum_space(2),
             plane_space(8),
@@ -660,11 +628,12 @@
             pltpu.VMEM((ROWS, 128), F32),
             pltpu.VMEM((9, 16, PLANE), BF16),
         ],
-        compiler_params=vmem(20),
-        cost_estimate=pl.CostEstimate(flops=2**32, bytes_accessed=2**22, transcendentals=0),
-        name="backward",
+        compiler_params=vmem(24),
+        cost_estimate=pl.CostEstimate(flops=2**33, bytes_accessed=2**23, transcendentals=2**18),
+        name="outer",
     )(
-        device, g_out, g_in, slope_out, slope_in, x_taps, x_pair, w2_back, keep_two, send_two,
+        device, outer, cot_planes, layer_mask, w1, w2, w2_back, *biases, taps, x_taps, one, two,
+        slope_in, g_in, part_two,
     )
     keep, send = pl.pallas_call(
         output_kernel,

time: 62 us -> 61.1 us (0.985)
  Pallas kernels: 18.7 us -> 17.8 us
    pallas_call x2 -> x1, Pallas kernels: 7.52 us -> 6.66 us  [local(): pl.pallas_call(outer_kernel, out_shape=(jax.ShapeDtypeStruct(halves, F32)...]
  transfers between devices with their start and end apart: 8 -> 8, of which waited for: 4 -> 4; matrix products, arithmetic and copies ran while one was open for 6% -> 7% of each run, Pallas kernels for 12% -> 12%
where the time goes in v11:
time: 61.1 us; the launch traced here: 60.7 us
  Pallas kernels  17.8 us (29%)
  blocking collectives  14.2 us (23%)
  waiting for transfers between devices  12.2 us (20%)
  starting transfers between devices  11.5 us (19%)
  other arithmetic  4.21 us (7%)
  between operations  0.77 us (1%)
    all_to_all x1, blocking collectives, shared_sum(): parts = lax.all_to_all(parts, both, 0, 0, axis_index_groups=groups)  14.2 us
    pallas_call x1, Pallas kernels, local(): pl.pallas_call(outer_kernel, out_shape=(jax.ShapeDtypeStruct(halves, F32)...  6.66 us
    all_to_all x1, waiting for transfers between devices, shared_sum(): copies = lax.all_to_all(copies, both, 0, 0, axis_index_groups=groups)  6.3 us
    pallas_call x1, Pallas kernels, local(): pl.pallas_call(inner_kernel, out_shape=(jax.ShapeDtypeStruct((4, KDIM, 2...  5.94 us
    ppermute x1, starting transfers between devices, shared_sum(): parts = (keep + lax.ppermute(send, 'space', swap).astype(F32)).astype(BF16)  4.03 us
    all_to_all x1, starting transfers between devices, shared_sum(): copies = lax.all_to_all(copies, both, 0, 0, axis_index_groups=groups)  3.49 us
    ppermute x1, waiting for transfers between devices, shared_sum(): moved = lax.ppermute(total, 'dp', [(v, v ^ step) for v in range(volumes)])  3.28 us
    ppermute x1, starting transfers between devices, shared_sum(): moved = lax.ppermute(total, 'dp', [(v, v ^ step) for v in range(volumes)])  2.66 us
  transfers between devices with their start and end apart: 8, of which 4 were waited for; matrix products, arithmetic and copies ran while one was open for 7% of the time, Pallas kernels for 12%

profile of v11, /device:TPU:0, one launch (start us, length us, event | category | flops | bytes accessed | tf_op | source)
XLA Modules:
  0.0 60.7 jit_solution(3454592519139189063)
XLA Ops:
  0.6 0.5 collective-permute-start
  1.1 0.1 collective-permute-start.1
  1.2 1.2 %pad_maximum_fusion.1.own_ref = bf16[8,96,512]{2,1,0:T(8,128)(2,1)S(1)} fusion(bf16[4,96,512]{2,1,0:T(8,128)(2,1)} %bitcast.18, bf16[4,96,512]{2,1,0:T(8,128)(2,1)} %bitcast.16), kind=kLoop, calls=%fused_computation.2 | loop fusion | flops 393216 | bytes 1572864 | tf_op jit(solution)/shard_map/concatenate | solution.py:542
  2.4 0.7 %pad_add_fusion.table = s32[27,1,32]{2,1,0:T(1,128)S(1)} fusion(s32[1,1,32]{2,1,0:T(1,128)} %bitcast.20, s32[26,1,32]{2,1,0:T(1,128)} %bitcast.19), kind=kLoop, calls=%fused_computation.4 | loop fusion | flops 864 | bytes 6912 | tf_op jit(solution)/shard_map/concatenate | solution.py:544
  3.2 1.3 %pad_maximum_fusion.weight_ref = bf16[192,2592]{1,0:T(8,128)(2,1)S(1)} fusion(bf16[96,2592]{1,0:T(8,128)(2,1)} %param.13, bf16[96,2592]{1,0:T(8,128)(2,1)} %param.12), kind=kLoop, calls=%fused_computation.1 | loop fusion | flops 1990656 | bytes 1990656 | tf_op jit(solution)/shard_map/concatenate | solution.py:541
  4.5 1.7 %layout.1 = (bf16[12,96,256]{2,1,0:T(8,128)(2,1)S(1)}, bf16[9,96,256]{2,1,0:T(8,128)(2,1)S(1)}, bf16[4,96,256]{2,1,0:T(8,128)(2,1)S(1)}, f32[3,8,256]{2,1,0:T(8,128)S(1)}) custom-call(s32[1]{0:T(128)} %bitcast.device, s32[27,1,32]{2,1,0:T(1,128)S(1)} %pad_add_fusion.table, bf16[8,96,512]{2,1,0:T(8,128)(2,1)S(1)} %pad_maximum_fusion.1.own_ref, ...), custom_call_target="tpu_custom_call" | custom-call | tf_op jit(solution)/shard_map/layout/pallas_call | solution.py:559
  6.2 0.7 %collective-permute-start.2 = (bf16[4,96,256]{2,1,0:T(8,128)(2,1)S(1)}, bf16[4,96,256]{2,1,0:T(8,128)(2,1)S(1)}, u32[]{:S(2)}, u32[]{:S(2)}) collective-permute-start(bf16[4,96,256]{2,1,0:T(8,128)(2,1)S(1)} %get-tuple-element.29), channel_id=1, source_target_pairs={{4,12},{8,16},{20,28},{12,4},{16,8},{28,20},{5,13},{9,17},{21,29},... | collective-permute-start | bytes 589832 | tf_op jit(solution)/shard_map/ppermute | solution.py:571
  6.9 5.9 %inner.1 = (bf16[4,896,512]{2,1,0:T(8,128)(2,1)S(1)}, bf16[5,896,512]{2,1,0:T(8,128)(2,1)S(1)}, f32[2,96,256]{2,1,0:T(8,128)S(1)}, f32[2,96,256]{2,1,0:T(8,128)S...) custom-call(s32[1]{0:T(128)} %bitcast.device, ...), custom_call_target="tpu_custom_call" | custom-call | flops 8589934592 | bytes 8388608 | tf_op jit(solution)/shard_map/inner/pallas_call | solution.py:574
  12.8 6.7 %outer.1 = (f32[8,2,128,128]{3,2,1,0:T(8,128)S(1)}, bf16[8,2,128,128]{3,2,1,0:T(8,128)(2,1)S(1)}, bf16[2,96,256]{2,1,0:T(8,128)(2,1)S(1)}) custom-call(s32[1]{0:T(128)} %bitcast.device, bf16[4,96,256]{2,1,0:T(8,128)(2,1)S(1)} %collective-permute-done.2.edge_ref, bf16[9,96,256]{2,1,0:T(8,128)(2,1)S(1)} %get-tuple-element.30.cot_ref, ...), custom_call_target="tpu_custom_call" | custom-call | flops 8589934592 | bytes 8388608 | tf_op jit(solution)/shard_map/outer/pallas_call | solution.py:607
  19.5 4.0 %collective-permute-start.4 = (bf16[8,2,128,128]{3,2,1,0:T(8,128)(2,1)S(1)}, bf16[8,2,128,128]{3,2,1,0:T(8,128)(2,1)S(1)}, u32[]{:S(2)}, u32[]{:S(2)}) collective-permute-start(bf16[8,2,128,128]{3,2,1,0:T(8,128)(2,1)S(1)} %get-tuple-element.48), channel_id=1, source_target_pairs={{0,4},{4,0},{8,12},{12,8},{16,20},{20,16},{24,28},{28,24},{1,5},{5... | collective-permute-start | bytes 1572872 | tf_op jit(solution)/shard_map/ppermute | solution.py:507
  23.5 1.5 %collective-permute-done.4 = bf16[8,2,128,128]{3,2,1,0:T(8,128)(2,1)S(1)} collective-permute-done((bf16[8,2,128,128]{3,2,1,0:T(8,128)(2,1)S(1)}, bf16[8,2,128,128]{3,2,1,0:T(8,128)(2,1)S(1)}, u32[]{:S(2)}, u32[]{:S(2)}) %collective-permute-start.4) | collective-permute-done | bytes 524320 | tf_op jit(solution)/shard_map/ppermute | solution.py:507
  25.1 0.1 add_convert_fusion
  25.2 14.2 %all_to_all.10 = bf16[8,2,128,128]{3,2,1,0:T(8,128)(2,1)S(1)} all-to-all(bf16[8,2,128,128]{3,2,1,0:T(8,128)(2,1)S(1)} %add_convert_fusion), channel_id=1, replica_groups={{0,8,16,24,1,9,17,25},{2,10,18,26,3,11,19,27},{4,12,20,28,5,13,21,29},{..., dimensions={0} | all-to-all | bytes 1048576 | tf_op jit(solution)/shard_map/all_to_all | solution.py:508
  39.4 0.1 reduce_sum.12.first_ref
  39.5 2.7 %collective-permute-start.5 = (bf16[2,128,128]{2,1,0:T(8,128)(2,1)S(1)}, bf16[2,128,128]{2,1,0:T(8,128)(2,1)S(1)}, u32[]{:S(2)}, u32[]{:S(2)}) collective-permute-start(bf16[2,128,128]{2,1,0:T(8,128)(2,1)S(1)} %reduce_sum.12.first_ref), channel_id=1, source_target_pairs={{0,2},{1,3},{2,0},{3,1},{4,6},{5,7},{6,4},{7,5},{8,10},{9,11},{10,... | collective-permute-start | bytes 196616 | tf_op jit(solution)/shard_map/ppermute | solution.py:512
  42.1 3.3 %collective-permute-done.5.second_ref = bf16[2,128,128]{2,1,0:T(8,128)(2,1)S(1)} collective-permute-done((bf16[2,128,128]{2,1,0:T(8,128)(2,1)S(1)}, bf16[2,128,128]{2,1,0:T(8,128)(2,1)S(1)}, u32[]{:S(2)}, u32[]{:S(2)}) %collective-permute-start.5) | collective-permute-done | bytes 65568 | tf_op jit(solution)/shard_map/ppermute | solution.py:512
  45.4 0.8 %copies.1 = bf16[8,2,128,128]{3,2,1,0:T(8,128)(2,1)} custom-call(bf16[2,128,128]{2,1,0:T(8,128)(2,1)S(1)} %reduce_sum.12.first_ref, bf16[2,128,128]{2,1,0:T(8,128)(2,1)S(1)} %collective-permute-done.5.second_ref), custom_call_target="tpu_custom_call" | custom-call | tf_op jit(solution)/shard_map/copies/pallas_call | solution.py:516
  46.3 3.5 %all-to-all-start.1 = ((bf16[8,2,128,128]{3,2,1,0:T(8,128)(2,1)}), bf16[8,2,128,128]{3,2,1,0:T(8,128)(2,1)S(1)}, u32[]{:S(2)}, u32[]{:S(2)}) async-start(bf16[8,2,128,128]{3,2,1,0:T(8,128)(2,1)} %copies.1), calls=%async_computation.1 | async-start | bytes 1048576 | tf_op jit(solution)/shard_map/all_to_all | solution.py:524
  49.8 1.2 %output.1 = (bf16[4,96,512]{2,1,0:T(8,128)(2,1)S(1)}, bf16[4,96,512]{2,1,0:T(8,128)(2,1)S(1)}) custom-call(s32[1]{0:T(128)} %bitcast.device, s32[27,1,32]{2,1,0:T(1,128)S(1)} %pad_add_fusion.table, bf16[2,96,256]{2,1,0:T(8,128)(2,1)S(1)} %get-tuple-element.43.first_ref, bf16[6,96,256]{2,1,0:T(8,128)(2,1)S(1)} %get-tuple-element.44.second_ref), custom_call_target="tpu_custom_call" | custom-call | flops 268435456 | bytes 2097152 | tf_op jit(solution)/shard_map/output/pallas_call | solution.py:638
  51.0 0.1 collective-permute-start.3
  51.1 6.3 %all-to-all-done.1.own_ref = bf16[8,2,128,128]{3,2,1,0:T(8,128)(2,1)S(1)} async-done(((bf16[8,2,128,128]{3,2,1,0:T(8,128)(2,1)}), bf16[8,2,128,128]{3,2,1,0:T(8,128)(2,1)S(1)}, u32[]{:S(2)}, u32[]{:S(2)}) %all-to-all-start.1) | async-done | bytes 524320 | tf_op jit(solution)/shard_map/all_to_all | solution.py:524
  57.4 0.8 %add_bitcast_fusion = bf16[1,4,96,512]{3,2,1,0:T(8,128)(2,1)} fusion(bf16[4,96,512]{2,1,0:T(8,128)(2,1)S(1)} %get-tuple-element.45, bf16[4,96,512]{2,1,0:T(8,128)(2,1)S(1)} %collective-permute-done.3), kind=kLoop, calls=%fused_computation.3 | loop fusion | flops 196608 | bytes 1179648 | tf_op jit(solution)/shard_map/broadcast_in_dim | solution.py:648
  58.2 1.1 %collective-permute-done.6.other_ref = bf16[8,2,128,128]{3,2,1,0:T(8,128)(2,1)S(1)} collective-permute-done((bf16[8,2,128,128]{3,2,1,0:T(8,128)(2,1)S(1)}, bf16[8,2,128,128]{3,2,1,0:T(8,128)(2,1)S(1)}, u32[]{:S(2)}, u32[]{:S(2)}) %collective-permute-start.6) | collective-permute-done | bytes 524320 | tf_op jit(solution)/shard_map/ppermute | solution.py:525
  59.3 1.5 %gather.1 = (f32[96,2592]{1,0:T(8,128)}, f32[96,2592]{1,0:T(8,128)}, f32[1,96]{1,0:T(1,128)}, f32[1,96]{1,0:T(1,128)}) custom-call(s32[1]{0:T(128)} %bitcast.device, bf16[8,2,128,128]{3,2,1,0:T(8,128)(2,1)S(1)} %all-to-all-done.1.own_ref, bf16[8,2,128,128]{3,2,1,0:T(8,128)(2,1)S(1)} %collective-permute-done.6.other_ref), custom_call_target="tpu_custom_call" | custom-call | tf_op jit(solution)/shard_map/gather/pallas_call | solution.py:652
  (9 shorter events, 0.0 us)
Async XLA Ops:
  0.6 3.8 %collective-permute-start = (bf16[4,96,512]{2,1,0:T(8,128)(2,1)}, bf16[4,96,512]{2,1,0:T(8,128)(2,1)S(1)}, u32[]{:S(2)}, u32[]{:S(2)}) collective-permute-start(bf16[4,96,512]{2,1,0:T(8,128)(2,1)} %bitcast.15), channel_id=1, source_target_pairs={{0,4},{4,0},{8,12},{12,8},{16,20},{20,16},{24,28},{28,24},{1,5},{5... | collective-permute-start | bytes 1179656 | tf_op jit(solution)/shard_map/ppermute | solution.py:538
  1.1 3.3 %collective-permute-start.1 = (bf16[4,96,512]{2,1,0:T(8,128)(2,1)}, bf16[4,96,512]{2,1,0:T(8,128)(2,1)S(1)}, u32[]{:S(2)}, u32[]{:S(2)}) collective-permute-start(bf16[4,96,512]{2,1,0:T(8,128)(2,1)} %bitcast.17), channel_id=1, source_target_pairs={{0,4},{4,0},{8,12},{12,8},{16,20},{20,16},{24,28},{28,24},{1,5},{5... | collective-permute-start | bytes 1179656 | tf_op jit(solution)/shard_map/ppermute | solution.py:539
  2.4 4.4 %copy-start = (f32[96]{0:T(128)S(1)}, f32[96]{0:T(128)}, u32[]{:S(2)}) copy-start(f32[96]{0:T(128)} %param.14) | copy-start | bytes 1156
  2.4 4.4 %copy-start.1 = (f32[96]{0:T(128)S(1)}, f32[96]{0:T(128)}, u32[]{:S(2)}) copy-start(f32[96]{0:T(128)} %param.15) | copy-start | bytes 1156
  6.2 6.7 %collective-permute-start.2 = (bf16[4,96,256]{2,1,0:T(8,128)(2,1)S(1)}, bf16[4,96,256]{2,1,0:T(8,128)(2,1)S(1)}, u32[]{:S(2)}, u32[]{:S(2)}) collective-permute-start(bf16[4,96,256]{2,1,0:T(8,128)(2,1)S(1)} %get-tuple-element.29), channel_id=1, source_target_pairs={{4,12},{8,16},{20,28},{12,4},{16,8},{28,20},{5,13},{9,17},{21,29},... | collective-permute-start | bytes 589832 | tf_op jit(solution)/shard_map/ppermute | solution.py:571
  19.5 5.6 %collective-permute-start.4 = (bf16[8,2,128,128]{3,2,1,0:T(8,128)(2,1)S(1)}, bf16[8,2,128,128]{3,2,1,0:T(8,128)(2,1)S(1)}, u32[]{:S(2)}, u32[]{:S(2)}) collective-permute-start(bf16[8,2,128,128]{3,2,1,0:T(8,128)(2,1)S(1)} %get-tuple-element.48), channel_id=1, source_target_pairs={{0,4},{4,0},{8,12},{12,8},{16,20},{20,16},{24,28},{28,24},{1,5},{5... | collective-permute-start | bytes 1572872 | tf_op jit(solution)/shard_map/ppermute | solution.py:507
  39.5 5.9 %collective-permute-start.5 = (bf16[2,128,128]{2,1,0:T(8,128)(2,1)S(1)}, bf16[2,128,128]{2,1,0:T(8,128)(2,1)S(1)}, u32[]{:S(2)}, u32[]{:S(2)}) collective-permute-start(bf16[2,128,128]{2,1,0:T(8,128)(2,1)S(1)} %reduce_sum.12.first_ref), channel_id=1, source_target_pairs={{0,2},{1,3},{2,0},{3,1},{4,6},{5,7},{6,4},{7,5},{8,10},{9,11},{10,... | collective-permute-start | bytes 196616 | tf_op jit(solution)/shard_map/ppermute | solution.py:512
  46.3 11.1 %all-to-all-start.1 = ((bf16[8,2,128,128]{3,2,1,0:T(8,128)(2,1)}), bf16[8,2,128,128]{3,2,1,0:T(8,128)(2,1)S(1)}, u32[]{:S(2)}, u32[]{:S(2)}) async-start(bf16[8,2,128,128]{3,2,1,0:T(8,128)(2,1)} %copies.1), calls=%async_computation.1 | async-start | bytes 1048576 | tf_op jit(solution)/shard_map/all_to_all | solution.py:524
  51.0 6.4 %collective-permute-start.3 = (bf16[4,96,512]{2,1,0:T(8,128)(2,1)S(1)}, bf16[4,96,512]{2,1,0:T(8,128)(2,1)S(1)}, u32[]{:S(2)}, u32[]{:S(2)}) collective-permute-start(bf16[4,96,512]{2,1,0:T(8,128)(2,1)S(1)} %get-tuple-element.46), channel_id=1, source_target_pairs={{0,4},{4,0},{8,12},{12,8},{16,20},{20,16},{24,28},{28,24},{1,5},{5... | collective-permute-start | bytes 1179656 | tf_op jit(solution)/shard_map/ppermute | solution.py:648
  57.4 1.9 %collective-permute-start.6 = (bf16[8,2,128,128]{3,2,1,0:T(8,128)(2,1)S(1)}, bf16[8,2,128,128]{3,2,1,0:T(8,128)(2,1)S(1)}, u32[]{:S(2)}, u32[]{:S(2)}) collective-permute-start(bf16[8,2,128,128]{3,2,1,0:T(8,128)(2,1)S(1)} %all-to-all-done.1.own_ref), channel_id=1, source_target_pairs={{0,4},{4,0},{8,12},{12,8},{16,20},{20,16},{24,28},{28,24},{1,5},{5... | collective-permute-start | bytes 1572872 | tf_op jit(solution)/shard_map/ppermute | solution.py:525

commit v12 on v11

--- a/solution.py
+++ b/solution.py
@@ -348,7 +348,7 @@
     def taps(p, rows):
         return taps_ref[p // 2, rows]
 
-    weight_products(total_ref, lambda q: g_ref[q - 2], (3, 5, 7), taps)
+    weight_products(total_ref, lambda q: g_ref[q - 2], (5, 7), taps)
 
 
 def outer_kernel(
@@ -416,6 +416,7 @@
             total[...] = total_ref[...] + part
         if j == 1:
             total[...] = total[...] + weight_part(pair_grads(grads, 1), taps_ref[0])
+            total[...] = total[...] + weight_part(pair_grads(grads, 3), taps_ref[1])
         if j == 2:
             write_tiles(flat, total, channels, even)
             split_tiles(keep_ref.at[:, 1], send_ref.at[:, 1], flat, device)
@@ -538,7 +539,6 @@
     pair_volume = lax.ppermute(volume, "space", swap)
     pair_cot = lax.ppermute(cotangent, "space", swap)
     biases = (bias_one[None], bias_two[None])
-    weights = jnp.concatenate([weight_one, weight_two], axis=0)
     own = jnp.concatenate([volume, cotangent], axis=0)
     device = (2 * me + ((me ^ (me >> 1)) & 1))[None]
     table = jnp.concatenate([neighbours.transpose(2, 0, 1), active[None]], axis=0)
@@ -568,7 +568,9 @@
         compiler_params=vmem(8),
         name="layout",
     )(device, table, own, pair_volume, pair_cot)
+    edge, weight_one, weight_two = lax.optimization_barrier((edge, weight_one, weight_two))
     outer = lax.ppermute(edge, "space", hop)
+    weights = jnp.concatenate([weight_one, weight_two], axis=0)
 
     rearranged = jax.ShapeDtypeStruct((3, channels, KDIM), BF16)
     taps, x_taps, one, two, slope_in, g_in, out_in, part_two, w1, w2, w2_back = pl.pallas_call(

time: 61.1 us -> 60.1 us (0.984)
  other arithmetic: 4.21 us -> 3.02 us
    concatenate x1, other arithmetic: 1.27 us -> 0.08 us  [local(): weights = jnp.concatenate([weight_one, weight_two], axis=0)]
  transfers between devices with their start and end apart: 8 -> 8, of which waited for: 4 -> 5; matrix products, arithmetic and copies ran while one was open for 7% -> 5% of each run, Pallas kernels for 12% -> 11%
where the time goes in v12:
time: 60.1 us; the launch traced here: 59.8 us
  Pallas kernels  17.6 us (29%)
  blocking collectives  14.6 us (24%)
  waiting for transfers between devices  12.3 us (20%)
  starting transfers between devices  11.5 us (19%)
  other arithmetic  3.02 us (5%)
  between operations  0.79 us (1%)
    all_to_all x1, blocking collectives, shared_sum(): parts = lax.all_to_all(parts, both, 0, 0, axis_index_groups=groups)  14.6 us
    pallas_call x1, Pallas kernels, local(): pl.pallas_call(outer_kernel, out_shape=(jax.ShapeDtypeStruct(halves, F32)...  6.97 us
    all_to_all x1, waiting for transfers between devices, shared_sum(): copies = lax.all_to_all(copies, both, 0, 0, axis_index_groups=groups)  6.3 us
    pallas_call x1, Pallas kernels, local(): pl.pallas_call(inner_kernel, out_shape=(jax.ShapeDtypeStruct((4, KDIM, 2...  5.42 us
    ppermute x1, starting transfers between devices, shared_sum(): parts = (keep + lax.ppermute(send, 'space', swap).astype(F32)).astype(BF16)  4.02 us
    all_to_all x1, starting transfers between devices, shared_sum(): copies = lax.all_to_all(copies, both, 0, 0, axis_index_groups=groups)  3.49 us
    ppermute x1, waiting for transfers between devices, shared_sum(): moved = lax.ppermute(total, 'dp', [(v, v ^ step) for v in range(volumes)])  3.28 us
    ppermute x1, starting transfers between devices, shared_sum(): moved = lax.ppermute(total, 'dp', [(v, v ^ step) for v in range(volumes)])  2.65 us
  transfers between devices with their start and end apart: 8, of which 5 were waited for; matrix products, arithmetic and copies ran while one was open for 5% of the time, Pallas kernels for 11%

profile of v12, /device:TPU:0, one launch (start us, length us, event | category | flops | bytes accessed | tf_op | source)
XLA Modules:
  0.0 59.8 jit_solution(14628931882625772365)
XLA Ops:
  0.7 0.5 collective-permute-start
  1.2 0.1 collective-permute-start.1
  1.3 0.7 %pad_add_fusion.table = s32[27,1,32]{2,1,0:T(1,128)S(1)} fusion(s32[1,1,32]{2,1,0:T(1,128)} %bitcast.20, s32[26,1,32]{2,1,0:T(1,128)} %bitcast.19), kind=kLoop, calls=%fused_computation.4 | loop fusion | flops 864 | bytes 6912 | tf_op jit(solution)/shard_map/concatenate | solution.py:544
  2.0 1.2 %pad_maximum_fusion.1.own_ref = bf16[8,96,512]{2,1,0:T(8,128)(2,1)S(1)} fusion(bf16[4,96,512]{2,1,0:T(8,128)(2,1)} %bitcast.18, bf16[4,96,512]{2,1,0:T(8,128)(2,1)} %bitcast.16), kind=kLoop, calls=%fused_computation.2 | loop fusion | flops 393216 | bytes 1572864 | tf_op jit(solution)/shard_map/concatenate | solution.py:542
  3.2 0.1 collective-permute-done.1.cot_pair_ref
  3.3 1.7 %layout.1 = (bf16[12,96,256]{2,1,0:T(8,128)(2,1)S(1)}, bf16[9,96,256]{2,1,0:T(8,128)(2,1)S(1)}, bf16[4,96,256]{2,1,0:T(8,128)(2,1)S(1)}, f32[3,8,256]{2,1,0:T(8,128)S(1)}) custom-call(s32[1]{0:T(128)} %bitcast.device, s32[27,1,32]{2,1,0:T(1,128)S(1)} %pad_add_fusion.table, bf16[8,96,512]{2,1,0:T(8,128)(2,1)S(1)} %pad_maximum_fusion.1.own_ref, ...), custom_call_target="tpu_custom_call" | custom-call | tf_op jit(solution)/shard_map/layout/pallas_call | solution.py:559
  5.0 0.7 %collective-permute-start.2 = (bf16[4,96,256]{2,1,0:T(8,128)(2,1)S(1)}, bf16[4,96,256]{2,1,0:T(8,128)(2,1)S(1)}, u32[]{:S(2)}, u32[]{:S(2)}) collective-permute-start(bf16[4,96,256]{2,1,0:T(8,128)(2,1)S(1)} %get-tuple-element.33), channel_id=1, source_target_pairs={{4,12},{8,16},{20,28},{12,4},{16,8},{28,20},{5,13},{9,17},{21,29},... | collective-permute-start | bytes 589832 | tf_op jit(solution)/shard_map/ppermute | solution.py:572
  5.7 0.1 pad_maximum_fusion.weight_ref
  5.8 5.4 %inner.1 = (bf16[4,896,512]{2,1,0:T(8,128)(2,1)S(1)}, bf16[5,896,512]{2,1,0:T(8,128)(2,1)S(1)}, f32[2,96,256]{2,1,0:T(8,128)S(1)}, f32[2,96,256]{2,1,0:T(8,128)S...) custom-call(s32[1]{0:T(128)} %bitcast.device, ...), custom_call_target="tpu_custom_call" | custom-call | flops 8589934592 | bytes 8388608 | tf_op jit(solution)/shard_map/inner/pallas_call | solution.py:576
  11.2 7.0 %outer.1 = (f32[8,2,128,128]{3,2,1,0:T(8,128)S(1)}, bf16[8,2,128,128]{3,2,1,0:T(8,128)(2,1)S(1)}, bf16[2,96,256]{2,1,0:T(8,128)(2,1)S(1)}) custom-call(s32[1]{0:T(128)} %bitcast.device, bf16[4,96,256]{2,1,0:T(8,128)(2,1)S(1)} %collective-permute-done.2.edge_ref, bf16[9,96,256]{2,1,0:T(8,128)(2,1)S(1)} %get-tuple-element.34.cot_ref, ...), custom_call_target="tpu_custom_call" | custom-call | flops 8589934592 | bytes 8388608 | tf_op jit(solution)/shard_map/outer/pallas_call | solution.py:609
  18.2 4.0 %collective-permute-start.4 = (bf16[8,2,128,128]{3,2,1,0:T(8,128)(2,1)S(1)}, bf16[8,2,128,128]{3,2,1,0:T(8,128)(2,1)S(1)}, u32[]{:S(2)}, u32[]{:S(2)}) collective-permute-start(bf16[8,2,128,128]{3,2,1,0:T(8,128)(2,1)S(1)} %get-tuple-element.54), channel_id=1, source_target_pairs={{0,4},{4,0},{8,12},{12,8},{16,20},{20,16},{24,28},{28,24},{1,5},{5... | collective-permute-start | bytes 1572872 | tf_op jit(solution)/shard_map/ppermute | solution.py:508
  22.2 1.5 %collective-permute-done.4 = bf16[8,2,128,128]{3,2,1,0:T(8,128)(2,1)S(1)} collective-permute-done((bf16[8,2,128,128]{3,2,1,0:T(8,128)(2,1)S(1)}, bf16[8,2,128,128]{3,2,1,0:T(8,128)(2,1)S(1)}, u32[]{:S(2)}, u32[]{:S(2)}) %collective-permute-start.4) | collective-permute-done | bytes 524320 | tf_op jit(solution)/shard_map/ppermute | solution.py:508
  23.7 0.1 add_convert_fusion
  23.9 14.6 %all_to_all.10 = bf16[8,2,128,128]{3,2,1,0:T(8,128)(2,1)S(1)} all-to-all(bf16[8,2,128,128]{3,2,1,0:T(8,128)(2,1)S(1)} %add_convert_fusion), channel_id=1, replica_groups={{0,8,16,24,1,9,17,25},{2,10,18,26,3,11,19,27},{4,12,20,28,5,13,21,29},{..., dimensions={0} | all-to-all | bytes 1048576 | tf_op jit(solution)/shard_map/all_to_all | solution.py:509
  38.5 0.1 reduce_sum.12.first_ref
  38.6 2.7 %collective-permute-start.5 = (bf16[2,128,128]{2,1,0:T(8,128)(2,1)S(1)}, bf16[2,128,128]{2,1,0:T(8,128)(2,1)S(1)}, u32[]{:S(2)}, u32[]{:S(2)}) collective-permute-start(bf16[2,128,128]{2,1,0:T(8,128)(2,1)S(1)} %reduce_sum.12.first_ref), channel_id=1, source_target_pairs={{0,2},{1,3},{2,0},{3,1},{4,6},{5,7},{6,4},{7,5},{8,10},{9,11},{10,... | collective-permute-start | bytes 196616 | tf_op jit(solution)/shard_map/ppermute | solution.py:513
  41.2 3.3 %collective-permute-done.5.second_ref = bf16[2,128,128]{2,1,0:T(8,128)(2,1)S(1)} collective-permute-done((bf16[2,128,128]{2,1,0:T(8,128)(2,1)S(1)}, bf16[2,128,128]{2,1,0:T(8,128)(2,1)S(1)}, u32[]{:S(2)}, u32[]{:S(2)}) %collective-permute-start.5) | collective-permute-done | bytes 65568 | tf_op jit(solution)/shard_map/ppermute | solution.py:513
  44.5 0.8 %copies.1 = bf16[8,2,128,128]{3,2,1,0:T(8,128)(2,1)} custom-call(bf16[2,128,128]{2,1,0:T(8,128)(2,1)S(1)} %reduce_sum.12.first_ref, bf16[2,128,128]{2,1,0:T(8,128)(2,1)S(1)} %collective-permute-done.5.second_ref), custom_call_target="tpu_custom_call" | custom-call | tf_op jit(solution)/shard_map/copies/pallas_call | solution.py:517
  45.4 3.5 %all-to-all-start.1 = ((bf16[8,2,128,128]{3,2,1,0:T(8,128)(2,1)}), bf16[8,2,128,128]{3,2,1,0:T(8,128)(2,1)S(1)}, u32[]{:S(2)}, u32[]{:S(2)}) async-start(bf16[8,2,128,128]{3,2,1,0:T(8,128)(2,1)} %copies.1), calls=%async_computation.1 | async-start | bytes 1048576 | tf_op jit(solution)/shard_map/all_to_all | solution.py:525
  48.9 1.2 %output.1 = (bf16[4,96,512]{2,1,0:T(8,128)(2,1)S(1)}, bf16[4,96,512]{2,1,0:T(8,128)(2,1)S(1)}) custom-call(s32[1]{0:T(128)} %bitcast.device, s32[27,1,32]{2,1,0:T(1,128)S(1)} %pad_add_fusion.table, bf16[2,96,256]{2,1,0:T(8,128)(2,1)S(1)} %get-tuple-element.49.first_ref, bf16[6,96,256]{2,1,0:T(8,128)(2,1)S(1)} %get-tuple-element.50.second_ref), custom_call_target="tpu_custom_call" | custom-call | flops 268435456 | bytes 2097152 | tf_op jit(solution)/shard_map/output/pallas_call | solution.py:640
  50.2 6.3 %all-to-all-done.1.own_ref = bf16[8,2,128,128]{3,2,1,0:T(8,128)(2,1)S(1)} async-done(((bf16[8,2,128,128]{3,2,1,0:T(8,128)(2,1)}), bf16[8,2,128,128]{3,2,1,0:T(8,128)(2,1)S(1)}, u32[]{:S(2)}, u32[]{:S(2)}) %all-to-all-start.1) | async-done | bytes 524320 | tf_op jit(solution)/shard_map/all_to_all | solution.py:525
  56.5 0.8 %add_bitcast_fusion = bf16[1,4,96,512]{3,2,1,0:T(8,128)(2,1)} fusion(bf16[4,96,512]{2,1,0:T(8,128)(2,1)S(1)} %get-tuple-element.51, bf16[4,96,512]{2,1,0:T(8,128)(2,1)S(1)} %collective-permute-done.3), kind=kLoop, calls=%fused_computation.3 | loop fusion | flops 196608 | bytes 1179648 | tf_op jit(solution)/shard_map/broadcast_in_dim | solution.py:650
  57.3 1.1 %collective-permute-done.6.other_ref = bf16[8,2,128,128]{3,2,1,0:T(8,128)(2,1)S(1)} collective-permute-done((bf16[8,2,128,128]{3,2,1,0:T(8,128)(2,1)S(1)}, bf16[8,2,128,128]{3,2,1,0:T(8,128)(2,1)S(1)}, u32[]{:S(2)}, u32[]{:S(2)}) %collective-permute-start.6) | collective-permute-done | bytes 524320 | tf_op jit(solution)/shard_map/ppermute | solution.py:526
  58.4 1.5 %gather.1 = (f32[96,2592]{1,0:T(8,128)}, f32[96,2592]{1,0:T(8,128)}, f32[1,96]{1,0:T(1,128)}, f32[1,96]{1,0:T(1,128)}) custom-call(s32[1]{0:T(128)} %bitcast.device, bf16[8,2,128,128]{3,2,1,0:T(8,128)(2,1)S(1)} %all-to-all-done.1.own_ref, bf16[8,2,128,128]{3,2,1,0:T(8,128)(2,1)S(1)} %collective-permute-done.6.other_ref), custom_call_target="tpu_custom_call" | custom-call | tf_op jit(solution)/shard_map/gather/pallas_call | solution.py:654
  (13 shorter events, 0.1 us)
Async XLA Ops:
  0.6 5.0 %copy-start.2 = (bf16[96,2592]{1,0:T(8,128)(2,1)S(1)}, bf16[96,2592]{1,0:T(8,128)(2,1)}, u32[]{:S(2)}) copy-start(bf16[96,2592]{1,0:T(8,128)(2,1)} %param.13) | copy-start | bytes 1492996
  0.6 5.0 %copy-start.3 = (bf16[96,2592]{1,0:T(8,128)(2,1)S(1)}, bf16[96,2592]{1,0:T(8,128)(2,1)}, u32[]{:S(2)}) copy-start(bf16[96,2592]{1,0:T(8,128)(2,1)} %param.12) | copy-start | bytes 1492996
  0.7 2.6 %collective-permute-start = (bf16[4,96,512]{2,1,0:T(8,128)(2,1)}, bf16[4,96,512]{2,1,0:T(8,128)(2,1)S(1)}, u32[]{:S(2)}, u32[]{:S(2)}) collective-permute-start(bf16[4,96,512]{2,1,0:T(8,128)(2,1)} %bitcast.15), channel_id=1, source_target_pairs={{0,4},{4,0},{8,12},{12,8},{16,20},{20,16},{24,28},{28,24},{1,5},{5... | collective-permute-start | bytes 1179656 | tf_op jit(solution)/shard_map/ppermute | solution.py:539
  1.2 2.1 %collective-permute-start.1 = (bf16[4,96,512]{2,1,0:T(8,128)(2,1)}, bf16[4,96,512]{2,1,0:T(8,128)(2,1)S(1)}, u32[]{:S(2)}, u32[]{:S(2)}) collective-permute-start(bf16[4,96,512]{2,1,0:T(8,128)(2,1)} %bitcast.17), channel_id=1, source_target_pairs={{0,4},{4,0},{8,12},{12,8},{16,20},{20,16},{24,28},{28,24},{1,5},{5... | collective-permute-start | bytes 1179656 | tf_op jit(solution)/shard_map/ppermute | solution.py:540
  3.2 2.6 %copy-start = (f32[96]{0:T(128)S(1)}, f32[96]{0:T(128)}, u32[]{:S(2)}) copy-start(f32[96]{0:T(128)} %param.14) | copy-start | bytes 1156
  3.2 2.6 %copy-start.1 = (f32[96]{0:T(128)S(1)}, f32[96]{0:T(128)}, u32[]{:S(2)}) copy-start(f32[96]{0:T(128)} %param.15) | copy-start | bytes 1156
  5.0 6.2 %collective-permute-start.2 = (bf16[4,96,256]{2,1,0:T(8,128)(2,1)S(1)}, bf16[4,96,256]{2,1,0:T(8,128)(2,1)S(1)}, u32[]{:S(2)}, u32[]{:S(2)}) collective-permute-start(bf16[4,96,256]{2,1,0:T(8,128)(2,1)S(1)} %get-tuple-element.33), channel_id=1, source_target_pairs={{4,12},{8,16},{20,28},{12,4},{16,8},{28,20},{5,13},{9,17},{21,29},... | collective-permute-start | bytes 589832 | tf_op jit(solution)/shard_map/ppermute | solution.py:572
  18.2 5.6 %collective-permute-start.4 = (bf16[8,2,128,128]{3,2,1,0:T(8,128)(2,1)S(1)}, bf16[8,2,128,128]{3,2,1,0:T(8,128)(2,1)S(1)}, u32[]{:S(2)}, u32[]{:S(2)}) collective-permute-start(bf16[8,2,128,128]{3,2,1,0:T(8,128)(2,1)S(1)} %get-tuple-element.54), channel_id=1, source_target_pairs={{0,4},{4,0},{8,12},{12,8},{16,20},{20,16},{24,28},{28,24},{1,5},{5... | collective-permute-start | bytes 1572872 | tf_op jit(solution)/shard_map/ppermute | solution.py:508
  38.6 5.9 %collective-permute-start.5 = (bf16[2,128,128]{2,1,0:T(8,128)(2,1)S(1)}, bf16[2,128,128]{2,1,0:T(8,128)(2,1)S(1)}, u32[]{:S(2)}, u32[]{:S(2)}) collective-permute-start(bf16[2,128,128]{2,1,0:T(8,128)(2,1)S(1)} %reduce_sum.12.first_ref), channel_id=1, source_target_pairs={{0,2},{1,3},{2,0},{3,1},{4,6},{5,7},{6,4},{7,5},{8,10},{9,11},{10,... | collective-permute-start | bytes 196616 | tf_op jit(solution)/shard_map/ppermute | solution.py:513
  45.4 11.1 %all-to-all-start.1 = ((bf16[8,2,128,128]{3,2,1,0:T(8,128)(2,1)}), bf16[8,2,128,128]{3,2,1,0:T(8,128)(2,1)S(1)}, u32[]{:S(2)}, u32[]{:S(2)}) async-start(bf16[8,2,128,128]{3,2,1,0:T(8,128)(2,1)} %copies.1), calls=%async_computation.1 | async-start | bytes 1048576 | tf_op jit(solution)/shard_map/all_to_all | solution.py:525
  50.1 6.4 %collective-permute-start.3 = (bf16[4,96,512]{2,1,0:T(8,128)(2,1)S(1)}, bf16[4,96,512]{2,1,0:T(8,128)(2,1)S(1)}, u32[]{:S(2)}, u32[]{:S(2)}) collective-permute-start(bf16[4,96,512]{2,1,0:T(8,128)(2,1)S(1)} %get-tuple-element.52), channel_id=1, source_target_pairs={{0,4},{4,0},{8,12},{12,8},{16,20},{20,16},{24,28},{28,24},{1,5},{5... | collective-permute-start | bytes 1179656 | tf_op jit(solution)/shard_map/ppermute | solution.py:650
  56.5 1.9 %collective-permute-start.6 = (bf16[8,2,128,128]{3,2,1,0:T(8,128)(2,1)S(1)}, bf16[8,2,128,128]{3,2,1,0:T(8,128)(2,1)S(1)}, u32[]{:S(2)}, u32[]{:S(2)}) collective-permute-start(bf16[8,2,128,128]{3,2,1,0:T(8,128)(2,1)S(1)} %all-to-all-done.1.own_ref), channel_id=1, source_target_pairs={{0,4},{4,0},{8,12},{12,8},{16,20},{20,16},{24,28},{28,24},{1,5},{5... | collective-permute-start | bytes 1572872 | tf_op jit(solution)/shard_map/ppermute | solution.py:526
